TPU v7x, 32 devices: a whole 2x2x4 slice. The times are simulated.
32 devices in a mesh: groups: 2 (over y), space: 4 (over z), feat: 2 (over x), edge: 2 (over core).
Axes of the slice: x: 2, y: 2, z: 4, core: 2. Of those that a mesh axis runs over, the one named last changes fastest.
Arguments:
- grid_latent: bfloat16 [32768, 512], P(('groups', 'space', 'edge'), 'feat'), parts along dimension 0, may hold values from -6 to 6
- enc_weight: bfloat16 [512, 512], P(None, 'feat'), may hold values from -0.25 to 0.25
- mesh_latent: bfloat16 [10240, 512], P(('groups', 'space', 'edge'), 'feat'), parts along dimension 0, may hold values from -6 to 6
- g2m_src: int32 [16, 7, 256], P(('groups', 'space', 'edge')), parts along dimension 0, may hold values from 0 to 2047
- g2m_dst: int32 [16, 7, 256], P(('groups', 'space', 'edge')), parts along dimension 0, may hold values from 0 to 640, as said below
- g2m_coef: float32 [16, 7, 256], P(('groups', 'space', 'edge')), parts along dimension 0, may hold values from 0.2 to 0.6
- src_weights: bfloat16 [2, 512, 512], P(None, None, 'feat'), may hold values from -0.25 to 0.25
- dst_weights: bfloat16 [2, 512, 512], P(None, None, 'feat'), may hold values from -0.25 to 0.25
- halo_send: int32 [16, 6, 64], P(('groups', 'space', 'edge')), parts along dimension 0, may hold values from 0 to 639
- m2m_src: int32 [16, 5120], P(('groups', 'space', 'edge')), parts along dimension 0, may hold values from 0 to 1023, as said below
- m2m_dst: int32 [16, 5120], P(('groups', 'space', 'edge')), parts along dimension 0, may hold values from 0 to 639
- m2m_coef: float32 [16, 5120], P(('groups', 'space', 'edge')), parts along dimension 0, may hold values from 0.15 to 0.5
Outputs:
- mesh_state: bfloat16 [10240, 512], P(('groups', 'space', 'edge'), 'feat'), parts along dimension 0
There are 2 independent parts, one for each index of `groups`. A program takes and returns all parts, laid end to end along the dimension named above; an argument that names none is the same for every part. Nothing has to cross between parts.
Inputs may be any that keep to these rules, and one draw needn't show every extreme that they name: `g2m_dst`: block j of region half s goes to owner s + j - 3. In each block the used slots come first and hold local mesh rows of that owner; the others hold 640. Blocks whose owner lies outside the region halves hold only 640; every other block has at least one used slot, the own block (3) is full, and some owner receives 256 used slots from each of its 7 senders. `m2m_src`: A listed block whose region half p lies outside the region halves is never named; every other value from 640 up appears in each region half's row.
All inputs are finite; a program needn't handle non-finite values.
Results may differ from a plain program's by a relative error of at most 0.012.
Values may be sent and summed in bfloat16 or wider, within the bound.
No kernel may reach another device: no remote copies, remote signals or barrier semaphores. Data moves between devices by JAX's collectives and lax.ppermute only.
A program may use at most 128 MiB of HBM per device.

v0:
```python
import math

import jax
import jax.numpy as jnp
from jax import lax
from jax.sharding import PartitionSpec as P


def passed_along(value, axis, steps):
    count = lax.axis_size(axis)
    first, last = (max(0, -steps), min(count, count - steps))
    return lax.ppermute(value, axis, [(source, source + steps) for source in range(first, last)])


def segment_total(values, targets, count):
    length = values.shape[0]
    width = values.shape[1]
    block = math.gcd(length, 1024)
    turns = length // block
    blocked_values = values.reshape(turns, block, width)
    blocked_targets = targets.reshape(turns, block)
    node_ids = lax.iota(jnp.int32, count)

    def accumulate(total, pair):
        piece_values, piece_targets = pair
        onehot = (node_ids[:, None] == piece_targets[None, :]).astype(jnp.bfloat16)
        return (total + jnp.dot(onehot, piece_values, preferred_element_type=jnp.float32), None)

    start_total = jnp.zeros((count, width), jnp.float32)
    result, unused = lax.scan(accumulate, start_total, (blocked_values, blocked_targets))
    return result


def pick_rows(table, indices):
    length = indices.shape[0]
    width = table.shape[1]
    block = math.gcd(length, 512)
    turns = length // block
    row_ids = lax.iota(jnp.int32, table.shape[0])

    def select(carry, piece_indices):
        onehot = (piece_indices[:, None] == row_ids[None, :]).astype(jnp.bfloat16)
        return (carry, jnp.dot(onehot, table, preferred_element_type=jnp.float32))

    unused, picked = lax.scan(select, 0, indices.reshape(turns, block))
    return picked.reshape(length, width)


def pick_float_rows(table, indices):
    width = table.shape[1]
    upper = table.astype(jnp.bfloat16)
    lower = (table - upper.astype(jnp.float32)).astype(jnp.bfloat16)
    picked = pick_rows(jnp.concatenate([upper, lower], axis=1), indices)
    return picked[:, :width] + picked[:, width:]


def on_device(
    grid_latent,
    enc_weight,
    mesh_latent,
    g2m_src,
    g2m_dst,
    g2m_coef,
    src_weights,
    dst_weights,
    halo_send,
    m2m_src,
    m2m_dst,
    m2m_coef,
):
    mesh_rows = mesh_latent.shape[0]
    channels = grid_latent.shape[1]
    block_count = g2m_src.shape[1]
    capacity = g2m_src.shape[2]
    reach = (block_count - 1) // 2
    link_count = halo_send.shape[1]
    listed_count = halo_send.shape[2]
    projected = jnp.dot(
        lax.all_gather(grid_latent, "feat", axis=1, tiled=True),
        enc_weight,
        preferred_element_type=jnp.float32,
    )
    picked = pick_float_rows(projected, g2m_src[0].reshape(-1))
    edge_scale = g2m_coef[0].reshape(-1, 1)
    encoded = (
        (edge_scale * jax.nn.silu(picked))
        .astype(jnp.bfloat16)
        .reshape(block_count, capacity, channels)
    )
    targets = g2m_dst[0]
    arrived_list = []
    target_list = []
    for position in range(block_count):
        offset = position - reach
        if offset == 0:
            values_here, targets_here = (encoded[position], targets[position])
        else:
            values_here, targets_here = passed_along(
                (encoded[position], targets[position]), ("space", "edge"), offset
            )
        arrived_list.append(values_here)
        target_list.append(targets_here)
    arrived = jnp.stack(arrived_list, axis=0)
    arrived_targets = jnp.stack(target_list, axis=0)
    gathered_in = segment_total(
        arrived.reshape(-1, channels), arrived_targets.reshape(-1), mesh_rows
    )
    state = (mesh_latent.astype(jnp.float32) + gathered_in).astype(jnp.bfloat16)
    senders = m2m_src[0]
    receivers = m2m_dst[0]
    mesh_scale = m2m_coef[0].reshape(-1, 1)
    listed_rows = halo_send[0].reshape(-1)
    half_links = link_count // 2
    for layer in range(src_weights.shape[0]):
        sender_weight = src_weights[layer]
        receiver_weight = dst_weights[layer]
        piece = lax.all_gather(state, "feat", axis=1, tiled=True)
        sender_full = jnp.dot(piece, sender_weight, preferred_element_type=jnp.float32)
        receiver = jnp.dot(piece, receiver_weight, preferred_element_type=jnp.float32)
        sender = sender_full.astype(jnp.bfloat16)
        outgoing = (
            pick_rows(sender, listed_rows)
            .astype(jnp.bfloat16)
            .reshape(link_count, listed_count, channels)
        )
        received = []
        for position in range(link_count):
            offset = position - half_links if position < half_links else position - half_links + 1
            received.append(passed_along(outgoing[position], ("space", "edge"), offset))
        extended = jnp.concatenate([sender] + received, axis=0)
        from_rows = pick_rows(extended, senders)
        to_rows = pick_float_rows(receiver, receivers)
        message = (mesh_scale * jax.nn.silu(from_rows + to_rows)).astype(jnp.bfloat16)
        update = segment_total(message, receivers, mesh_rows)
        state = (state.astype(jnp.float32) + update).astype(jnp.bfloat16)
    return state


def solution(mesh):
    placed = (
        P(("groups", "space", "edge"), "feat"),
        P(None, "feat"),
        P(("groups", "space", "edge"), "feat"),
        P(("groups", "space", "edge"), None, None),
        P(("groups", "space", "edge"), None, None),
        P(("groups", "space", "edge"), None, None),
        P(None, None, "feat"),
        P(None, None, "feat"),
        P(("groups", "space", "edge"), None, None),
        P(("groups", "space", "edge"), None),
        P(("groups", "space", "edge"), None),
        P(("groups", "space", "edge"), None),
    )
    return jax.shard_map(
        on_device,
        mesh=mesh,
        in_specs=placed,
        out_specs=P(("groups", "space", "edge"), "feat"),
        check_vma=False,
    )
```

profile of v0, /device:TPU:0, one launch (start us, length us, event | category | flops | bytes accessed | tf_op | source)
XLA Modules:
  0.0 304.4 jit_solution(14960033935131076483)
XLA Ops:
  8.7 36.0 %all-gather.2.cloned.1.call-done = bf16[2048,512]{1,0:T(8,128)(2,1)} async-done(((bf16[2048,256]{1,0:T(8,128)(2,1)}), bf16[2048,512]{1,0:T(8,128)(2,1)}) %all-gather.2.cloned.1.call-update) | async-done | bytes 2097168 | tf_op jit(solution)/shard_map/all_gather | solution.py:79
  44.7 2.3 subtract_convert_fusion
  47.2 2.5 copy.13
  49.7 22.1 %while.110 = (s32[]{:T(128)}, f32[7,256,512]{2,1,0:T(8,128)}, s32[7,256]{1,0:T(8,128)S(1)}, bf16[2048,512]{1,0:T(8,128)(2,1)}, s32[]{:T(128)}) while((s32[]{:T(128)}, f32[7,256,512]{2,1,0:T(8,128)}, s32[7,256]{1,0:T(8,128)S(1)}, bf16[2048,512]{1,0:T(8,128)(2,1)}, s32[]{:T(128)}) %tuple.234), condition=%wide.region_1.2_spmd.clone, body=%wide.region_0.1_spmd.clone.sunk | while | flops 537395200 | bytes 2625089 | solution.py:45
  49.8 3.1 %fusion.110 = f32[7,256,512]{2,1,0:T(8,128)} fusion(f32[7,256,512]{2,1,0:T(8,128)} %get-tuple-element.789, s32[]{:T(128)} %get-tuple-element.788, bf16[2048,512]{1,0:T(8,128)(2,1)} %get-tuple-element.796, s32[256]{0:T(256)S(1)} %bitcast.203), kind=kOutput, calls=%fused_computation.13.clone.1 | convolution fusion | flops 537395200 | bytes 2622976 | tf_op jit(solution)/shard_map/while/body/eval_jaxpr/dot_general | solution.py:43
  52.9 3.2 %fusion.110 = f32[7,256,512]{2,1,0:T(8,128)} fusion(f32[7,256,512]{2,1,0:T(8,128)} %get-tuple-element.789, s32[]{:T(128)} %get-tuple-element.788, bf16[2048,512]{1,0:T(8,128)(2,1)} %get-tuple-element.796, s32[256]{0:T(256)S(1)} %bitcast.203), kind=kOutput, calls=%fused_computation.13.clone.1 | convolution fusion | flops 537395200 | bytes 2622976 | tf_op jit(solution)/shard_map/while/body/eval_jaxpr/dot_general | solution.py:43
  56.1 3.2 %fusion.110 = f32[7,256,512]{2,1,0:T(8,128)} fusion(f32[7,256,512]{2,1,0:T(8,128)} %get-tuple-element.789, s32[]{:T(128)} %get-tuple-element.788, bf16[2048,512]{1,0:T(8,128)(2,1)} %get-tuple-element.796, s32[256]{0:T(256)S(1)} %bitcast.203), kind=kOutput, calls=%fused_computation.13.clone.1 | convolution fusion | flops 537395200 | bytes 2622976 | tf_op jit(solution)/shard_map/while/body/eval_jaxpr/dot_general | solution.py:43
  59.2 3.1 %fusion.110 = f32[7,256,512]{2,1,0:T(8,128)} fusion(f32[7,256,512]{2,1,0:T(8,128)} %get-tuple-element.789, s32[]{:T(128)} %get-tuple-element.788, bf16[2048,512]{1,0:T(8,128)(2,1)} %get-tuple-element.796, s32[256]{0:T(256)S(1)} %bitcast.203), kind=kOutput, calls=%fused_computation.13.clone.1 | convolution fusion | flops 537395200 | bytes 2622976 | tf_op jit(solution)/shard_map/while/body/eval_jaxpr/dot_general | solution.py:43
  62.4 3.2 %fusion.110 = f32[7,256,512]{2,1,0:T(8,128)} fusion(f32[7,256,512]{2,1,0:T(8,128)} %get-tuple-element.789, s32[]{:T(128)} %get-tuple-element.788, bf16[2048,512]{1,0:T(8,128)(2,1)} %get-tuple-element.796, s32[256]{0:T(256)S(1)} %bitcast.203), kind=kOutput, calls=%fused_computation.13.clone.1 | convolution fusion | flops 537395200 | bytes 2622976 | tf_op jit(solution)/shard_map/while/body/eval_jaxpr/dot_general | solution.py:43
  65.5 3.1 %fusion.110 = f32[7,256,512]{2,1,0:T(8,128)} fusion(f32[7,256,512]{2,1,0:T(8,128)} %get-tuple-element.789, s32[]{:T(128)} %get-tuple-element.788, bf16[2048,512]{1,0:T(8,128)(2,1)} %get-tuple-element.796, s32[256]{0:T(256)S(1)} %bitcast.203), kind=kOutput, calls=%fused_computation.13.clone.1 | convolution fusion | flops 537395200 | bytes 2622976 | tf_op jit(solution)/shard_map/while/body/eval_jaxpr/dot_general | solution.py:43
  68.7 3.1 %fusion.110 = f32[7,256,512]{2,1,0:T(8,128)} fusion(f32[7,256,512]{2,1,0:T(8,128)} %get-tuple-element.789, s32[]{:T(128)} %get-tuple-element.788, bf16[2048,512]{1,0:T(8,128)(2,1)} %get-tuple-element.796, s32[256]{0:T(256)S(1)} %bitcast.203), kind=kOutput, calls=%fused_computation.13.clone.1 | convolution fusion | flops 537395200 | bytes 2622976 | tf_op jit(solution)/shard_map/while/body/eval_jaxpr/dot_general | solution.py:43
  71.8 2.6 multiply_convert_fusion.2
  77.9 3.4 %collective-permute-start.4 = (s32[256]{0:T(256)S(1)}, s32[256]{0:T(256)S(1)}, u32[]{:S(2)}, u32[]{:S(2)}) collective-permute-start(s32[256]{0:T(256)S(1)} %bitcast.209), channel_id=1, source_target_pairs={{0,4},{1,5},{4,8},{5,9},{8,12},{9,13},{2,6},{3,7},{6,10},{7,11},{1... | collective-permute-start | bytes 3080 | tf_op jit(solution)/shard_map/ppermute | solution.py:12
  81.3 4.0 %collective-permute-start.5 = (s32[256]{0:T(256)S(1)}, s32[256]{0:T(256)S(1)}, u32[]{:S(2)}, u32[]{:S(2)}) collective-permute-start(s32[256]{0:T(256)S(1)} %bitcast.208), channel_id=1, source_target_pairs={{0,5},{1,8},{4,9},{5,12},{8,13},{2,7},{3,10},{6,11},{7,14},{10,15}... | collective-permute-start | bytes 3080 | tf_op jit(solution)/shard_map/ppermute | solution.py:12
  87.9 5.0 %collective-permute-start.3 = (s32[256]{0:T(256)S(1)}, s32[256]{0:T(256)S(1)}, u32[]{:S(2)}, u32[]{:S(2)}) collective-permute-start(s32[256]{0:T(256)S(1)} %bitcast.205), channel_id=1, source_target_pairs={{0,1},{1,4},{4,5},{5,8},{8,9},{9,12},{12,13},{2,3},{3,6},{6,7},{7,... | collective-permute-start | bytes 3080 | tf_op jit(solution)/shard_map/ppermute | solution.py:12
  97.8 4.3 %collective-permute-start.9 = (bf16[256,256]{1,0:T(8,128)(2,1)}, bf16[256,256]{1,0:T(8,128)(2,1)S(1)}, u32[]{:S(2)}, u32[]{:S(2)}) collective-permute-start(bf16[256,256]{1,0:T(8,128)(2,1)} %get-tuple-element.506), channel_id=1, source_target_pairs={{0,1},{1,4},{4,5},{5,8},{8,9},{9,12},{12,13},{2,3},{3,6},{6,7},{7,... | collective-permute-start | bytes 393224 | tf_op jit(solution)/shard_map/ppermute | solution.py:12
  102.1 4.9 %collective-permute-start.10 = (bf16[256,256]{1,0:T(8,128)(2,1)}, bf16[256,256]{1,0:T(8,128)(2,1)S(1)}, u32[]{:S(2)}, u32[]{:S(2)}) collective-permute-start(bf16[256,256]{1,0:T(8,128)(2,1)} %get-tuple-element.505), channel_id=1, source_target_pairs={{0,4},{1,5},{4,8},{5,9},{8,12},{9,13},{2,6},{3,7},{6,10},{7,11},{1... | collective-permute-start | bytes 393224 | tf_op jit(solution)/shard_map/ppermute | solution.py:12
  107.7 4.7 %collective-permute-start.11 = (bf16[256,256]{1,0:T(8,128)(2,1)}, bf16[256,256]{1,0:T(8,128)(2,1)S(1)}, u32[]{:S(2)}, u32[]{:S(2)}) collective-permute-start(bf16[256,256]{1,0:T(8,128)(2,1)} %get-tuple-element.504), channel_id=1, source_target_pairs={{0,5},{1,8},{4,9},{5,12},{8,13},{2,7},{3,10},{6,11},{7,14},{10,15}... | collective-permute-start | bytes 393224 | tf_op jit(solution)/shard_map/ppermute | solution.py:12
  113.4 2.6 collective-permute-done.11
  116.0 2.6 while.117
  118.7 10.0 %all_gather.10 = bf16[640,512]{1,0:T(8,128)(2,1)S(1)} all-gather(bf16[640,256]{1,0:T(8,128)(2,1)S(1)} %add_convert_fusion.2), channel_id=1, replica_groups=mesh['groups'=2,'space'=4,'feat'=2,'edge'=2] {'feat'}, dimensions={1}, use_global_device_ids=true | all-gather | bytes 983040 | tf_op jit(solution)/shard_map/all_gather | solution.py:117
  128.7 2.0 constant_dynamic-update-slice_fusion.6
  135.6 3.0 collective-permute-start.15
  138.6 5.1 %collective-permute-start.16 = (bf16[64,256]{1,0:T(8,128)(2,1)S(1)}, bf16[64,256]{1,0:T(8,128)(2,1)S(1)}, u32[]{:S(2)}, u32[]{:S(2)}) collective-permute-start(bf16[64,256]{1,0:T(8,128)(2,1)S(1)} %get-tuple-element.517), channel_id=1, source_target_pairs={{0,4},{1,5},{4,8},{5,9},{8,12},{9,13},{2,6},{3,7},{6,10},{7,11},{1... | collective-permute-start | bytes 98312 | tf_op jit(solution)/shard_map/ppermute | solution.py:12
  144.5 5.4 %broadcast.30.clone = f32[10,512,512]{2,1,0:T(8,128)} broadcast(f32[]{:T(128)} %constant.92.clone.1), dimensions={} | broadcast | bytes 10485764 | tf_op jit(solution)/shard_map/broadcast.8
  149.9 16.2 %while.113 = (s32[]{:T(128)}, f32[10,512,512]{2,1,0:T(8,128)}, s32[10,512]{1,0:T(8,128)S(1)}, bf16[640,512]{1,0:T(8,128)(2,1)S(1)}, s32[]{:T(128)}) while((s32[]{:T(128)}, f32[10,512,512]{2,1,0:T(8,128)}, s32[10,512]{1,0:T(8,128)S(1)}, bf16[640,512]{1,0:T(8,128)(2,1)S(1)}, s32[]{:T(128)}) %tuple.203), condition=%wide.region_9.10_spmd.clone, body=%wide.region_8.9_spmd.clone.sunk | while | flops 335872000 | bytes 1710657 | solution.py:45
  166.0 5.8 %collective-permute-start.17 = (bf16[64,256]{1,0:T(8,128)(2,1)S(1)}, bf16[64,256]{1,0:T(8,128)(2,1)S(1)}, u32[]{:S(2)}, u32[]{:S(2)}) collective-permute-start(bf16[64,256]{1,0:T(8,128)(2,1)S(1)} %get-tuple-element.516), channel_id=1, source_target_pairs={{0,5},{1,8},{4,9},{5,12},{8,13},{2,7},{3,10},{6,11},{7,14},{10,15}... | collective-permute-start | bytes 98312 | tf_op jit(solution)/shard_map/ppermute | solution.py:12
  173.4 2.7 broadcast.28.clone
  176.2 13.2 %while.112 = (s32[]{:T(128)}, f32[10,512,256]{2,1,0:T(8,128)}, s32[10,512]{1,0:T(8,128)S(1)}, bf16[1024,256]{1,0:T(8,128)(2,1)S(1)}, s32[]{:T(128)}) while((s32[]{:T(128)}, f32[10,512,256]{2,1,0:T(8,128)}, s32[10,512]{1,0:T(8,128)S(1)}, bf16[1024,256]{1,0:T(8,128)(2,1)S(1)}, s32[]{:T(128)}) %tuple.209), condition=%wide.region_7.8_spmd.clone, body=%wide.region_6.7_spmd.clone.sunk | while | flops 268959744 | bytes 1055297 | solution.py:45
  189.4 8.0 %multiply_convert_fusion.1 = bf16[5120,256]{1,0:T(8,128)(2,1)} fusion(f32[5120,512]{1,0:T(8,128)} %bitcast.186, f32[10,512,256]{2,1,0:T(8,128)} %get-tuple-element.278, f32[5120]{0:T(1024)S(1)} %bitcast.196), kind=kLoop, calls=%fused_computation.78 | loop fusion | flops 10485760 | bytes 18370560 | tf_op jit(solution)/shard_map/convert_element_type | solution.py:133
  197.5 8.7 %while.118 = (s32[]{:T(128)}, f32[640,256]{1,0:T(8,128)S(1)}, s32[5,1024]{1,0:T(8,128)S(1)}, bf16[5,1024,256]{2,1,0:T(8,128)(2,1)}, s32[]{:T(128)}, /*index=5*/s32[]{:T(128)}) while((s32[]{:T(128)}, f32[640,256]{1,0:T(8,128)S(1)}, s32[5,1024]{1,0:T(8,128)S(1)}, bf16[5,1024,256]{2,1,0:T(8,128)(2,1)}, s32[]{:T(128)}, ...), condition=%wide.region_11.12_spmd.clone, body=%wide.region_10.11_spmd.clone.sunk | while | flops 336527360 | bytes 1847891 | solution.py:30
  197.5 1.7 fusion.127
  202.7 1.7 fusion.127
  206.3 9.8 %all_gather.11 = bf16[640,512]{1,0:T(8,128)(2,1)S(1)} all-gather(bf16[640,256]{1,0:T(8,128)(2,1)S(1)} %add_convert_fusion.1), channel_id=1, replica_groups=mesh['groups'=2,'space'=4,'feat'=2,'edge'=2] {'feat'}, dimensions={1}, use_global_device_ids=true | all-gather | bytes 983040 | tf_op jit(solution)/shard_map/all_gather | solution.py:117
  221.7 3.0 collective-permute-start.21
  224.7 5.0 %collective-permute-start.22 = (bf16[64,256]{1,0:T(8,128)(2,1)S(1)}, bf16[64,256]{1,0:T(8,128)(2,1)S(1)}, u32[]{:S(2)}, u32[]{:S(2)}) collective-permute-start(bf16[64,256]{1,0:T(8,128)(2,1)S(1)} %get-tuple-element.511), channel_id=1, source_target_pairs={{0,4},{1,5},{4,8},{5,9},{8,12},{9,13},{2,6},{3,7},{6,10},{7,11},{1... | collective-permute-start | bytes 98312 | tf_op jit(solution)/shard_map/ppermute | solution.py:12
  230.1 5.4 %broadcast.30 = f32[10,512,512]{2,1,0:T(8,128)} broadcast(f32[]{:T(128)} %constant.92.clone.1), dimensions={} | broadcast | bytes 10485764 | tf_op jit(solution)/shard_map/broadcast.8
  235.4 16.2 %while.116 = (s32[]{:T(128)}, f32[10,512,512]{2,1,0:T(8,128)}, s32[10,512]{1,0:T(8,128)S(1)}, bf16[640,512]{1,0:T(8,128)(2,1)S(1)}, s32[]{:T(128)}) while((s32[]{:T(128)}, f32[10,512,512]{2,1,0:T(8,128)}, s32[10,512]{1,0:T(8,128)S(1)}, bf16[640,512]{1,0:T(8,128)(2,1)S(1)}, s32[]{:T(128)}) %tuple.233), condition=%wide.region_17.18_spmd.clone, body=%wide.region_16.17_spmd.clone.sunk | while | flops 335872000 | bytes 1710657 | solution.py:45
  251.6 4.7 %collective-permute-start.23 = (bf16[64,256]{1,0:T(8,128)(2,1)S(1)}, bf16[64,256]{1,0:T(8,128)(2,1)S(1)}, u32[]{:S(2)}, u32[]{:S(2)}) collective-permute-start(bf16[64,256]{1,0:T(8,128)(2,1)S(1)} %get-tuple-element.510), channel_id=1, source_target_pairs={{0,5},{1,8},{4,9},{5,12},{8,13},{2,7},{3,10},{6,11},{7,14},{10,15}... | collective-permute-start | bytes 98312 | tf_op jit(solution)/shard_map/ppermute | solution.py:12
  257.9 2.7 broadcast.28
  260.6 13.2 %while.115 = (s32[]{:T(128)}, f32[10,512,256]{2,1,0:T(8,128)}, s32[10,512]{1,0:T(8,128)S(1)}, bf16[1024,256]{1,0:T(8,128)(2,1)S(1)}, s32[]{:T(128)}) while((s32[]{:T(128)}, f32[10,512,256]{2,1,0:T(8,128)}, s32[10,512]{1,0:T(8,128)S(1)}, bf16[1024,256]{1,0:T(8,128)(2,1)S(1)}, s32[]{:T(128)}) %tuple.232), condition=%wide.region_15.16_spmd.clone, body=%wide.region_14.15_spmd.clone.sunk | while | flops 268959744 | bytes 1055297 | solution.py:45
  273.8 6.7 %multiply_convert_fusion = bf16[5120,256]{1,0:T(8,128)(2,1)S(1)} fusion(f32[5120,512]{1,0:T(8,128)} %bitcast.187, f32[10,512,256]{2,1,0:T(8,128)} %get-tuple-element.282, f32[5120]{0:T(1024)S(1)} %bitcast.197), kind=kLoop, calls=%fused_computation.77 | loop fusion | flops 10485760 | bytes 18370560 | tf_op jit(solution)/shard_map/convert_element_type | solution.py:133
  280.5 15.1 %while.119 = (s32[]{:T(128)}, f32[640,256]{1,0:T(8,128)}, s32[5,1024]{1,0:T(8,128)}, bf16[5,1024,256]{2,1,0:T(8,128)(2,1)S(1)}, s32[]{:T(128)}, /*index=5*/s32[]{:T(128)}) while((s32[]{:T(128)}, f32[640,256]{1,0:T(8,128)}, s32[5,1024]{1,0:T(8,128)}, bf16[5,1024,256]{2,1,0:T(8,128)(2,1)S(1)}, s32[]{:T(128)}, ...), condition=%wide.region_19.20_spmd.clone, body=%wide.region_18.19_spmd.clone.sunk | while | flops 336527360 | bytes 1847383 | solution.py:30
  283.5 2.5 fusion.129
  286.7 2.5 fusion.129
  290.0 2.5 fusion.129
  293.2 2.5 fusion.129
  295.7 1.9 add_convert_fusion
  (243 shorter events, 102.3 us)
Async XLA Ops:
  6.5 38.2 %copy-start = (bf16[512,256]{1,0:T(8,128)(2,1)S(1)}, bf16[512,256]{1,0:T(8,128)(2,1)}, u32[]{:S(2)}) copy-start(bf16[512,256]{1,0:T(8,128)(2,1)} %param.33) | copy-start | bytes 786436
  6.5 38.2 %all-gather.2.cloned.1.call-start = ((), (), s32[]{:S(2)}) async-start(), calls=%async_computation | async-start | bytes 3145728 | tf_op jit(solution)/shard_map/all_gather | solution.py:79
  71.8 4.7 %copy-start.9 = (s32[1,7,256]{2,0,1:T(1,128)S(1)}, s32[1,7,256]{2,0,1:T(1,128)}, u32[]{:S(2)}) copy-start(s32[1,7,256]{2,0,1:T(1,128)} %param.36) | copy-start | bytes 21508
  71.8 21.1 %copy-start.10 = (s32[1,6,64]{2,0,1:T(1,128)S(1)}, s32[1,6,64]{2,0,1:T(1,128)}, u32[]{:S(2)}) copy-start(s32[1,6,64]{2,0,1:T(1,128)} %param.40) | copy-start | bytes 4612
  71.8 21.8 %copy-start.8 = (s32[1,5120]{1,0:T(1,128)S(1)}, s32[1,5120]{1,0:T(1,128)}, u32[]{:S(2)}) copy-start(s32[1,5120]{1,0:T(1,128)} %param.41) | copy-start | bytes 61444
  71.8 22.5 %copy-start.7 = (s32[1,5120]{1,0:T(1,128)S(1)}, s32[1,5120]{1,0:T(1,128)}, u32[]{:S(2)}) copy-start(s32[1,5120]{1,0:T(1,128)} %param.42) | copy-start | bytes 61444
  75.3 31.7 %collective-permute-start.6 = (bf16[256,256]{1,0:T(8,128)(2,1)S(1)}, bf16[256,256]{1,0:T(8,128)(2,1)S(1)}, u32[]{:S(2)}, u32[]{:S(2)}) collective-permute-start(bf16[256,256]{1,0:T(8,128)(2,1)S(1)} %get-tuple-element.509), channel_id=1, source_target_pairs={{5,0},{8,1},{9,4},{12,5},{13,8},{7,2},{10,3},{11,6},{14,7},{15,10}... | collective-permute-start | bytes 393224 | tf_op jit(solution)/shard_map/ppermute | solution.py:12
  76.6 10.0 %collective-permute-start = (s32[256]{0:T(256)S(1)}, s32[256]{0:T(256)S(1)}, u32[]{:S(2)}, u32[]{:S(2)}) collective-permute-start(s32[256]{0:T(256)S(1)} %bitcast.210), channel_id=1, source_target_pairs={{5,0},{8,1},{9,4},{12,5},{13,8},{7,2},{10,3},{11,6},{14,7},{15,10}... | collective-permute-start | bytes 3080 | tf_op jit(solution)/shard_map/ppermute | solution.py:12
  77.9 10.0 %collective-permute-start.4 = (s32[256]{0:T(256)S(1)}, s32[256]{0:T(256)S(1)}, u32[]{:S(2)}, u32[]{:S(2)}) collective-permute-start(s32[256]{0:T(256)S(1)} %bitcast.209), channel_id=1, source_target_pairs={{0,4},{1,5},{4,8},{5,9},{8,12},{9,13},{2,6},{3,7},{6,10},{7,11},{1... | collective-permute-start | bytes 3080 | tf_op jit(solution)/shard_map/ppermute | solution.py:12
  81.3 13.9 %collective-permute-start.5 = (s32[256]{0:T(256)S(1)}, s32[256]{0:T(256)S(1)}, u32[]{:S(2)}, u32[]{:S(2)}) collective-permute-start(s32[256]{0:T(256)S(1)} %bitcast.208), channel_id=1, source_target_pairs={{0,5},{1,8},{4,9},{5,12},{8,13},{2,7},{3,10},{6,11},{7,14},{10,15}... | collective-permute-start | bytes 3080 | tf_op jit(solution)/shard_map/ppermute | solution.py:12
  85.3 9.9 %collective-permute-start.1 = (s32[256]{0:T(256)S(1)}, s32[256]{0:T(256)S(1)}, u32[]{:S(2)}, u32[]{:S(2)}) collective-permute-start(s32[256]{0:T(256)S(1)} %bitcast.207), channel_id=1, source_target_pairs={{4,0},{5,1},{8,4},{9,5},{12,8},{13,9},{6,2},{7,3},{10,6},{11,7},{1... | collective-permute-start | bytes 3080 | tf_op jit(solution)/shard_map/ppermute | solution.py:12
  86.6 8.6 %collective-permute-start.2 = (s32[256]{0:T(256)S(1)}, s32[256]{0:T(256)S(1)}, u32[]{:S(2)}, u32[]{:S(2)}) collective-permute-start(s32[256]{0:T(256)S(1)} %bitcast.206), channel_id=1, source_target_pairs={{1,0},{4,1},{5,4},{8,5},{9,8},{12,9},{13,12},{3,2},{6,3},{7,6},{10... | collective-permute-start | bytes 3080 | tf_op jit(solution)/shard_map/ppermute | solution.py:12
  87.9 7.2 %collective-permute-start.3 = (s32[256]{0:T(256)S(1)}, s32[256]{0:T(256)S(1)}, u32[]{:S(2)}, u32[]{:S(2)}) collective-permute-start(s32[256]{0:T(256)S(1)} %bitcast.205), channel_id=1, source_target_pairs={{0,1},{1,4},{4,5},{5,8},{8,9},{9,12},{12,13},{2,3},{3,6},{6,7},{7,... | collective-permute-start | bytes 3080 | tf_op jit(solution)/shard_map/ppermute | solution.py:12
  95.2 18.1 %collective-permute-start.7 = (bf16[256,256]{1,0:T(8,128)(2,1)}, bf16[256,256]{1,0:T(8,128)(2,1)S(1)}, u32[]{:S(2)}, u32[]{:S(2)}) collective-permute-start(bf16[256,256]{1,0:T(8,128)(2,1)} %get-tuple-element.508), channel_id=1, source_target_pairs={{4,0},{5,1},{8,4},{9,5},{12,8},{13,9},{6,2},{7,3},{10,6},{11,7},{1... | collective-permute-start | bytes 393224 | tf_op jit(solution)/shard_map/ppermute | solution.py:12
  96.5 16.8 %collective-permute-start.8 = (bf16[256,256]{1,0:T(8,128)(2,1)}, bf16[256,256]{1,0:T(8,128)(2,1)S(1)}, u32[]{:S(2)}, u32[]{:S(2)}) collective-permute-start(bf16[256,256]{1,0:T(8,128)(2,1)} %get-tuple-element.507), channel_id=1, source_target_pairs={{1,0},{4,1},{5,4},{8,5},{9,8},{12,9},{13,12},{3,2},{6,3},{7,6},{10... | collective-permute-start | bytes 393224 | tf_op jit(solution)/shard_map/ppermute | solution.py:12
  97.8 15.5 %collective-permute-start.9 = (bf16[256,256]{1,0:T(8,128)(2,1)}, bf16[256,256]{1,0:T(8,128)(2,1)S(1)}, u32[]{:S(2)}, u32[]{:S(2)}) collective-permute-start(bf16[256,256]{1,0:T(8,128)(2,1)} %get-tuple-element.506), channel_id=1, source_target_pairs={{0,1},{1,4},{4,5},{5,8},{8,9},{9,12},{12,13},{2,3},{3,6},{6,7},{7,... | collective-permute-start | bytes 393224 | tf_op jit(solution)/shard_map/ppermute | solution.py:12
  102.1 11.3 %collective-permute-start.10 = (bf16[256,256]{1,0:T(8,128)(2,1)}, bf16[256,256]{1,0:T(8,128)(2,1)S(1)}, u32[]{:S(2)}, u32[]{:S(2)}) collective-permute-start(bf16[256,256]{1,0:T(8,128)(2,1)} %get-tuple-element.505), channel_id=1, source_target_pairs={{0,4},{1,5},{4,8},{5,9},{8,12},{9,13},{2,6},{3,7},{6,10},{7,11},{1... | collective-permute-start | bytes 393224 | tf_op jit(solution)/shard_map/ppermute | solution.py:12
  107.0 0.6 copy-start.4
  107.7 8.3 %collective-permute-start.11 = (bf16[256,256]{1,0:T(8,128)(2,1)}, bf16[256,256]{1,0:T(8,128)(2,1)S(1)}, u32[]{:S(2)}, u32[]{:S(2)}) collective-permute-start(bf16[256,256]{1,0:T(8,128)(2,1)} %get-tuple-element.504), channel_id=1, source_target_pairs={{0,5},{1,8},{4,9},{5,12},{8,13},{2,7},{3,10},{6,11},{7,14},{10,15}... | collective-permute-start | bytes 393224 | tf_op jit(solution)/shard_map/ppermute | solution.py:12
  116.0 2.6 copy-start.2
  118.6 25.1 %copy-start.1 = (bf16[2,512,256]{2,1,0:T(8,128)(2,1)S(1)}, bf16[2,512,256]{2,1,0:T(8,128)(2,1)}, u32[]{:S(2)}) copy-start(bf16[2,512,256]{2,1,0:T(8,128)(2,1)} %param.39) | copy-start | bytes 1572868
  131.7 34.4 %collective-permute-start.12 = (bf16[64,256]{1,0:T(8,128)(2,1)S(1)}, bf16[64,256]{1,0:T(8,128)(2,1)}, u32[]{:S(2)}, u32[]{:S(2)}) collective-permute-start(bf16[64,256]{1,0:T(8,128)(2,1)S(1)} %get-tuple-element.521), channel_id=1, source_target_pairs={{5,0},{8,1},{9,4},{12,5},{13,8},{7,2},{10,3},{11,6},{14,7},{15,10}... | collective-permute-start | bytes 98312 | tf_op jit(solution)/shard_map/ppermute | solution.py:12
  133.0 39.6 %collective-permute-start.13 = (bf16[64,256]{1,0:T(8,128)(2,1)S(1)}, bf16[64,256]{1,0:T(8,128)(2,1)S(1)}, u32[]{:S(2)}, u32[]{:S(2)}) collective-permute-start(bf16[64,256]{1,0:T(8,128)(2,1)S(1)} %get-tuple-element.520), channel_id=1, source_target_pairs={{4,0},{5,1},{8,4},{9,5},{12,8},{13,9},{6,2},{7,3},{10,6},{11,7},{1... | collective-permute-start | bytes 98312 | tf_op jit(solution)/shard_map/ppermute | solution.py:12
  134.3 38.3 %collective-permute-start.14 = (bf16[64,256]{1,0:T(8,128)(2,1)S(1)}, bf16[64,256]{1,0:T(8,128)(2,1)S(1)}, u32[]{:S(2)}, u32[]{:S(2)}) collective-permute-start(bf16[64,256]{1,0:T(8,128)(2,1)S(1)} %get-tuple-element.519), channel_id=1, source_target_pairs={{1,0},{4,1},{5,4},{8,5},{9,8},{12,9},{13,12},{3,2},{6,3},{7,6},{10... | collective-permute-start | bytes 98312 | tf_op jit(solution)/shard_map/ppermute | solution.py:12
  135.6 37.1 %collective-permute-start.15 = (bf16[64,256]{1,0:T(8,128)(2,1)S(1)}, bf16[64,256]{1,0:T(8,128)(2,1)S(1)}, u32[]{:S(2)}, u32[]{:S(2)}) collective-permute-start(bf16[64,256]{1,0:T(8,128)(2,1)S(1)} %get-tuple-element.518), channel_id=1, source_target_pairs={{0,1},{1,4},{4,5},{5,8},{8,9},{9,12},{12,13},{2,3},{3,6},{6,7},{7,... | collective-permute-start | bytes 98312 | tf_op jit(solution)/shard_map/ppermute | solution.py:12
  138.6 34.1 %collective-permute-start.16 = (bf16[64,256]{1,0:T(8,128)(2,1)S(1)}, bf16[64,256]{1,0:T(8,128)(2,1)S(1)}, u32[]{:S(2)}, u32[]{:S(2)}) collective-permute-start(bf16[64,256]{1,0:T(8,128)(2,1)S(1)} %get-tuple-element.517), channel_id=1, source_target_pairs={{0,4},{1,5},{4,8},{5,9},{8,12},{9,13},{2,6},{3,7},{6,10},{7,11},{1... | collective-permute-start | bytes 98312 | tf_op jit(solution)/shard_map/ppermute | solution.py:12
  149.9 22.0 %copy-start.12 = (bf16[1024,256]{1,0:T(8,128)(2,1)S(1)}, bf16[1024,256]{1,0:T(8,128)(2,1)}, u32[]{:S(2)}) copy-start(bf16[1024,256]{1,0:T(8,128)(2,1)} %get-tuple-element.529) | copy-start | bytes 1572868
  166.0 7.4 %collective-permute-start.17 = (bf16[64,256]{1,0:T(8,128)(2,1)S(1)}, bf16[64,256]{1,0:T(8,128)(2,1)S(1)}, u32[]{:S(2)}, u32[]{:S(2)}) collective-permute-start(bf16[64,256]{1,0:T(8,128)(2,1)S(1)} %get-tuple-element.516), channel_id=1, source_target_pairs={{0,5},{1,8},{4,9},{5,12},{8,13},{2,7},{3,10},{6,11},{7,14},{10,15}... | collective-permute-start | bytes 98312 | tf_op jit(solution)/shard_map/ppermute | solution.py:12
  176.2 13.2 %copy-start.5 = (f32[1,5120]{1,0:T(1,128)S(1)}, f32[1,5120]{1,0:T(1,128)}, u32[]{:S(2)}) copy-start(f32[1,5120]{1,0:T(1,128)} %param.43) | copy-start | bytes 61444
  197.5 18.6 %copy-start.11 = (bf16[2,512,256]{2,1,0:T(8,128)(2,1)S(1)}, bf16[2,512,256]{2,1,0:T(8,128)(2,1)}, u32[]{:S(2)}) copy-start(bf16[2,512,256]{2,1,0:T(8,128)(2,1)} %param.38) | copy-start | bytes 1572868
  206.2 10.7 %copy-start.3 = (s32[5,1024]{1,0:T(8,128)}, s32[5,1024]{1,0:T(8,128)S(1)}, u32[]{:S(2)}) copy-start(s32[5,1024]{1,0:T(8,128)S(1)} %get-tuple-element.946) | copy-start | bytes 61444
  217.8 33.8 %collective-permute-start.18 = (bf16[64,256]{1,0:T(8,128)(2,1)S(1)}, bf16[64,256]{1,0:T(8,128)(2,1)S(1)}, u32[]{:S(2)}, u32[]{:S(2)}) collective-permute-start(bf16[64,256]{1,0:T(8,128)(2,1)S(1)} %get-tuple-element.515), channel_id=1, source_target_pairs={{5,0},{8,1},{9,4},{12,5},{13,8},{7,2},{10,3},{11,6},{14,7},{15,10}... | collective-permute-start | bytes 98312 | tf_op jit(solution)/shard_map/ppermute | solution.py:12
  219.1 37.2 %collective-permute-start.19 = (bf16[64,256]{1,0:T(8,128)(2,1)S(1)}, bf16[64,256]{1,0:T(8,128)(2,1)S(1)}, u32[]{:S(2)}, u32[]{:S(2)}) collective-permute-start(bf16[64,256]{1,0:T(8,128)(2,1)S(1)} %get-tuple-element.514), channel_id=1, source_target_pairs={{4,0},{5,1},{8,4},{9,5},{12,8},{13,9},{6,2},{7,3},{10,6},{11,7},{1... | collective-permute-start | bytes 98312 | tf_op jit(solution)/shard_map/ppermute | solution.py:12
  220.4 35.9 %collective-permute-start.20 = (bf16[64,256]{1,0:T(8,128)(2,1)S(1)}, bf16[64,256]{1,0:T(8,128)(2,1)S(1)}, u32[]{:S(2)}, u32[]{:S(2)}) collective-permute-start(bf16[64,256]{1,0:T(8,128)(2,1)S(1)} %get-tuple-element.513), channel_id=1, source_target_pairs={{1,0},{4,1},{5,4},{8,5},{9,8},{12,9},{13,12},{3,2},{6,3},{7,6},{10... | collective-permute-start | bytes 98312 | tf_op jit(solution)/shard_map/ppermute | solution.py:12
  221.7 34.6 %collective-permute-start.21 = (bf16[64,256]{1,0:T(8,128)(2,1)S(1)}, bf16[64,256]{1,0:T(8,128)(2,1)S(1)}, u32[]{:S(2)}, u32[]{:S(2)}) collective-permute-start(bf16[64,256]{1,0:T(8,128)(2,1)S(1)} %get-tuple-element.512), channel_id=1, source_target_pairs={{0,1},{1,4},{4,5},{5,8},{8,9},{9,12},{12,13},{2,3},{3,6},{6,7},{7,... | collective-permute-start | bytes 98312 | tf_op jit(solution)/shard_map/ppermute | solution.py:12
  224.7 31.6 %collective-permute-start.22 = (bf16[64,256]{1,0:T(8,128)(2,1)S(1)}, bf16[64,256]{1,0:T(8,128)(2,1)S(1)}, u32[]{:S(2)}, u32[]{:S(2)}) collective-permute-start(bf16[64,256]{1,0:T(8,128)(2,1)S(1)} %get-tuple-element.511), channel_id=1, source_target_pairs={{0,4},{1,5},{4,8},{5,9},{8,12},{9,13},{2,6},{3,7},{6,10},{7,11},{1... | collective-permute-start | bytes 98312 | tf_op jit(solution)/shard_map/ppermute | solution.py:12
  251.6 6.3 %collective-permute-start.23 = (bf16[64,256]{1,0:T(8,128)(2,1)S(1)}, bf16[64,256]{1,0:T(8,128)(2,1)S(1)}, u32[]{:S(2)}, u32[]{:S(2)}) collective-permute-start(bf16[64,256]{1,0:T(8,128)(2,1)S(1)} %get-tuple-element.510), channel_id=1, source_target_pairs={{0,5},{1,8},{4,9},{5,12},{8,13},{2,7},{3,10},{6,11},{7,14},{10,15}... | collective-permute-start | bytes 98312 | tf_op jit(solution)/shard_map/ppermute | solution.py:12
  260.6 13.2 %copy-start.6 = (f32[1,5120]{1,0:T(1,128)S(1)}, f32[1,5120]{1,0:T(1,128)}, u32[]{:S(2)}) copy-start(f32[1,5120]{1,0:T(1,128)} %param.43) | copy-start | bytes 61444
Sparse Core Ops, SparseCore 0:
  8.9 35.7 all-gather.1
where the time goes:
time: 306 us; the launch traced here: 304 us
  matrix products  110 us (36%)
  starting transfers between devices  68.4 us (22%)
  waiting for transfers between devices  41.5 us (14%)
  local copies, waits for them, and re-layouts  28.3 us (9%)
  other arithmetic  21.8 us (7%)
  blocking collectives  19.9 us (7%)
  between operations  14.2 us (5%)
    dot_general x53, matrix products, select(): return (carry, jnp.dot(onehot, table, preferred_element_type=jnp.float32))  82.1 us
    ppermute x24, starting transfers between devices, passed_along(): lax.ppermute(value, axis, [(source, source + steps) for source in range(f...  68.4 us
    all_gather x1, waiting for transfers between devices, on_device(): lax.all_gather(grid_latent, 'feat', axis=1, tiled=True)  36 us
    dot_general x17, matrix products, accumulate(): jnp.dot(onehot, piece_values, preferred_element_type=jnp.float32)  22.1 us
    all_gather x2, blocking collectives, on_device(): piece = lax.all_gather(state, 'feat', axis=1, tiled=True)  19.9 us
    another operation x6, local copies, waits for them, and re-layouts  16.2 us
    convert_element_type x2, other arithmetic, on_device(): (mesh_scale * jax.nn.silu(from_rows + to_rows)).astype(jnp.bfloat16)  14.7 us
    unnamed x47, local copies, waits for them, and re-layouts  6.78 us
  transfers between devices with their start and end apart: 25, of which 4 were waited for; matrix products, arithmetic and copies ran while one was open for 16% of the time, Pallas kernels for 0%

commit v1 on v0

v1 whole, which is shorter than its diff:
```python
import functools

import jax
import jax.numpy as jnp
from jax import lax
from jax.experimental import pallas as pl
from jax.experimental.pallas import tpu as pltpu
from jax.sharding import PartitionSpec as P

REGION = ("space", "edge")
PAD = 16
VMEM_BYTES = 56 * 1024 * 1024


def params():
    return pltpu.CompilerParams(vmem_limit_bytes=VMEM_BYTES)


def vmem_specs(count):
    return [pl.BlockSpec(memory_space=pltpu.VMEM)] * count


def passed_along(value, steps):
    count = lax.axis_size(REGION)
    first, last = (max(0, -steps), min(count, count - steps))
    return lax.ppermute(value, REGION, [(i, i + steps) for i in range(first, last)])


def from_others(value):
    n = lax.axis_size("feat")
    return [
        lax.ppermute(value, "feat", [(i, (i + k) % n) for i in range(n)]) for k in range(1, n)
    ]


def own_and_others_rows(weight_ref, channels, others):
    n = others + 1
    me = lax.axis_index("feat")
    blocks = []
    for k in range(n):
        owner = lax.rem(me - k + n, n)
        start = pl.multiple_of(owner * channels, channels)
        blocks.append(weight_ref[0, pl.ds(start, channels), :])
    return blocks


def silu(v):
    half = 0.5 * v
    return half + half * jnp.tanh(half)


def column(row):
    length = row.shape[1]
    parts = [
        jnp.broadcast_to(row[:, c * 128 : (c + 1) * 128], (128, 128)).T for c in range(length // 128)
    ]
    return parts[0] if len(parts) == 1 else jnp.concatenate(parts, axis=0)


def lane_iota(count):
    return lax.broadcasted_iota(jnp.int32, (16, count), 1).astype(jnp.int16)


def row_iota(count):
    return lax.broadcasted_iota(jnp.int32, (count, 128), 0).astype(jnp.int16)


def tiled(value, rows, lanes):
    if value.shape[0] != rows:
        value = jnp.concatenate([value] * (rows // value.shape[0]), axis=0)
    if value.shape[1] != lanes:
        value = jnp.concatenate([value] * (lanes // value.shape[1]), axis=1)
    return value


def pick_mask(column16, lane16):
    rows, lanes = (column16.shape[0], lane16.shape[1])
    same = tiled(column16, rows, lanes) == tiled(lane16, rows, lanes)
    return jnp.where(same, jnp.bfloat16(1), jnp.bfloat16(0))


def sum_mask(row, rows16, scale=None):
    count, length = (rows16.shape[0], row.shape[1])
    targets = jnp.broadcast_to(row, (16, length)).astype(jnp.int16)
    same = tiled(rows16, count, length) == tiled(targets, count, length)
    if scale is None:
        here = jnp.bfloat16(1)
    else:
        here = tiled(jnp.broadcast_to(scale, (16, length)).astype(jnp.bfloat16), count, length)
    return jnp.where(same, here, jnp.bfloat16(0))


def dot(a, b):
    return jnp.dot(a, b, preferred_element_type=jnp.float32)


def pick_kernel(order, index_ref, table_ref, out_ref):
    lanes = lane_iota(table_ref.shape[0])
    for place, j in enumerate(order):
        col = column(index_ref[0, pl.ds(j, 1), :]).astype(jnp.int16)
        out_ref[place] = dot(pick_mask(col, lanes), table_ref[...]).astype(jnp.bfloat16)


def pick(order, g2m_src, grid_latent):
    capacity = g2m_src.shape[2]
    rows, channels = grid_latent.shape
    return pl.pallas_call(
        functools.partial(pick_kernel, order),
        out_shape=jax.ShapeDtypeStruct((len(order), capacity, channels), jnp.bfloat16),
        in_specs=vmem_specs(2),
        out_specs=pl.BlockSpec(memory_space=pltpu.VMEM),
        compiler_params=params(),
        cost_estimate=pl.CostEstimate(
            flops=2 * len(order) * capacity * rows * channels,
            bytes_accessed=2 * (rows + len(order) * capacity) * channels,
            transcendentals=0,
        ),
    )(g2m_src, grid_latent)


def encode_kernel(order, others, weight_ref, coef_ref, target_ref, *refs):
    sources, outs = (refs[: others + 1], refs[others + 1 :])
    capacity, channels = sources[0].shape[1:]
    weights = own_and_others_rows(weight_ref, channels, others)
    line = lax.broadcasted_iota(jnp.int32, (PAD, channels), 0)
    pieces = capacity // channels
    for place, j in enumerate(order):
        projected = dot(sources[0][place], weights[0])
        for source, weight in zip(sources[1:], weights[1:]):
            projected += dot(source[place], weight)
        scale = tiled(column(coef_ref[0, pl.ds(j, 1), :]), capacity, channels)
        outs[place][pl.ds(0, capacity), :] = (scale * silu(projected)).astype(jnp.bfloat16)
        target = target_ref[0, pl.ds(j, 1), :]
        code = jnp.zeros((PAD, channels), jnp.float32)
        for number, part in enumerate((target >> 3, target & 7)):
            part = part.astype(jnp.float32)
            for piece in range(pieces):
                values = part[:, piece * channels : (piece + 1) * channels]
                code = jnp.where(line == number * pieces + piece, values, code)
        outs[place][pl.ds(capacity, PAD), :] = code.astype(jnp.bfloat16)


def encode(order, picked, arrived, enc_weight, g2m_coef, g2m_dst):
    count, capacity, channels = picked.shape
    sent = jax.ShapeDtypeStruct((capacity + PAD, channels), jnp.bfloat16)
    return pl.pallas_call(
        functools.partial(encode_kernel, order, len(arrived)),
        out_shape=[sent] * count,
        in_specs=vmem_specs(4 + len(arrived)),
        out_specs=vmem_specs(count),
        compiler_params=params(),
        cost_estimate=pl.CostEstimate(
            flops=2 * count * capacity * enc_weight.shape[0] * channels,
            bytes_accessed=2 * (3 * count * capacity + enc_weight.shape[0]) * channels,
            transcendentals=count * capacity * channels,
        ),
    )(enc_weight[None], g2m_coef, g2m_dst, picked, *arrived)


def gather_in_kernel(latent_ref, *refs):
    blocks, out_ref = (refs[:-1], refs[-1])
    nodes, channels = latent_ref.shape
    capacity = blocks[0].shape[0] - PAD
    rows16 = row_iota(nodes)
    pieces = capacity // channels
    total = latent_ref[...].astype(jnp.float32)
    for block in blocks:
        code = block[pl.ds(capacity, PAD), :].astype(jnp.float32)
        lines = [code[i : i + 1, :] for i in range(2 * pieces)]
        upper = lines[0] if pieces == 1 else jnp.concatenate(lines[:pieces], axis=1)
        lower = lines[1] if pieces == 1 else jnp.concatenate(lines[pieces:], axis=1)
        target = (8.0 * upper + lower).astype(jnp.int32)
        total += dot(sum_mask(target, rows16), block[pl.ds(0, capacity), :])
    out_ref[...] = total.astype(jnp.bfloat16)


def gather_in(mesh_latent, blocks):
    nodes, channels = mesh_latent.shape
    slots = len(blocks) * blocks[0].shape[0]
    return pl.pallas_call(
        gather_in_kernel,
        out_shape=jax.ShapeDtypeStruct((nodes, channels), jnp.bfloat16),
        in_specs=vmem_specs(1 + len(blocks)),
        out_specs=pl.BlockSpec(memory_space=pltpu.VMEM),
        compiler_params=params(),
        cost_estimate=pl.CostEstimate(
            flops=2 * nodes * slots * channels,
            bytes_accessed=2 * (slots + 2 * nodes) * channels,
            transcendentals=0,
        ),
    )(mesh_latent, *blocks)


def project_kernel(others, regions, offsets, src_ref, dst_ref, listed_ref, *refs):
    states, (sender_ref, receiver_ref, sent_ref) = (refs[: others + 1], refs[others + 1 :])
    nodes, channels = states[0].shape
    totals = []
    for weight_ref in (src_ref, dst_ref):
        weights = own_and_others_rows(weight_ref, channels, others)
        total = dot(states[0][...], weights[0])
        for state, weight in zip(states[1:], weights[1:]):
            total += dot(state[...], weight)
        totals.append(total.astype(jnp.bfloat16))
    sender_ref[...] = totals[0]
    receiver_ref[...] = totals[1]
    width = listed_ref.shape[2]
    lanes = lane_iota(nodes)
    region = lax.axis_index(REGION)
    sent_ref[...] = jnp.zeros_like(sent_ref)
    for j in range(0, len(offsets), 2):
        row = jnp.concatenate([listed_ref[0, pl.ds(j + i, 1), :] for i in range(2)], axis=1)
        rows = dot(pick_mask(column(row).astype(jnp.int16), lanes), totals[0]).astype(jnp.bfloat16)
        for i in range(2):
            to = region + offsets[j + i]

            @pl.when((to >= 0) & (to < regions))
            def _():
                sent_ref[jnp.clip(to, 0, regions - 1)] = rows[i * width : (i + 1) * width]


def project(layer, state, arrived, src_weights, dst_weights, halo_send, offsets):
    nodes, channels = state.shape
    links, width = halo_send.shape[1:]
    regions = lax.axis_size(REGION)
    depth = src_weights.shape[1]
    weight_spec = pl.BlockSpec((1, depth, channels), lambda i: (layer, 0, 0))
    table = jax.ShapeDtypeStruct((nodes, channels), jnp.bfloat16)
    return pl.pallas_call(
        functools.partial(project_kernel, len(arrived), regions, offsets),
        out_shape=[table, table, jax.ShapeDtypeStruct((regions, width, channels), jnp.bfloat16)],
        grid=(1,),
        in_specs=[weight_spec, weight_spec] + vmem_specs(2 + len(arrived)),
        out_specs=vmem_specs(3),
        compiler_params=params(),
        cost_estimate=pl.CostEstimate(
            flops=4 * nodes * depth * channels + 2 * links * width * nodes * channels,
            bytes_accessed=2 * (2 * depth + 4 * nodes + regions * width) * channels,
            transcendentals=0,
        ),
    )(src_weights, dst_weights, halo_send, state, *arrived)


def message_kernel(
    offsets, regions, turn, source_ref, target_ref, coef_ref, state_ref, sender_ref, receiver_ref, got_ref,
    out_ref, table_ref, total_ref,
):
    nodes, channels = state_ref.shape
    width = got_ref.shape[1]
    named = nodes + len(offsets) * width
    table_ref[pl.ds(0, nodes), :] = sender_ref[...]
    region = lax.axis_index(REGION)
    for j, offset in enumerate(offsets):
        origin = jnp.clip(region - offset, 0, regions - 1)
        table_ref[pl.ds(nodes + j * width, width), :] = got_ref[origin]
    table_ref[pl.ds(named, nodes), :] = receiver_ref[...]
    total_ref[...] = state_ref[...].astype(jnp.float32)
    source_lanes = lane_iota(named)
    target_lanes = lane_iota(nodes)
    rows16 = row_iota(nodes)

    def body(step, carry):
        start = pl.multiple_of(step * turn, turn)
        target = target_ref[:, pl.ds(start, turn)]
        source16 = column(source_ref[:, pl.ds(start, turn)]).astype(jnp.int16)
        target16 = column(target).astype(jnp.int16)
        mask = jnp.concatenate(
            [pick_mask(source16, source_lanes), pick_mask(target16, target_lanes)], axis=1
        )
        message = silu(dot(mask, table_ref[...])).astype(jnp.bfloat16)
        total_ref[...] += dot(sum_mask(target, rows16, coef_ref[:, pl.ds(start, turn)]), message)
        return carry

    lax.fori_loop(0, source_ref.shape[1] // turn, body, 0)
    out_ref[...] = total_ref[...].astype(jnp.bfloat16)


def messages(state, sender, receiver, got, m2m_src, m2m_dst, m2m_coef, offsets):
    nodes, channels = state.shape
    edges = m2m_src.shape[1]
    named = nodes + len(offsets) * got.shape[1]
    return pl.pallas_call(
        functools.partial(message_kernel, offsets, lax.axis_size(REGION), 512),
        out_shape=jax.ShapeDtypeStruct((nodes, channels), jnp.bfloat16),
        in_specs=vmem_specs(7),
        out_specs=pl.BlockSpec(memory_space=pltpu.VMEM),
        scratch_shapes=[
            pltpu.VMEM((named + nodes, channels), jnp.bfloat16),
            pltpu.VMEM((nodes, channels), jnp.float32),
        ],
        compiler_params=params(),
        cost_estimate=pl.CostEstimate(
            flops=2 * edges * (named + 2 * nodes) * channels,
            bytes_accessed=2 * (named + 3 * nodes) * channels,
            transcendentals=edges * channels,
        ),
    )(m2m_src, m2m_dst, m2m_coef, state, sender, receiver, got)


def on_device(
    grid_latent,
    enc_weight,
    mesh_latent,
    g2m_src,
    g2m_dst,
    g2m_coef,
    src_weights,
    dst_weights,
    halo_send,
    m2m_src,
    m2m_dst,
    m2m_coef,
):
    reach = (g2m_src.shape[1] - 1) // 2
    offsets = tuple(o for o in range(-reach, reach + 1) if o != 0)
    by_distance = sorted(range(2 * reach + 1), key=lambda j: -abs(j - reach))
    cut = len(by_distance) // 2 + 1
    groups = [tuple(by_distance[:cut]), tuple(by_distance[cut:])]
    blocks = []
    picked = [pick(order, g2m_src, grid_latent) for order in groups]
    arrived = [from_others(rows) for rows in picked]
    for order, rows, others in zip(groups, picked, arrived):
        encoded = encode(order, rows, others, enc_weight, g2m_coef, g2m_dst)
        for j, block in zip(order, encoded):
            blocks.append(block if j == reach else passed_along(block, j - reach))
    state = gather_in(mesh_latent, blocks)
    for layer in range(src_weights.shape[0]):
        sender, receiver, sent = project(
            layer, state, from_others(state), src_weights, dst_weights, halo_send, offsets
        )
        got = lax.all_to_all(sent, REGION, 0, 0, tiled=True)
        state = messages(state, sender, receiver, got, m2m_src, m2m_dst, m2m_coef, offsets)
    return state


def solution(mesh):
    placed = (
        P(("groups", "space", "edge"), "feat"),
        P(None, "feat"),
        P(("groups", "space", "edge"), "feat"),
        P(("groups", "space", "edge"), None, None),
        P(("groups", "space", "edge"), None, None),
        P(("groups", "space", "edge"), None, None),
        P(None, None, "feat"),
        P(None, None, "feat"),
        P(("groups", "space", "edge"), None, None),
        P(("groups", "space", "edge"), None),
        P(("groups", "space", "edge"), None),
        P(("groups", "space", "edge"), None),
    )
    return jax.shard_map(
        on_device,
        mesh=mesh,
        in_specs=placed,
        out_specs=P(("groups", "space", "edge"), "feat"),
        check_vma=False,
    )
```

time: 306 us -> 136 us (0.44)
  matrix products: 110 us -> 0 us
  Pallas kernels: 0 us -> 50.8 us
  starting transfers between devices: 68.4 us -> 21.4 us
  other arithmetic: 21.8 us -> 0 us
  local copies, waits for them, and re-layouts: 28.3 us -> 6.85 us
  between operations: 14.2 us -> 0.15 us
  waiting for transfers between devices: 41.5 us -> 28.6 us
  blocking collectives: 19.9 us -> 27.5 us
    dot_general x75 -> x0, matrix products: 110 us -> none  [the longest x53 82.1 us: select(): return (carry, jnp.dot(onehot, table, preferred_element_type=jnp.float32))]
    pallas_call x0 -> x9, Pallas kernels: none -> 50.8 us  [the longest x2 29.5 us: messages(): pl.pallas_call(functools.partial(message_kernel, offsets, lax.axis_size(R...]
    ppermute x24 -> x10, starting transfers between devices: 68.4 us -> 21.4 us  [the longest x6 15.7 us: passed_along(): lax.ppermute(value, REGION, [(i, i + steps) for i in range(first, last)])]
    all_gather x1 -> x0, waiting for transfers between devices: 36 us -> none  [on_device(): lax.all_gather(grid_latent, 'feat', axis=1, tiled=True)]
    all_to_all x0 -> x2, blocking collectives: none -> 27.5 us  [on_device(): got = lax.all_to_all(sent, REGION, 0, 0, tiled=True)]
    ppermute x24 -> x10, waiting for transfers between devices: 4.82 us -> 28.6 us  [the longest x4 24.3 us: from_others(): lax.ppermute(value, 'feat', [(i, (i + k) % n) for i in range(n)])]
    all_gather x2 -> x0, blocking collectives: 19.9 us -> none  [on_device(): piece = lax.all_gather(state, 'feat', axis=1, tiled=True)]
    convert_element_type x6 -> x0, other arithmetic: 19.4 us -> none  [the longest x2 14.7 us: on_device(): (mesh_scale * jax.nn.silu(from_rows + to_rows)).astype(jnp.bfloat16)]
  transfers between devices with their start and end apart: 25 -> 10, of which waited for: 4 -> 6; matrix products, arithmetic and copies ran while one was open for 16% -> 1% of each run, Pallas kernels for 0% -> 6%
where the time goes in v1:
time: 136 us; the launch traced here: 135 us
  Pallas kernels  50.8 us (37%)
  waiting for transfers between devices  28.6 us (21%)
  blocking collectives  27.5 us (20%)
  starting transfers between devices  21.4 us (16%)
  local copies, waits for them, and re-layouts  6.85 us (5%)
    pallas_call x2, Pallas kernels, messages(): pl.pallas_call(functools.partial(message_kernel, offsets, lax.axis_size(R...  29.5 us
    all_to_all x2, blocking collectives, on_device(): got = lax.all_to_all(sent, REGION, 0, 0, tiled=True)  27.5 us
    ppermute x4, waiting for transfers between devices, from_others(): lax.ppermute(value, 'feat', [(i, (i + k) % n) for i in range(n)])  24.3 us
    ppermute x6, starting transfers between devices, passed_along(): lax.ppermute(value, REGION, [(i, i + steps) for i in range(first, last)])  15.7 us
    pallas_call x2, Pallas kernels, project(): pl.pallas_call(functools.partial(project_kernel, len(arrived), regions, o...  7.02 us
    unnamed x30, local copies, waits for them, and re-layouts  6.85 us
    pallas_call x2, Pallas kernels, pick(): pl.pallas_call(functools.partial(pick_kernel, order), out_shape=jax.Shape...  6.34 us
    ppermute x4, starting transfers between devices, from_others(): lax.ppermute(value, 'feat', [(i, (i + k) % n) for i in range(n)])  5.65 us
  transfers between devices with their start and end apart: 10, of which 6 were waited for; matrix products, arithmetic and copies ran while one was open for 1% of the time, Pallas kernels for 6%

profile of v1, /device:TPU:0, one launch (start us, length us, event | category | flops | bytes accessed | tf_op | source)
XLA Modules:
  0.0 135.3 jit_solution(14654888258977231369)
XLA Ops:
  0.0 1.3 copy.13.index_ref
  1.3 3.0 %shard_map.120.refs_0_ = bf16[3,256,256]{2,1,0:T(8,128)(2,1)} custom-call(s32[1,7,256]{2,1,0:T(8,128)} %copy.13.index_ref, bf16[2048,256]{1,0:T(8,128)(2,1)} %table_ref.3), custom_call_target="tpu_custom_call" | custom-call | flops 805306368 | bytes 1441792 | tf_op jit(solution)/shard_map/pallas_call | solution.py:107
  4.3 2.9 %collective-permute-start.5 = (bf16[3,256,256]{2,1,0:T(8,128)(2,1)}, bf16[3,256,256]{2,1,0:T(8,128)(2,1)S(1)}, u32[]{:S(2)}, u32[]{:S(2)}) collective-permute-start(bf16[3,256,256]{2,1,0:T(8,128)(2,1)} %shard_map.120.refs_0_), channel_id=1, source_target_pairs={{0,2},{2,0},{1,3},{3,1},{4,6},{6,4},{5,7},{7,5},{8,10},{10,8},{9,1... | collective-permute-start | bytes 1179656 | tf_op jit(solution)/shard_map/ppermute | solution.py:32
  7.3 3.3 %shard_map.118.refs_0_ = bf16[4,256,256]{2,1,0:T(8,128)(2,1)} custom-call(s32[1,7,256]{2,1,0:T(8,128)} %copy.13.index_ref, bf16[2048,256]{1,0:T(8,128)(2,1)} %table_ref.3), custom_call_target="tpu_custom_call" | custom-call | flops 1073741824 | bytes 1572864 | tf_op jit(solution)/shard_map/pallas_call | solution.py:107
  10.6 0.0 collective-permute-start
  10.6 0.0 copy-done.4
  10.6 0.6 copy.14.coef_ref
  11.2 0.1 copy-done.5
  11.3 0.6 copy.15.target_ref
  11.9 5.5 %collective-permute-done.5.refs_1_ = bf16[3,256,256]{2,1,0:T(8,128)(2,1)S(1)} collective-permute-done((bf16[3,256,256]{2,1,0:T(8,128)(2,1)}, bf16[3,256,256]{2,1,0:T(8,128)(2,1)S(1)}, u32[]{:S(2)}, u32[]{:S(2)}) %collective-permute-start.5) | collective-permute-done | bytes 393248 | tf_op jit(solution)/shard_map/ppermute | solution.py:32
  17.4 0.8 copy-done.1
  18.2 2.5 %shard_map.121 = (bf16[272,256]{1,0:T(8,128)(2,1)}, bf16[272,256]{1,0:T(8,128)(2,1)}, bf16[272,256]{1,0:T(8,128)(2,1)}) custom-call(bf16[1,512,256]{2,1,0:T(8,128)(2,1)} %bitcast.1, f32[1,7,256]{2,1,0:T(8,128)} %copy.14.coef_ref, s32[1,7,256]{2,1,0:T(8,128)} %copy.15.target_ref, bf16[3,256,256]{2,1,0:T(8,128)(2,1)} %shard_map.120.refs_0_, ...), custom_call_target="tpu_custom_call" | custom-call | flops 201326592 | bytes 1441792 | tf_op jit(solution)/shard_map/pallas_call | solution.py:146
  20.6 1.3 collective-permute-start.6
  21.9 3.0 %collective-permute-start.7 = (bf16[272,256]{1,0:T(8,128)(2,1)}, bf16[272,256]{1,0:T(8,128)(2,1)S(1)}, u32[]{:S(2)}, u32[]{:S(2)}) collective-permute-start(bf16[272,256]{1,0:T(8,128)(2,1)} %get-tuple-element.23), channel_id=1, source_target_pairs={{0,1},{1,4},{4,5},{5,8},{8,9},{9,12},{12,13},{2,3},{3,6},{6,7},{7,... | collective-permute-start | bytes 417800 | tf_op jit(solution)/shard_map/ppermute | solution.py:26
  25.0 2.8 %collective-permute-done.refs_1_ = bf16[4,256,256]{2,1,0:T(8,128)(2,1)S(1)} collective-permute-done((bf16[4,256,256]{2,1,0:T(8,128)(2,1)}, bf16[4,256,256]{2,1,0:T(8,128)(2,1)S(1)}, u32[]{:S(2)}, u32[]{:S(2)}) %collective-permute-start) | collective-permute-done | bytes 524320 | tf_op jit(solution)/shard_map/ppermute | solution.py:32
  27.8 0.8 copy-done
  28.6 2.6 %shard_map.119 = (bf16[272,256]{1,0:T(8,128)(2,1)}, bf16[272,256]{1,0:T(8,128)(2,1)}, bf16[272,256]{1,0:T(8,128)(2,1)}, bf16[272,256]{1,0:T(8,128)(2,1)}) custom-call(bf16[1,512,256]{2,1,0:T(8,128)(2,1)} %bitcast.2, f32[1,7,256]{2,1,0:T(8,128)} %copy.14.coef_ref, s32[1,7,256]{2,1,0:T(8,128)} %copy.15.target_ref, bf16[4,256,256]{2,1,0:T(8,128)(2,1)} %shard_map.118.refs_0_, ...), custom_call_target="tpu_custom_call" | custom-call | flops 268435456 | bytes 1835008 | tf_op jit(solution)/shard_map/pallas_call | solution.py:146
  31.2 1.3 collective-permute-start.1
  32.5 4.3 %collective-permute-start.2 = (bf16[272,256]{1,0:T(8,128)(2,1)}, bf16[272,256]{1,0:T(8,128)(2,1)S(1)}, u32[]{:S(2)}, u32[]{:S(2)}) collective-permute-start(bf16[272,256]{1,0:T(8,128)(2,1)} %get-tuple-element.19), channel_id=1, source_target_pairs={{0,5},{1,8},{4,9},{5,12},{8,13},{2,7},{3,10},{6,11},{7,14},{10,15}... | collective-permute-start | bytes 417800 | tf_op jit(solution)/shard_map/ppermute | solution.py:26
  36.8 1.3 collective-permute-start.3
  38.1 0.0 collective-permute-done.6.refs_4_
  38.1 0.0 copy-start.7
  38.1 4.6 %collective-permute-start.4 = (bf16[272,256]{1,0:T(8,128)(2,1)}, bf16[272,256]{1,0:T(8,128)(2,1)S(1)}, u32[]{:S(2)}, u32[]{:S(2)}) collective-permute-start(bf16[272,256]{1,0:T(8,128)(2,1)} %get-tuple-element.21), channel_id=1, source_target_pairs={{0,4},{1,5},{4,8},{5,9},{8,12},{9,13},{2,6},{3,7},{6,10},{7,11},{1... | collective-permute-start | bytes 417800 | tf_op jit(solution)/shard_map/ppermute | solution.py:26
  42.7 0.0 collective-permute-done.7.refs_5_
  42.7 0.0 copy-start.8
  42.7 0.0 collective-permute-done.1.refs_0_
  42.7 0.0 copy-start.9
  42.7 0.0 collective-permute-done.2.refs_1_
  42.7 0.0 copy-start.10
  42.7 2.4 %collective-permute-done.3.refs_2_ = bf16[272,256]{1,0:T(8,128)(2,1)S(1)} collective-permute-done((bf16[272,256]{1,0:T(8,128)(2,1)}, bf16[272,256]{1,0:T(8,128)(2,1)S(1)}, u32[]{:S(2)}, u32[]{:S(2)}) %collective-permute-start.3) | collective-permute-done | bytes 139296 | tf_op jit(solution)/shard_map/ppermute | solution.py:26
  45.2 1.8 %collective-permute-done.4.refs_3_ = bf16[272,256]{1,0:T(8,128)(2,1)S(1)} collective-permute-done((bf16[272,256]{1,0:T(8,128)(2,1)}, bf16[272,256]{1,0:T(8,128)(2,1)S(1)}, u32[]{:S(2)}, u32[]{:S(2)}) %collective-permute-start.4) | collective-permute-done | bytes 139296 | tf_op jit(solution)/shard_map/ppermute | solution.py:26
  47.0 0.0 copy-done.7
  47.0 0.0 copy-done.8
  47.0 0.6 copy-done.12
  47.6 2.8 %shard_map.122.refs_0_.state_ref = bf16[640,256]{1,0:T(8,128)(2,1)} custom-call(bf16[640,256]{1,0:T(8,128)(2,1)} %latent_ref.1, bf16[272,256]{1,0:T(8,128)(2,1)} %copy-done.9, bf16[272,256]{1,0:T(8,128)(2,1)} %copy-done.10, bf16[272,256]{1,0:T(8,128)(2,1)} %copy-done.11, bf16[272,256]{1,0:T(8,128)(2,1)} %copy-done.12, bf16[272,256]{1,0:T(8,128)(2,1)} %copy-done.7, ...), custom_call_target="tpu_custom_call" | custom-call | flops 623902720 | bytes 1630208 | tf_op jit(solution)/shard_map/pallas_call | solution.py:180
  50.5 1.5 %collective-permute-start.8 = (bf16[640,256]{1,0:T(8,128)(2,1)}, bf16[640,256]{1,0:T(8,128)(2,1)S(1)}, u32[]{:S(2)}, u32[]{:S(2)}) collective-permute-start(bf16[640,256]{1,0:T(8,128)(2,1)} %shard_map.122.refs_0_.state_ref), channel_id=1, source_target_pairs={{0,2},{2,0},{1,3},{3,1},{4,6},{6,4},{5,7},{7,5},{8,10},{10,8},{9,1... | collective-permute-start | bytes 983048 | tf_op jit(solution)/shard_map/ppermute | solution.py:32
  52.0 0.6 copy.19.listed_ref
  52.6 7.8 %collective-permute-done.8.refs_1_ = bf16[640,256]{1,0:T(8,128)(2,1)S(1)} collective-permute-done((bf16[640,256]{1,0:T(8,128)(2,1)}, bf16[640,256]{1,0:T(8,128)(2,1)S(1)}, u32[]{:S(2)}, u32[]{:S(2)}) %collective-permute-start.8) | collective-permute-done | bytes 327712 | tf_op jit(solution)/shard_map/ppermute | solution.py:32
  60.4 0.7 copy-done.2
  61.1 3.5 %shard_map.123 = (bf16[640,256]{1,0:T(8,128)(2,1)}, bf16[640,256]{1,0:T(8,128)(2,1)}, bf16[8,64,256]{2,1,0:T(8,128)(2,1)}) custom-call(bf16[2,512,256]{2,1,0:T(8,128)(2,1)} %src_ref.3, bf16[2,512,256]{2,1,0:T(8,128)(2,1)} %dst_ref.3, s32[1,6,64]{2,1,0:T(8,128)} %copy.19.listed_ref, bf16[640,256]{1,0:T(8,128)(2,1)} %shard_map.122.refs_0_.state_ref, ...), custom_call_target="tpu_custom_call" | custom-call | flops 461373440 | bytes 2097152 | tf_op jit(solution)/shard_map/pallas_call | solution.py:228
  64.7 13.8 %all_to_all.10.got_ref = bf16[8,64,256]{2,1,0:T(8,128)(2,1)} all-to-all(bf16[8,64,256]{2,1,0:T(8,128)(2,1)} %get-tuple-element.27), channel_id=1, replica_groups=mesh['groups'=2,'space'=4,'feat'=2,'edge'=2] {'space','edge'}, dimensions={0} | all-to-all | bytes 524288 | tf_op jit(solution)/shard_map/all_to_all | solution.py:330
  78.4 14.8 %shard_map.124.refs_0_.state_ref = bf16[640,256]{1,0:T(8,128)(2,1)} custom-call(s32[1,5120]{1,0:T(1,128)} %source_ref.3, s32[1,5120]{1,0:T(1,128)} %target_ref.5, f32[1,5120]{1,0:T(1,128)} %coef_ref.5, bf16[640,256]{1,0:T(8,128)(2,1)} %shard_map.122.refs_0_.state_ref, bf16[640,256]{1,0:T(8,128)(2,1)} %get-tuple-element.25.sender_ref, ...), custom_call_target="tpu_custom_call" | custom-call | flops 6039797760 | bytes 1507328 | tf_op jit(solution)/shard_map/pallas_call | solution.py:281
  93.2 1.2 collective-permute-start.9
  94.4 8.1 %collective-permute-done.9.refs_1_ = bf16[640,256]{1,0:T(8,128)(2,1)S(1)} collective-permute-done((bf16[640,256]{1,0:T(8,128)(2,1)}, bf16[640,256]{1,0:T(8,128)(2,1)S(1)}, u32[]{:S(2)}, u32[]{:S(2)}) %collective-permute-start.9) | collective-permute-done | bytes 327712 | tf_op jit(solution)/shard_map/ppermute | solution.py:32
  102.5 0.7 copy-done.3
  103.2 3.5 %shard_map.125 = (bf16[640,256]{1,0:T(8,128)(2,1)}, bf16[640,256]{1,0:T(8,128)(2,1)}, bf16[8,64,256]{2,1,0:T(8,128)(2,1)}) custom-call(bf16[2,512,256]{2,1,0:T(8,128)(2,1)} %src_ref.3, bf16[2,512,256]{2,1,0:T(8,128)(2,1)} %dst_ref.3, s32[1,6,64]{2,1,0:T(8,128)} %copy.19.listed_ref, bf16[640,256]{1,0:T(8,128)(2,1)} %shard_map.124.refs_0_.state_ref, ...), custom_call_target="tpu_custom_call" | custom-call | flops 461373440 | bytes 2097152 | tf_op jit(solution)/shard_map/pallas_call | solution.py:228
  106.7 13.8 %all_to_all.11.got_ref = bf16[8,64,256]{2,1,0:T(8,128)(2,1)} all-to-all(bf16[8,64,256]{2,1,0:T(8,128)(2,1)} %get-tuple-element.30), channel_id=1, replica_groups=mesh['groups'=2,'space'=4,'feat'=2,'edge'=2] {'space','edge'}, dimensions={0} | all-to-all | bytes 524288 | tf_op jit(solution)/shard_map/all_to_all | solution.py:330
  120.5 14.8 %shard_map.126 = bf16[640,256]{1,0:T(8,128)(2,1)} custom-call(s32[1,5120]{1,0:T(1,128)} %source_ref.3, s32[1,5120]{1,0:T(1,128)} %target_ref.5, f32[1,5120]{1,0:T(1,128)} %coef_ref.5, bf16[640,256]{1,0:T(8,128)(2,1)} %shard_map.124.refs_0_.state_ref, bf16[640,256]{1,0:T(8,128)(2,1)} %get-tuple-element.28.sender_ref, ...), custom_call_target="tpu_custom_call" | custom-call | flops 6039797760 | bytes 1507328 | tf_op jit(solution)/shard_map/pallas_call | solution.py:281
  (13 shorter events, 0.0 us)
Async XLA Ops:
  4.3 6.3 %copy-start.4 = (f32[1,7,256]{2,0,1:T(1,128)S(1)}, f32[1,7,256]{2,0,1:T(1,128)}, u32[]{:S(2)}) copy-start(f32[1,7,256]{2,0,1:T(1,128)} %param.17) | copy-start | bytes 21508
  4.3 13.1 %collective-permute-start.5 = (bf16[3,256,256]{2,1,0:T(8,128)(2,1)}, bf16[3,256,256]{2,1,0:T(8,128)(2,1)S(1)}, u32[]{:S(2)}, u32[]{:S(2)}) collective-permute-start(bf16[3,256,256]{2,1,0:T(8,128)(2,1)} %shard_map.120.refs_0_), channel_id=1, source_target_pairs={{0,2},{2,0},{1,3},{3,1},{4,6},{6,4},{5,7},{7,5},{8,10},{10,8},{9,1... | collective-permute-start | bytes 1179656 | tf_op jit(solution)/shard_map/ppermute | solution.py:32
  10.6 0.7 copy-start.5
  10.6 17.2 %collective-permute-start = (bf16[4,256,256]{2,1,0:T(8,128)(2,1)}, bf16[4,256,256]{2,1,0:T(8,128)(2,1)S(1)}, u32[]{:S(2)}, u32[]{:S(2)}) collective-permute-start(bf16[4,256,256]{2,1,0:T(8,128)(2,1)} %shard_map.118.refs_0_), channel_id=1, source_target_pairs={{0,2},{2,0},{1,3},{3,1},{4,6},{6,4},{5,7},{7,5},{8,10},{10,8},{9,1... | collective-permute-start | bytes 1572872 | tf_op jit(solution)/shard_map/ppermute | solution.py:32
  17.4 0.8 copy-start.1
  20.6 17.4 %collective-permute-start.6 = (bf16[272,256]{1,0:T(8,128)(2,1)}, bf16[272,256]{1,0:T(8,128)(2,1)S(1)}, u32[]{:S(2)}, u32[]{:S(2)}) collective-permute-start(bf16[272,256]{1,0:T(8,128)(2,1)} %get-tuple-element.22), channel_id=1, source_target_pairs={{1,0},{4,1},{5,4},{8,5},{9,8},{12,9},{13,12},{3,2},{6,3},{7,6},{10... | collective-permute-start | bytes 417800 | tf_op jit(solution)/shard_map/ppermute | solution.py:26
  21.9 20.7 %collective-permute-start.7 = (bf16[272,256]{1,0:T(8,128)(2,1)}, bf16[272,256]{1,0:T(8,128)(2,1)S(1)}, u32[]{:S(2)}, u32[]{:S(2)}) collective-permute-start(bf16[272,256]{1,0:T(8,128)(2,1)} %get-tuple-element.23), channel_id=1, source_target_pairs={{0,1},{1,4},{4,5},{5,8},{8,9},{9,12},{12,13},{2,3},{3,6},{6,7},{7,... | collective-permute-start | bytes 417800 | tf_op jit(solution)/shard_map/ppermute | solution.py:26
  27.8 0.8 copy-start
  31.2 11.5 %collective-permute-start.1 = (bf16[272,256]{1,0:T(8,128)(2,1)}, bf16[272,256]{1,0:T(8,128)(2,1)S(1)}, u32[]{:S(2)}, u32[]{:S(2)}) collective-permute-start(bf16[272,256]{1,0:T(8,128)(2,1)} %get-tuple-element.18), channel_id=1, source_target_pairs={{5,0},{8,1},{9,4},{12,5},{13,8},{7,2},{10,3},{11,6},{14,7},{15,10}... | collective-permute-start | bytes 417800 | tf_op jit(solution)/shard_map/ppermute | solution.py:26
  32.5 10.2 %collective-permute-start.2 = (bf16[272,256]{1,0:T(8,128)(2,1)}, bf16[272,256]{1,0:T(8,128)(2,1)S(1)}, u32[]{:S(2)}, u32[]{:S(2)}) collective-permute-start(bf16[272,256]{1,0:T(8,128)(2,1)} %get-tuple-element.19), channel_id=1, source_target_pairs={{0,5},{1,8},{4,9},{5,12},{8,13},{2,7},{3,10},{6,11},{7,14},{10,15}... | collective-permute-start | bytes 417800 | tf_op jit(solution)/shard_map/ppermute | solution.py:26
  36.8 8.4 %collective-permute-start.3 = (bf16[272,256]{1,0:T(8,128)(2,1)}, bf16[272,256]{1,0:T(8,128)(2,1)S(1)}, u32[]{:S(2)}, u32[]{:S(2)}) collective-permute-start(bf16[272,256]{1,0:T(8,128)(2,1)} %get-tuple-element.20), channel_id=1, source_target_pairs={{4,0},{5,1},{8,4},{9,5},{12,8},{13,9},{6,2},{7,3},{10,6},{11,7},{1... | collective-permute-start | bytes 417800 | tf_op jit(solution)/shard_map/ppermute | solution.py:26
  38.1 8.9 %copy-start.7 = (bf16[272,256]{1,0:T(8,128)(2,1)}, bf16[272,256]{1,0:T(8,128)(2,1)S(1)}, u32[]{:S(2)}) copy-start(bf16[272,256]{1,0:T(8,128)(2,1)S(1)} %collective-permute-done.6.refs_4_) | copy-start | bytes 417796
  38.1 8.9 %collective-permute-start.4 = (bf16[272,256]{1,0:T(8,128)(2,1)}, bf16[272,256]{1,0:T(8,128)(2,1)S(1)}, u32[]{:S(2)}, u32[]{:S(2)}) collective-permute-start(bf16[272,256]{1,0:T(8,128)(2,1)} %get-tuple-element.21), channel_id=1, source_target_pairs={{0,4},{1,5},{4,8},{5,9},{8,12},{9,13},{2,6},{3,7},{6,10},{7,11},{1... | collective-permute-start | bytes 417800 | tf_op jit(solution)/shard_map/ppermute | solution.py:26
  42.7 4.3 %copy-start.8 = (bf16[272,256]{1,0:T(8,128)(2,1)}, bf16[272,256]{1,0:T(8,128)(2,1)S(1)}, u32[]{:S(2)}) copy-start(bf16[272,256]{1,0:T(8,128)(2,1)S(1)} %collective-permute-done.7.refs_5_) | copy-start | bytes 417796
  42.7 4.3 %copy-start.9 = (bf16[272,256]{1,0:T(8,128)(2,1)}, bf16[272,256]{1,0:T(8,128)(2,1)S(1)}, u32[]{:S(2)}) copy-start(bf16[272,256]{1,0:T(8,128)(2,1)S(1)} %collective-permute-done.1.refs_0_) | copy-start | bytes 417796
  42.7 4.3 %copy-start.10 = (bf16[272,256]{1,0:T(8,128)(2,1)}, bf16[272,256]{1,0:T(8,128)(2,1)S(1)}, u32[]{:S(2)}) copy-start(bf16[272,256]{1,0:T(8,128)(2,1)S(1)} %collective-permute-done.2.refs_1_) | copy-start | bytes 417796
  45.2 1.9 %copy-start.11 = (bf16[272,256]{1,0:T(8,128)(2,1)}, bf16[272,256]{1,0:T(8,128)(2,1)S(1)}, u32[]{:S(2)}) copy-start(bf16[272,256]{1,0:T(8,128)(2,1)S(1)} %collective-permute-done.3.refs_2_) | copy-start | bytes 417796
  47.0 0.7 copy-start.12
  47.6 4.3 %copy-start.6 = (s32[1,6,64]{2,0,1:T(1,128)S(1)}, s32[1,6,64]{2,0,1:T(1,128)}, u32[]{:S(2)}) copy-start(s32[1,6,64]{2,0,1:T(1,128)} %param.20) | copy-start | bytes 4612
  50.5 9.9 %collective-permute-start.8 = (bf16[640,256]{1,0:T(8,128)(2,1)}, bf16[640,256]{1,0:T(8,128)(2,1)S(1)}, u32[]{:S(2)}, u32[]{:S(2)}) collective-permute-start(bf16[640,256]{1,0:T(8,128)(2,1)} %shard_map.122.refs_0_.state_ref), channel_id=1, source_target_pairs={{0,2},{2,0},{1,3},{3,1},{4,6},{6,4},{5,7},{7,5},{8,10},{10,8},{9,1... | collective-permute-start | bytes 983048 | tf_op jit(solution)/shard_map/ppermute | solution.py:32
  60.4 0.7 copy-start.2
  93.2 9.3 %collective-permute-start.9 = (bf16[640,256]{1,0:T(8,128)(2,1)}, bf16[640,256]{1,0:T(8,128)(2,1)S(1)}, u32[]{:S(2)}, u32[]{:S(2)}) collective-permute-start(bf16[640,256]{1,0:T(8,128)(2,1)} %shard_map.124.refs_0_.state_ref), channel_id=1, source_target_pairs={{0,2},{2,0},{1,3},{3,1},{4,6},{6,4},{5,7},{7,5},{8,10},{10,8},{9,1... | collective-permute-start | bytes 983048 | tf_op jit(solution)/shard_map/ppermute | solution.py:32
  102.5 0.7 copy-start.3

commit v2 on v1

v2 whole, which is shorter than its diff:
```python
import functools

import jax
import jax.numpy as jnp
from jax import lax
from jax.experimental import pallas as pl
from jax.experimental.pallas import tpu as pltpu
from jax.sharding import PartitionSpec as P

REGION = ("space", "edge")
PAD = 16
VMEM_BYTES = 28 * 1024 * 1024


def made_in_vmem(output):
    return pltpu.VMEM(output.shape, output.dtype)


def taken_from_vmem(array):
    return pltpu.with_memory_space_constraint(array, pltpu.VMEM)


def call(kernel, outputs, inputs, flops, transcendentals=0, scratch=(), final=False):
    size = lambda a: int(a.size) * a.dtype.itemsize
    shapes = outputs if final else [made_in_vmem(o) for o in outputs]
    return pl.pallas_call(
        kernel,
        out_shape=shapes,
        in_specs=[pl.BlockSpec(memory_space=pltpu.VMEM)] * len(inputs),
        out_specs=[pl.BlockSpec(memory_space=pltpu.VMEM)] * len(outputs),
        scratch_shapes=list(scratch),
        compiler_params=pltpu.CompilerParams(vmem_limit_bytes=VMEM_BYTES),
        cost_estimate=pl.CostEstimate(
            flops=flops,
            bytes_accessed=sum(size(a) for a in list(inputs) + list(outputs)),
            transcendentals=transcendentals,
        ),
    )(*[taken_from_vmem(a) for a in inputs])


def shape(dims, dtype=jnp.bfloat16):
    return jax.ShapeDtypeStruct(dims, dtype)


def passed_along(value, steps):
    count = lax.axis_size(REGION)
    first, last = (max(0, -steps), min(count, count - steps))
    return lax.ppermute(value, REGION, [(i, i + steps) for i in range(first, last)])


def from_others(value):
    n = lax.axis_size("feat")
    return [
        lax.ppermute(value, "feat", [(i, (i + k) % n) for i in range(n)]) for k in range(1, n)
    ]


def own_and_others_rows(weight_ref, channels, others):
    n = others + 1
    me = lax.axis_index("feat")
    blocks = []
    for k in range(n):
        owner = lax.rem(me - k + n, n)
        start = pl.multiple_of(owner * channels, channels)
        blocks.append(weight_ref[pl.ds(start, channels), :])
    return blocks


def silu(v):
    half = 0.5 * v
    return half + half * jnp.tanh(half)


def column(row):
    length = row.shape[1]
    parts = [
        jnp.broadcast_to(row[:, c * 128 : (c + 1) * 128], (128, 128)).T for c in range(length // 128)
    ]
    return parts[0] if len(parts) == 1 else jnp.concatenate(parts, axis=0)


def lane_iota(count):
    return lax.broadcasted_iota(jnp.int32, (16, count), 1).astype(jnp.int16)


def row_iota(count):
    return lax.broadcasted_iota(jnp.int32, (count, 128), 0).astype(jnp.int16)


def tiled(value, rows, lanes):
    if value.shape[0] != rows:
        value = jnp.concatenate([value] * (rows // value.shape[0]), axis=0)
    if value.shape[1] != lanes:
        value = jnp.concatenate([value] * (lanes // value.shape[1]), axis=1)
    return value


def pick_mask(column16, lane16):
    rows, lanes = (column16.shape[0], lane16.shape[1])
    same = tiled(column16, rows, lanes) == tiled(lane16, rows, lanes)
    return jnp.where(same, jnp.bfloat16(1), jnp.bfloat16(0))


def sum_mask(row, rows16, scale=None):
    count, length = (rows16.shape[0], row.shape[1])
    targets = jnp.broadcast_to(row, (16, length)).astype(jnp.int16)
    same = tiled(rows16, count, length) == tiled(targets, count, length)
    if scale is None:
        here = jnp.bfloat16(1)
    else:
        here = tiled(jnp.broadcast_to(scale, (16, length)).astype(jnp.bfloat16), count, length)
    return jnp.where(same, here, jnp.bfloat16(0))


def dot(a, b):
    return jnp.dot(a, b, preferred_element_type=jnp.float32)


def pick_kernel(orders, index_ref, table_ref, *out_refs):
    lanes = lane_iota(table_ref.shape[0])
    for order, out_ref in zip(orders, out_refs):
        for place, j in enumerate(order):
            col = column(index_ref[j]).astype(jnp.int16)
            out_ref[place] = dot(pick_mask(col, lanes), table_ref[...]).astype(jnp.bfloat16)


def pick(orders, g2m_src, grid_latent):
    capacity = g2m_src.shape[2]
    rows, channels = grid_latent.shape
    return call(
        functools.partial(pick_kernel, orders),
        [shape((len(order), capacity, channels)) for order in orders],
        [g2m_src, grid_latent],
        2 * sum(map(len, orders)) * capacity * rows * channels,
    )


def encode_kernel(order, others, weight_ref, coef_ref, target_ref, *refs):
    sources, outs = (refs[: others + 1], refs[-len(order) :])
    capacity, channels = sources[0].shape[1:]
    weights = own_and_others_rows(weight_ref, channels, others)
    line = lax.broadcasted_iota(jnp.int32, (PAD, channels), 0)
    pieces = capacity // channels
    for place, j in enumerate(order):
        projected = dot(sources[0][place], weights[0])
        for source, weight in zip(sources[1:], weights[1:]):
            projected += dot(source[place], weight)
        scale = tiled(column(coef_ref[j]), capacity, channels)
        outs[place][pl.ds(0, capacity), :] = (scale * silu(projected)).astype(jnp.bfloat16)
        target = target_ref[j]
        code = jnp.zeros((PAD, channels), jnp.float32)
        for number, part in enumerate((target >> 3, target & 7)):
            part = part.astype(jnp.float32)
            for piece in range(pieces):
                values = part[:, piece * channels : (piece + 1) * channels]
                code = jnp.where(line == number * pieces + piece, values, code)
        outs[place][pl.ds(capacity, PAD), :] = code.astype(jnp.bfloat16)


def encode(order, picked, arrived, enc_weight, g2m_coef, g2m_dst, after=()):
    count, capacity, channels = picked.shape
    return call(
        functools.partial(encode_kernel, order, len(arrived)),
        [shape((capacity + PAD, channels))] * count,
        [enc_weight, g2m_coef, g2m_dst, picked, *arrived, *after],
        2 * count * capacity * enc_weight.shape[0] * channels,
        count * capacity * channels,
    )


def gather_in_kernel(before_ref, *refs):
    blocks, out_ref = (refs[:-1], refs[-1])
    nodes, channels = before_ref.shape
    capacity = blocks[0].shape[0] - PAD
    rows16 = row_iota(nodes)
    pieces = capacity // channels
    total = before_ref[...].astype(jnp.float32)
    for block in blocks:
        code = block[pl.ds(capacity, PAD), :].astype(jnp.float32)
        lines = [code[i : i + 1, :] for i in range(2 * pieces)]
        upper = lines[0] if pieces == 1 else jnp.concatenate(lines[:pieces], axis=1)
        lower = lines[1] if pieces == 1 else jnp.concatenate(lines[pieces:], axis=1)
        target = (8.0 * upper + lower).astype(jnp.int32)
        total += dot(sum_mask(target, rows16), block[pl.ds(0, capacity), :])
    out_ref[...] = total.astype(out_ref.dtype)


def gather_in(before, blocks, dtype):
    nodes, channels = before.shape
    slots = len(blocks) * blocks[0].shape[0]
    return call(
        gather_in_kernel,
        [shape((nodes, channels), dtype)],
        [before, *blocks],
        2 * nodes * slots * channels,
    )[0]


def columns_kernel(*refs):
    half = len(refs) // 2
    for row_ref, out_ref in zip(refs[:half], refs[half:]):
        out_ref[...] = column(row_ref[...]).astype(jnp.int16)


def columns(*rows):
    count = rows[0].shape[1]
    return call(
        columns_kernel, [shape((count, 128), jnp.int16)] * len(rows), rows, len(rows) * count * 128 * 8
    )


def project_kernel(
    others, reach, src_ref, dst_ref, listed_ref, *refs
):
    states, (sender_ref, receiver_ref, up_ref, down_ref, far_ref, near_ref) = (
        refs[: others + 1],
        refs[others + 1 :],
    )
    nodes, channels = states[0].shape
    for weight_ref, out_ref in ((src_ref, sender_ref), (dst_ref, receiver_ref)):
        weights = own_and_others_rows(weight_ref, channels, others)
        total = dot(states[0][...], weights[0])
        for state, weight in zip(states[1:], weights[1:]):
            total += dot(state[...], weight)
        out_ref[...] = total.astype(jnp.bfloat16)
    width = listed_ref.shape[2]
    lanes = lane_iota(nodes)
    core = lax.axis_index("edge")
    wanted = [2 - core, 3 - core, -2 - core, -1 - core, 6 * core - 3, 1 - 2 * core]
    wanted = [offset + reach - jnp.where(offset > 0, 1, 0) for offset in wanted]
    for k in range(0, len(wanted), 2):
        row = jnp.concatenate([listed_ref[wanted[k + i]] for i in range(2)], axis=1)
        rows = dot(pick_mask(column(row).astype(jnp.int16), lanes), sender_ref[...])
        rows = rows.astype(jnp.bfloat16)
        for i in range(2):
            part = rows[i * width : (i + 1) * width]
            if k == 0:
                up_ref[i] = part
            elif k == 2:
                down_ref[i] = part
            elif i == 0:
                far_ref[...] = part
            else:
                near_ref[...] = part


def project(state, arrived, src_weight, dst_weight, halo_send, reach):
    nodes, channels = state.shape
    links, unused, width = halo_send.shape
    depth = src_weight.shape[0]
    table, one, two = [shape(d) for d in ((nodes, channels), (width, channels), (2, width, channels))]
    return call(
        functools.partial(project_kernel, len(arrived), reach),
        [table, table, two, two, one, one],
        [src_weight, dst_weight, halo_send, state, *arrived],
        4 * nodes * depth * channels + 2 * links * width * nodes * channels,
    )


def forward_kernel(near_ref, from_below_ref, from_above_ref, out_ref):
    other = 1 - lax.axis_index("edge")
    out_ref[0] = near_ref[...]
    out_ref[1] = from_below_ref[other]
    out_ref[2] = from_above_ref[other]


def listed_rows(up, down, far, near):
    count = lax.axis_size(REGION)
    below = lax.ppermute(up, REGION, [(i, i + 2) for i in range(count - 2)])
    above = lax.ppermute(down, REGION, [(i, i - 2) for i in range(2, count)])
    odd = [(i, i + 3) for i in range(1, count - 3, 2)]
    even = [(i, i - 3) for i in range(4, count, 2)]
    distant = lax.ppermute(far, REGION, odd + even)
    width, channels = near.shape
    sent = call(forward_kernel, [shape((3, width, channels))], [near, below, above], 0)[0]
    across = lax.ppermute(sent, "edge", [(0, 1), (1, 0)])
    return below, above, distant, across


def first_kernel(turn, source_ref, target_ref, sender_ref, receiver_ref, out_ref):
    nodes = sender_ref.shape[0]
    lanes = lane_iota(nodes)
    for start in range(0, source_ref.shape[0], turn):
        here = pl.ds(start, turn)
        out_ref[here, :] = dot(pick_mask(source_ref[here, :], lanes), sender_ref[...]) + dot(
            pick_mask(target_ref[here, :], lanes), receiver_ref[...]
        )


def first_part(source_col, target_col, sender, receiver):
    nodes, channels = sender.shape
    edges = source_col.shape[0]
    return call(
        functools.partial(first_kernel, 512),
        [shape((edges, channels), jnp.float32)],
        [source_col, target_col, sender, receiver],
        4 * edges * nodes * channels,
    )[0]


def message_kernel(
    turn, source_ref, target_ref, coef_ref, state_ref, first_ref, below_ref, above_ref, distant_ref, across_ref,
    out_ref, table_ref,
):
    nodes, channels = state_ref.shape
    width = distant_ref.shape[0]
    core = lax.axis_index("edge")
    own_below, own_above = (below_ref[core], above_ref[core])
    even = core == 0
    rows = (
        jnp.where(even, across_ref[2], distant_ref[...]),
        own_above,
        jnp.where(even, across_ref[0], across_ref[2]),
        jnp.where(even, across_ref[1], across_ref[0]),
        own_below,
        jnp.where(even, distant_ref[...], across_ref[1]),
    )
    for j, part in enumerate(rows):
        table_ref[pl.ds(j * width, width), :] = part
    lanes = (lane_iota(len(rows) * width).astype(jnp.int32) + nodes).astype(jnp.int16)
    rows16 = row_iota(nodes)
    total = state_ref[...].astype(jnp.float32)
    for start in range(0, source_ref.shape[0], turn):
        here = pl.ds(start, turn)
        summed = first_ref[here, :] + dot(pick_mask(source_ref[here, :], lanes), table_ref[...])
        mask = sum_mask(target_ref[:, here], rows16, coef_ref[:, here])
        total += dot(mask, silu(summed).astype(jnp.bfloat16))
    out_ref[...] = total.astype(jnp.bfloat16)


def messages(source_col, m2m_dst, m2m_coef, state, first, listed, final):
    nodes, channels = state.shape
    edges = m2m_dst.shape[1]
    named = 6 * listed[2].shape[0]
    return call(
        functools.partial(message_kernel, 512),
        [shape((nodes, channels))],
        [source_col, m2m_dst, m2m_coef, state, first, *listed],
        2 * edges * (named + nodes) * channels,
        edges * channels,
        [pltpu.VMEM((named, channels), jnp.bfloat16)],
        final,
    )[0]


def on_device(
    grid_latent,
    enc_weight,
    mesh_latent,
    g2m_src,
    g2m_dst,
    g2m_coef,
    src_weights,
    dst_weights,
    halo_send,
    m2m_src,
    m2m_dst,
    m2m_coef,
):
    reach = (g2m_src.shape[1] - 1) // 2
    assert reach == 3 and lax.axis_size("edge") == 2
    g2m_src, g2m_dst, g2m_coef, halo_send = [
        jnp.swapaxes(a, 0, 1) for a in (g2m_src, g2m_dst, g2m_coef, halo_send)
    ]
    groups = [(reach - d, reach + d) for d in range(reach, 0, -1)] + [(reach,)]
    picked = pick(groups[:1], g2m_src, grid_latent) + pick(groups[1:], g2m_src, grid_latent)
    arrived = [from_others(rows) for rows in picked]
    source_col, target_col = columns(m2m_src, m2m_dst)
    blocks = []
    for order, rows, others in zip(groups, picked, arrived):
        after = () if blocks else (source_col, target_col)
        encoded = encode(order, rows, others, enc_weight, g2m_coef, g2m_dst, after)
        for j, block in zip(order, encoded):
            blocks.append(block if j == reach else passed_along(block, j - reach))
    state = gather_in(mesh_latent, blocks[:4], jnp.float32)
    state = gather_in(state, blocks[4:], jnp.bfloat16)
    layers = src_weights.shape[0]
    for layer in range(layers):
        sender, receiver, *sent = project(
            state, from_others(state), src_weights[layer], dst_weights[layer], halo_send, reach
        )
        listed = listed_rows(*sent)
        first = first_part(source_col, target_col, sender, receiver)
        state = messages(source_col, m2m_dst, m2m_coef, state, first, listed, layer == layers - 1)
    return state


def solution(mesh):
    placed = (
        P(("groups", "space", "edge"), "feat"),
        P(None, "feat"),
        P(("groups", "space", "edge"), "feat"),
        P(("groups", "space", "edge"), None, None),
        P(("groups", "space", "edge"), None, None),
        P(("groups", "space", "edge"), None, None),
        P(None, None, "feat"),
        P(None, None, "feat"),
        P(("groups", "space", "edge"), None, None),
        P(("groups", "space", "edge"), None),
        P(("groups", "space", "edge"), None),
        P(("groups", "space", "edge"), None),
    )
    return jax.shard_map(
        on_device,
        mesh=mesh,
        in_specs=placed,
        out_specs=P(("groups", "space", "edge"), "feat"),
        check_vma=False,
    )
```

time: 136 us -> 94.5 us (0.69)
  blocking collectives: 27.5 us -> 0 us
  Pallas kernels: 50.8 us -> 25.2 us
  starting transfers between devices: 21.4 us -> 37.9 us
  local copies, waits for them, and re-layouts: 6.85 us -> 2.07 us
    all_to_all x2 -> x0, blocking collectives: 27.5 us -> none  [on_device(): got = lax.all_to_all(sent, REGION, 0, 0, tiled=True)]
    pallas_call x9 -> x17, Pallas kernels: 50.8 us -> 25.2 us  [call(): pl.pallas_call(kernel, out_shape=shapes, in_specs=[pl.BlockSpec(memory_sp...]
    ppermute x0 -> x8, starting transfers between devices: none -> 12.6 us  [the longest x2 8.33 us: listed_rows(): below = lax.ppermute(up, REGION, [(i, i + 2) for i in range(count - 2)])]
    ppermute x0 -> x8, waiting for transfers between devices: none -> 8.19 us  [the longest x2 8.18 us: listed_rows(): above = lax.ppermute(down, REGION, [(i, i - 2) for i in range(2, count)])]
    unnamed x30 -> x24, local copies, waits for them, and re-layouts: 6.85 us -> 2.01 us
    ppermute x4 -> x6, starting transfers between devices: 5.65 us -> 10.3 us  [from_others(): lax.ppermute(value, 'feat', [(i, (i + k) % n) for i in range(n)])]
    ppermute x4 -> x6, waiting for transfers between devices: 24.3 us -> 20.1 us  [from_others(): lax.ppermute(value, 'feat', [(i, (i + k) % n) for i in range(n)])]
    ppermute x6, waiting for transfers between devices: 4.28 us -> 0.16 us  [passed_along(): lax.ppermute(value, REGION, [(i, i + steps) for i in range(first, last)])]
  transfers between devices with their start and end apart: 10 -> 20, of which waited for: 6 -> 7; matrix products, arithmetic and copies ran while one was open for 1% -> 0% of each run, Pallas kernels for 6% -> 14%
where the time goes in v2:
time: 94.5 us; the launch traced here: 94 us
  starting transfers between devices  37.9 us (40%)
  waiting for transfers between devices  28.5 us (30%)
  Pallas kernels  25.2 us (27%)
  local copies, waits for them, and re-layouts  2.07 us (2%)
    pallas_call x17, Pallas kernels, call(): pl.pallas_call(kernel, out_shape=shapes, in_specs=[pl.BlockSpec(memory_sp...  25.2 us
    ppermute x6, waiting for transfers between devices, from_others(): lax.ppermute(value, 'feat', [(i, (i + k) % n) for i in range(n)])  20.1 us
    ppermute x6, starting transfers between devices, passed_along(): lax.ppermute(value, REGION, [(i, i + steps) for i in range(first, last)])  14.9 us
    ppermute x6, starting transfers between devices, from_others(): lax.ppermute(value, 'feat', [(i, (i + k) % n) for i in range(n)])  10.3 us
    ppermute x2, starting transfers between devices, listed_rows(): below = lax.ppermute(up, REGION, [(i, i + 2) for i in range(count - 2)])  8.33 us
    ppermute x2, waiting for transfers between devices, listed_rows(): above = lax.ppermute(down, REGION, [(i, i - 2) for i in range(2, count)])  8.18 us
    ppermute x2, starting transfers between devices, listed_rows(): above = lax.ppermute(down, REGION, [(i, i - 2) for i in range(2, count)])  2.58 us
    unnamed x24, local copies, waits for them, and re-layouts  2.01 us
  transfers between devices with their start and end apart: 20, of which 7 were waited for; matrix products, arithmetic and copies ran while one was open for 0% of the time, Pallas kernels for 14%

profile of v2, /device:TPU:0, one launch (start us, length us, event | category | flops | bytes accessed | tf_op | source)
XLA Modules:
  0.0 94.0 jit_solution(5377341162239550885)
XLA Ops:
  0.0 1.3 %copy-done.6 = bf16[2048,256]{1,0:T(8,128)(2,1)S(1)} copy-done((bf16[2048,256]{1,0:T(8,128)(2,1)S(1)}, bf16[2048,256]{1,0:T(8,128)(2,1)}, u32[]{:S(2)}) %copy-start.6) | copy-done | bytes 1048600
  1.3 0.7 copy-done.8
  2.0 0.7 shard_map.119.refs_0_
  2.7 0.0 copy-start.1
  2.7 3.0 %collective-permute-start = (bf16[2,256,256]{2,1,0:T(8,128)(2,1)S(1)}, bf16[2,256,256]{2,1,0:T(8,128)(2,1)S(1)}, u32[]{:S(2)}, u32[]{:S(2)}) collective-permute-start(bf16[2,256,256]{2,1,0:T(8,128)(2,1)S(1)} %shard_map.119.refs_0_), channel_id=1, source_target_pairs={{0,2},{2,0},{1,3},{3,1},{4,6},{6,4},{5,7},{7,5},{8,10},{10,8},{9,1... | collective-permute-start | bytes 786440 | tf_op jit(solution)/shard_map/ppermute | solution.py:54
  5.8 1.5 %shard_map.121 = (bf16[2,256,256]{2,1,0:T(8,128)(2,1)S(1)}, bf16[2,256,256]{2,1,0:T(8,128)(2,1)S(1)}, bf16[1,256,256]{2,1,0:T(8,128)(2,1)S(1)}) custom-call(s32[7,1,256]{2,1,0:T(1,128)S(1)} %bitcast.21, bf16[2048,256]{1,0:T(8,128)(2,1)S(1)} %copy-done.6), custom_call_target="tpu_custom_call" | custom-call | flops 1342177280 | bytes 1711104 | tf_op jit(solution)/shard_map/pallas_call | solution.py:26
  7.3 0.0 copy-start.10
  7.3 0.0 copy-start.11
  7.3 0.1 collective-permute-start.3
  7.4 2.0 %collective-permute-start.6 = (bf16[2,256,256]{2,1,0:T(8,128)(2,1)S(1)}, bf16[2,256,256]{2,1,0:T(8,128)(2,1)S(1)}, u32[]{:S(2)}, u32[]{:S(2)}) collective-permute-start(bf16[2,256,256]{2,1,0:T(8,128)(2,1)S(1)} %get-tuple-element.35.refs_0_), channel_id=1, source_target_pairs={{0,2},{2,0},{1,3},{3,1},{4,6},{6,4},{5,7},{7,5},{8,10},{10,8},{9,1... | collective-permute-start | bytes 786440 | tf_op jit(solution)/shard_map/ppermute | solution.py:54
  9.4 1.4 %shard_map.118 = (s16[5120,128]{1,0:T(8,128)(2,1)S(1)}, s16[5120,128]{1,0:T(8,128)(2,1)S(1)}) custom-call(s32[1,5120]{1,0:T(1,128)S(1)} %copy-done.4, s32[1,5120]{1,0:T(1,128)S(1)} %copy-done.5), custom_call_target="tpu_custom_call" | custom-call | flops 10485760 | bytes 2662400 | tf_op jit(solution)/shard_map/pallas_call | solution.py:26
  10.9 2.0 %collective-permute-done.refs_1_ = bf16[2,256,256]{2,1,0:T(8,128)(2,1)S(1)} collective-permute-done((bf16[2,256,256]{2,1,0:T(8,128)(2,1)S(1)}, bf16[2,256,256]{2,1,0:T(8,128)(2,1)S(1)}, u32[]{:S(2)}, u32[]{:S(2)}) %collective-permute-start) | collective-permute-done | bytes 262176 | tf_op jit(solution)/shard_map/ppermute | solution.py:54
  12.9 0.4 shard_map.120
  13.3 1.3 %collective-permute-start.1 = (bf16[272,256]{1,0:T(8,128)(2,1)S(1)}, bf16[272,256]{1,0:T(8,128)(2,1)S(1)}, u32[]{:S(2)}, u32[]{:S(2)}) collective-permute-start(bf16[272,256]{1,0:T(8,128)(2,1)S(1)} %get-tuple-element.30), channel_id=1, source_target_pairs={{5,0},{8,1},{9,4},{12,5},{13,8},{7,2},{10,3},{11,6},{14,7},{15,10}... | collective-permute-start | bytes 417800 | tf_op jit(solution)/shard_map/ppermute | solution.py:48
  14.6 2.1 %collective-permute-start.9 = (bf16[1,256,256]{2,1,0:T(8,128)(2,1)S(1)}, bf16[1,256,256]{2,1,0:T(8,128)(2,1)S(1)}, u32[]{:S(2)}, u32[]{:S(2)}) collective-permute-start(bf16[1,256,256]{2,1,0:T(8,128)(2,1)S(1)} %get-tuple-element.38.refs_0_), channel_id=1, source_target_pairs={{0,2},{2,0},{1,3},{3,1},{4,6},{6,4},{5,7},{7,5},{8,10},{10,8},{9,1... | collective-permute-start | bytes 393224 | tf_op jit(solution)/shard_map/ppermute | solution.py:54
  16.7 4.0 %collective-permute-start.2 = (bf16[272,256]{1,0:T(8,128)(2,1)S(1)}, bf16[272,256]{1,0:T(8,128)(2,1)S(1)}, u32[]{:S(2)}, u32[]{:S(2)}) collective-permute-start(bf16[272,256]{1,0:T(8,128)(2,1)S(1)} %get-tuple-element.31), channel_id=1, source_target_pairs={{0,5},{1,8},{4,9},{5,12},{8,13},{2,7},{3,10},{6,11},{7,14},{10,15}... | collective-permute-start | bytes 417800 | tf_op jit(solution)/shard_map/ppermute | solution.py:48
  20.7 0.4 shard_map.122
  21.1 1.3 %collective-permute-start.4 = (bf16[272,256]{1,0:T(8,128)(2,1)S(1)}, bf16[272,256]{1,0:T(8,128)(2,1)S(1)}, u32[]{:S(2)}, u32[]{:S(2)}) collective-permute-start(bf16[272,256]{1,0:T(8,128)(2,1)S(1)} %get-tuple-element.33), channel_id=1, source_target_pairs={{4,0},{5,1},{8,4},{9,5},{12,8},{13,9},{6,2},{7,3},{10,6},{11,7},{1... | collective-permute-start | bytes 417800 | tf_op jit(solution)/shard_map/ppermute | solution.py:48
  22.4 1.7 %collective-permute-done.6.refs_1_ = bf16[2,256,256]{2,1,0:T(8,128)(2,1)S(1)} collective-permute-done((bf16[2,256,256]{2,1,0:T(8,128)(2,1)S(1)}, bf16[2,256,256]{2,1,0:T(8,128)(2,1)S(1)}, u32[]{:S(2)}, u32[]{:S(2)}) %collective-permute-start.6) | collective-permute-done | bytes 262176 | tf_op jit(solution)/shard_map/ppermute | solution.py:54
  24.1 4.0 %collective-permute-start.5 = (bf16[272,256]{1,0:T(8,128)(2,1)S(1)}, bf16[272,256]{1,0:T(8,128)(2,1)S(1)}, u32[]{:S(2)}, u32[]{:S(2)}) collective-permute-start(bf16[272,256]{1,0:T(8,128)(2,1)S(1)} %get-tuple-element.34), channel_id=1, source_target_pairs={{0,4},{1,5},{4,8},{5,9},{8,12},{9,13},{2,6},{3,7},{6,10},{7,11},{1... | collective-permute-start | bytes 417800 | tf_op jit(solution)/shard_map/ppermute | solution.py:48
  28.2 0.4 shard_map.124
  28.6 1.3 %collective-permute-start.7 = (bf16[272,256]{1,0:T(8,128)(2,1)S(1)}, bf16[272,256]{1,0:T(8,128)(2,1)S(1)}, u32[]{:S(2)}, u32[]{:S(2)}) collective-permute-start(bf16[272,256]{1,0:T(8,128)(2,1)S(1)} %get-tuple-element.36), channel_id=1, source_target_pairs={{1,0},{4,1},{5,4},{8,5},{9,8},{12,9},{13,12},{3,2},{6,3},{7,6},{10... | collective-permute-start | bytes 417800 | tf_op jit(solution)/shard_map/ppermute | solution.py:48
  29.9 3.0 %collective-permute-start.8 = (bf16[272,256]{1,0:T(8,128)(2,1)S(1)}, bf16[272,256]{1,0:T(8,128)(2,1)S(1)}, u32[]{:S(2)}, u32[]{:S(2)}) collective-permute-start(bf16[272,256]{1,0:T(8,128)(2,1)S(1)} %get-tuple-element.37), channel_id=1, source_target_pairs={{0,1},{1,4},{4,5},{5,8},{8,9},{9,12},{12,13},{2,3},{3,6},{6,7},{7,... | collective-permute-start | bytes 417800 | tf_op jit(solution)/shard_map/ppermute | solution.py:48
  32.9 0.3 shard_map.125.refs_2_
  33.2 0.5 shard_map.123.before_ref
  33.8 0.1 collective-permute-done.8.refs_1_
  33.9 0.4 shard_map.126.refs_0_.state_ref
  34.3 1.6 %collective-permute-start.10 = (bf16[640,256]{1,0:T(8,128)(2,1)S(1)}, bf16[640,256]{1,0:T(8,128)(2,1)S(1)}, u32[]{:S(2)}, u32[]{:S(2)}) collective-permute-start(bf16[640,256]{1,0:T(8,128)(2,1)S(1)} %shard_map.126.refs_0_.state_ref), channel_id=1, source_target_pairs={{0,2},{2,0},{1,3},{3,1},{4,6},{6,4},{5,7},{7,5},{8,10},{10,8},{9,1... | collective-permute-start | bytes 983048 | tf_op jit(solution)/shard_map/ppermute | solution.py:54
  35.9 0.1 slice_bitcast_fusion
  36.0 7.7 %collective-permute-done.10.refs_1_ = bf16[640,256]{1,0:T(8,128)(2,1)S(1)} collective-permute-done((bf16[640,256]{1,0:T(8,128)(2,1)S(1)}, bf16[640,256]{1,0:T(8,128)(2,1)S(1)}, u32[]{:S(2)}, u32[]{:S(2)}) %collective-permute-start.10) | collective-permute-done | bytes 327712 | tf_op jit(solution)/shard_map/ppermute | solution.py:54
  43.7 0.7 shard_map.127
  44.4 6.0 %collective-permute-start.11 = (bf16[2,64,256]{2,1,0:T(8,128)(2,1)S(1)}, bf16[2,64,256]{2,1,0:T(8,128)(2,1)S(1)}, u32[]{:S(2)}, u32[]{:S(2)}) collective-permute-start(bf16[2,64,256]{2,1,0:T(8,128)(2,1)S(1)} %get-tuple-element.41), channel_id=1, source_target_pairs={{0,4},{1,5},{4,8},{5,9},{8,12},{9,13},{2,6},{3,7},{6,10},{7,11},{1... | collective-permute-start | bytes 196616 | tf_op jit(solution)/shard_map/ppermute | solution.py:269
  50.4 1.3 %collective-permute-start.12 = (bf16[2,64,256]{2,1,0:T(8,128)(2,1)S(1)}, bf16[2,64,256]{2,1,0:T(8,128)(2,1)S(1)}, u32[]{:S(2)}, u32[]{:S(2)}) collective-permute-start(bf16[2,64,256]{2,1,0:T(8,128)(2,1)S(1)} %get-tuple-element.42), channel_id=1, source_target_pairs={{4,0},{5,1},{8,4},{9,5},{12,8},{13,9},{6,2},{7,3},{10,6},{11,7},{1... | collective-permute-start | bytes 196616 | tf_op jit(solution)/shard_map/ppermute | solution.py:270
  51.7 0.7 collective-permute-start.13
  52.4 4.2 %collective-permute-done.12.from_above_ref.above_ref = bf16[2,64,256]{2,1,0:T(8,128)(2,1)S(1)} collective-permute-done((bf16[2,64,256]{2,1,0:T(8,128)(2,1)S(1)}, bf16[2,64,256]{2,1,0:T(8,128)(2,1)S(1)}, u32[]{:S(2)}, u32[]{:S(2)}) %collective-permute-start.12) | collective-permute-done | bytes 65568 | tf_op jit(solution)/shard_map/ppermute | solution.py:270
  56.6 0.1 collective-permute-start.14
  56.7 4.2 %shard_map.128.first_ref = f32[5120,256]{1,0:T(8,128)S(1)} custom-call(s16[5120,128]{1,0:T(8,128)(2,1)S(1)} %get-tuple-element.28.refs_2_.source_ref, s16[5120,128]{1,0:T(8,128)(2,1)S(1)} %get-tuple-element.29.refs_3_.target_ref, bf16[640,256]{1,0:T(8,128)(2,1)S(1)} %get-tuple-element.39.sender_ref, bf16[640,256]{1,0:T(8,128)(2,1)S(1)} %get-tuple-element.40.receiver_ref), custom_call_target="tpu_custom_call" | custom-call | flops 3355443200 | bytes 8519680 | tf_op jit(solution)/shard_map/pallas_call | solution.py:26
  61.0 4.3 %shard_map.130.refs_0_.state_ref = bf16[640,256]{1,0:T(8,128)(2,1)S(1)} custom-call(s16[5120,128]{1,0:T(8,128)(2,1)S(1)} %get-tuple-element.28.refs_2_.source_ref, s32[1,5120]{1,0:T(1,128)S(1)} %copy-done.5, f32[1,5120]{1,0:T(1,128)S(1)} %copy-done.7, bf16[640,256]{1,0:T(8,128)(2,1)S(1)} %shard_map.126.refs_0_.state_ref, ...), custom_call_target="tpu_custom_call" | custom-call | flops 2684354560 | bytes 7512064 | tf_op jit(solution)/shard_map/pallas_call | solution.py:26
  65.2 1.6 %collective-permute-start.15 = (bf16[640,256]{1,0:T(8,128)(2,1)S(1)}, bf16[640,256]{1,0:T(8,128)(2,1)S(1)}, u32[]{:S(2)}, u32[]{:S(2)}) collective-permute-start(bf16[640,256]{1,0:T(8,128)(2,1)S(1)} %shard_map.130.refs_0_.state_ref), channel_id=1, source_target_pairs={{0,2},{2,0},{1,3},{3,1},{4,6},{6,4},{5,7},{7,5},{8,10},{10,8},{9,1... | collective-permute-start | bytes 983048 | tf_op jit(solution)/shard_map/ppermute | solution.py:54
  66.8 8.6 %collective-permute-done.15.refs_1_ = bf16[640,256]{1,0:T(8,128)(2,1)S(1)} collective-permute-done((bf16[640,256]{1,0:T(8,128)(2,1)S(1)}, bf16[640,256]{1,0:T(8,128)(2,1)S(1)}, u32[]{:S(2)}, u32[]{:S(2)}) %collective-permute-start.15) | collective-permute-done | bytes 327712 | tf_op jit(solution)/shard_map/ppermute | solution.py:54
  75.4 0.7 shard_map.131
  76.1 2.3 %collective-permute-start.16 = (bf16[2,64,256]{2,1,0:T(8,128)(2,1)S(1)}, bf16[2,64,256]{2,1,0:T(8,128)(2,1)S(1)}, u32[]{:S(2)}, u32[]{:S(2)}) collective-permute-start(bf16[2,64,256]{2,1,0:T(8,128)(2,1)S(1)} %get-tuple-element.47), channel_id=1, source_target_pairs={{0,4},{1,5},{4,8},{5,9},{8,12},{9,13},{2,6},{3,7},{6,10},{7,11},{1... | collective-permute-start | bytes 196616 | tf_op jit(solution)/shard_map/ppermute | solution.py:269
  78.4 1.3 %collective-permute-start.17 = (bf16[2,64,256]{2,1,0:T(8,128)(2,1)S(1)}, bf16[2,64,256]{2,1,0:T(8,128)(2,1)S(1)}, u32[]{:S(2)}, u32[]{:S(2)}) collective-permute-start(bf16[2,64,256]{2,1,0:T(8,128)(2,1)S(1)} %get-tuple-element.48), channel_id=1, source_target_pairs={{4,0},{5,1},{8,4},{9,5},{12,8},{13,9},{6,2},{7,3},{10,6},{11,7},{1... | collective-permute-start | bytes 196616 | tf_op jit(solution)/shard_map/ppermute | solution.py:270
  79.7 0.8 collective-permute-start.18
  80.6 4.0 %collective-permute-done.17.from_above_ref.above_ref = bf16[2,64,256]{2,1,0:T(8,128)(2,1)S(1)} collective-permute-done((bf16[2,64,256]{2,1,0:T(8,128)(2,1)S(1)}, bf16[2,64,256]{2,1,0:T(8,128)(2,1)S(1)}, u32[]{:S(2)}, u32[]{:S(2)}) %collective-permute-start.17) | collective-permute-done | bytes 65568 | tf_op jit(solution)/shard_map/ppermute | solution.py:270
  84.6 0.1 collective-permute-start.19
  84.7 4.2 %shard_map.132.first_ref = f32[5120,256]{1,0:T(8,128)S(1)} custom-call(s16[5120,128]{1,0:T(8,128)(2,1)S(1)} %get-tuple-element.28.refs_2_.source_ref, s16[5120,128]{1,0:T(8,128)(2,1)S(1)} %get-tuple-element.29.refs_3_.target_ref, bf16[640,256]{1,0:T(8,128)(2,1)S(1)} %get-tuple-element.45.sender_ref, bf16[640,256]{1,0:T(8,128)(2,1)S(1)} %get-tuple-element.46.receiver_ref), custom_call_target="tpu_custom_call" | custom-call | flops 3355443200 | bytes 8519680 | tf_op jit(solution)/shard_map/pallas_call | solution.py:26
  88.9 5.0 %shard_map.134 = bf16[640,256]{1,0:T(8,128)(2,1)} custom-call(s16[5120,128]{1,0:T(8,128)(2,1)S(1)} %get-tuple-element.28.refs_2_.source_ref, s32[1,5120]{1,0:T(1,128)S(1)} %copy-done.5, f32[1,5120]{1,0:T(1,128)S(1)} %copy-done.7, bf16[640,256]{1,0:T(8,128)(2,1)S(1)} %shard_map.130.refs_0_.state_ref, f32[5120,256]{1,0:T(8,128)S(1)} %shard_map.132.first_ref, ...), custom_call_target="tpu_custom_call" | custom-call | flops 2684354560 | bytes 7512064 | tf_op jit(solution)/shard_map/pallas_call | solution.py:26
  (34 shorter events, 0.1 us)
Async XLA Ops:
  0.0 9.4 %copy-start.4 = (s32[1,5120]{1,0:T(1,128)S(1)}, s32[1,5120]{1,0:T(1,128)}, u32[]{:S(2)}) copy-start(s32[1,5120]{1,0:T(1,128)} %refs_0_.1) | copy-start | bytes 61444
  0.0 9.4 %copy-start.5 = (s32[1,5120]{1,0:T(1,128)S(1)}, s32[1,5120]{1,0:T(1,128)}, u32[]{:S(2)}) copy-start(s32[1,5120]{1,0:T(1,128)} %target_ref.3) | copy-start | bytes 61444
  0.0 12.9 %copy-start = (bf16[512,256]{1,0:T(8,128)(2,1)S(1)}, bf16[512,256]{1,0:T(8,128)(2,1)}, u32[]{:S(2)}) copy-start(bf16[512,256]{1,0:T(8,128)(2,1)} %weight_ref.7) | copy-start | bytes 786436
  0.0 12.9 %copy-start.2 = (f32[1,7,256]{2,0,1:T(1,128)S(1)}, f32[1,7,256]{2,0,1:T(1,128)}, u32[]{:S(2)}) copy-start(f32[1,7,256]{2,0,1:T(1,128)} %param.17) | copy-start | bytes 21508
  0.0 12.9 %copy-start.3 = (s32[1,7,256]{2,0,1:T(1,128)S(1)}, s32[1,7,256]{2,0,1:T(1,128)}, u32[]{:S(2)}) copy-start(s32[1,7,256]{2,0,1:T(1,128)} %param.16) | copy-start | bytes 21508
  0.0 1.3 %copy-start.6 = (bf16[2048,256]{1,0:T(8,128)(2,1)S(1)}, bf16[2048,256]{1,0:T(8,128)(2,1)}, u32[]{:S(2)}) copy-start(bf16[2048,256]{1,0:T(8,128)(2,1)} %table_ref.3) | copy-start | bytes 3145732
  1.3 0.7 copy-start.8
  2.7 30.5 %copy-start.1 = (bf16[640,256]{1,0:T(8,128)(2,1)S(1)}, bf16[640,256]{1,0:T(8,128)(2,1)}, u32[]{:S(2)}) copy-start(bf16[640,256]{1,0:T(8,128)(2,1)} %before_ref.1) | copy-start | bytes 983044
  2.7 10.2 %collective-permute-start = (bf16[2,256,256]{2,1,0:T(8,128)(2,1)S(1)}, bf16[2,256,256]{2,1,0:T(8,128)(2,1)S(1)}, u32[]{:S(2)}, u32[]{:S(2)}) collective-permute-start(bf16[2,256,256]{2,1,0:T(8,128)(2,1)S(1)} %shard_map.119.refs_0_), channel_id=1, source_target_pairs={{0,2},{2,0},{1,3},{3,1},{4,6},{6,4},{5,7},{7,5},{8,10},{10,8},{9,1... | collective-permute-start | bytes 786440 | tf_op jit(solution)/shard_map/ppermute | solution.py:54
  7.3 28.6 %copy-start.10 = (bf16[2,512,256]{2,1,0:T(8,128)(2,1)S(1)}, bf16[2,512,256]{2,1,0:T(8,128)(2,1)}, u32[]{:S(2)}) copy-start(bf16[2,512,256]{2,1,0:T(8,128)(2,1)} %param.19) | copy-start | bytes 1572868
  7.3 28.6 %copy-start.11 = (bf16[2,512,256]{2,1,0:T(8,128)(2,1)S(1)}, bf16[2,512,256]{2,1,0:T(8,128)(2,1)}, u32[]{:S(2)}) copy-start(bf16[2,512,256]{2,1,0:T(8,128)(2,1)} %param.18) | copy-start | bytes 1572868
  7.3 13.4 %collective-permute-start.3 = (bf16[2,256,256]{2,1,0:T(8,128)(2,1)S(1)}, bf16[2,256,256]{2,1,0:T(8,128)(2,1)S(1)}, u32[]{:S(2)}, u32[]{:S(2)}) collective-permute-start(bf16[2,256,256]{2,1,0:T(8,128)(2,1)S(1)} %get-tuple-element.32.refs_0_), channel_id=1, source_target_pairs={{0,2},{2,0},{1,3},{3,1},{4,6},{6,4},{5,7},{7,5},{8,10},{10,8},{9,1... | collective-permute-start | bytes 786440 | tf_op jit(solution)/shard_map/ppermute | solution.py:54
  7.4 16.7 %collective-permute-start.6 = (bf16[2,256,256]{2,1,0:T(8,128)(2,1)S(1)}, bf16[2,256,256]{2,1,0:T(8,128)(2,1)S(1)}, u32[]{:S(2)}, u32[]{:S(2)}) collective-permute-start(bf16[2,256,256]{2,1,0:T(8,128)(2,1)S(1)} %get-tuple-element.35.refs_0_), channel_id=1, source_target_pairs={{0,2},{2,0},{1,3},{3,1},{4,6},{6,4},{5,7},{7,5},{8,10},{10,8},{9,1... | collective-permute-start | bytes 786440 | tf_op jit(solution)/shard_map/ppermute | solution.py:54
  12.9 30.8 %copy-start.9 = (s32[1,6,64]{2,0,1:T(1,128)S(1)}, s32[1,6,64]{2,0,1:T(1,128)}, u32[]{:S(2)}) copy-start(s32[1,6,64]{2,0,1:T(1,128)} %param.20) | copy-start | bytes 4612
  13.3 16.6 %collective-permute-start.1 = (bf16[272,256]{1,0:T(8,128)(2,1)S(1)}, bf16[272,256]{1,0:T(8,128)(2,1)S(1)}, u32[]{:S(2)}, u32[]{:S(2)}) collective-permute-start(bf16[272,256]{1,0:T(8,128)(2,1)S(1)} %get-tuple-element.30), channel_id=1, source_target_pairs={{5,0},{8,1},{9,4},{12,5},{13,8},{7,2},{10,3},{11,6},{14,7},{15,10}... | collective-permute-start | bytes 417800 | tf_op jit(solution)/shard_map/ppermute | solution.py:48
  14.6 14.0 %collective-permute-start.9 = (bf16[1,256,256]{2,1,0:T(8,128)(2,1)S(1)}, bf16[1,256,256]{2,1,0:T(8,128)(2,1)S(1)}, u32[]{:S(2)}, u32[]{:S(2)}) collective-permute-start(bf16[1,256,256]{2,1,0:T(8,128)(2,1)S(1)} %get-tuple-element.38.refs_0_), channel_id=1, source_target_pairs={{0,2},{2,0},{1,3},{3,1},{4,6},{6,4},{5,7},{7,5},{8,10},{10,8},{9,1... | collective-permute-start | bytes 393224 | tf_op jit(solution)/shard_map/ppermute | solution.py:54
  16.7 16.5 %collective-permute-start.2 = (bf16[272,256]{1,0:T(8,128)(2,1)S(1)}, bf16[272,256]{1,0:T(8,128)(2,1)S(1)}, u32[]{:S(2)}, u32[]{:S(2)}) collective-permute-start(bf16[272,256]{1,0:T(8,128)(2,1)S(1)} %get-tuple-element.31), channel_id=1, source_target_pairs={{0,5},{1,8},{4,9},{5,12},{8,13},{2,7},{3,10},{6,11},{7,14},{10,15}... | collective-permute-start | bytes 417800 | tf_op jit(solution)/shard_map/ppermute | solution.py:48
  21.1 12.1 %collective-permute-start.4 = (bf16[272,256]{1,0:T(8,128)(2,1)S(1)}, bf16[272,256]{1,0:T(8,128)(2,1)S(1)}, u32[]{:S(2)}, u32[]{:S(2)}) collective-permute-start(bf16[272,256]{1,0:T(8,128)(2,1)S(1)} %get-tuple-element.33), channel_id=1, source_target_pairs={{4,0},{5,1},{8,4},{9,5},{12,8},{13,9},{6,2},{7,3},{10,6},{11,7},{1... | collective-permute-start | bytes 417800 | tf_op jit(solution)/shard_map/ppermute | solution.py:48
  24.1 9.1 %collective-permute-start.5 = (bf16[272,256]{1,0:T(8,128)(2,1)S(1)}, bf16[272,256]{1,0:T(8,128)(2,1)S(1)}, u32[]{:S(2)}, u32[]{:S(2)}) collective-permute-start(bf16[272,256]{1,0:T(8,128)(2,1)S(1)} %get-tuple-element.34), channel_id=1, source_target_pairs={{0,4},{1,5},{4,8},{5,9},{8,12},{9,13},{2,6},{3,7},{6,10},{7,11},{1... | collective-permute-start | bytes 417800 | tf_op jit(solution)/shard_map/ppermute | solution.py:48
  28.6 5.2 %collective-permute-start.7 = (bf16[272,256]{1,0:T(8,128)(2,1)S(1)}, bf16[272,256]{1,0:T(8,128)(2,1)S(1)}, u32[]{:S(2)}, u32[]{:S(2)}) collective-permute-start(bf16[272,256]{1,0:T(8,128)(2,1)S(1)} %get-tuple-element.36), channel_id=1, source_target_pairs={{1,0},{4,1},{5,4},{8,5},{9,8},{12,9},{13,12},{3,2},{6,3},{7,6},{10... | collective-permute-start | bytes 417800 | tf_op jit(solution)/shard_map/ppermute | solution.py:48
  29.9 4.0 %collective-permute-start.8 = (bf16[272,256]{1,0:T(8,128)(2,1)S(1)}, bf16[272,256]{1,0:T(8,128)(2,1)S(1)}, u32[]{:S(2)}, u32[]{:S(2)}) collective-permute-start(bf16[272,256]{1,0:T(8,128)(2,1)S(1)} %get-tuple-element.37), channel_id=1, source_target_pairs={{0,1},{1,4},{4,5},{5,8},{8,9},{9,12},{12,13},{2,3},{3,6},{6,7},{7,... | collective-permute-start | bytes 417800 | tf_op jit(solution)/shard_map/ppermute | solution.py:48
  34.3 9.4 %collective-permute-start.10 = (bf16[640,256]{1,0:T(8,128)(2,1)S(1)}, bf16[640,256]{1,0:T(8,128)(2,1)S(1)}, u32[]{:S(2)}, u32[]{:S(2)}) collective-permute-start(bf16[640,256]{1,0:T(8,128)(2,1)S(1)} %shard_map.126.refs_0_.state_ref), channel_id=1, source_target_pairs={{0,2},{2,0},{1,3},{3,1},{4,6},{6,4},{5,7},{7,5},{8,10},{10,8},{9,1... | collective-permute-start | bytes 983048 | tf_op jit(solution)/shard_map/ppermute | solution.py:54
  44.4 8.0 %collective-permute-start.11 = (bf16[2,64,256]{2,1,0:T(8,128)(2,1)S(1)}, bf16[2,64,256]{2,1,0:T(8,128)(2,1)S(1)}, u32[]{:S(2)}, u32[]{:S(2)}) collective-permute-start(bf16[2,64,256]{2,1,0:T(8,128)(2,1)S(1)} %get-tuple-element.41), channel_id=1, source_target_pairs={{0,4},{1,5},{4,8},{5,9},{8,12},{9,13},{2,6},{3,7},{6,10},{7,11},{1... | collective-permute-start | bytes 196616 | tf_op jit(solution)/shard_map/ppermute | solution.py:269
  50.4 6.2 %collective-permute-start.12 = (bf16[2,64,256]{2,1,0:T(8,128)(2,1)S(1)}, bf16[2,64,256]{2,1,0:T(8,128)(2,1)S(1)}, u32[]{:S(2)}, u32[]{:S(2)}) collective-permute-start(bf16[2,64,256]{2,1,0:T(8,128)(2,1)S(1)} %get-tuple-element.42), channel_id=1, source_target_pairs={{4,0},{5,1},{8,4},{9,5},{12,8},{13,9},{6,2},{7,3},{10,6},{11,7},{1... | collective-permute-start | bytes 196616 | tf_op jit(solution)/shard_map/ppermute | solution.py:270
  51.7 9.2 %collective-permute-start.13 = (bf16[64,256]{1,0:T(8,128)(2,1)S(1)}, bf16[64,256]{1,0:T(8,128)(2,1)S(1)}, u32[]{:S(2)}, u32[]{:S(2)}) collective-permute-start(bf16[64,256]{1,0:T(8,128)(2,1)S(1)} %get-tuple-element.43), channel_id=1, source_target_pairs={{1,8},{5,12},{8,1},{12,5},{3,10},{7,14},{10,3},{14,7},{17,24},{21,... | collective-permute-start | bytes 98312 | tf_op jit(solution)/shard_map/ppermute | solution.py:273
  56.6 4.3 %collective-permute-start.14 = (bf16[3,64,256]{2,1,0:T(8,128)(2,1)S(1)}, bf16[3,64,256]{2,1,0:T(8,128)(2,1)S(1)}, u32[]{:S(2)}, u32[]{:S(2)}) collective-permute-start(bf16[3,64,256]{2,1,0:T(8,128)(2,1)S(1)} %shard_map.129), channel_id=1, source_target_pairs={{0,1},{1,0},{2,3},{3,2},{4,5},{5,4},{6,7},{7,6},{8,9},{9,8},{10,11... | collective-permute-start | bytes 294920 | tf_op jit(solution)/shard_map/ppermute | solution.py:276
  56.7 4.3 %copy-start.7 = (f32[1,5120]{1,0:T(1,128)S(1)}, f32[1,5120]{1,0:T(1,128)}, u32[]{:S(2)}) copy-start(f32[1,5120]{1,0:T(1,128)} %coef_ref.3) | copy-start | bytes 61444
  65.2 10.2 %collective-permute-start.15 = (bf16[640,256]{1,0:T(8,128)(2,1)S(1)}, bf16[640,256]{1,0:T(8,128)(2,1)S(1)}, u32[]{:S(2)}, u32[]{:S(2)}) collective-permute-start(bf16[640,256]{1,0:T(8,128)(2,1)S(1)} %shard_map.130.refs_0_.state_ref), channel_id=1, source_target_pairs={{0,2},{2,0},{1,3},{3,1},{4,6},{6,4},{5,7},{7,5},{8,10},{10,8},{9,1... | collective-permute-start | bytes 983048 | tf_op jit(solution)/shard_map/ppermute | solution.py:54
  76.1 4.5 %collective-permute-start.16 = (bf16[2,64,256]{2,1,0:T(8,128)(2,1)S(1)}, bf16[2,64,256]{2,1,0:T(8,128)(2,1)S(1)}, u32[]{:S(2)}, u32[]{:S(2)}) collective-permute-start(bf16[2,64,256]{2,1,0:T(8,128)(2,1)S(1)} %get-tuple-element.47), channel_id=1, source_target_pairs={{0,4},{1,5},{4,8},{5,9},{8,12},{9,13},{2,6},{3,7},{6,10},{7,11},{1... | collective-permute-start | bytes 196616 | tf_op jit(solution)/shard_map/ppermute | solution.py:269
  78.4 6.2 %collective-permute-start.17 = (bf16[2,64,256]{2,1,0:T(8,128)(2,1)S(1)}, bf16[2,64,256]{2,1,0:T(8,128)(2,1)S(1)}, u32[]{:S(2)}, u32[]{:S(2)}) collective-permute-start(bf16[2,64,256]{2,1,0:T(8,128)(2,1)S(1)} %get-tuple-element.48), channel_id=1, source_target_pairs={{4,0},{5,1},{8,4},{9,5},{12,8},{13,9},{6,2},{7,3},{10,6},{11,7},{1... | collective-permute-start | bytes 196616 | tf_op jit(solution)/shard_map/ppermute | solution.py:270
  79.7 9.2 %collective-permute-start.18 = (bf16[64,256]{1,0:T(8,128)(2,1)S(1)}, bf16[64,256]{1,0:T(8,128)(2,1)S(1)}, u32[]{:S(2)}, u32[]{:S(2)}) collective-permute-start(bf16[64,256]{1,0:T(8,128)(2,1)S(1)} %get-tuple-element.49), channel_id=1, source_target_pairs={{1,8},{5,12},{8,1},{12,5},{3,10},{7,14},{10,3},{14,7},{17,24},{21,... | collective-permute-start | bytes 98312 | tf_op jit(solution)/shard_map/ppermute | solution.py:273
  84.6 4.3 %collective-permute-start.19 = (bf16[3,64,256]{2,1,0:T(8,128)(2,1)S(1)}, bf16[3,64,256]{2,1,0:T(8,128)(2,1)S(1)}, u32[]{:S(2)}, u32[]{:S(2)}) collective-permute-start(bf16[3,64,256]{2,1,0:T(8,128)(2,1)S(1)} %shard_map.133), channel_id=1, source_target_pairs={{0,1},{1,0},{2,3},{3,2},{4,5},{5,4},{6,7},{7,6},{8,9},{9,8},{10,11... | collective-permute-start | bytes 294920 | tf_op jit(solution)/shard_map/ppermute | solution.py:276

commit v3 on v2

--- a/solution.py
+++ b/solution.py
@@ -20,7 +20,7 @@
     return pltpu.with_memory_space_constraint(array, pltpu.VMEM)
 
 
-def call(kernel, outputs, inputs, flops, transcendentals=0, scratch=(), final=False):
+def call(kernel, outputs, inputs, flops, transcendentals=0, scratch=(), final=False, fetched=0):
     size = lambda a: int(a.size) * a.dtype.itemsize
     shapes = outputs if final else [made_in_vmem(o) for o in outputs]
     return pl.pallas_call(
@@ -35,23 +35,63 @@
             bytes_accessed=sum(size(a) for a in list(inputs) + list(outputs)),
             transcendentals=transcendentals,
         ),
-    )(*[taken_from_vmem(a) for a in inputs])
+    )(*inputs[:fetched], *[taken_from_vmem(a) for a in inputs[fetched:]])
 
 
 def shape(dims, dtype=jnp.bfloat16):
     return jax.ShapeDtypeStruct(dims, dtype)
 
 
-def passed_along(value, steps):
+def meets_core(r):
+    return r + 1 - 2 * (r % 2)
+
+
+def meets_next(r):
+    return r - 1 + 2 * (r % 2)
+
+
+def meets_two(r):
+    return r + 2 - 4 * (r // 2 % 2)
+
+
+def meets_other_two(r):
+    return r - 2 + 4 * (r // 2 % 2)
+
+
+def meets_three(r):
+    return r + 3 - 6 * (r % 2)
+
+
+def meets_other_three(r):
+    return r - 3 + 6 * (r % 2)
+
+
+def pairs(meets):
     count = lax.axis_size(REGION)
-    first, last = (max(0, -steps), min(count, count - steps))
-    return lax.ppermute(value, REGION, [(i, i + steps) for i in range(first, last)])
-
-
-def from_others(value):
+    return [(r, meets(r)) for r in range(count) if 0 <= meets(r) < count]
+
+
+def swapped(value, meets):
+    return lax.ppermute(value, REGION, pairs(meets))
+
+
+def block_for(meets, reach):
+    region = lax.axis_index(REGION)
+    return meets(region) - region + reach
+
+
+def from_others(value, meets=None):
     n = lax.axis_size("feat")
+    if meets is None:
+        axes, rings = ("feat", [[i for i in range(n)]])
+    else:
+        axes, cores = (("space", "feat", "edge"), lax.axis_size("edge"))
+        rings = [
+            [(r // cores * n + i) * cores + r % cores for i in range(n)] for r, unused in pairs(meets)
+        ]
     return [
-        lax.ppermute(value, "feat", [(i, (i + k) % n) for i in range(n)]) for k in range(1, n)
+        lax.ppermute(value, axes, [(ring[i], ring[(i + k) % n]) for ring in rings for i in range(n)])
+        for k in range(1, n)
     ]
 
 
@@ -116,32 +156,40 @@
     return jnp.dot(a, b, preferred_element_type=jnp.float32)
 
 
-def pick_kernel(orders, index_ref, table_ref, *out_refs):
+def block_index(meets, reach):
+    return reach if meets is None else block_for(meets, reach)
+
+
+def pick_kernel(groups, index_ref, table_ref, *refs):
+    out_refs = refs[-len(groups) :]
     lanes = lane_iota(table_ref.shape[0])
-    for order, out_ref in zip(orders, out_refs):
-        for place, j in enumerate(order):
-            col = column(index_ref[j]).astype(jnp.int16)
+    reach = index_ref.shape[0] // 2
+    for group, out_ref in zip(groups, out_refs):
+        for place, meets in enumerate(group):
+            col = column(index_ref[block_index(meets, reach)]).astype(jnp.int16)
             out_ref[place] = dot(pick_mask(col, lanes), table_ref[...]).astype(jnp.bfloat16)
 
 
-def pick(orders, g2m_src, grid_latent):
+def pick(groups, g2m_src, grid_latent, after=()):
     capacity = g2m_src.shape[2]
     rows, channels = grid_latent.shape
     return call(
-        functools.partial(pick_kernel, orders),
-        [shape((len(order), capacity, channels)) for order in orders],
-        [g2m_src, grid_latent],
-        2 * sum(map(len, orders)) * capacity * rows * channels,
-    )
-
-
-def encode_kernel(order, others, weight_ref, coef_ref, target_ref, *refs):
-    sources, outs = (refs[: others + 1], refs[-len(order) :])
+        functools.partial(pick_kernel, groups),
+        [shape((len(group), capacity, channels)) for group in groups],
+        [g2m_src, grid_latent, *after],
+        2 * sum(map(len, groups)) * capacity * rows * channels,
+    )
+
+
+def encode_kernel(group, others, weight_ref, coef_ref, target_ref, *refs):
+    sources, outs = (refs[: others + 1], refs[-len(group) :])
     capacity, channels = sources[0].shape[1:]
     weights = own_and_others_rows(weight_ref, channels, others)
     line = lax.broadcasted_iota(jnp.int32, (PAD, channels), 0)
     pieces = capacity // channels
-    for place, j in enumerate(order):
+    reach = coef_ref.shape[0] // 2
+    for place, meets in enumerate(group):
+        j = block_index(meets, reach)
         projected = dot(sources[0][place], weights[0])
         for source, weight in zip(sources[1:], weights[1:]):
             projected += dot(source[place], weight)
@@ -157,10 +205,10 @@
         outs[place][pl.ds(capacity, PAD), :] = code.astype(jnp.bfloat16)
 
 
-def encode(order, picked, arrived, enc_weight, g2m_coef, g2m_dst, after=()):
+def encode(group, picked, arrived, enc_weight, g2m_coef, g2m_dst, after=()):
     count, capacity, channels = picked.shape
     return call(
-        functools.partial(encode_kernel, order, len(arrived)),
+        functools.partial(encode_kernel, group, len(arrived)),
         [shape((capacity + PAD, channels))] * count,
         [enc_weight, g2m_coef, g2m_dst, picked, *arrived, *after],
         2 * count * capacity * enc_weight.shape[0] * channels,
@@ -196,23 +244,26 @@
     )[0]
 
 
-def columns_kernel(*refs):
-    half = len(refs) // 2
-    for row_ref, out_ref in zip(refs[:half], refs[half:]):
-        out_ref[...] = column(row_ref[...]).astype(jnp.int16)
-
-
-def columns(*rows):
-    count = rows[0].shape[1]
-    return call(
-        columns_kernel, [shape((count, 128), jnp.int16)] * len(rows), rows, len(rows) * count * 128 * 8
-    )
-
-
-def project_kernel(
-    others, reach, src_ref, dst_ref, listed_ref, *refs
-):
-    states, (sender_ref, receiver_ref, up_ref, down_ref, far_ref, near_ref) = (
+def columns_kernel(pieces, *refs):
+    rows = len(refs) // (pieces + 1)
+    for k in range(rows):
+        for piece, out_ref in enumerate(refs[rows + k * pieces : rows + (k + 1) * pieces]):
+            count = out_ref.shape[0]
+            out_ref[...] = column(refs[k][:, pl.ds(piece * count, count)]).astype(jnp.int16)
+
+
+def columns(pieces, *rows):
+    count = rows[0].shape[1] // pieces
+    return call(
+        functools.partial(columns_kernel, pieces),
+        [shape((count, 128), jnp.int16)] * (pieces * len(rows)),
+        rows,
+        pieces * len(rows) * count * 128 * 8,
+    )
+
+
+def project_kernel(others, reach, src_ref, dst_ref, listed_ref, *refs):
+    states, (sender_ref, receiver_ref, one_ref, two_ref, far_ref, near_ref) = (
         refs[: others + 1],
         refs[others + 1 :],
     )
@@ -225,23 +276,25 @@
         out_ref[...] = total.astype(jnp.bfloat16)
     width = listed_ref.shape[2]
     lanes = lane_iota(nodes)
-    core = lax.axis_index("edge")
-    wanted = [2 - core, 3 - core, -2 - core, -1 - core, 6 * core - 3, 1 - 2 * core]
+    region = lax.axis_index(REGION)
+    core = region % 2
+    wanted = [
+        meets(region) - core + i - region for meets in (meets_two, meets_other_two) for i in range(2)
+    ]
+    wanted += [meets_other_three(region) - region, meets_core(region) - region]
     wanted = [offset + reach - jnp.where(offset > 0, 1, 0) for offset in wanted]
     for k in range(0, len(wanted), 2):
         row = jnp.concatenate([listed_ref[wanted[k + i]] for i in range(2)], axis=1)
         rows = dot(pick_mask(column(row).astype(jnp.int16), lanes), sender_ref[...])
         rows = rows.astype(jnp.bfloat16)
-        for i in range(2):
-            part = rows[i * width : (i + 1) * width]
-            if k == 0:
-                up_ref[i] = part
-            elif k == 2:
-                down_ref[i] = part
-            elif i == 0:
-                far_ref[...] = part
-            else:
-                near_ref[...] = part
+        parts = [rows[i * width : (i + 1) * width] for i in range(2)]
+        if k < 4:
+            ref = one_ref if k == 0 else two_ref
+            for i in range(2):
+                ref[i] = parts[i]
+        else:
+            far_ref[...] = parts[0]
+            near_ref[...] = parts[1]
 
 
 def project(state, arrived, src_weight, dst_weight, halo_send, reach):
@@ -257,27 +310,15 @@
     )
 
 
-def forward_kernel(near_ref, from_below_ref, from_above_ref, out_ref):
+def forward_kernel(near_ref, one_ref, two_ref, unused_ref, out_ref):
     other = 1 - lax.axis_index("edge")
     out_ref[0] = near_ref[...]
-    out_ref[1] = from_below_ref[other]
-    out_ref[2] = from_above_ref[other]
-
-
-def listed_rows(up, down, far, near):
-    count = lax.axis_size(REGION)
-    below = lax.ppermute(up, REGION, [(i, i + 2) for i in range(count - 2)])
-    above = lax.ppermute(down, REGION, [(i, i - 2) for i in range(2, count)])
-    odd = [(i, i + 3) for i in range(1, count - 3, 2)]
-    even = [(i, i - 3) for i in range(4, count, 2)]
-    distant = lax.ppermute(far, REGION, odd + even)
-    width, channels = near.shape
-    sent = call(forward_kernel, [shape((3, width, channels))], [near, below, above], 0)[0]
-    across = lax.ppermute(sent, "edge", [(0, 1), (1, 0)])
-    return below, above, distant, across
-
-
-def first_kernel(turn, source_ref, target_ref, sender_ref, receiver_ref, out_ref):
+    out_ref[1] = one_ref[other]
+    out_ref[2] = two_ref[other]
+
+
+def first_kernel(turn, source_ref, target_ref, sender_ref, receiver_ref, *refs):
+    out_ref = refs[-1]
     nodes = sender_ref.shape[0]
     lanes = lane_iota(nodes)
     for start in range(0, source_ref.shape[0], turn):
@@ -287,55 +328,66 @@
         )
 
 
-def first_part(source_col, target_col, sender, receiver):
+def first_part(source_col, target_col, sender, receiver, after=()):
     nodes, channels = sender.shape
     edges = source_col.shape[0]
     return call(
         functools.partial(first_kernel, 512),
         [shape((edges, channels), jnp.float32)],
-        [source_col, target_col, sender, receiver],
+        [source_col, target_col, sender, receiver, *after],
         4 * edges * nodes * channels,
     )[0]
 
 
 def message_kernel(
-    turn, source_ref, target_ref, coef_ref, state_ref, first_ref, below_ref, above_ref, distant_ref, across_ref,
-    out_ref, table_ref,
+    turn, halves, target_ref, coef_ref, state_ref, one_ref, two_ref, distant_ref, across_ref, *refs
 ):
+    sources, firsts, (out_ref, table_ref) = (refs[:halves], refs[halves : 2 * halves], refs[2 * halves :])
     nodes, channels = state_ref.shape
     width = distant_ref.shape[0]
-    core = lax.axis_index("edge")
-    own_below, own_above = (below_ref[core], above_ref[core])
+    region = lax.axis_index(REGION)
+    core = region % 2
+    low_even = region // 2 % 2 == 0
+    own = (one_ref[core], two_ref[core])
+    across = (across_ref[1], across_ref[2])
+    before, after = [
+        [jnp.where(low_even == first, pair[0], pair[1]) for pair in (own, across)] for first in (False, True)
+    ]
+    near = across_ref[0]
+    distant = distant_ref[...]
     even = core == 0
     rows = (
-        jnp.where(even, across_ref[2], distant_ref[...]),
-        own_above,
-        jnp.where(even, across_ref[0], across_ref[2]),
-        jnp.where(even, across_ref[1], across_ref[0]),
-        own_below,
-        jnp.where(even, distant_ref[...], across_ref[1]),
+        jnp.where(even, after[1], distant),
+        after[0],
+        jnp.where(even, near, after[1]),
+        jnp.where(even, before[1], near),
+        before[0],
+        jnp.where(even, distant, before[1]),
     )
     for j, part in enumerate(rows):
         table_ref[pl.ds(j * width, width), :] = part
     lanes = (lane_iota(len(rows) * width).astype(jnp.int32) + nodes).astype(jnp.int16)
     rows16 = row_iota(nodes)
     total = state_ref[...].astype(jnp.float32)
-    for start in range(0, source_ref.shape[0], turn):
-        here = pl.ds(start, turn)
-        summed = first_ref[here, :] + dot(pick_mask(source_ref[here, :], lanes), table_ref[...])
-        mask = sum_mask(target_ref[:, here], rows16, coef_ref[:, here])
-        total += dot(mask, silu(summed).astype(jnp.bfloat16))
+    for half, (source_ref, first_ref) in enumerate(zip(sources, firsts)):
+        count = source_ref.shape[0]
+        for start in range(0, count, turn):
+            here = pl.ds(start, turn)
+            there = pl.ds(half * count + start, turn)
+            summed = first_ref[here, :] + dot(pick_mask(source_ref[here, :], lanes), table_ref[...])
+            mask = sum_mask(target_ref[:, there], rows16, coef_ref[:, there])
+            total += dot(mask, silu(summed).astype(jnp.bfloat16))
     out_ref[...] = total.astype(jnp.bfloat16)
 
 
-def messages(source_col, m2m_dst, m2m_coef, state, first, listed, final):
+def messages(m2m_dst, m2m_coef, state, listed, sources, firsts, final):
     nodes, channels = state.shape
     edges = m2m_dst.shape[1]
     named = 6 * listed[2].shape[0]
     return call(
-        functools.partial(message_kernel, 512),
+        functools.partial(message_kernel, 512, len(sources)),
         [shape((nodes, channels))],
-        [source_col, m2m_dst, m2m_coef, state, first, *listed],
+        [m2m_dst, m2m_coef, state, *listed, *sources, *firsts],
         2 * edges * (named + nodes) * channels,
         edges * channels,
         [pltpu.VMEM((named, channels), jnp.bfloat16)],
@@ -362,26 +414,44 @@
     g2m_src, g2m_dst, g2m_coef, halo_send = [
         jnp.swapaxes(a, 0, 1) for a in (g2m_src, g2m_dst, g2m_coef, halo_send)
     ]
-    groups = [(reach - d, reach + d) for d in range(reach, 0, -1)] + [(reach,)]
-    picked = pick(groups[:1], g2m_src, grid_latent) + pick(groups[1:], g2m_src, grid_latent)
-    arrived = [from_others(rows) for rows in picked]
-    source_col, target_col = columns(m2m_src, m2m_dst)
-    blocks = []
-    for order, rows, others in zip(groups, picked, arrived):
-        after = () if blocks else (source_col, target_col)
-        encoded = encode(order, rows, others, enc_weight, g2m_coef, g2m_dst, after)
-        for j, block in zip(order, encoded):
-            blocks.append(block if j == reach else passed_along(block, j - reach))
-    state = gather_in(mesh_latent, blocks[:4], jnp.float32)
-    state = gather_in(state, blocks[4:], jnp.bfloat16)
+    cols = columns(2, m2m_src, m2m_dst)
+    source_cols, target_cols = cols[:2], cols[2:]
+    groups = [(meets_three,), (meets_other_three,), (meets_two, meets_other_two, meets_next), (meets_core, None)]
+    picked = pick(groups[:2], g2m_src, grid_latent)
+    arrived = [from_others(rows, group[0]) for group, rows in zip(groups, picked)]
+    for place in (2, 3):
+        picked += pick(groups[place : place + 1], g2m_src, grid_latent, arrived[place - 2])
+        arrived.append(from_others(picked[place]))
+    state = mesh_latent
+    after = cols
+    waiting = []
+    for place, (group, rows, others) in enumerate(zip(groups, picked, arrived)):
+        encoded = encode(group, rows, others, enc_weight, g2m_coef, g2m_dst, after)
+        waiting += [
+            block if meets is None else swapped(block, meets) for meets, block in zip(group, encoded)
+        ]
+        if place == 1:
+            state = gather_in(state, waiting, jnp.float32)
+            waiting, after = ([], [state])
+    state = gather_in(state, waiting[:2], jnp.float32)
+    state = gather_in(state, waiting[2:], jnp.bfloat16)
     layers = src_weights.shape[0]
     for layer in range(layers):
-        sender, receiver, *sent = project(
+        sender, receiver, one, two, far, near = project(
             state, from_others(state), src_weights[layer], dst_weights[layer], halo_send, reach
         )
-        listed = listed_rows(*sent)
-        first = first_part(source_col, target_col, sender, receiver)
-        state = messages(source_col, m2m_dst, m2m_coef, state, first, listed, layer == layers - 1)
+        one, two = swapped(one, meets_two), swapped(two, meets_other_two)
+        distant = swapped(far, meets_other_three)
+        firsts = [first_part(source_cols[0], target_cols[0], sender, receiver)]
+        width, channels = near.shape
+        sent = call(
+            forward_kernel, [shape((3, width, channels))], [near, one, two, firsts[0]], 3 * width * channels
+        )[0]
+        across = swapped(sent, meets_core)
+        firsts.append(first_part(source_cols[1], target_cols[1], sender, receiver, [sent]))
+        state = messages(
+            m2m_dst, m2m_coef, state, (one, two, distant, across), source_cols, firsts, layer == layers - 1
+        )
     return state
 
 

time: 94.5 us -> 94.2 us (level)
  waiting for transfers between devices: 28.5 us -> 25.7 us
  starting transfers between devices: 37.9 us -> 39.7 us
    ppermute x20, waiting for transfers between devices: 28.5 us -> 25.7 us  [the longest x6 18.5 us: from_others(): lax.ppermute(value, axes, [(ring[i], ring[(i + k) % n]) for ring in rings...]
    ppermute x20, starting transfers between devices: 37.9 us -> 39.7 us  [the longest x14 30 us: swapped(): return lax.ppermute(value, REGION, pairs(meets))]
    pallas_call x17 -> x21, Pallas kernels: 25.2 us -> 25.9 us  [call(): pl.pallas_call(kernel, out_shape=shapes, in_specs=[pl.BlockSpec(memory_sp...]
  transfers between devices with their start and end apart: 20 -> 20, of which waited for: 7 -> 6; matrix products, arithmetic and copies ran while one was open for 0% -> 0% of each run, Pallas kernels for 14% -> 15%
where the time goes in v3:
time: 94.2 us; the launch traced here: 93.8 us
  starting transfers between devices  39.7 us (42%)
  Pallas kernels  25.9 us (27%)
  waiting for transfers between devices  25.7 us (27%)
  local copies, waits for them, and re-layouts  2.05 us (2%)
    ppermute x14, starting transfers between devices, swapped(): return lax.ppermute(value, REGION, pairs(meets))  30 us
    pallas_call x21, Pallas kernels, call(): pl.pallas_call(kernel, out_shape=shapes, in_specs=[pl.BlockSpec(memory_sp...  25.9 us
    ppermute x6, waiting for transfers between devices, from_others(): lax.ppermute(value, axes, [(ring[i], ring[(i + k) % n]) for ring in rings...  18.5 us
    ppermute x6, starting transfers between devices, from_others(): lax.ppermute(value, axes, [(ring[i], ring[(i + k) % n]) for ring in rings...  9.7 us
    ppermute x14, waiting for transfers between devices, swapped(): return lax.ppermute(value, REGION, pairs(meets))  7.14 us
    unnamed x24, local copies, waits for them, and re-layouts  1.98 us
  transfers between devices with their start and end apart: 20, of which 6 were waited for; matrix products, arithmetic and copies ran while one was open for 0% of the time, Pallas kernels for 15%

profile of v3, /device:TPU:0, one launch (start us, length us, event | category | flops | bytes accessed | tf_op | source)
XLA Modules:
  0.0 93.8 jit_solution(948075555906661567)
XLA Ops:
  0.0 1.2 %copy-done.6 = bf16[2048,256]{1,0:T(8,128)(2,1)S(1)} copy-done((bf16[2048,256]{1,0:T(8,128)(2,1)S(1)}, bf16[2048,256]{1,0:T(8,128)(2,1)}, u32[]{:S(2)}) %copy-start.6) | copy-done | bytes 1048600
  1.2 0.7 copy-done.8
  1.9 0.8 shard_map.118
  2.8 5.0 %collective-permute-start = (bf16[1,256,256]{2,1,0:T(8,128)(2,1)S(1)}, bf16[1,256,256]{2,1,0:T(8,128)(2,1)S(1)}, u32[]{:S(2)}, u32[]{:S(2)}) collective-permute-start(bf16[1,256,256]{2,1,0:T(8,128)(2,1)S(1)} %get-tuple-element.28.refs_0_), channel_id=1, source_target_pairs={{0,2},{2,0},{4,6},{6,4},{5,7},{7,5},{8,10},{10,8},{9,11},{11,9},{1... | collective-permute-start | bytes 393224 | tf_op jit(solution)/shard_map/ppermute | solution.py:93
  7.7 0.7 collective-permute-start.2
  8.4 3.7 %collective-permute-done.refs_1_.refs_0_ = bf16[1,256,256]{2,1,0:T(8,128)(2,1)S(1)} collective-permute-done((bf16[1,256,256]{2,1,0:T(8,128)(2,1)S(1)}, bf16[1,256,256]{2,1,0:T(8,128)(2,1)S(1)}, u32[]{:S(2)}, u32[]{:S(2)}) %collective-permute-start) | collective-permute-done | bytes 131104 | tf_op jit(solution)/shard_map/ppermute | solution.py:93
  12.1 1.0 %shard_map.123.refs_0_ = bf16[3,256,256]{2,1,0:T(8,128)(2,1)S(1)} custom-call(s32[7,1,256]{2,1,0:T(1,128)S(1)} %bitcast.21, bf16[2048,256]{1,0:T(8,128)(2,1)S(1)} %copy-done.6, bf16[1,256,256]{2,1,0:T(8,128)(2,1)S(1)} %collective-permute-done.refs_1_.refs_0_), custom_call_target="tpu_custom_call" | custom-call | flops 805306368 | bytes 1580032 | tf_op jit(solution)/shard_map/pallas_call | solution.py:26
  13.1 2.0 %collective-permute-start.4 = (bf16[3,256,256]{2,1,0:T(8,128)(2,1)S(1)}, bf16[3,256,256]{2,1,0:T(8,128)(2,1)S(1)}, u32[]{:S(2)}, u32[]{:S(2)}) collective-permute-start(bf16[3,256,256]{2,1,0:T(8,128)(2,1)S(1)} %shard_map.123.refs_0_), channel_id=1, source_target_pairs={{0,2},{2,0},{1,3},{3,1},{4,6},{6,4},{5,7},{7,5},{8,10},{10,8},{9,1... | collective-permute-start | bytes 1179656 | tf_op jit(solution)/shard_map/ppermute | solution.py:93
  15.1 0.8 shard_map.126.refs_0_
  15.9 0.2 collective-permute-start.8
  16.0 1.4 %shard_map.119 = (s16[2560,128]{1,0:T(8,128)(2,1)S(1)}, s16[2560,128]{1,0:T(8,128)(2,1)S(1)}, s16[2560,128]{1,0:T(8,128)(2,1)S(1)}, s16[2560,128]{1,0:T(8,128)(2,1)S(1)}) custom-call(s32[1,5120]{1,0:T(1,128)S(1)} %copy-done.4, s32[1,5120]{1,0:T(1,128)S(1)} %copy-done.5), custom_call_target="tpu_custom_call" | custom-call | flops 10485760 | bytes 2662400 | tf_op jit(solution)/shard_map/pallas_call | solution.py:26
  17.5 0.3 shard_map.121
  17.8 0.7 collective-permute-start.3
  18.4 0.3 shard_map.120
  18.7 5.2 %collective-permute-start.1 = (bf16[272,256]{1,0:T(8,128)(2,1)S(1)}, bf16[272,256]{1,0:T(8,128)(2,1)S(1)}, u32[]{:S(2)}, u32[]{:S(2)}) collective-permute-start(bf16[272,256]{1,0:T(8,128)(2,1)S(1)} %shard_map.120), channel_id=1, source_target_pairs={{0,5},{4,9},{5,0},{8,13},{9,4},{13,8},{2,7},{6,11},{7,2},{10,15},{... | collective-permute-start | bytes 417800 | tf_op jit(solution)/shard_map/ppermute | solution.py:75
  23.9 4.1 %collective-permute-done.1.refs_0_ = bf16[272,256]{1,0:T(8,128)(2,1)S(1)} collective-permute-done((bf16[272,256]{1,0:T(8,128)(2,1)S(1)}, bf16[272,256]{1,0:T(8,128)(2,1)S(1)}, u32[]{:S(2)}, u32[]{:S(2)}) %collective-permute-start.1) | collective-permute-done | bytes 139296 | tf_op jit(solution)/shard_map/ppermute | solution.py:75
  28.0 0.3 shard_map.122.refs_2_.before_ref
  28.3 0.4 shard_map.124
  28.8 0.5 collective-permute-start.5
  29.4 0.7 collective-permute-start.6
  30.0 0.4 shard_map.127
  30.4 0.4 collective-permute-start.9
  30.8 0.7 collective-permute-start.7
  31.5 2.7 %collective-permute-done.5.refs_0_ = bf16[272,256]{1,0:T(8,128)(2,1)S(1)} collective-permute-done((bf16[272,256]{1,0:T(8,128)(2,1)S(1)}, bf16[272,256]{1,0:T(8,128)(2,1)S(1)}, u32[]{:S(2)}, u32[]{:S(2)}) %collective-permute-start.5) | collective-permute-done | bytes 139296 | tf_op jit(solution)/shard_map/ppermute | solution.py:75
  34.2 0.3 shard_map.125.before_ref
  34.5 0.4 shard_map.128.refs_0_.state_ref
  35.0 0.9 collective-permute-start.10
  35.8 0.1 slice_bitcast_fusion
  35.9 6.2 %collective-permute-done.10.refs_1_ = bf16[640,256]{1,0:T(8,128)(2,1)S(1)} collective-permute-done((bf16[640,256]{1,0:T(8,128)(2,1)S(1)}, bf16[640,256]{1,0:T(8,128)(2,1)S(1)}, u32[]{:S(2)}, u32[]{:S(2)}) %collective-permute-start.10) | collective-permute-done | bytes 327712 | tf_op jit(solution)/shard_map/ppermute | solution.py:93
  42.1 0.7 shard_map.129
  42.8 8.8 %collective-permute-start.11 = (bf16[2,64,256]{2,1,0:T(8,128)(2,1)S(1)}, bf16[2,64,256]{2,1,0:T(8,128)(2,1)S(1)}, u32[]{:S(2)}, u32[]{:S(2)}) collective-permute-start(bf16[2,64,256]{2,1,0:T(8,128)(2,1)S(1)} %get-tuple-element.39), channel_id=1, source_target_pairs={{0,4},{1,5},{4,0},{5,1},{8,12},{9,13},{12,8},{13,9},{2,6},{3,7},{6... | collective-permute-start | bytes 196616 | tf_op jit(solution)/shard_map/ppermute | solution.py:75
  51.6 0.7 collective-permute-start.12
  52.3 0.8 collective-permute-start.13
  53.2 2.2 %shard_map.130.unused_ref.refs_2_ = f32[2560,256]{1,0:T(8,128)S(1)} custom-call(s16[2560,128]{1,0:T(8,128)(2,1)S(1)} %get-tuple-element.29.refs_2_.source_ref.refs_0_, s16[2560,128]{1,0:T(8,128)(2,1)S(1)} %get-tuple-element.31.refs_4_.target_ref, bf16[640,256]{1,0:T(8,128)(2,1)S(1)} %get-tuple-element.43.sender_ref, ...), custom_call_target="tpu_custom_call" | custom-call | flops 1677721600 | bytes 4587520 | tf_op jit(solution)/shard_map/pallas_call | solution.py:26
  55.4 4.2 %collective-permute-start.14 = (bf16[3,64,256]{2,1,0:T(8,128)(2,1)S(1)}, bf16[3,64,256]{2,1,0:T(8,128)(2,1)S(1)}, u32[]{:S(2)}, u32[]{:S(2)}) collective-permute-start(bf16[3,64,256]{2,1,0:T(8,128)(2,1)S(1)} %shard_map.131.refs_0_), channel_id=1, source_target_pairs={{0,1},{1,0},{4,5},{5,4},{8,9},{9,8},{12,13},{13,12},{2,3},{3,2},{6... | collective-permute-start | bytes 294920 | tf_op jit(solution)/shard_map/ppermute | solution.py:75
  59.6 2.2 %shard_map.132.refs_3_ = f32[2560,256]{1,0:T(8,128)S(1)} custom-call(s16[2560,128]{1,0:T(8,128)(2,1)S(1)} %get-tuple-element.30.refs_3_.source_ref.refs_1_, s16[2560,128]{1,0:T(8,128)(2,1)S(1)} %get-tuple-element.32.refs_5_.target_ref, bf16[640,256]{1,0:T(8,128)(2,1)S(1)} %get-tuple-element.43.sender_ref, ...), custom_call_target="tpu_custom_call" | custom-call | flops 1677721600 | bytes 4685824 | tf_op jit(solution)/shard_map/pallas_call | solution.py:26
  61.8 4.3 %shard_map.133.refs_0_.state_ref = bf16[640,256]{1,0:T(8,128)(2,1)S(1)} custom-call(s32[1,5120]{1,0:T(1,128)S(1)} %copy-done.5, f32[1,5120]{1,0:T(1,128)S(1)} %copy-done.7, bf16[640,256]{1,0:T(8,128)(2,1)S(1)} %shard_map.128.refs_0_.state_ref, bf16[2,64,256]{2,1,0:T(8,128)(2,1)S(1)} %collective-permute-done.11.one_ref, ...), custom_call_target="tpu_custom_call" | custom-call | flops 2684354560 | bytes 7512064 | tf_op jit(solution)/shard_map/pallas_call | solution.py:26
  66.1 1.0 %collective-permute-start.15 = (bf16[640,256]{1,0:T(8,128)(2,1)S(1)}, bf16[640,256]{1,0:T(8,128)(2,1)S(1)}, u32[]{:S(2)}, u32[]{:S(2)}) collective-permute-start(bf16[640,256]{1,0:T(8,128)(2,1)S(1)} %shard_map.133.refs_0_.state_ref), channel_id=1, source_target_pairs={{0,2},{2,0},{1,3},{3,1},{4,6},{6,4},{5,7},{7,5},{8,10},{10,8},{9,1... | collective-permute-start | bytes 983048 | tf_op jit(solution)/shard_map/ppermute | solution.py:93
  67.1 8.7 %collective-permute-done.15.refs_1_ = bf16[640,256]{1,0:T(8,128)(2,1)S(1)} collective-permute-done((bf16[640,256]{1,0:T(8,128)(2,1)S(1)}, bf16[640,256]{1,0:T(8,128)(2,1)S(1)}, u32[]{:S(2)}, u32[]{:S(2)}) %collective-permute-start.15) | collective-permute-done | bytes 327712 | tf_op jit(solution)/shard_map/ppermute | solution.py:93
  75.8 0.7 shard_map.134
  76.5 0.2 collective-permute-start.16
  76.8 0.7 collective-permute-start.17
  77.4 0.9 collective-permute-start.18
  78.3 2.2 %shard_map.135.unused_ref.refs_2_ = f32[2560,256]{1,0:T(8,128)S(1)} custom-call(s16[2560,128]{1,0:T(8,128)(2,1)S(1)} %get-tuple-element.29.refs_2_.source_ref.refs_0_, s16[2560,128]{1,0:T(8,128)(2,1)S(1)} %get-tuple-element.31.refs_4_.target_ref, bf16[640,256]{1,0:T(8,128)(2,1)S(1)} %get-tuple-element.49.sender_ref, ...), custom_call_target="tpu_custom_call" | custom-call | flops 1677721600 | bytes 4587520 | tf_op jit(solution)/shard_map/pallas_call | solution.py:26
  80.5 0.3 collective-permute-done.16.one_ref
  80.9 5.7 %collective-permute-start.19 = (bf16[3,64,256]{2,1,0:T(8,128)(2,1)S(1)}, bf16[3,64,256]{2,1,0:T(8,128)(2,1)S(1)}, u32[]{:S(2)}, u32[]{:S(2)}) collective-permute-start(bf16[3,64,256]{2,1,0:T(8,128)(2,1)S(1)} %shard_map.136.refs_0_), channel_id=1, source_target_pairs={{0,1},{1,0},{4,5},{5,4},{8,9},{9,8},{12,13},{13,12},{2,3},{3,2},{6... | collective-permute-start | bytes 294920 | tf_op jit(solution)/shard_map/ppermute | solution.py:75
  86.6 2.2 %shard_map.137.refs_3_ = f32[2560,256]{1,0:T(8,128)S(1)} custom-call(s16[2560,128]{1,0:T(8,128)(2,1)S(1)} %get-tuple-element.30.refs_3_.source_ref.refs_1_, s16[2560,128]{1,0:T(8,128)(2,1)S(1)} %get-tuple-element.32.refs_5_.target_ref, bf16[640,256]{1,0:T(8,128)(2,1)S(1)} %get-tuple-element.49.sender_ref, ...), custom_call_target="tpu_custom_call" | custom-call | flops 1677721600 | bytes 4685824 | tf_op jit(solution)/shard_map/pallas_call | solution.py:26
  88.8 5.0 %shard_map.138 = bf16[640,256]{1,0:T(8,128)(2,1)} custom-call(s32[1,5120]{1,0:T(1,128)S(1)} %copy-done.5, f32[1,5120]{1,0:T(1,128)S(1)} %copy-done.7, bf16[640,256]{1,0:T(8,128)(2,1)S(1)} %shard_map.133.refs_0_.state_ref, bf16[2,64,256]{2,1,0:T(8,128)(2,1)S(1)} %collective-permute-done.16.one_ref, bf16[2,64,256]{2,1,0:T(8,128)(2,1)S(1)} %collective-permute-done.17.two_ref, ...), custom_call_target="tpu_custom_call" | custom-call | flops 2684354560 | bytes 7512064 | tf_op jit(solution)/shard_map/pallas_call | solution.py:26
  (38 shorter events, 0.1 us)
Async XLA Ops:
  0.0 1.2 %copy-start.6 = (bf16[2048,256]{1,0:T(8,128)(2,1)S(1)}, bf16[2048,256]{1,0:T(8,128)(2,1)}, u32[]{:S(2)}) copy-start(bf16[2048,256]{1,0:T(8,128)(2,1)} %table_ref.5) | copy-start | bytes 3145732
  1.2 0.7 copy-start.8
  2.7 13.4 %copy-start.4 = (s32[1,5120]{1,0:T(1,128)S(1)}, s32[1,5120]{1,0:T(1,128)}, u32[]{:S(2)}) copy-start(s32[1,5120]{1,0:T(1,128)} %refs_0_.1) | copy-start | bytes 61444
  2.7 13.3 %copy-start.5 = (s32[1,5120]{1,0:T(1,128)S(1)}, s32[1,5120]{1,0:T(1,128)}, u32[]{:S(2)}) copy-start(s32[1,5120]{1,0:T(1,128)} %target_ref.3) | copy-start | bytes 61444
  2.7 14.7 %copy-start = (bf16[512,256]{1,0:T(8,128)(2,1)S(1)}, bf16[512,256]{1,0:T(8,128)(2,1)}, u32[]{:S(2)}) copy-start(bf16[512,256]{1,0:T(8,128)(2,1)} %weight_ref.7) | copy-start | bytes 786436
  2.7 14.7 %copy-start.2 = (f32[1,7,256]{2,0,1:T(1,128)S(1)}, f32[1,7,256]{2,0,1:T(1,128)}, u32[]{:S(2)}) copy-start(f32[1,7,256]{2,0,1:T(1,128)} %param.17) | copy-start | bytes 21508
  2.7 14.7 %copy-start.3 = (s32[1,7,256]{2,0,1:T(1,128)S(1)}, s32[1,7,256]{2,0,1:T(1,128)}, u32[]{:S(2)}) copy-start(s32[1,7,256]{2,0,1:T(1,128)} %param.16) | copy-start | bytes 21508
  2.8 9.3 %collective-permute-start = (bf16[1,256,256]{2,1,0:T(8,128)(2,1)S(1)}, bf16[1,256,256]{2,1,0:T(8,128)(2,1)S(1)}, u32[]{:S(2)}, u32[]{:S(2)}) collective-permute-start(bf16[1,256,256]{2,1,0:T(8,128)(2,1)S(1)} %get-tuple-element.28.refs_0_), channel_id=1, source_target_pairs={{0,2},{2,0},{4,6},{6,4},{5,7},{7,5},{8,10},{10,8},{9,11},{11,9},{1... | collective-permute-start | bytes 393224 | tf_op jit(solution)/shard_map/ppermute | solution.py:93
  7.7 7.4 %collective-permute-start.2 = (bf16[1,256,256]{2,1,0:T(8,128)(2,1)S(1)}, bf16[1,256,256]{2,1,0:T(8,128)(2,1)S(1)}, u32[]{:S(2)}, u32[]{:S(2)}) collective-permute-start(bf16[1,256,256]{2,1,0:T(8,128)(2,1)S(1)} %get-tuple-element.33.refs_0_), channel_id=1, source_target_pairs={{1,3},{3,1},{5,7},{7,5},{8,10},{10,8},{12,14},{14,12},{17,19},{19,... | collective-permute-start | bytes 393224 | tf_op jit(solution)/shard_map/ppermute | solution.py:93
  13.1 15.2 %collective-permute-start.4 = (bf16[3,256,256]{2,1,0:T(8,128)(2,1)S(1)}, bf16[3,256,256]{2,1,0:T(8,128)(2,1)S(1)}, u32[]{:S(2)}, u32[]{:S(2)}) collective-permute-start(bf16[3,256,256]{2,1,0:T(8,128)(2,1)S(1)} %shard_map.123.refs_0_), channel_id=1, source_target_pairs={{0,2},{2,0},{1,3},{3,1},{4,6},{6,4},{5,7},{7,5},{8,10},{10,8},{9,1... | collective-permute-start | bytes 1179656 | tf_op jit(solution)/shard_map/ppermute | solution.py:93
  15.9 14.1 %collective-permute-start.8 = (bf16[2,256,256]{2,1,0:T(8,128)(2,1)S(1)}, bf16[2,256,256]{2,1,0:T(8,128)(2,1)S(1)}, u32[]{:S(2)}, u32[]{:S(2)}) collective-permute-start(bf16[2,256,256]{2,1,0:T(8,128)(2,1)S(1)} %shard_map.126.refs_0_), channel_id=1, source_target_pairs={{0,2},{2,0},{1,3},{3,1},{4,6},{6,4},{5,7},{7,5},{8,10},{10,8},{9,1... | collective-permute-start | bytes 786440 | tf_op jit(solution)/shard_map/ppermute | solution.py:93
  17.5 10.5 %copy-start.1 = (bf16[640,256]{1,0:T(8,128)(2,1)S(1)}, bf16[640,256]{1,0:T(8,128)(2,1)}, u32[]{:S(2)}) copy-start(bf16[640,256]{1,0:T(8,128)(2,1)} %before_ref.1) | copy-start | bytes 983044
  17.8 6.1 %collective-permute-start.3 = (bf16[272,256]{1,0:T(8,128)(2,1)S(1)}, bf16[272,256]{1,0:T(8,128)(2,1)S(1)}, u32[]{:S(2)}, u32[]{:S(2)}) collective-permute-start(bf16[272,256]{1,0:T(8,128)(2,1)S(1)} %shard_map.121), channel_id=1, source_target_pairs={{1,8},{5,12},{8,1},{12,5},{3,10},{7,14},{10,3},{14,7},{17,24},{21,... | collective-permute-start | bytes 417800 | tf_op jit(solution)/shard_map/ppermute | solution.py:75
  18.7 9.3 %collective-permute-start.1 = (bf16[272,256]{1,0:T(8,128)(2,1)S(1)}, bf16[272,256]{1,0:T(8,128)(2,1)S(1)}, u32[]{:S(2)}, u32[]{:S(2)}) collective-permute-start(bf16[272,256]{1,0:T(8,128)(2,1)S(1)} %shard_map.120), channel_id=1, source_target_pairs={{0,5},{4,9},{5,0},{8,13},{9,4},{13,8},{2,7},{6,11},{7,2},{10,15},{... | collective-permute-start | bytes 417800 | tf_op jit(solution)/shard_map/ppermute | solution.py:75
  28.8 7.0 %copy-start.10 = (bf16[2,512,256]{2,1,0:T(8,128)(2,1)S(1)}, bf16[2,512,256]{2,1,0:T(8,128)(2,1)}, u32[]{:S(2)}) copy-start(bf16[2,512,256]{2,1,0:T(8,128)(2,1)} %param.19) | copy-start | bytes 1572868
  28.8 7.0 %copy-start.11 = (bf16[2,512,256]{2,1,0:T(8,128)(2,1)S(1)}, bf16[2,512,256]{2,1,0:T(8,128)(2,1)}, u32[]{:S(2)}) copy-start(bf16[2,512,256]{2,1,0:T(8,128)(2,1)} %param.18) | copy-start | bytes 1572868
  28.8 5.3 %collective-permute-start.5 = (bf16[272,256]{1,0:T(8,128)(2,1)S(1)}, bf16[272,256]{1,0:T(8,128)(2,1)S(1)}, u32[]{:S(2)}, u32[]{:S(2)}) collective-permute-start(bf16[272,256]{1,0:T(8,128)(2,1)S(1)} %get-tuple-element.34), channel_id=1, source_target_pairs={{0,4},{1,5},{4,0},{5,1},{8,12},{9,13},{12,8},{13,9},{2,6},{3,7},{6... | collective-permute-start | bytes 417800 | tf_op jit(solution)/shard_map/ppermute | solution.py:75
  29.4 4.8 %collective-permute-start.6 = (bf16[272,256]{1,0:T(8,128)(2,1)S(1)}, bf16[272,256]{1,0:T(8,128)(2,1)S(1)}, u32[]{:S(2)}, u32[]{:S(2)}) collective-permute-start(bf16[272,256]{1,0:T(8,128)(2,1)S(1)} %get-tuple-element.35), channel_id=1, source_target_pairs={{4,8},{5,9},{8,4},{9,5},{6,10},{7,11},{10,6},{11,7},{20,24},{21,25... | collective-permute-start | bytes 417800 | tf_op jit(solution)/shard_map/ppermute | solution.py:75
  30.4 11.7 %copy-start.9 = (s32[1,6,64]{2,0,1:T(1,128)S(1)}, s32[1,6,64]{2,0,1:T(1,128)}, u32[]{:S(2)}) copy-start(s32[1,6,64]{2,0,1:T(1,128)} %param.20) | copy-start | bytes 4612
  30.4 4.1 %collective-permute-start.9 = (bf16[272,256]{1,0:T(8,128)(2,1)S(1)}, bf16[272,256]{1,0:T(8,128)(2,1)S(1)}, u32[]{:S(2)}, u32[]{:S(2)}) collective-permute-start(bf16[272,256]{1,0:T(8,128)(2,1)S(1)} %get-tuple-element.37), channel_id=1, source_target_pairs={{0,1},{1,0},{4,5},{5,4},{8,9},{9,8},{12,13},{13,12},{2,3},{3,2},{6... | collective-permute-start | bytes 417800 | tf_op jit(solution)/shard_map/ppermute | solution.py:75
  30.8 3.7 %collective-permute-start.7 = (bf16[272,256]{1,0:T(8,128)(2,1)S(1)}, bf16[272,256]{1,0:T(8,128)(2,1)S(1)}, u32[]{:S(2)}, u32[]{:S(2)}) collective-permute-start(bf16[272,256]{1,0:T(8,128)(2,1)S(1)} %get-tuple-element.36), channel_id=1, source_target_pairs={{1,4},{4,1},{5,8},{8,5},{9,12},{12,9},{3,6},{6,3},{7,10},{10,7},{1... | collective-permute-start | bytes 417800 | tf_op jit(solution)/shard_map/ppermute | solution.py:75
  35.0 7.1 %collective-permute-start.10 = (bf16[640,256]{1,0:T(8,128)(2,1)S(1)}, bf16[640,256]{1,0:T(8,128)(2,1)S(1)}, u32[]{:S(2)}, u32[]{:S(2)}) collective-permute-start(bf16[640,256]{1,0:T(8,128)(2,1)S(1)} %shard_map.128.refs_0_.state_ref), channel_id=1, source_target_pairs={{0,2},{2,0},{1,3},{3,1},{4,6},{6,4},{5,7},{7,5},{8,10},{10,8},{9,1... | collective-permute-start | bytes 983048 | tf_op jit(solution)/shard_map/ppermute | solution.py:93
  42.8 12.5 %collective-permute-start.11 = (bf16[2,64,256]{2,1,0:T(8,128)(2,1)S(1)}, bf16[2,64,256]{2,1,0:T(8,128)(2,1)S(1)}, u32[]{:S(2)}, u32[]{:S(2)}) collective-permute-start(bf16[2,64,256]{2,1,0:T(8,128)(2,1)S(1)} %get-tuple-element.39), channel_id=1, source_target_pairs={{0,4},{1,5},{4,0},{5,1},{8,12},{9,13},{12,8},{13,9},{2,6},{3,7},{6... | collective-permute-start | bytes 196616 | tf_op jit(solution)/shard_map/ppermute | solution.py:75
  51.6 3.7 %collective-permute-start.12 = (bf16[2,64,256]{2,1,0:T(8,128)(2,1)S(1)}, bf16[2,64,256]{2,1,0:T(8,128)(2,1)S(1)}, u32[]{:S(2)}, u32[]{:S(2)}) collective-permute-start(bf16[2,64,256]{2,1,0:T(8,128)(2,1)S(1)} %get-tuple-element.40), channel_id=1, source_target_pairs={{4,8},{5,9},{8,4},{9,5},{6,10},{7,11},{10,6},{11,7},{20,24},{21,25... | collective-permute-start | bytes 196616 | tf_op jit(solution)/shard_map/ppermute | solution.py:75
  52.3 9.5 %collective-permute-start.13 = (bf16[64,256]{1,0:T(8,128)(2,1)S(1)}, bf16[64,256]{1,0:T(8,128)(2,1)S(1)}, u32[]{:S(2)}, u32[]{:S(2)}) collective-permute-start(bf16[64,256]{1,0:T(8,128)(2,1)S(1)} %get-tuple-element.41), channel_id=1, source_target_pairs={{1,8},{5,12},{8,1},{12,5},{3,10},{7,14},{10,3},{14,7},{17,24},{21,... | collective-permute-start | bytes 98312 | tf_op jit(solution)/shard_map/ppermute | solution.py:75
  55.4 6.4 %copy-start.7 = (f32[1,5120]{1,0:T(1,128)S(1)}, f32[1,5120]{1,0:T(1,128)}, u32[]{:S(2)}) copy-start(f32[1,5120]{1,0:T(1,128)} %coef_ref.3) | copy-start | bytes 61444
  55.4 6.4 %collective-permute-start.14 = (bf16[3,64,256]{2,1,0:T(8,128)(2,1)S(1)}, bf16[3,64,256]{2,1,0:T(8,128)(2,1)S(1)}, u32[]{:S(2)}, u32[]{:S(2)}) collective-permute-start(bf16[3,64,256]{2,1,0:T(8,128)(2,1)S(1)} %shard_map.131.refs_0_), channel_id=1, source_target_pairs={{0,1},{1,0},{4,5},{5,4},{8,9},{9,8},{12,13},{13,12},{2,3},{3,2},{6... | collective-permute-start | bytes 294920 | tf_op jit(solution)/shard_map/ppermute | solution.py:75
  66.1 9.7 %collective-permute-start.15 = (bf16[640,256]{1,0:T(8,128)(2,1)S(1)}, bf16[640,256]{1,0:T(8,128)(2,1)S(1)}, u32[]{:S(2)}, u32[]{:S(2)}) collective-permute-start(bf16[640,256]{1,0:T(8,128)(2,1)S(1)} %shard_map.133.refs_0_.state_ref), channel_id=1, source_target_pairs={{0,2},{2,0},{1,3},{3,1},{4,6},{6,4},{5,7},{7,5},{8,10},{10,8},{9,1... | collective-permute-start | bytes 983048 | tf_op jit(solution)/shard_map/ppermute | solution.py:93
  76.5 4.3 %collective-permute-start.16 = (bf16[2,64,256]{2,1,0:T(8,128)(2,1)S(1)}, bf16[2,64,256]{2,1,0:T(8,128)(2,1)S(1)}, u32[]{:S(2)}, u32[]{:S(2)}) collective-permute-start(bf16[2,64,256]{2,1,0:T(8,128)(2,1)S(1)} %get-tuple-element.45), channel_id=1, source_target_pairs={{0,4},{1,5},{4,0},{5,1},{8,12},{9,13},{12,8},{13,9},{2,6},{3,7},{6... | collective-permute-start | bytes 196616 | tf_op jit(solution)/shard_map/ppermute | solution.py:75
  76.8 4.1 %collective-permute-start.17 = (bf16[2,64,256]{2,1,0:T(8,128)(2,1)S(1)}, bf16[2,64,256]{2,1,0:T(8,128)(2,1)S(1)}, u32[]{:S(2)}, u32[]{:S(2)}) collective-permute-start(bf16[2,64,256]{2,1,0:T(8,128)(2,1)S(1)} %get-tuple-element.46), channel_id=1, source_target_pairs={{4,8},{5,9},{8,4},{9,5},{6,10},{7,11},{10,6},{11,7},{20,24},{21,25... | collective-permute-start | bytes 196616 | tf_op jit(solution)/shard_map/ppermute | solution.py:75
  77.4 11.3 %collective-permute-start.18 = (bf16[64,256]{1,0:T(8,128)(2,1)S(1)}, bf16[64,256]{1,0:T(8,128)(2,1)S(1)}, u32[]{:S(2)}, u32[]{:S(2)}) collective-permute-start(bf16[64,256]{1,0:T(8,128)(2,1)S(1)} %get-tuple-element.47), channel_id=1, source_target_pairs={{1,8},{5,12},{8,1},{12,5},{3,10},{7,14},{10,3},{14,7},{17,24},{21,... | collective-permute-start | bytes 98312 | tf_op jit(solution)/shard_map/ppermute | solution.py:75
  80.9 7.9 %collective-permute-start.19 = (bf16[3,64,256]{2,1,0:T(8,128)(2,1)S(1)}, bf16[3,64,256]{2,1,0:T(8,128)(2,1)S(1)}, u32[]{:S(2)}, u32[]{:S(2)}) collective-permute-start(bf16[3,64,256]{2,1,0:T(8,128)(2,1)S(1)} %shard_map.136.refs_0_), channel_id=1, source_target_pairs={{0,1},{1,0},{4,5},{5,4},{8,9},{9,8},{12,13},{13,12},{2,3},{3,2},{6... | collective-permute-start | bytes 294920 | tf_op jit(solution)/shard_map/ppermute | solution.py:75

commit v4 on v3

--- a/solution.py
+++ b/solution.py
@@ -32,7 +32,7 @@
         compiler_params=pltpu.CompilerParams(vmem_limit_bytes=VMEM_BYTES),
         cost_estimate=pl.CostEstimate(
             flops=flops,
-            bytes_accessed=sum(size(a) for a in list(inputs) + list(outputs)),
+            bytes_accessed=sum(size(a) for a in list(inputs) + list(outputs)) if flops else 0,
             transcendentals=transcendentals,
         ),
     )(*inputs[:fetched], *[taken_from_vmem(a) for a in inputs[fetched:]])
@@ -262,18 +262,8 @@
     )
 
 
-def project_kernel(others, reach, src_ref, dst_ref, listed_ref, *refs):
-    states, (sender_ref, receiver_ref, one_ref, two_ref, far_ref, near_ref) = (
-        refs[: others + 1],
-        refs[others + 1 :],
-    )
-    nodes, channels = states[0].shape
-    for weight_ref, out_ref in ((src_ref, sender_ref), (dst_ref, receiver_ref)):
-        weights = own_and_others_rows(weight_ref, channels, others)
-        total = dot(states[0][...], weights[0])
-        for state, weight in zip(states[1:], weights[1:]):
-            total += dot(state[...], weight)
-        out_ref[...] = total.astype(jnp.bfloat16)
+def list_kernel(reach, listed_ref, state_ref, one_ref, two_ref, far_ref, near_ref):
+    nodes = state_ref.shape[0]
     width = listed_ref.shape[2]
     lanes = lane_iota(nodes)
     region = lax.axis_index(REGION)
@@ -285,7 +275,7 @@
     wanted = [offset + reach - jnp.where(offset > 0, 1, 0) for offset in wanted]
     for k in range(0, len(wanted), 2):
         row = jnp.concatenate([listed_ref[wanted[k + i]] for i in range(2)], axis=1)
-        rows = dot(pick_mask(column(row).astype(jnp.int16), lanes), sender_ref[...])
+        rows = dot(pick_mask(column(row).astype(jnp.int16), lanes), state_ref[...])
         rows = rows.astype(jnp.bfloat16)
         parts = [rows[i * width : (i + 1) * width] for i in range(2)]
         if k < 4:
@@ -297,53 +287,26 @@
             near_ref[...] = parts[1]
 
 
-def project(state, arrived, src_weight, dst_weight, halo_send, reach):
+def list_rows(state, halo_send, reach):
     nodes, channels = state.shape
     links, unused, width = halo_send.shape
-    depth = src_weight.shape[0]
-    table, one, two = [shape(d) for d in ((nodes, channels), (width, channels), (2, width, channels))]
-    return call(
-        functools.partial(project_kernel, len(arrived), reach),
-        [table, table, two, two, one, one],
-        [src_weight, dst_weight, halo_send, state, *arrived],
-        4 * nodes * depth * channels + 2 * links * width * nodes * channels,
-    )
-
-
-def forward_kernel(near_ref, one_ref, two_ref, unused_ref, out_ref):
+    one, two = [shape(d) for d in ((width, channels), (2, width, channels))]
+    return call(
+        functools.partial(list_kernel, reach),
+        [two, two, one, one],
+        [halo_send, state],
+        0,
+    )
+
+
+def forward_kernel(near_ref, one_ref, two_ref, out_ref):
     other = 1 - lax.axis_index("edge")
     out_ref[0] = near_ref[...]
     out_ref[1] = one_ref[other]
     out_ref[2] = two_ref[other]
 
 
-def first_kernel(turn, source_ref, target_ref, sender_ref, receiver_ref, *refs):
-    out_ref = refs[-1]
-    nodes = sender_ref.shape[0]
-    lanes = lane_iota(nodes)
-    for start in range(0, source_ref.shape[0], turn):
-        here = pl.ds(start, turn)
-        out_ref[here, :] = dot(pick_mask(source_ref[here, :], lanes), sender_ref[...]) + dot(
-            pick_mask(target_ref[here, :], lanes), receiver_ref[...]
-        )
-
-
-def first_part(source_col, target_col, sender, receiver, after=()):
-    nodes, channels = sender.shape
-    edges = source_col.shape[0]
-    return call(
-        functools.partial(first_kernel, 512),
-        [shape((edges, channels), jnp.float32)],
-        [source_col, target_col, sender, receiver, *after],
-        4 * edges * nodes * channels,
-    )[0]
-
-
-def message_kernel(
-    turn, halves, target_ref, coef_ref, state_ref, one_ref, two_ref, distant_ref, across_ref, *refs
-):
-    sources, firsts, (out_ref, table_ref) = (refs[:halves], refs[halves : 2 * halves], refs[2 * halves :])
-    nodes, channels = state_ref.shape
+def order_kernel(one_ref, two_ref, distant_ref, across_ref, out_ref):
     width = distant_ref.shape[0]
     region = lax.axis_index(REGION)
     core = region % 2
@@ -365,32 +328,94 @@
         jnp.where(even, distant, before[1]),
     )
     for j, part in enumerate(rows):
-        table_ref[pl.ds(j * width, width), :] = part
-    lanes = (lane_iota(len(rows) * width).astype(jnp.int32) + nodes).astype(jnp.int16)
+        out_ref[pl.ds(j * width, width), :] = part
+
+
+def exchange_listed(one, two, far, near):
+    width, channels = near.shape
+    one, two = swapped(one, meets_two), swapped(two, meets_other_two)
+    distant = swapped(far, meets_other_three)
+    sent = call(forward_kernel, [shape((3, width, channels))], [near, one, two], 0)[0]
+    across = swapped(sent, meets_core)
+    return call(
+        order_kernel, [shape((6 * width, channels))], [one, two, distant, across], 0
+    )[0]
+
+
+def projected_rows(weight_ref, parts):
+    weights = own_and_others_rows(weight_ref, parts[0].shape[1], len(parts) - 1)
+    total = dot(parts[0][...], weights[0])
+    for part, weight in zip(parts[1:], weights[1:]):
+        total += dot(part[...], weight)
+    return total.astype(jnp.bfloat16)
+
+
+def project_kernel(src_ref, dst_ref, *refs):
+    states, table_ref = (refs[:-1], refs[-1])
+    nodes = states[0].shape[0]
+    table_ref[pl.ds(0, nodes), :] = projected_rows(src_ref, states)
+    table_ref[pl.ds(nodes, nodes), :] = projected_rows(dst_ref, states)
+
+
+def project(states, src_weight, dst_weight):
+    nodes, channels = states[0].shape
+    depth = src_weight.shape[0]
+    return call(
+        project_kernel,
+        [shape((2 * nodes, channels))],
+        [src_weight, dst_weight, *states],
+        4 * nodes * depth * channels,
+    )[0]
+
+
+def first_kernel(turn, source_ref, target_ref, table_ref, out_ref):
+    lanes = lane_iota(table_ref.shape[0] // 2)
+    for start in range(0, source_ref.shape[0], turn):
+        here = pl.ds(start, turn)
+        mask = jnp.concatenate(
+            [pick_mask(source_ref[here, :], lanes), pick_mask(target_ref[here, :], lanes)], axis=1
+        )
+        out_ref[here, :] = dot(mask, table_ref[...])
+
+
+def first_part(source_col, target_col, table):
+    rows, channels = table.shape
+    edges = source_col.shape[0]
+    return call(
+        functools.partial(first_kernel, 512),
+        [shape((edges, channels), jnp.float32)],
+        [source_col, target_col, table],
+        2 * edges * rows * channels,
+    )[0]
+
+
+def message_kernel(turn, source_ref, target_ref, coef_ref, state_ref, first_ref, weight_ref, *refs):
+    listed, (out_ref, message_ref) = (refs[:-2], refs[-2:])
+    nodes, channels = state_ref.shape
+    table = projected_rows(weight_ref, listed)
+    lanes = (lane_iota(table.shape[0]).astype(jnp.int32) + nodes).astype(jnp.int16)
     rows16 = row_iota(nodes)
     total = state_ref[...].astype(jnp.float32)
-    for half, (source_ref, first_ref) in enumerate(zip(sources, firsts)):
-        count = source_ref.shape[0]
-        for start in range(0, count, turn):
-            here = pl.ds(start, turn)
-            there = pl.ds(half * count + start, turn)
-            summed = first_ref[here, :] + dot(pick_mask(source_ref[here, :], lanes), table_ref[...])
-            mask = sum_mask(target_ref[:, there], rows16, coef_ref[:, there])
-            total += dot(mask, silu(summed).astype(jnp.bfloat16))
+    for start in range(0, source_ref.shape[0], turn):
+        here = pl.ds(start, turn)
+        summed = first_ref[here, :] + dot(pick_mask(source_ref[here, :], lanes), table)
+        message_ref[here, :] = silu(summed).astype(jnp.bfloat16)
+        mask = sum_mask(target_ref[:, here], rows16, coef_ref[:, here])
+        total += dot(mask, message_ref[here, :])
     out_ref[...] = total.astype(jnp.bfloat16)
 
 
-def messages(m2m_dst, m2m_coef, state, listed, sources, firsts, final):
+def messages(source_col, m2m_dst, m2m_coef, state, first, src_weight, listed, final):
     nodes, channels = state.shape
     edges = m2m_dst.shape[1]
-    named = 6 * listed[2].shape[0]
-    return call(
-        functools.partial(message_kernel, 512, len(sources)),
+    named = listed[0].shape[0]
+    return call(
+        functools.partial(message_kernel, 1024),
         [shape((nodes, channels))],
-        [m2m_dst, m2m_coef, state, *listed, *sources, *firsts],
+        [source_col, m2m_dst, m2m_coef, state, first, src_weight, *listed],
         2 * edges * (named + nodes) * channels,
         edges * channels,
-        [pltpu.VMEM((named, channels), jnp.bfloat16)],
+        [pltpu.VMEM((edges, channels), jnp.bfloat16)],
         final,
     )[0]
 
@@ -414,43 +439,37 @@
     g2m_src, g2m_dst, g2m_coef, halo_send = [
         jnp.swapaxes(a, 0, 1) for a in (g2m_src, g2m_dst, g2m_coef, halo_send)
     ]
-    cols = columns(2, m2m_src, m2m_dst)
-    source_cols, target_cols = cols[:2], cols[2:]
-    groups = [(meets_three,), (meets_other_three,), (meets_two, meets_other_two, meets_next), (meets_core, None)]
+    source_col, target_col = cols = columns(1, m2m_src, m2m_dst)
+    groups = [
+        (meets_three,), (meets_other_three,), (meets_two, meets_other_two), (meets_next,), (meets_core, None)
+    ]
     picked = pick(groups[:2], g2m_src, grid_latent)
     arrived = [from_others(rows, group[0]) for group, rows in zip(groups, picked)]
-    for place in (2, 3):
-        picked += pick(groups[place : place + 1], g2m_src, grid_latent, arrived[place - 2])
+    for place, before in ((2, 0), (3, 1), (4, 3)):
+        picked += pick(groups[place : place + 1], g2m_src, grid_latent, arrived[before])
         arrived.append(from_others(picked[place]))
+    sent = []
     state = mesh_latent
-    after = cols
-    waiting = []
-    for place, (group, rows, others) in enumerate(zip(groups, picked, arrived)):
-        encoded = encode(group, rows, others, enc_weight, g2m_coef, g2m_dst, after)
-        waiting += [
-            block if meets is None else swapped(block, meets) for meets, block in zip(group, encoded)
+    for place in (0, 1, 3, 2, 4):
+        after = {0: cols, 2: [state]}.get(place, ())
+        encoded = encode(groups[place], picked[place], arrived[place], enc_weight, g2m_coef, g2m_dst, after)
+        sent += [
+            block if meets is None else swapped(block, meets) for meets, block in zip(groups[place], encoded)
         ]
-        if place == 1:
-            state = gather_in(state, waiting, jnp.float32)
-            waiting, after = ([], [state])
-    state = gather_in(state, waiting[:2], jnp.float32)
-    state = gather_in(state, waiting[2:], jnp.bfloat16)
+        if place == 3:
+            state = gather_in(state, sent[:2], jnp.float32)
+    state = gather_in(state, sent[2:5], jnp.float32)
+    state = gather_in(state, sent[5:], jnp.bfloat16)
     layers = src_weights.shape[0]
     for layer in range(layers):
-        sender, receiver, one, two, far, near = project(
-            state, from_others(state), src_weights[layer], dst_weights[layer], halo_send, reach
-        )
-        one, two = swapped(one, meets_two), swapped(two, meets_other_two)
-        distant = swapped(far, meets_other_three)
-        firsts = [first_part(source_cols[0], target_cols[0], sender, receiver)]
-        width, channels = near.shape
-        sent = call(
-            forward_kernel, [shape((3, width, channels))], [near, one, two, firsts[0]], 3 * width * channels
-        )[0]
-        across = swapped(sent, meets_core)
-        firsts.append(first_part(source_cols[1], target_cols[1], sender, receiver, [sent]))
+        src_weight, dst_weight = src_weights[layer], dst_weights[layer]
+        others = from_others(state)
+        listed = exchange_listed(*list_rows(state, halo_send, reach))
+        table = project([state, *others], src_weight, dst_weight)
+        listed = [listed, *from_others(listed)]
+        first = first_part(source_col, target_col, table)
         state = messages(
-            m2m_dst, m2m_coef, state, (one, two, distant, across), source_cols, firsts, layer == layers - 1
+            source_col, m2m_dst, m2m_coef, state, first, src_weight, listed, layer == layers - 1
         )
     return state
 

time: 94.2 us -> 89.3 us (0.948)
  the two profiles are of different devices: /device:TPU:0 before, /device:TPU:9 now
where the time goes in v4:
time: 89.3 us; the launch traced here: 88.9 us
  starting transfers between devices  44.3 us (50%)
  Pallas kernels  25.6 us (29%)
  waiting for transfers between devices  16.5 us (18%)
  local copies, waits for them, and re-layouts  2.08 us (2%)
    ppermute x14, starting transfers between devices, swapped(): return lax.ppermute(value, REGION, pairs(meets))  33 us
    pallas_call x25, Pallas kernels, call(): pl.pallas_call(kernel, out_shape=shapes, in_specs=[pl.BlockSpec(memory_sp...  25.6 us
    ppermute x14, waiting for transfers between devices, swapped(): return lax.ppermute(value, REGION, pairs(meets))  11.5 us
    ppermute x9, starting transfers between devices, from_others(): lax.ppermute(value, axes, [(ring[i], ring[(i + k) % n]) for ring in rings...  11.4 us
    ppermute x9, waiting for transfers between devices, from_others(): lax.ppermute(value, axes, [(ring[i], ring[(i + k) % n]) for ring in rings...  4.99 us
    unnamed x24, local copies, waits for them, and re-layouts  2.01 us
  transfers between devices with their start and end apart: 23, of which 10 were waited for; matrix products, arithmetic and copies ran while one was open for 0% of the time, Pallas kernels for 16%

profile of v4, /device:TPU:9, one launch (start us, length us, event | category | flops | bytes accessed | tf_op | source)
XLA Modules:
  0.0 88.9 jit_solution(3095752587419978177)
XLA Ops:
  0.0 1.3 %copy-done.1 = bf16[2048,256]{1,0:T(8,128)(2,1)S(1)} copy-done((bf16[2048,256]{1,0:T(8,128)(2,1)S(1)}, bf16[2048,256]{1,0:T(8,128)(2,1)}, u32[]{:S(2)}) %copy-start.1) | copy-done | bytes 1048600
  1.3 0.7 copy-done.8
  2.0 0.8 shard_map.119
  2.8 3.2 %collective-permute-start.2 = (bf16[1,256,256]{2,1,0:T(8,128)(2,1)S(1)}, bf16[1,256,256]{2,1,0:T(8,128)(2,1)S(1)}, u32[]{:S(2)}, u32[]{:S(2)}) collective-permute-start(bf16[1,256,256]{2,1,0:T(8,128)(2,1)S(1)} %get-tuple-element.24.refs_0_), channel_id=1, source_target_pairs={{1,3},{3,1},{5,7},{7,5},{8,10},{10,8},{12,14},{14,12},{17,19},{19,... | collective-permute-start | bytes 393224 | tf_op jit(solution)/shard_map/ppermute | solution.py:93
  6.0 2.2 %collective-permute-start = (bf16[1,256,256]{2,1,0:T(8,128)(2,1)S(1)}, bf16[1,256,256]{2,1,0:T(8,128)(2,1)S(1)}, u32[]{:S(2)}, u32[]{:S(2)}) collective-permute-start(bf16[1,256,256]{2,1,0:T(8,128)(2,1)S(1)} %get-tuple-element.22.refs_0_), channel_id=1, source_target_pairs={{0,2},{2,0},{4,6},{6,4},{5,7},{7,5},{8,10},{10,8},{9,11},{11,9},{1... | collective-permute-start | bytes 393224 | tf_op jit(solution)/shard_map/ppermute | solution.py:93
  8.2 0.4 collective-permute-done.2.refs_1_.refs_0_
  8.6 0.5 shard_map.123.refs_0_
  9.1 1.3 %collective-permute-start.4 = (bf16[1,256,256]{2,1,0:T(8,128)(2,1)S(1)}, bf16[1,256,256]{2,1,0:T(8,128)(2,1)S(1)}, u32[]{:S(2)}, u32[]{:S(2)}) collective-permute-start(bf16[1,256,256]{2,1,0:T(8,128)(2,1)S(1)} %shard_map.123.refs_0_), channel_id=1, source_target_pairs={{0,2},{2,0},{1,3},{3,1},{4,6},{6,4},{5,7},{7,5},{8,10},{10,8},{9,1... | collective-permute-start | bytes 393224 | tf_op jit(solution)/shard_map/ppermute | solution.py:93
  10.4 2.5 %collective-permute-done.refs_1_.refs_0_ = bf16[1,256,256]{2,1,0:T(8,128)(2,1)S(1)} collective-permute-done((bf16[1,256,256]{2,1,0:T(8,128)(2,1)S(1)}, bf16[1,256,256]{2,1,0:T(8,128)(2,1)S(1)}, u32[]{:S(2)}, u32[]{:S(2)}) %collective-permute-start) | collective-permute-done | bytes 131104 | tf_op jit(solution)/shard_map/ppermute | solution.py:93
  12.9 0.8 shard_map.125.refs_0_
  13.6 0.8 collective-permute-start.6
  14.6 0.8 shard_map.128.refs_0_
  15.4 1.3 %collective-permute-start.9 = (bf16[2,256,256]{2,1,0:T(8,128)(2,1)S(1)}, bf16[2,256,256]{2,1,0:T(8,128)(2,1)S(1)}, u32[]{:S(2)}, u32[]{:S(2)}) collective-permute-start(bf16[2,256,256]{2,1,0:T(8,128)(2,1)S(1)} %shard_map.128.refs_0_), channel_id=1, source_target_pairs={{0,2},{2,0},{1,3},{3,1},{4,6},{6,4},{5,7},{7,5},{8,10},{10,8},{9,1... | collective-permute-start | bytes 786440 | tf_op jit(solution)/shard_map/ppermute | solution.py:93
  16.7 1.4 %shard_map.118 = (s16[5120,128]{1,0:T(8,128)(2,1)S(1)}, s16[5120,128]{1,0:T(8,128)(2,1)S(1)}) custom-call(s32[1,5120]{1,0:T(1,128)S(1)} %copy-done.5, s32[1,5120]{1,0:T(1,128)S(1)} %copy-done.6), custom_call_target="tpu_custom_call" | custom-call | flops 10485760 | bytes 2662400 | tf_op jit(solution)/shard_map/pallas_call | solution.py:26
  18.4 2.1 %collective-permute-start.1 = (bf16[272,256]{1,0:T(8,128)(2,1)S(1)}, bf16[272,256]{1,0:T(8,128)(2,1)S(1)}, u32[]{:S(2)}, u32[]{:S(2)}) collective-permute-start(bf16[272,256]{1,0:T(8,128)(2,1)S(1)} %shard_map.120), channel_id=1, source_target_pairs={{0,5},{4,9},{5,0},{8,13},{9,4},{13,8},{2,7},{6,11},{7,2},{10,15},{... | collective-permute-start | bytes 417800 | tf_op jit(solution)/shard_map/ppermute | solution.py:75
  20.8 7.2 %collective-permute-start.3 = (bf16[272,256]{1,0:T(8,128)(2,1)S(1)}, bf16[272,256]{1,0:T(8,128)(2,1)S(1)}, u32[]{:S(2)}, u32[]{:S(2)}) collective-permute-start(bf16[272,256]{1,0:T(8,128)(2,1)S(1)} %shard_map.121), channel_id=1, source_target_pairs={{1,8},{5,12},{8,1},{12,5},{3,10},{7,14},{10,3},{14,7},{17,24},{21,... | collective-permute-start | bytes 417800 | tf_op jit(solution)/shard_map/ppermute | solution.py:75
  28.2 2.2 %collective-permute-start.5 = (bf16[272,256]{1,0:T(8,128)(2,1)S(1)}, bf16[272,256]{1,0:T(8,128)(2,1)S(1)}, u32[]{:S(2)}, u32[]{:S(2)}) collective-permute-start(bf16[272,256]{1,0:T(8,128)(2,1)S(1)} %shard_map.124), channel_id=1, source_target_pairs={{1,4},{4,1},{5,8},{8,5},{9,12},{12,9},{3,6},{6,3},{7,10},{10,7},{1... | collective-permute-start | bytes 417800 | tf_op jit(solution)/shard_map/ppermute | solution.py:75
  30.4 1.0 %collective-permute-done.3.refs_1_ = bf16[272,256]{1,0:T(8,128)(2,1)S(1)} collective-permute-done((bf16[272,256]{1,0:T(8,128)(2,1)S(1)}, bf16[272,256]{1,0:T(8,128)(2,1)S(1)}, u32[]{:S(2)}, u32[]{:S(2)}) %collective-permute-start.3) | collective-permute-done | bytes 139296 | tf_op jit(solution)/shard_map/ppermute | solution.py:75
  31.5 0.3 shard_map.122.refs_2_.before_ref
  31.8 0.4 shard_map.126
  32.2 2.1 %collective-permute-start.7 = (bf16[272,256]{1,0:T(8,128)(2,1)S(1)}, bf16[272,256]{1,0:T(8,128)(2,1)S(1)}, u32[]{:S(2)}, u32[]{:S(2)}) collective-permute-start(bf16[272,256]{1,0:T(8,128)(2,1)S(1)} %get-tuple-element.25), channel_id=1, source_target_pairs={{0,4},{1,5},{4,0},{5,1},{8,12},{9,13},{12,8},{13,9},{2,6},{3,7},{6... | collective-permute-start | bytes 417800 | tf_op jit(solution)/shard_map/ppermute | solution.py:75
  34.3 1.9 %collective-permute-start.8 = (bf16[272,256]{1,0:T(8,128)(2,1)S(1)}, bf16[272,256]{1,0:T(8,128)(2,1)S(1)}, u32[]{:S(2)}, u32[]{:S(2)}) collective-permute-start(bf16[272,256]{1,0:T(8,128)(2,1)S(1)} %get-tuple-element.26), channel_id=1, source_target_pairs={{4,8},{5,9},{8,4},{9,5},{6,10},{7,11},{10,6},{11,7},{20,24},{21,25... | collective-permute-start | bytes 417800 | tf_op jit(solution)/shard_map/ppermute | solution.py:75
  36.2 0.4 shard_map.129
  36.6 2.4 %collective-permute-start.10 = (bf16[272,256]{1,0:T(8,128)(2,1)S(1)}, bf16[272,256]{1,0:T(8,128)(2,1)S(1)}, u32[]{:S(2)}, u32[]{:S(2)}) collective-permute-start(bf16[272,256]{1,0:T(8,128)(2,1)S(1)} %get-tuple-element.27), channel_id=1, source_target_pairs={{0,1},{1,0},{4,5},{5,4},{8,9},{9,8},{12,13},{13,12},{2,3},{3,2},{6... | collective-permute-start | bytes 417800 | tf_op jit(solution)/shard_map/ppermute | solution.py:75
  39.1 2.0 %collective-permute-done.8.refs_2_ = bf16[272,256]{1,0:T(8,128)(2,1)S(1)} collective-permute-done((bf16[272,256]{1,0:T(8,128)(2,1)S(1)}, bf16[272,256]{1,0:T(8,128)(2,1)S(1)}, u32[]{:S(2)}, u32[]{:S(2)}) %collective-permute-start.8) | collective-permute-done | bytes 139296 | tf_op jit(solution)/shard_map/ppermute | solution.py:75
  41.1 0.4 shard_map.127.before_ref
  41.5 0.3 shard_map.130.refs_0_.state_ref
  41.9 0.5 shard_map.133
  42.4 1.9 %collective-permute-start.13 = (bf16[2,64,256]{2,1,0:T(8,128)(2,1)S(1)}, bf16[2,64,256]{2,1,0:T(8,128)(2,1)S(1)}, u32[]{:S(2)}, u32[]{:S(2)}) collective-permute-start(bf16[2,64,256]{2,1,0:T(8,128)(2,1)S(1)} %get-tuple-element.30), channel_id=1, source_target_pairs={{4,8},{5,9},{8,4},{9,5},{6,10},{7,11},{10,6},{11,7},{20,24},{21,25... | collective-permute-start | bytes 196616 | tf_op jit(solution)/shard_map/ppermute | solution.py:75
  44.7 4.7 %collective-permute-start.14 = (bf16[64,256]{1,0:T(8,128)(2,1)S(1)}, bf16[64,256]{1,0:T(8,128)(2,1)S(1)}, u32[]{:S(2)}, u32[]{:S(2)}) collective-permute-start(bf16[64,256]{1,0:T(8,128)(2,1)S(1)} %get-tuple-element.31), channel_id=1, source_target_pairs={{1,8},{5,12},{8,1},{12,5},{3,10},{7,14},{10,3},{14,7},{17,24},{21,... | collective-permute-start | bytes 98312 | tf_op jit(solution)/shard_map/ppermute | solution.py:75
  49.4 0.4 collective-permute-start.15
  49.9 0.9 collective-permute-done.14.distant_ref
  50.8 1.3 %collective-permute-start.16 = (bf16[384,256]{1,0:T(8,128)(2,1)S(1)}, bf16[384,256]{1,0:T(8,128)(2,1)S(1)}, u32[]{:S(2)}, u32[]{:S(2)}) collective-permute-start(bf16[384,256]{1,0:T(8,128)(2,1)S(1)} %shard_map.135.refs_0_), channel_id=1, source_target_pairs={{0,2},{2,0},{1,3},{3,1},{4,6},{6,4},{5,7},{7,5},{8,10},{10,8},{9,1... | collective-permute-start | bytes 589832 | tf_op jit(solution)/shard_map/ppermute | solution.py:93
  52.1 0.5 shard_map.131.table_ref
  52.6 3.5 %shard_map.132.first_ref = f32[5120,256]{1,0:T(8,128)S(1)} custom-call(s16[5120,128]{1,0:T(8,128)(2,1)S(1)} %get-tuple-element.21.refs_2_.source_ref, s16[5120,128]{1,0:T(8,128)(2,1)S(1)} %get-tuple-element.23.refs_3_.target_ref, bf16[1280,256]{1,0:T(8,128)(2,1)S(1)} %shard_map.131.table_ref), custom_call_target="tpu_custom_call" | custom-call | flops 3355443200 | bytes 8519680 | tf_op jit(solution)/shard_map/pallas_call | solution.py:26
  56.2 1.7 %collective-permute-done.16.refs_1_ = bf16[384,256]{1,0:T(8,128)(2,1)S(1)} collective-permute-done((bf16[384,256]{1,0:T(8,128)(2,1)S(1)}, bf16[384,256]{1,0:T(8,128)(2,1)S(1)}, u32[]{:S(2)}, u32[]{:S(2)}) %collective-permute-start.16) | collective-permute-done | bytes 196640 | tf_op jit(solution)/shard_map/ppermute | solution.py:93
  57.9 4.5 %shard_map.136.refs_0_.state_ref = bf16[640,256]{1,0:T(8,128)(2,1)S(1)} custom-call(s16[5120,128]{1,0:T(8,128)(2,1)S(1)} %get-tuple-element.21.refs_2_.source_ref, s32[1,5120]{1,0:T(1,128)S(1)} %copy-done.6, f32[1,5120]{1,0:T(1,128)S(1)} %copy-done.9, bf16[640,256]{1,0:T(8,128)(2,1)S(1)} %shard_map.130.refs_0_.state_ref, ...), custom_call_target="tpu_custom_call" | custom-call | flops 2684354560 | bytes 7905280 | tf_op jit(solution)/shard_map/pallas_call | solution.py:26
  62.4 0.7 collective-permute-start.17
  63.0 0.5 shard_map.139
  63.5 1.7 %collective-permute-start.18 = (bf16[2,64,256]{2,1,0:T(8,128)(2,1)S(1)}, bf16[2,64,256]{2,1,0:T(8,128)(2,1)S(1)}, u32[]{:S(2)}, u32[]{:S(2)}) collective-permute-start(bf16[2,64,256]{2,1,0:T(8,128)(2,1)S(1)} %get-tuple-element.33), channel_id=1, source_target_pairs={{0,4},{1,5},{4,0},{5,1},{8,12},{9,13},{12,8},{13,9},{2,6},{3,7},{6... | collective-permute-start | bytes 196616 | tf_op jit(solution)/shard_map/ppermute | solution.py:75
  65.2 1.9 %collective-permute-start.19 = (bf16[2,64,256]{2,1,0:T(8,128)(2,1)S(1)}, bf16[2,64,256]{2,1,0:T(8,128)(2,1)S(1)}, u32[]{:S(2)}, u32[]{:S(2)}) collective-permute-start(bf16[2,64,256]{2,1,0:T(8,128)(2,1)S(1)} %get-tuple-element.34), channel_id=1, source_target_pairs={{4,8},{5,9},{8,4},{9,5},{6,10},{7,11},{10,6},{11,7},{20,24},{21,25... | collective-permute-start | bytes 196616 | tf_op jit(solution)/shard_map/ppermute | solution.py:75
  67.1 3.3 %collective-permute-done.19.two_ref = bf16[2,64,256]{2,1,0:T(8,128)(2,1)S(1)} collective-permute-done((bf16[2,64,256]{2,1,0:T(8,128)(2,1)S(1)}, bf16[2,64,256]{2,1,0:T(8,128)(2,1)S(1)}, u32[]{:S(2)}, u32[]{:S(2)}) %collective-permute-start.19) | collective-permute-done | bytes 65568 | tf_op jit(solution)/shard_map/ppermute | solution.py:75
  70.5 2.4 %collective-permute-start.21 = (bf16[3,64,256]{2,1,0:T(8,128)(2,1)S(1)}, bf16[3,64,256]{2,1,0:T(8,128)(2,1)S(1)}, u32[]{:S(2)}, u32[]{:S(2)}) collective-permute-start(bf16[3,64,256]{2,1,0:T(8,128)(2,1)S(1)} %shard_map.140), channel_id=1, source_target_pairs={{0,1},{1,0},{4,5},{5,4},{8,9},{9,8},{12,13},{13,12},{2,3},{3,2},{6... | collective-permute-start | bytes 294920 | tf_op jit(solution)/shard_map/ppermute | solution.py:75
  72.9 1.9 %collective-permute-start.20 = (bf16[64,256]{1,0:T(8,128)(2,1)S(1)}, bf16[64,256]{1,0:T(8,128)(2,1)S(1)}, u32[]{:S(2)}, u32[]{:S(2)}) collective-permute-start(bf16[64,256]{1,0:T(8,128)(2,1)S(1)} %get-tuple-element.35), channel_id=1, source_target_pairs={{1,8},{5,12},{8,1},{12,5},{3,10},{7,14},{10,3},{14,7},{17,24},{21,... | collective-permute-start | bytes 98312 | tf_op jit(solution)/shard_map/ppermute | solution.py:75
  74.8 4.2 %collective-permute-done.20.distant_ref = bf16[64,256]{1,0:T(8,128)(2,1)S(1)} collective-permute-done((bf16[64,256]{1,0:T(8,128)(2,1)S(1)}, bf16[64,256]{1,0:T(8,128)(2,1)S(1)}, u32[]{:S(2)}, u32[]{:S(2)}) %collective-permute-start.20) | collective-permute-done | bytes 32800 | tf_op jit(solution)/shard_map/ppermute | solution.py:75
  79.4 0.5 shard_map.137.table_ref
  79.9 3.5 %shard_map.138.first_ref = f32[5120,256]{1,0:T(8,128)S(1)} custom-call(s16[5120,128]{1,0:T(8,128)(2,1)S(1)} %get-tuple-element.21.refs_2_.source_ref, s16[5120,128]{1,0:T(8,128)(2,1)S(1)} %get-tuple-element.23.refs_3_.target_ref, bf16[1280,256]{1,0:T(8,128)(2,1)S(1)} %shard_map.137.table_ref), custom_call_target="tpu_custom_call" | custom-call | flops 3355443200 | bytes 8519680 | tf_op jit(solution)/shard_map/pallas_call | solution.py:26
  83.7 5.2 %shard_map.142 = bf16[640,256]{1,0:T(8,128)(2,1)} custom-call(s16[5120,128]{1,0:T(8,128)(2,1)S(1)} %get-tuple-element.21.refs_2_.source_ref, s32[1,5120]{1,0:T(1,128)S(1)} %copy-done.6, f32[1,5120]{1,0:T(1,128)S(1)} %copy-done.9, bf16[640,256]{1,0:T(8,128)(2,1)S(1)} %shard_map.136.refs_0_.state_ref, f32[5120,256]{1,0:T(8,128)S(1)} %shard_map.138.first_ref, ...), custom_call_target="tpu_custom_call" | custom-call | flops 2684354560 | bytes 7905280 | tf_op jit(solution)/shard_map/pallas_call | solution.py:26
  (48 shorter events, 2.2 us)
Async XLA Ops:
  0.0 18.1 %copy-start = (bf16[512,256]{1,0:T(8,128)(2,1)S(1)}, bf16[512,256]{1,0:T(8,128)(2,1)}, u32[]{:S(2)}) copy-start(bf16[512,256]{1,0:T(8,128)(2,1)} %weight_ref.9) | copy-start | bytes 786436
  0.0 1.3 %copy-start.1 = (bf16[2048,256]{1,0:T(8,128)(2,1)S(1)}, bf16[2048,256]{1,0:T(8,128)(2,1)}, u32[]{:S(2)}) copy-start(bf16[2048,256]{1,0:T(8,128)(2,1)} %table_ref.7) | copy-start | bytes 3145732
  1.3 0.7 copy-start.8
  2.0 14.7 %copy-start.5 = (s32[1,5120]{1,0:T(1,128)S(1)}, s32[1,5120]{1,0:T(1,128)}, u32[]{:S(2)}) copy-start(s32[1,5120]{1,0:T(1,128)} %refs_0_.1) | copy-start | bytes 61444
  2.0 14.7 %copy-start.6 = (s32[1,5120]{1,0:T(1,128)S(1)}, s32[1,5120]{1,0:T(1,128)}, u32[]{:S(2)}) copy-start(s32[1,5120]{1,0:T(1,128)} %target_ref.3) | copy-start | bytes 61444
  2.0 16.2 %copy-start.3 = (f32[1,7,256]{2,0,1:T(1,128)S(1)}, f32[1,7,256]{2,0,1:T(1,128)}, u32[]{:S(2)}) copy-start(f32[1,7,256]{2,0,1:T(1,128)} %param.17) | copy-start | bytes 21508
  2.0 16.2 %copy-start.4 = (s32[1,7,256]{2,0,1:T(1,128)S(1)}, s32[1,7,256]{2,0,1:T(1,128)}, u32[]{:S(2)}) copy-start(s32[1,7,256]{2,0,1:T(1,128)} %param.16) | copy-start | bytes 21508
  2.8 28.7 %copy-start.2 = (bf16[640,256]{1,0:T(8,128)(2,1)S(1)}, bf16[640,256]{1,0:T(8,128)(2,1)}, u32[]{:S(2)}) copy-start(bf16[640,256]{1,0:T(8,128)(2,1)} %before_ref.1) | copy-start | bytes 983044
  2.8 5.8 %collective-permute-start.2 = (bf16[1,256,256]{2,1,0:T(8,128)(2,1)S(1)}, bf16[1,256,256]{2,1,0:T(8,128)(2,1)S(1)}, u32[]{:S(2)}, u32[]{:S(2)}) collective-permute-start(bf16[1,256,256]{2,1,0:T(8,128)(2,1)S(1)} %get-tuple-element.24.refs_0_), channel_id=1, source_target_pairs={{1,3},{3,1},{5,7},{7,5},{8,10},{10,8},{12,14},{14,12},{17,19},{19,... | collective-permute-start | bytes 393224 | tf_op jit(solution)/shard_map/ppermute | solution.py:93
  6.0 6.8 %collective-permute-start = (bf16[1,256,256]{2,1,0:T(8,128)(2,1)S(1)}, bf16[1,256,256]{2,1,0:T(8,128)(2,1)S(1)}, u32[]{:S(2)}, u32[]{:S(2)}) collective-permute-start(bf16[1,256,256]{2,1,0:T(8,128)(2,1)S(1)} %get-tuple-element.22.refs_0_), channel_id=1, source_target_pairs={{0,2},{2,0},{4,6},{6,4},{5,7},{7,5},{8,10},{10,8},{9,11},{11,9},{1... | collective-permute-start | bytes 393224 | tf_op jit(solution)/shard_map/ppermute | solution.py:93
  9.1 5.5 %collective-permute-start.4 = (bf16[1,256,256]{2,1,0:T(8,128)(2,1)S(1)}, bf16[1,256,256]{2,1,0:T(8,128)(2,1)S(1)}, u32[]{:S(2)}, u32[]{:S(2)}) collective-permute-start(bf16[1,256,256]{2,1,0:T(8,128)(2,1)S(1)} %shard_map.123.refs_0_), channel_id=1, source_target_pairs={{0,2},{2,0},{1,3},{3,1},{4,6},{6,4},{5,7},{7,5},{8,10},{10,8},{9,1... | collective-permute-start | bytes 393224 | tf_op jit(solution)/shard_map/ppermute | solution.py:93
  13.6 18.1 %collective-permute-start.6 = (bf16[2,256,256]{2,1,0:T(8,128)(2,1)S(1)}, bf16[2,256,256]{2,1,0:T(8,128)(2,1)S(1)}, u32[]{:S(2)}, u32[]{:S(2)}) collective-permute-start(bf16[2,256,256]{2,1,0:T(8,128)(2,1)S(1)} %shard_map.125.refs_0_), channel_id=1, source_target_pairs={{0,2},{2,0},{1,3},{3,1},{4,6},{6,4},{5,7},{7,5},{8,10},{10,8},{9,1... | collective-permute-start | bytes 786440 | tf_op jit(solution)/shard_map/ppermute | solution.py:93
  15.4 20.8 %collective-permute-start.9 = (bf16[2,256,256]{2,1,0:T(8,128)(2,1)S(1)}, bf16[2,256,256]{2,1,0:T(8,128)(2,1)S(1)}, u32[]{:S(2)}, u32[]{:S(2)}) collective-permute-start(bf16[2,256,256]{2,1,0:T(8,128)(2,1)S(1)} %shard_map.128.refs_0_), channel_id=1, source_target_pairs={{0,2},{2,0},{1,3},{3,1},{4,6},{6,4},{5,7},{7,5},{8,10},{10,8},{9,1... | collective-permute-start | bytes 786440 | tf_op jit(solution)/shard_map/ppermute | solution.py:93
  18.2 23.7 %copy-start.7 = (s32[1,6,64]{2,0,1:T(1,128)S(1)}, s32[1,6,64]{2,0,1:T(1,128)}, u32[]{:S(2)}) copy-start(s32[1,6,64]{2,0,1:T(1,128)} %param.20) | copy-start | bytes 4612
  18.2 31.7 %copy-start.10 = (bf16[2,512,256]{2,1,0:T(8,128)(2,1)S(1)}, bf16[2,512,256]{2,1,0:T(8,128)(2,1)}, u32[]{:S(2)}) copy-start(bf16[2,512,256]{2,1,0:T(8,128)(2,1)} %param.19) | copy-start | bytes 1572868
  18.2 31.7 %copy-start.11 = (bf16[2,512,256]{2,1,0:T(8,128)(2,1)S(1)}, bf16[2,512,256]{2,1,0:T(8,128)(2,1)}, u32[]{:S(2)}) copy-start(bf16[2,512,256]{2,1,0:T(8,128)(2,1)} %param.18) | copy-start | bytes 1572868
  18.4 12.0 %collective-permute-start.1 = (bf16[272,256]{1,0:T(8,128)(2,1)S(1)}, bf16[272,256]{1,0:T(8,128)(2,1)S(1)}, u32[]{:S(2)}, u32[]{:S(2)}) collective-permute-start(bf16[272,256]{1,0:T(8,128)(2,1)S(1)} %shard_map.120), channel_id=1, source_target_pairs={{0,5},{4,9},{5,0},{8,13},{9,4},{13,8},{2,7},{6,11},{7,2},{10,15},{... | collective-permute-start | bytes 417800 | tf_op jit(solution)/shard_map/ppermute | solution.py:75
  20.8 10.7 %collective-permute-start.3 = (bf16[272,256]{1,0:T(8,128)(2,1)S(1)}, bf16[272,256]{1,0:T(8,128)(2,1)S(1)}, u32[]{:S(2)}, u32[]{:S(2)}) collective-permute-start(bf16[272,256]{1,0:T(8,128)(2,1)S(1)} %shard_map.121), channel_id=1, source_target_pairs={{1,8},{5,12},{8,1},{12,5},{3,10},{7,14},{10,3},{14,7},{17,24},{21,... | collective-permute-start | bytes 417800 | tf_op jit(solution)/shard_map/ppermute | solution.py:75
  28.2 10.8 %collective-permute-start.5 = (bf16[272,256]{1,0:T(8,128)(2,1)S(1)}, bf16[272,256]{1,0:T(8,128)(2,1)S(1)}, u32[]{:S(2)}, u32[]{:S(2)}) collective-permute-start(bf16[272,256]{1,0:T(8,128)(2,1)S(1)} %shard_map.124), channel_id=1, source_target_pairs={{1,4},{4,1},{5,8},{8,5},{9,12},{12,9},{3,6},{6,3},{7,10},{10,7},{1... | collective-permute-start | bytes 417800 | tf_op jit(solution)/shard_map/ppermute | solution.py:75
  32.2 6.9 %collective-permute-start.7 = (bf16[272,256]{1,0:T(8,128)(2,1)S(1)}, bf16[272,256]{1,0:T(8,128)(2,1)S(1)}, u32[]{:S(2)}, u32[]{:S(2)}) collective-permute-start(bf16[272,256]{1,0:T(8,128)(2,1)S(1)} %get-tuple-element.25), channel_id=1, source_target_pairs={{0,4},{1,5},{4,0},{5,1},{8,12},{9,13},{12,8},{13,9},{2,6},{3,7},{6... | collective-permute-start | bytes 417800 | tf_op jit(solution)/shard_map/ppermute | solution.py:75
  34.3 6.8 %collective-permute-start.8 = (bf16[272,256]{1,0:T(8,128)(2,1)S(1)}, bf16[272,256]{1,0:T(8,128)(2,1)S(1)}, u32[]{:S(2)}, u32[]{:S(2)}) collective-permute-start(bf16[272,256]{1,0:T(8,128)(2,1)S(1)} %get-tuple-element.26), channel_id=1, source_target_pairs={{4,8},{5,9},{8,4},{9,5},{6,10},{7,11},{10,6},{11,7},{20,24},{21,25... | collective-permute-start | bytes 417800 | tf_op jit(solution)/shard_map/ppermute | solution.py:75
  36.6 4.9 %collective-permute-start.10 = (bf16[272,256]{1,0:T(8,128)(2,1)S(1)}, bf16[272,256]{1,0:T(8,128)(2,1)S(1)}, u32[]{:S(2)}, u32[]{:S(2)}) collective-permute-start(bf16[272,256]{1,0:T(8,128)(2,1)S(1)} %get-tuple-element.27), channel_id=1, source_target_pairs={{0,1},{1,0},{4,5},{5,4},{8,9},{9,8},{12,13},{13,12},{2,3},{3,2},{6... | collective-permute-start | bytes 417800 | tf_op jit(solution)/shard_map/ppermute | solution.py:75
  42.3 7.0 %collective-permute-start.12 = (bf16[2,64,256]{2,1,0:T(8,128)(2,1)S(1)}, bf16[2,64,256]{2,1,0:T(8,128)(2,1)S(1)}, u32[]{:S(2)}, u32[]{:S(2)}) collective-permute-start(bf16[2,64,256]{2,1,0:T(8,128)(2,1)S(1)} %get-tuple-element.29), channel_id=1, source_target_pairs={{0,4},{1,5},{4,0},{5,1},{8,12},{9,13},{12,8},{13,9},{2,6},{3,7},{6... | collective-permute-start | bytes 196616 | tf_op jit(solution)/shard_map/ppermute | solution.py:75
  42.4 7.0 %collective-permute-start.13 = (bf16[2,64,256]{2,1,0:T(8,128)(2,1)S(1)}, bf16[2,64,256]{2,1,0:T(8,128)(2,1)S(1)}, u32[]{:S(2)}, u32[]{:S(2)}) collective-permute-start(bf16[2,64,256]{2,1,0:T(8,128)(2,1)S(1)} %get-tuple-element.30), channel_id=1, source_target_pairs={{4,8},{5,9},{8,4},{9,5},{6,10},{7,11},{10,6},{11,7},{20,24},{21,25... | collective-permute-start | bytes 196616 | tf_op jit(solution)/shard_map/ppermute | solution.py:75
  44.3 7.8 %collective-permute-start.11 = (bf16[640,256]{1,0:T(8,128)(2,1)S(1)}, bf16[640,256]{1,0:T(8,128)(2,1)S(1)}, u32[]{:S(2)}, u32[]{:S(2)}) collective-permute-start(bf16[640,256]{1,0:T(8,128)(2,1)S(1)} %shard_map.130.refs_0_.state_ref), channel_id=1, source_target_pairs={{0,2},{2,0},{1,3},{3,1},{4,6},{6,4},{5,7},{7,5},{8,10},{10,8},{9,1... | collective-permute-start | bytes 983048 | tf_op jit(solution)/shard_map/ppermute | solution.py:93
  44.7 6.1 %collective-permute-start.14 = (bf16[64,256]{1,0:T(8,128)(2,1)S(1)}, bf16[64,256]{1,0:T(8,128)(2,1)S(1)}, u32[]{:S(2)}, u32[]{:S(2)}) collective-permute-start(bf16[64,256]{1,0:T(8,128)(2,1)S(1)} %get-tuple-element.31), channel_id=1, source_target_pairs={{1,8},{5,12},{8,1},{12,5},{3,10},{7,14},{10,3},{14,7},{17,24},{21,... | collective-permute-start | bytes 98312 | tf_op jit(solution)/shard_map/ppermute | solution.py:75
  49.4 1.4 %collective-permute-start.15 = (bf16[3,64,256]{2,1,0:T(8,128)(2,1)S(1)}, bf16[3,64,256]{2,1,0:T(8,128)(2,1)S(1)}, u32[]{:S(2)}, u32[]{:S(2)}) collective-permute-start(bf16[3,64,256]{2,1,0:T(8,128)(2,1)S(1)} %shard_map.134), channel_id=1, source_target_pairs={{0,1},{1,0},{4,5},{5,4},{8,9},{9,8},{12,13},{13,12},{2,3},{3,2},{6... | collective-permute-start | bytes 294920 | tf_op jit(solution)/shard_map/ppermute | solution.py:75
  50.8 7.0 %collective-permute-start.16 = (bf16[384,256]{1,0:T(8,128)(2,1)S(1)}, bf16[384,256]{1,0:T(8,128)(2,1)S(1)}, u32[]{:S(2)}, u32[]{:S(2)}) collective-permute-start(bf16[384,256]{1,0:T(8,128)(2,1)S(1)} %shard_map.135.refs_0_), channel_id=1, source_target_pairs={{0,2},{2,0},{1,3},{3,1},{4,6},{6,4},{5,7},{7,5},{8,10},{10,8},{9,1... | collective-permute-start | bytes 589832 | tf_op jit(solution)/shard_map/ppermute | solution.py:93
  52.6 5.3 %copy-start.9 = (f32[1,5120]{1,0:T(1,128)S(1)}, f32[1,5120]{1,0:T(1,128)}, u32[]{:S(2)}) copy-start(f32[1,5120]{1,0:T(1,128)} %coef_ref.3) | copy-start | bytes 61444
  62.4 17.1 %collective-permute-start.17 = (bf16[640,256]{1,0:T(8,128)(2,1)S(1)}, bf16[640,256]{1,0:T(8,128)(2,1)S(1)}, u32[]{:S(2)}, u32[]{:S(2)}) collective-permute-start(bf16[640,256]{1,0:T(8,128)(2,1)S(1)} %shard_map.136.refs_0_.state_ref), channel_id=1, source_target_pairs={{0,2},{2,0},{1,3},{3,1},{4,6},{6,4},{5,7},{7,5},{8,10},{10,8},{9,1... | collective-permute-start | bytes 983048 | tf_op jit(solution)/shard_map/ppermute | solution.py:93
  63.5 3.7 %collective-permute-start.18 = (bf16[2,64,256]{2,1,0:T(8,128)(2,1)S(1)}, bf16[2,64,256]{2,1,0:T(8,128)(2,1)S(1)}, u32[]{:S(2)}, u32[]{:S(2)}) collective-permute-start(bf16[2,64,256]{2,1,0:T(8,128)(2,1)S(1)} %get-tuple-element.33), channel_id=1, source_target_pairs={{0,4},{1,5},{4,0},{5,1},{8,12},{9,13},{12,8},{13,9},{2,6},{3,7},{6... | collective-permute-start | bytes 196616 | tf_op jit(solution)/shard_map/ppermute | solution.py:75
  65.2 5.3 %collective-permute-start.19 = (bf16[2,64,256]{2,1,0:T(8,128)(2,1)S(1)}, bf16[2,64,256]{2,1,0:T(8,128)(2,1)S(1)}, u32[]{:S(2)}, u32[]{:S(2)}) collective-permute-start(bf16[2,64,256]{2,1,0:T(8,128)(2,1)S(1)} %get-tuple-element.34), channel_id=1, source_target_pairs={{4,8},{5,9},{8,4},{9,5},{6,10},{7,11},{10,6},{11,7},{20,24},{21,25... | collective-permute-start | bytes 196616 | tf_op jit(solution)/shard_map/ppermute | solution.py:75
  70.5 8.6 %collective-permute-start.21 = (bf16[3,64,256]{2,1,0:T(8,128)(2,1)S(1)}, bf16[3,64,256]{2,1,0:T(8,128)(2,1)S(1)}, u32[]{:S(2)}, u32[]{:S(2)}) collective-permute-start(bf16[3,64,256]{2,1,0:T(8,128)(2,1)S(1)} %shard_map.140), channel_id=1, source_target_pairs={{0,1},{1,0},{4,5},{5,4},{8,9},{9,8},{12,13},{13,12},{2,3},{3,2},{6... | collective-permute-start | bytes 294920 | tf_op jit(solution)/shard_map/ppermute | solution.py:75
  72.9 6.1 %collective-permute-start.20 = (bf16[64,256]{1,0:T(8,128)(2,1)S(1)}, bf16[64,256]{1,0:T(8,128)(2,1)S(1)}, u32[]{:S(2)}, u32[]{:S(2)}) collective-permute-start(bf16[64,256]{1,0:T(8,128)(2,1)S(1)} %get-tuple-element.35), channel_id=1, source_target_pairs={{1,8},{5,12},{8,1},{12,5},{3,10},{7,14},{10,3},{14,7},{17,24},{21,... | collective-permute-start | bytes 98312 | tf_op jit(solution)/shard_map/ppermute | solution.py:75
  79.1 4.6 %collective-permute-start.22 = (bf16[384,256]{1,0:T(8,128)(2,1)S(1)}, bf16[384,256]{1,0:T(8,128)(2,1)S(1)}, u32[]{:S(2)}, u32[]{:S(2)}) collective-permute-start(bf16[384,256]{1,0:T(8,128)(2,1)S(1)} %shard_map.141.refs_0_), channel_id=1, source_target_pairs={{0,2},{2,0},{1,3},{3,1},{4,6},{6,4},{5,7},{7,5},{8,10},{10,8},{9,1... | collective-permute-start | bytes 589832 | tf_op jit(solution)/shard_map/ppermute | solution.py:93

commit v5 on v4

--- a/solution.py
+++ b/solution.py
@@ -18,6 +18,10 @@
 
 def taken_from_vmem(array):
     return pltpu.with_memory_space_constraint(array, pltpu.VMEM)
+
+
+def taken_from_hbm(array):
+    return pltpu.with_memory_space_constraint(array, pltpu.HBM)
 
 
 def call(kernel, outputs, inputs, flops, transcendentals=0, scratch=(), final=False, fetched=0):
@@ -179,6 +183,80 @@
         [g2m_src, grid_latent, *after],
         2 * sum(map(len, groups)) * capacity * rows * channels,
     )
+
+
+def first_pick_kernel(groups, parts, index_hbm, table_hbm, *refs):
+    out_refs, (index_ref, table_ref, index_sem, table_sems) = (refs[: len(groups)], refs[len(groups) :])
+    rows = table_ref.shape[0] // parts
+    index_copy = pltpu.make_async_copy(index_hbm, index_ref, index_sem)
+    index_copy.start()
+    copies = []
+    for part in range(parts):
+        here = pl.ds(part * rows, rows)
+        copies.append(pltpu.make_async_copy(table_hbm.at[here, :], table_ref.at[here, :], table_sems.at[part]))
+        copies[-1].start()
+    index_copy.wait()
+    reach = index_ref.shape[0] // 2
+    cols = [
+        column(index_ref[block_index(meets, reach)]).astype(jnp.int16) for group in groups for meets in group
+    ]
+    totals = [None] * len(cols)
+    for part, copy in enumerate(copies):
+        copy.wait()
+        lanes = (lane_iota(rows).astype(jnp.int32) + part * rows).astype(jnp.int16)
+        for k, col in enumerate(cols):
+            found = dot(pick_mask(col, lanes), table_ref[pl.ds(part * rows, rows), :])
+            totals[k] = found if part == 0 else totals[k] + found
+    for group, out_ref in zip(groups, out_refs):
+        for place in range(len(group)):
+            out_ref[place] = totals.pop(0).astype(jnp.bfloat16)
+
+
+def first_pick(groups, g2m_src, grid_latent):
+    capacity = g2m_src.shape[2]
+    rows, channels = grid_latent.shape
+    parts = 4
+    outputs = [shape((len(group), capacity, channels)) for group in groups]
+    outputs += [shape(g2m_src.shape, g2m_src.dtype), shape(grid_latent.shape, grid_latent.dtype)]
+    *picked, index, table = pl.pallas_call(
+        functools.partial(first_pick_kernel, groups, parts),
+        out_shape=[made_in_vmem(o) for o in outputs],
+        in_specs=[pl.BlockSpec(memory_space=pl.ANY)] * 2,
+        out_specs=[pl.BlockSpec(memory_space=pltpu.VMEM)] * len(outputs),
+        scratch_shapes=[pltpu.SemaphoreType.DMA, pltpu.SemaphoreType.DMA((parts,))],
+        compiler_params=pltpu.CompilerParams(vmem_limit_bytes=VMEM_BYTES),
+    )(taken_from_hbm(g2m_src), taken_from_hbm(grid_latent))
+    return picked, index, table
+
+
+def fetch_kernel(after_ref, *refs):
+    count = (len(refs) - 3) // 2
+    sources, copied, (source_col_ref, target_col_ref, sems) = (
+        refs[:count],
+        refs[count : 2 * count],
+        refs[2 * count :],
+    )
+    copies = [pltpu.make_async_copy(sources[k], copied[k], sems.at[k]) for k in range(count)]
+    for copy in copies:
+        copy.start()
+    for copy, row_ref, out_ref in zip(copies, copied, (source_col_ref, target_col_ref)):
+        copy.wait()
+        out_ref[...] = column(row_ref[...]).astype(jnp.int16)
+    for copy in copies[2:]:
+        copy.wait()
+
+
+def fetch(after, *arrays):
+    outputs = [shape(a.shape, a.dtype) for a in arrays]
+    outputs += [shape((a.shape[1], 128), jnp.int16) for a in arrays[:2]]
+    return pl.pallas_call(
+        fetch_kernel,
+        out_shape=[made_in_vmem(o) for o in outputs],
+        in_specs=[pl.BlockSpec(memory_space=pltpu.VMEM)] + [pl.BlockSpec(memory_space=pl.ANY)] * len(arrays),
+        out_specs=[pl.BlockSpec(memory_space=pltpu.VMEM)] * len(outputs),
+        scratch_shapes=[pltpu.SemaphoreType.DMA((len(arrays),))],
+        compiler_params=pltpu.CompilerParams(vmem_limit_bytes=VMEM_BYTES),
+    )(taken_from_vmem(after), *[taken_from_hbm(a) for a in arrays])
 
 
 def encode_kernel(group, others, weight_ref, coef_ref, target_ref, *refs):
@@ -244,24 +322,6 @@
     )[0]
 
 
-def columns_kernel(pieces, *refs):
-    rows = len(refs) // (pieces + 1)
-    for k in range(rows):
-        for piece, out_ref in enumerate(refs[rows + k * pieces : rows + (k + 1) * pieces]):
-            count = out_ref.shape[0]
-            out_ref[...] = column(refs[k][:, pl.ds(piece * count, count)]).astype(jnp.int16)
-
-
-def columns(pieces, *rows):
-    count = rows[0].shape[1] // pieces
-    return call(
-        functools.partial(columns_kernel, pieces),
-        [shape((count, 128), jnp.int16)] * (pieces * len(rows)),
-        rows,
-        pieces * len(rows) * count * 128 * 8,
-    )
-
-
 def list_kernel(reach, listed_ref, state_ref, one_ref, two_ref, far_ref, near_ref):
     nodes = state_ref.shape[0]
     width = listed_ref.shape[2]
@@ -350,20 +410,20 @@
     return total.astype(jnp.bfloat16)
 
 
-def project_kernel(src_ref, dst_ref, *refs):
+def project_kernel(layer, src_ref, dst_ref, *refs):
     states, table_ref = (refs[:-1], refs[-1])
     nodes = states[0].shape[0]
-    table_ref[pl.ds(0, nodes), :] = projected_rows(src_ref, states)
-    table_ref[pl.ds(nodes, nodes), :] = projected_rows(dst_ref, states)
-
-
-def project(states, src_weight, dst_weight):
+    table_ref[pl.ds(0, nodes), :] = projected_rows(src_ref.at[layer], states)
+    table_ref[pl.ds(nodes, nodes), :] = projected_rows(dst_ref.at[layer], states)
+
+
+def project(layer, states, src_weights, dst_weights):
     nodes, channels = states[0].shape
-    depth = src_weight.shape[0]
-    return call(
-        project_kernel,
+    depth = src_weights.shape[1]
+    return call(
+        functools.partial(project_kernel, layer),
         [shape((2 * nodes, channels))],
-        [src_weight, dst_weight, *states],
+        [src_weights, dst_weights, *states],
         4 * nodes * depth * channels,
     )[0]
 
@@ -389,30 +449,39 @@
     )[0]
 
 
-def message_kernel(turn, source_ref, target_ref, coef_ref, state_ref, first_ref, weight_ref, *refs):
+def message_kernel(turn, layer, source_ref, target_ref, coef_ref, state_ref, first_ref, weight_ref, *refs):
     listed, (out_ref, message_ref) = (refs[:-2], refs[-2:])
     nodes, channels = state_ref.shape
-    table = projected_rows(weight_ref, listed)
+    table = projected_rows(weight_ref.at[layer], listed)
     lanes = (lane_iota(table.shape[0]).astype(jnp.int32) + nodes).astype(jnp.int16)
     rows16 = row_iota(nodes)
     total = state_ref[...].astype(jnp.float32)
-    for start in range(0, source_ref.shape[0], turn):
+    edges = source_ref.shape[0]
+
+    def gathered(start):
         here = pl.ds(start, turn)
-        summed = first_ref[here, :] + dot(pick_mask(source_ref[here, :], lanes), table)
+        return first_ref[here, :] + dot(pick_mask(source_ref[here, :], lanes), table)
+
+    ahead = gathered(0)
+    for start in range(0, edges, turn):
+        here = pl.ds(start, turn)
+        summed = ahead
+        if start + turn < edges:
+            ahead = gathered(start + turn)
         message_ref[here, :] = silu(summed).astype(jnp.bfloat16)
         mask = sum_mask(target_ref[:, here], rows16, coef_ref[:, here])
         total += dot(mask, message_ref[here, :])
     out_ref[...] = total.astype(jnp.bfloat16)
 
 
-def messages(source_col, m2m_dst, m2m_coef, state, first, src_weight, listed, final):
+def messages(layer, source_col, m2m_dst, m2m_coef, state, first, src_weights, listed, final):
     nodes, channels = state.shape
     edges = m2m_dst.shape[1]
     named = listed[0].shape[0]
     return call(
-        functools.partial(message_kernel, 1024),
+        functools.partial(message_kernel, 512, layer),
         [shape((nodes, channels))],
-        [source_col, m2m_dst, m2m_coef, state, first, src_weight, *listed],
+        [source_col, m2m_dst, m2m_coef, state, first, src_weights, *listed],
         2 * edges * (named + nodes) * channels,
         edges * channels,
         [pltpu.VMEM((edges, channels), jnp.bfloat16)],
@@ -439,37 +508,48 @@
     g2m_src, g2m_dst, g2m_coef, halo_send = [
         jnp.swapaxes(a, 0, 1) for a in (g2m_src, g2m_dst, g2m_coef, halo_send)
     ]
-    source_col, target_col = cols = columns(1, m2m_src, m2m_dst)
     groups = [
-        (meets_three,), (meets_other_three,), (meets_two, meets_other_two), (meets_next,), (meets_core, None)
-    ]
-    picked = pick(groups[:2], g2m_src, grid_latent)
+        (meets_three,), (meets_other_three,), (meets_two, meets_other_two), (meets_next, None), (meets_core,)
+    ]
+    picked, g2m_src, grid_latent = first_pick(groups[:2], g2m_src, grid_latent)
     arrived = [from_others(rows, group[0]) for group, rows in zip(groups, picked)]
-    for place, before in ((2, 0), (3, 1), (4, 3)):
-        picked += pick(groups[place : place + 1], g2m_src, grid_latent, arrived[before])
+    m2m_src, m2m_dst, m2m_coef, enc_weight, g2m_coef, g2m_dst, mesh_latent, halo_send, src_weights, dst_weights, *cols = (
+        fetch(
+            g2m_src, m2m_src, m2m_dst, m2m_coef, enc_weight, g2m_coef, g2m_dst, mesh_latent, halo_send,
+            src_weights, dst_weights,
+        )
+    )
+    source_col, target_col = cols
+
+    def pick_next(place, after):
+        picked.extend(pick(groups[place : place + 1], g2m_src, grid_latent, after))
         arrived.append(from_others(picked[place]))
-    sent = []
-    state = mesh_latent
-    for place in (0, 1, 3, 2, 4):
-        after = {0: cols, 2: [state]}.get(place, ())
-        encoded = encode(groups[place], picked[place], arrived[place], enc_weight, g2m_coef, g2m_dst, after)
-        sent += [
-            block if meets is None else swapped(block, meets) for meets, block in zip(groups[place], encoded)
-        ]
-        if place == 3:
-            state = gather_in(state, sent[:2], jnp.float32)
-    state = gather_in(state, sent[2:5], jnp.float32)
-    state = gather_in(state, sent[5:], jnp.bfloat16)
+
+    def encode_group(place, after=()):
+        return encode(groups[place], picked[place], arrived[place], enc_weight, g2m_coef, g2m_dst, after)
+
+    pick_next(2, arrived[0])
+    encoded = encode_group(0) + encode_group(1)
+    pick_next(3, encoded)
+    encoded += encode_group(2)
+    blocks = [swapped(block, meets) for block, meets in zip(encoded, groups[0] + groups[1] + groups[2])]
+    state = gather_in(mesh_latent, blocks[:2], jnp.float32)
+    pick_next(4, [state, *encoded[2:]])
+    following, own = encode_group(3)
+    (near,) = encode_group(4)
+    blocks.append(swapped(following, meets_next))
+    near = swapped(near, meets_core)
+    state = gather_in(state, blocks[2:4] + [own], jnp.float32)
+    state = gather_in(state, [blocks[4], near], jnp.bfloat16)
     layers = src_weights.shape[0]
     for layer in range(layers):
-        src_weight, dst_weight = src_weights[layer], dst_weights[layer]
         others = from_others(state)
         listed = exchange_listed(*list_rows(state, halo_send, reach))
-        table = project([state, *others], src_weight, dst_weight)
+        table = project(layer, [state, *others], src_weights, dst_weights)
         listed = [listed, *from_others(listed)]
         first = first_part(source_col, target_col, table)
         state = messages(
-            source_col, m2m_dst, m2m_coef, state, first, src_weight, listed, layer == layers - 1
+            layer, source_col, m2m_dst, m2m_coef, state, first, src_weights, listed, layer == layers - 1
         )
     return state
 

time: 89.3 us -> 89.8 us (level)
  the two profiles are of different devices: /device:TPU:9 before, /device:TPU:1 now
where the time goes in v5:
time: 89.8 us; the launch traced here: 89.4 us
  starting transfers between devices  49.6 us (55%)
  Pallas kernels  28.3 us (32%)
  waiting for transfers between devices  11.2 us (12%)
    ppermute x14, starting transfers between devices, swapped(): return lax.ppermute(value, REGION, pairs(meets))  39.1 us
    pallas_call x23, Pallas kernels, call(): pl.pallas_call(kernel, out_shape=shapes, in_specs=[pl.BlockSpec(memory_sp...  23.4 us
    ppermute x9, starting transfers between devices, from_others(): lax.ppermute(value, axes, [(ring[i], ring[(i + k) % n]) for ring in rings...  10.5 us
    ppermute x14, waiting for transfers between devices, swapped(): return lax.ppermute(value, REGION, pairs(meets))  10.3 us
    pallas_call x1, Pallas kernels, fetch(): pl.pallas_call(fetch_kernel, out_shape=[made_in_vmem(o) for o in outputs]...  2.94 us
    pallas_call x1, Pallas kernels, first_pick(): pl.pallas_call(functools.partial(first_pick_kernel, groups, parts), out_s...  2.01 us
  transfers between devices with their start and end apart: 23, of which 7 were waited for; matrix products, arithmetic and copies ran while one was open for 0% of the time, Pallas kernels for 18%

profile of v5, /device:TPU:1, one launch (start us, length us, event | category | flops | bytes accessed | tf_op | source)
XLA Modules:
  0.0 89.4 jit_solution(18427572144616102769)
XLA Ops:
  0.0 2.0 %shard_map.118 = (bf16[1,256,256]{2,1,0:T(8,128)(2,1)S(1)}, bf16[1,256,256]{2,1,0:T(8,128)(2,1)S(1)}, s32[7,1,256]{2,1,0:T(1,128)S(1)}, bf16[2048,256]{1,0:T(8,128)(2,1)S(1)}) custom-call(s32[7,1,256]{2,1,0:T(1,128)} %bitcast.4, bf16[2048,256]{1,0:T(8,128)(2,1)} %table_hbm.1), custom_call_target="tpu_custom_call" | custom-call | tf_op jit(solution)/shard_map/pallas_call | solution.py:221
  2.0 0.7 collective-permute-start
  2.7 3.9 %collective-permute-start.2 = (bf16[1,256,256]{2,1,0:T(8,128)(2,1)S(1)}, bf16[1,256,256]{2,1,0:T(8,128)(2,1)S(1)}, u32[]{:S(2)}, u32[]{:S(2)}) collective-permute-start(bf16[1,256,256]{2,1,0:T(8,128)(2,1)S(1)} %get-tuple-element.41.refs_0_), channel_id=1, source_target_pairs={{1,3},{3,1},{5,7},{7,5},{8,10},{10,8},{12,14},{14,12},{17,19},{19,... | collective-permute-start | bytes 393224 | tf_op jit(solution)/shard_map/ppermute | solution.py:97
  6.7 0.8 shard_map.123.refs_0_
  7.5 2.9 %shard_map.119 = (s32[1,5120]{1,0:T(1,128)}, s32[1,5120]{1,0:T(1,128)S(1)}, f32[1,5120]{1,0:T(1,128)S(1)}, bf16[512,256]{1,0:T(8,128)(2,1)S(1)}, f32[7,1,256]{2,...) custom-call(s32[7,1,256]{2,1,0:T(1,128)S(1)} %get-tuple-element.32.a, ...), custom_call_target="tpu_custom_call" | custom-call | tf_op jit(solution)/shard_map/pallas_call | solution.py:252
  10.5 0.3 shard_map.120.refs_0_
  10.7 0.7 collective-permute-start.1
  11.4 0.3 shard_map.121.refs_1_
  11.7 10.8 %collective-permute-start.3 = (bf16[272,256]{1,0:T(8,128)(2,1)S(1)}, bf16[272,256]{1,0:T(8,128)(2,1)S(1)}, u32[]{:S(2)}, u32[]{:S(2)}) collective-permute-start(bf16[272,256]{1,0:T(8,128)(2,1)S(1)} %shard_map.121.refs_1_), channel_id=1, source_target_pairs={{1,8},{5,12},{8,1},{12,5},{3,10},{7,14},{10,3},{14,7},{17,24},{21,... | collective-permute-start | bytes 417800 | tf_op jit(solution)/shard_map/ppermute | solution.py:79
  22.5 0.8 shard_map.125.refs_0_
  23.2 0.3 collective-permute-start.7
  23.6 1.6 %collective-permute-done.3.refs_1_ = bf16[272,256]{1,0:T(8,128)(2,1)S(1)} collective-permute-done((bf16[272,256]{1,0:T(8,128)(2,1)S(1)}, bf16[272,256]{1,0:T(8,128)(2,1)S(1)}, u32[]{:S(2)}, u32[]{:S(2)}) %collective-permute-start.3) | collective-permute-done | bytes 139296 | tf_op jit(solution)/shard_map/ppermute | solution.py:79
  25.2 0.3 shard_map.122.before_ref.refs_0_
  25.5 0.4 shard_map.124
  25.9 0.5 shard_map.128.refs_0_
  26.4 0.3 collective-permute-start.9
  26.7 2.7 %collective-permute-start.5 = (bf16[272,256]{1,0:T(8,128)(2,1)S(1)}, bf16[272,256]{1,0:T(8,128)(2,1)S(1)}, u32[]{:S(2)}, u32[]{:S(2)}) collective-permute-start(bf16[272,256]{1,0:T(8,128)(2,1)S(1)} %get-tuple-element.43.refs_1_), channel_id=1, source_target_pairs={{0,4},{1,5},{4,0},{5,1},{8,12},{9,13},{12,8},{13,9},{2,6},{3,7},{6... | collective-permute-start | bytes 417800 | tf_op jit(solution)/shard_map/ppermute | solution.py:79
  29.4 0.7 collective-permute-start.6
  30.1 0.9 collective-permute-done.7.refs_1_
  30.9 0.4 shard_map.126
  31.3 4.7 %collective-permute-start.8 = (bf16[272,256]{1,0:T(8,128)(2,1)S(1)}, bf16[272,256]{1,0:T(8,128)(2,1)S(1)}, u32[]{:S(2)}, u32[]{:S(2)}) collective-permute-start(bf16[272,256]{1,0:T(8,128)(2,1)S(1)} %get-tuple-element.46), channel_id=1, source_target_pairs={{1,4},{4,1},{5,8},{8,5},{9,12},{12,9},{3,6},{6,3},{7,10},{10,7},{1... | collective-permute-start | bytes 417800 | tf_op jit(solution)/shard_map/ppermute | solution.py:79
  36.0 0.3 shard_map.129
  36.4 0.4 shard_map.127.before_ref
  36.8 1.9 %collective-permute-done.8.refs_0_ = bf16[272,256]{1,0:T(8,128)(2,1)S(1)} collective-permute-done((bf16[272,256]{1,0:T(8,128)(2,1)S(1)}, bf16[272,256]{1,0:T(8,128)(2,1)S(1)}, u32[]{:S(2)}, u32[]{:S(2)}) %collective-permute-start.8) | collective-permute-done | bytes 139296 | tf_op jit(solution)/shard_map/ppermute | solution.py:79
  38.7 0.3 shard_map.130.refs_0_.state_ref
  39.1 1.7 %collective-permute-start.11 = (bf16[640,256]{1,0:T(8,128)(2,1)S(1)}, bf16[640,256]{1,0:T(8,128)(2,1)S(1)}, u32[]{:S(2)}, u32[]{:S(2)}) collective-permute-start(bf16[640,256]{1,0:T(8,128)(2,1)S(1)} %shard_map.130.refs_0_.state_ref), channel_id=1, source_target_pairs={{0,2},{2,0},{1,3},{3,1},{4,6},{6,4},{5,7},{7,5},{8,10},{10,8},{9,1... | collective-permute-start | bytes 983048 | tf_op jit(solution)/shard_map/ppermute | solution.py:97
  40.8 0.5 shard_map.133
  41.3 0.1 collective-permute-start.12
  41.4 0.7 collective-permute-start.13
  42.0 2.7 %collective-permute-done.12.one_ref = bf16[2,64,256]{2,1,0:T(8,128)(2,1)S(1)} collective-permute-done((bf16[2,64,256]{2,1,0:T(8,128)(2,1)S(1)}, bf16[2,64,256]{2,1,0:T(8,128)(2,1)S(1)}, u32[]{:S(2)}, u32[]{:S(2)}) %collective-permute-start.12) | collective-permute-done | bytes 65568 | tf_op jit(solution)/shard_map/ppermute | solution.py:79
  44.8 1.3 %collective-permute-start.15 = (bf16[3,64,256]{2,1,0:T(8,128)(2,1)S(1)}, bf16[3,64,256]{2,1,0:T(8,128)(2,1)S(1)}, u32[]{:S(2)}, u32[]{:S(2)}) collective-permute-start(bf16[3,64,256]{2,1,0:T(8,128)(2,1)S(1)} %shard_map.134), channel_id=1, source_target_pairs={{0,1},{1,0},{4,5},{5,4},{8,9},{9,8},{12,13},{13,12},{2,3},{3,2},{6... | collective-permute-start | bytes 294920 | tf_op jit(solution)/shard_map/ppermute | solution.py:79
  46.1 5.1 %collective-permute-start.14 = (bf16[64,256]{1,0:T(8,128)(2,1)S(1)}, bf16[64,256]{1,0:T(8,128)(2,1)S(1)}, u32[]{:S(2)}, u32[]{:S(2)}) collective-permute-start(bf16[64,256]{1,0:T(8,128)(2,1)S(1)} %get-tuple-element.53), channel_id=1, source_target_pairs={{1,8},{5,12},{8,1},{12,5},{3,10},{7,14},{10,3},{14,7},{17,24},{21,... | collective-permute-start | bytes 98312 | tf_op jit(solution)/shard_map/ppermute | solution.py:79
  51.1 1.4 %collective-permute-done.14.distant_ref = bf16[64,256]{1,0:T(8,128)(2,1)S(1)} collective-permute-done((bf16[64,256]{1,0:T(8,128)(2,1)S(1)}, bf16[64,256]{1,0:T(8,128)(2,1)S(1)}, u32[]{:S(2)}, u32[]{:S(2)}) %collective-permute-start.14) | collective-permute-done | bytes 32800 | tf_op jit(solution)/shard_map/ppermute | solution.py:79
  52.6 0.5 collective-permute-start.16
  53.1 0.5 shard_map.131.table_ref
  53.6 3.6 %shard_map.132.first_ref = f32[5120,256]{1,0:T(8,128)S(1)} custom-call(s16[5120,128]{1,0:T(8,128)(2,1)S(1)} %get-tuple-element.33.source_ref, s16[5120,128]{1,0:T(8,128)(2,1)S(1)} %get-tuple-element.47.target_ref, bf16[1280,256]{1,0:T(8,128)(2,1)S(1)} %shard_map.131.table_ref), custom_call_target="tpu_custom_call" | custom-call | flops 3355443200 | bytes 8519680 | tf_op jit(solution)/shard_map/pallas_call | solution.py:30
  57.2 4.5 %shard_map.136.refs_0_.state_ref = bf16[640,256]{1,0:T(8,128)(2,1)S(1)} custom-call(s16[5120,128]{1,0:T(8,128)(2,1)S(1)} %get-tuple-element.33.source_ref, s32[1,5120]{1,0:T(1,128)S(1)} %get-tuple-element.34.target_ref, f32[1,5120]{1,0:T(1,128)S(1)} %get-tuple-element.35.coef_ref, bf16[640,256]{1,0:T(8,128)(2,1)S(1)} %shard_map.130.refs_0_.state_ref, ...), custom_call_target="tpu_custom_call" | custom-call | flops 2684354560 | bytes 8167424 | tf_op jit(solution)/shard_map/pallas_call | solution.py:30
  61.6 1.1 %collective-permute-start.17 = (bf16[640,256]{1,0:T(8,128)(2,1)S(1)}, bf16[640,256]{1,0:T(8,128)(2,1)S(1)}, u32[]{:S(2)}, u32[]{:S(2)}) collective-permute-start(bf16[640,256]{1,0:T(8,128)(2,1)S(1)} %shard_map.136.refs_0_.state_ref), channel_id=1, source_target_pairs={{0,2},{2,0},{1,3},{3,1},{4,6},{6,4},{5,7},{7,5},{8,10},{10,8},{9,1... | collective-permute-start | bytes 983048 | tf_op jit(solution)/shard_map/ppermute | solution.py:97
  62.7 0.5 shard_map.139
  63.2 3.3 %collective-permute-start.18 = (bf16[2,64,256]{2,1,0:T(8,128)(2,1)S(1)}, bf16[2,64,256]{2,1,0:T(8,128)(2,1)S(1)}, u32[]{:S(2)}, u32[]{:S(2)}) collective-permute-start(bf16[2,64,256]{2,1,0:T(8,128)(2,1)S(1)} %get-tuple-element.55), channel_id=1, source_target_pairs={{0,4},{1,5},{4,0},{5,1},{8,12},{9,13},{12,8},{13,9},{2,6},{3,7},{6... | collective-permute-start | bytes 196616 | tf_op jit(solution)/shard_map/ppermute | solution.py:79
  66.6 0.7 collective-permute-start.19
  67.2 1.0 %collective-permute-done.18.one_ref = bf16[2,64,256]{2,1,0:T(8,128)(2,1)S(1)} collective-permute-done((bf16[2,64,256]{2,1,0:T(8,128)(2,1)S(1)}, bf16[2,64,256]{2,1,0:T(8,128)(2,1)S(1)}, u32[]{:S(2)}, u32[]{:S(2)}) %collective-permute-start.18) | collective-permute-done | bytes 65568 | tf_op jit(solution)/shard_map/ppermute | solution.py:79
  68.3 8.4 %collective-permute-start.20 = (bf16[64,256]{1,0:T(8,128)(2,1)S(1)}, bf16[64,256]{1,0:T(8,128)(2,1)S(1)}, u32[]{:S(2)}, u32[]{:S(2)}) collective-permute-start(bf16[64,256]{1,0:T(8,128)(2,1)S(1)} %get-tuple-element.57), channel_id=1, source_target_pairs={{1,8},{5,12},{8,1},{12,5},{3,10},{7,14},{10,3},{14,7},{17,24},{21,... | collective-permute-start | bytes 98312 | tf_op jit(solution)/shard_map/ppermute | solution.py:79
  76.7 1.6 %collective-permute-done.20.distant_ref = bf16[64,256]{1,0:T(8,128)(2,1)S(1)} collective-permute-done((bf16[64,256]{1,0:T(8,128)(2,1)S(1)}, bf16[64,256]{1,0:T(8,128)(2,1)S(1)}, u32[]{:S(2)}, u32[]{:S(2)}) %collective-permute-start.20) | collective-permute-done | bytes 32800 | tf_op jit(solution)/shard_map/ppermute | solution.py:79
  78.4 1.8 %collective-permute-start.22 = (bf16[384,256]{1,0:T(8,128)(2,1)S(1)}, bf16[384,256]{1,0:T(8,128)(2,1)S(1)}, u32[]{:S(2)}, u32[]{:S(2)}) collective-permute-start(bf16[384,256]{1,0:T(8,128)(2,1)S(1)} %shard_map.141.refs_0_), channel_id=1, source_target_pairs={{0,2},{2,0},{1,3},{3,1},{4,6},{6,4},{5,7},{7,5},{8,10},{10,8},{9,1... | collective-permute-start | bytes 589832 | tf_op jit(solution)/shard_map/ppermute | solution.py:97
  80.2 0.5 shard_map.137.table_ref
  80.7 3.6 %shard_map.138.first_ref = f32[5120,256]{1,0:T(8,128)S(1)} custom-call(s16[5120,128]{1,0:T(8,128)(2,1)S(1)} %get-tuple-element.33.source_ref, s16[5120,128]{1,0:T(8,128)(2,1)S(1)} %get-tuple-element.47.target_ref, bf16[1280,256]{1,0:T(8,128)(2,1)S(1)} %shard_map.137.table_ref), custom_call_target="tpu_custom_call" | custom-call | flops 3355443200 | bytes 8519680 | tf_op jit(solution)/shard_map/pallas_call | solution.py:30
  84.2 5.2 %shard_map.142 = bf16[640,256]{1,0:T(8,128)(2,1)} custom-call(s16[5120,128]{1,0:T(8,128)(2,1)S(1)} %get-tuple-element.33.source_ref, s32[1,5120]{1,0:T(1,128)S(1)} %get-tuple-element.34.target_ref, f32[1,5120]{1,0:T(1,128)S(1)} %get-tuple-element.35.coef_ref, bf16[640,256]{1,0:T(8,128)(2,1)S(1)} %shard_map.136.refs_0_.state_ref, ...), custom_call_target="tpu_custom_call" | custom-call | flops 2684354560 | bytes 8167424 | tf_op jit(solution)/shard_map/pallas_call | solution.py:30
  (23 shorter events, 0.4 us)
Async XLA Ops:
  2.0 4.6 %collective-permute-start = (bf16[1,256,256]{2,1,0:T(8,128)(2,1)S(1)}, bf16[1,256,256]{2,1,0:T(8,128)(2,1)S(1)}, u32[]{:S(2)}, u32[]{:S(2)}) collective-permute-start(bf16[1,256,256]{2,1,0:T(8,128)(2,1)S(1)} %get-tuple-element.40.refs_0_), channel_id=1, source_target_pairs={{0,2},{2,0},{4,6},{6,4},{5,7},{7,5},{8,10},{10,8},{9,11},{11,9},{1... | collective-permute-start | bytes 393224 | tf_op jit(solution)/shard_map/ppermute | solution.py:97
  2.7 8.7 %collective-permute-start.2 = (bf16[1,256,256]{2,1,0:T(8,128)(2,1)S(1)}, bf16[1,256,256]{2,1,0:T(8,128)(2,1)S(1)}, u32[]{:S(2)}, u32[]{:S(2)}) collective-permute-start(bf16[1,256,256]{2,1,0:T(8,128)(2,1)S(1)} %get-tuple-element.41.refs_0_), channel_id=1, source_target_pairs={{1,3},{3,1},{5,7},{7,5},{8,10},{10,8},{12,14},{14,12},{17,19},{19,... | collective-permute-start | bytes 393224 | tf_op jit(solution)/shard_map/ppermute | solution.py:97
  7.4 18.1 %collective-permute-start.4 = (bf16[2,256,256]{2,1,0:T(8,128)(2,1)S(1)}, bf16[2,256,256]{2,1,0:T(8,128)(2,1)S(1)}, u32[]{:S(2)}, u32[]{:S(2)}) collective-permute-start(bf16[2,256,256]{2,1,0:T(8,128)(2,1)S(1)} %shard_map.123.refs_0_), channel_id=1, source_target_pairs={{0,2},{2,0},{1,3},{3,1},{4,6},{6,4},{5,7},{7,5},{8,10},{10,8},{9,1... | collective-permute-start | bytes 786440 | tf_op jit(solution)/shard_map/ppermute | solution.py:97
  10.7 12.9 %collective-permute-start.1 = (bf16[272,256]{1,0:T(8,128)(2,1)S(1)}, bf16[272,256]{1,0:T(8,128)(2,1)S(1)}, u32[]{:S(2)}, u32[]{:S(2)}) collective-permute-start(bf16[272,256]{1,0:T(8,128)(2,1)S(1)} %shard_map.120.refs_0_), channel_id=1, source_target_pairs={{0,5},{4,9},{5,0},{8,13},{9,4},{13,8},{2,7},{6,11},{7,2},{10,15},{... | collective-permute-start | bytes 417800 | tf_op jit(solution)/shard_map/ppermute | solution.py:79
  11.7 13.5 %collective-permute-start.3 = (bf16[272,256]{1,0:T(8,128)(2,1)S(1)}, bf16[272,256]{1,0:T(8,128)(2,1)S(1)}, u32[]{:S(2)}, u32[]{:S(2)}) collective-permute-start(bf16[272,256]{1,0:T(8,128)(2,1)S(1)} %shard_map.121.refs_1_), channel_id=1, source_target_pairs={{1,8},{5,12},{8,1},{12,5},{3,10},{7,14},{10,3},{14,7},{17,24},{21,... | collective-permute-start | bytes 417800 | tf_op jit(solution)/shard_map/ppermute | solution.py:79
  23.2 7.7 %collective-permute-start.7 = (bf16[2,256,256]{2,1,0:T(8,128)(2,1)S(1)}, bf16[2,256,256]{2,1,0:T(8,128)(2,1)S(1)}, u32[]{:S(2)}, u32[]{:S(2)}) collective-permute-start(bf16[2,256,256]{2,1,0:T(8,128)(2,1)S(1)} %shard_map.125.refs_0_), channel_id=1, source_target_pairs={{0,2},{2,0},{1,3},{3,1},{4,6},{6,4},{5,7},{7,5},{8,10},{10,8},{9,1... | collective-permute-start | bytes 786440 | tf_op jit(solution)/shard_map/ppermute | solution.py:97
  26.4 9.6 %collective-permute-start.9 = (bf16[1,256,256]{2,1,0:T(8,128)(2,1)S(1)}, bf16[1,256,256]{2,1,0:T(8,128)(2,1)S(1)}, u32[]{:S(2)}, u32[]{:S(2)}) collective-permute-start(bf16[1,256,256]{2,1,0:T(8,128)(2,1)S(1)} %shard_map.128.refs_0_), channel_id=1, source_target_pairs={{0,2},{2,0},{1,3},{3,1},{4,6},{6,4},{5,7},{7,5},{8,10},{10,8},{9,1... | collective-permute-start | bytes 393224 | tf_op jit(solution)/shard_map/ppermute | solution.py:97
  26.7 9.6 %collective-permute-start.5 = (bf16[272,256]{1,0:T(8,128)(2,1)S(1)}, bf16[272,256]{1,0:T(8,128)(2,1)S(1)}, u32[]{:S(2)}, u32[]{:S(2)}) collective-permute-start(bf16[272,256]{1,0:T(8,128)(2,1)S(1)} %get-tuple-element.43.refs_1_), channel_id=1, source_target_pairs={{0,4},{1,5},{4,0},{5,1},{8,12},{9,13},{12,8},{13,9},{2,6},{3,7},{6... | collective-permute-start | bytes 417800 | tf_op jit(solution)/shard_map/ppermute | solution.py:79
  29.4 7.0 %collective-permute-start.6 = (bf16[272,256]{1,0:T(8,128)(2,1)S(1)}, bf16[272,256]{1,0:T(8,128)(2,1)S(1)}, u32[]{:S(2)}, u32[]{:S(2)}) collective-permute-start(bf16[272,256]{1,0:T(8,128)(2,1)S(1)} %get-tuple-element.44.refs_2_), channel_id=1, source_target_pairs={{4,8},{5,9},{8,4},{9,5},{6,10},{7,11},{10,6},{11,7},{20,24},{21,25... | collective-permute-start | bytes 417800 | tf_op jit(solution)/shard_map/ppermute | solution.py:79
  31.3 7.4 %collective-permute-start.8 = (bf16[272,256]{1,0:T(8,128)(2,1)S(1)}, bf16[272,256]{1,0:T(8,128)(2,1)S(1)}, u32[]{:S(2)}, u32[]{:S(2)}) collective-permute-start(bf16[272,256]{1,0:T(8,128)(2,1)S(1)} %get-tuple-element.46), channel_id=1, source_target_pairs={{1,4},{4,1},{5,8},{8,5},{9,12},{12,9},{3,6},{6,3},{7,10},{10,7},{1... | collective-permute-start | bytes 417800 | tf_op jit(solution)/shard_map/ppermute | solution.py:79
  36.3 2.4 %collective-permute-start.10 = (bf16[272,256]{1,0:T(8,128)(2,1)S(1)}, bf16[272,256]{1,0:T(8,128)(2,1)S(1)}, u32[]{:S(2)}, u32[]{:S(2)}) collective-permute-start(bf16[272,256]{1,0:T(8,128)(2,1)S(1)} %shard_map.129), channel_id=1, source_target_pairs={{0,1},{1,0},{4,5},{5,4},{8,9},{9,8},{12,13},{13,12},{2,3},{3,2},{6... | collective-permute-start | bytes 417800 | tf_op jit(solution)/shard_map/ppermute | solution.py:79
  39.1 14.0 %collective-permute-start.11 = (bf16[640,256]{1,0:T(8,128)(2,1)S(1)}, bf16[640,256]{1,0:T(8,128)(2,1)S(1)}, u32[]{:S(2)}, u32[]{:S(2)}) collective-permute-start(bf16[640,256]{1,0:T(8,128)(2,1)S(1)} %shard_map.130.refs_0_.state_ref), channel_id=1, source_target_pairs={{0,2},{2,0},{1,3},{3,1},{4,6},{6,4},{5,7},{7,5},{8,10},{10,8},{9,1... | collective-permute-start | bytes 983048 | tf_op jit(solution)/shard_map/ppermute | solution.py:97
  41.3 3.5 %collective-permute-start.12 = (bf16[2,64,256]{2,1,0:T(8,128)(2,1)S(1)}, bf16[2,64,256]{2,1,0:T(8,128)(2,1)S(1)}, u32[]{:S(2)}, u32[]{:S(2)}) collective-permute-start(bf16[2,64,256]{2,1,0:T(8,128)(2,1)S(1)} %get-tuple-element.51), channel_id=1, source_target_pairs={{0,4},{1,5},{4,0},{5,1},{8,12},{9,13},{12,8},{13,9},{2,6},{3,7},{6... | collective-permute-start | bytes 196616 | tf_op jit(solution)/shard_map/ppermute | solution.py:79
  41.4 3.4 %collective-permute-start.13 = (bf16[2,64,256]{2,1,0:T(8,128)(2,1)S(1)}, bf16[2,64,256]{2,1,0:T(8,128)(2,1)S(1)}, u32[]{:S(2)}, u32[]{:S(2)}) collective-permute-start(bf16[2,64,256]{2,1,0:T(8,128)(2,1)S(1)} %get-tuple-element.52), channel_id=1, source_target_pairs={{4,8},{5,9},{8,4},{9,5},{6,10},{7,11},{10,6},{11,7},{20,24},{21,25... | collective-permute-start | bytes 196616 | tf_op jit(solution)/shard_map/ppermute | solution.py:79
  44.8 7.8 %collective-permute-start.15 = (bf16[3,64,256]{2,1,0:T(8,128)(2,1)S(1)}, bf16[3,64,256]{2,1,0:T(8,128)(2,1)S(1)}, u32[]{:S(2)}, u32[]{:S(2)}) collective-permute-start(bf16[3,64,256]{2,1,0:T(8,128)(2,1)S(1)} %shard_map.134), channel_id=1, source_target_pairs={{0,1},{1,0},{4,5},{5,4},{8,9},{9,8},{12,13},{13,12},{2,3},{3,2},{6... | collective-permute-start | bytes 294920 | tf_op jit(solution)/shard_map/ppermute | solution.py:79
  46.1 6.5 %collective-permute-start.14 = (bf16[64,256]{1,0:T(8,128)(2,1)S(1)}, bf16[64,256]{1,0:T(8,128)(2,1)S(1)}, u32[]{:S(2)}, u32[]{:S(2)}) collective-permute-start(bf16[64,256]{1,0:T(8,128)(2,1)S(1)} %get-tuple-element.53), channel_id=1, source_target_pairs={{1,8},{5,12},{8,1},{12,5},{3,10},{7,14},{10,3},{14,7},{17,24},{21,... | collective-permute-start | bytes 98312 | tf_op jit(solution)/shard_map/ppermute | solution.py:79
  52.6 4.6 %collective-permute-start.16 = (bf16[384,256]{1,0:T(8,128)(2,1)S(1)}, bf16[384,256]{1,0:T(8,128)(2,1)S(1)}, u32[]{:S(2)}, u32[]{:S(2)}) collective-permute-start(bf16[384,256]{1,0:T(8,128)(2,1)S(1)} %shard_map.135.refs_0_), channel_id=1, source_target_pairs={{0,2},{2,0},{1,3},{3,1},{4,6},{6,4},{5,7},{7,5},{8,10},{10,8},{9,1... | collective-permute-start | bytes 589832 | tf_op jit(solution)/shard_map/ppermute | solution.py:97
  61.6 18.5 %collective-permute-start.17 = (bf16[640,256]{1,0:T(8,128)(2,1)S(1)}, bf16[640,256]{1,0:T(8,128)(2,1)S(1)}, u32[]{:S(2)}, u32[]{:S(2)}) collective-permute-start(bf16[640,256]{1,0:T(8,128)(2,1)S(1)} %shard_map.136.refs_0_.state_ref), channel_id=1, source_target_pairs={{0,2},{2,0},{1,3},{3,1},{4,6},{6,4},{5,7},{7,5},{8,10},{10,8},{9,1... | collective-permute-start | bytes 983048 | tf_op jit(solution)/shard_map/ppermute | solution.py:97
  63.2 5.0 %collective-permute-start.18 = (bf16[2,64,256]{2,1,0:T(8,128)(2,1)S(1)}, bf16[2,64,256]{2,1,0:T(8,128)(2,1)S(1)}, u32[]{:S(2)}, u32[]{:S(2)}) collective-permute-start(bf16[2,64,256]{2,1,0:T(8,128)(2,1)S(1)} %get-tuple-element.55), channel_id=1, source_target_pairs={{0,4},{1,5},{4,0},{5,1},{8,12},{9,13},{12,8},{13,9},{2,6},{3,7},{6... | collective-permute-start | bytes 196616 | tf_op jit(solution)/shard_map/ppermute | solution.py:79
  66.6 1.7 %collective-permute-start.19 = (bf16[2,64,256]{2,1,0:T(8,128)(2,1)S(1)}, bf16[2,64,256]{2,1,0:T(8,128)(2,1)S(1)}, u32[]{:S(2)}, u32[]{:S(2)}) collective-permute-start(bf16[2,64,256]{2,1,0:T(8,128)(2,1)S(1)} %get-tuple-element.56), channel_id=1, source_target_pairs={{4,8},{5,9},{8,4},{9,5},{6,10},{7,11},{10,6},{11,7},{20,24},{21,25... | collective-permute-start | bytes 196616 | tf_op jit(solution)/shard_map/ppermute | solution.py:79
  68.2 10.1 %collective-permute-start.21 = (bf16[3,64,256]{2,1,0:T(8,128)(2,1)S(1)}, bf16[3,64,256]{2,1,0:T(8,128)(2,1)S(1)}, u32[]{:S(2)}, u32[]{:S(2)}) collective-permute-start(bf16[3,64,256]{2,1,0:T(8,128)(2,1)S(1)} %shard_map.140), channel_id=1, source_target_pairs={{0,1},{1,0},{4,5},{5,4},{8,9},{9,8},{12,13},{13,12},{2,3},{3,2},{6... | collective-permute-start | bytes 294920 | tf_op jit(solution)/shard_map/ppermute | solution.py:79
  68.3 10.0 %collective-permute-start.20 = (bf16[64,256]{1,0:T(8,128)(2,1)S(1)}, bf16[64,256]{1,0:T(8,128)(2,1)S(1)}, u32[]{:S(2)}, u32[]{:S(2)}) collective-permute-start(bf16[64,256]{1,0:T(8,128)(2,1)S(1)} %get-tuple-element.57), channel_id=1, source_target_pairs={{1,8},{5,12},{8,1},{12,5},{3,10},{7,14},{10,3},{14,7},{17,24},{21,... | collective-permute-start | bytes 98312 | tf_op jit(solution)/shard_map/ppermute | solution.py:79
  78.4 5.9 %collective-permute-start.22 = (bf16[384,256]{1,0:T(8,128)(2,1)S(1)}, bf16[384,256]{1,0:T(8,128)(2,1)S(1)}, u32[]{:S(2)}, u32[]{:S(2)}) collective-permute-start(bf16[384,256]{1,0:T(8,128)(2,1)S(1)} %shard_map.141.refs_0_), channel_id=1, source_target_pairs={{0,2},{2,0},{1,3},{3,1},{4,6},{6,4},{5,7},{7,5},{8,10},{10,8},{9,1... | collective-permute-start | bytes 589832 | tf_op jit(solution)/shard_map/ppermute | solution.py:97

commit v6 on v5

--- a/solution.py
+++ b/solution.py
@@ -322,7 +322,7 @@
     )[0]
 
 
-def list_kernel(reach, listed_ref, state_ref, one_ref, two_ref, far_ref, near_ref):
+def list_kernel(reach, listed_ref, state_ref, far_ref, near_ref, one_ref, two_ref):
     nodes = state_ref.shape[0]
     width = listed_ref.shape[2]
     lanes = lane_iota(nodes)
@@ -343,7 +343,10 @@
             for i in range(2):
                 ref[i] = parts[i]
         else:
-            far_ref[...] = parts[0]
+            far_ref[pl.ds(0, width), :] = parts[0]
+            far_ref[pl.ds(width, far_ref.shape[0] - width), :] = jnp.zeros(
+                (far_ref.shape[0] - width, parts[0].shape[1]), jnp.bfloat16
+            )
             near_ref[...] = parts[1]
 
 
@@ -351,23 +354,24 @@
     nodes, channels = state.shape
     links, unused, width = halo_send.shape
     one, two = [shape(d) for d in ((width, channels), (2, width, channels))]
+    far = shape((2 * width + PAD, channels))
     return call(
         functools.partial(list_kernel, reach),
-        [two, two, one, one],
+        [far, one, two, two],
         [halo_send, state],
         0,
     )
 
 
-def forward_kernel(near_ref, one_ref, two_ref, out_ref):
+def forward_kernel(distant_ref, near_ref, one_ref, two_ref, out_ref):
     other = 1 - lax.axis_index("edge")
     out_ref[0] = near_ref[...]
     out_ref[1] = one_ref[other]
     out_ref[2] = two_ref[other]
 
 
-def order_kernel(one_ref, two_ref, distant_ref, across_ref, out_ref):
-    width = distant_ref.shape[0]
+def order_kernel(distant_ref, one_ref, two_ref, across_ref, out_ref):
+    width = across_ref.shape[1]
     region = lax.axis_index(REGION)
     core = region % 2
     low_even = region // 2 % 2 == 0
@@ -377,7 +381,7 @@
         [jnp.where(low_even == first, pair[0], pair[1]) for pair in (own, across)] for first in (False, True)
     ]
     near = across_ref[0]
-    distant = distant_ref[...]
+    distant = distant_ref[pl.ds(0, width), :]
     even = core == 0
     rows = (
         jnp.where(even, after[1], distant),
@@ -391,14 +395,14 @@
         out_ref[pl.ds(j * width, width), :] = part
 
 
-def exchange_listed(one, two, far, near):
+def exchange_listed(far, near, one, two):
     width, channels = near.shape
+    distant = swapped(far, meets_other_three)
     one, two = swapped(one, meets_two), swapped(two, meets_other_two)
-    distant = swapped(far, meets_other_three)
-    sent = call(forward_kernel, [shape((3, width, channels))], [near, one, two], 0)[0]
+    sent = call(forward_kernel, [shape((3, width, channels))], [distant, near, one, two], 0)[0]
     across = swapped(sent, meets_core)
     return call(
-        order_kernel, [shape((6 * width, channels))], [one, two, distant, across], 0
+        order_kernel, [shape((6 * width, channels))], [distant, one, two, across], 0
     )[0]
 
 
@@ -509,7 +513,7 @@
         jnp.swapaxes(a, 0, 1) for a in (g2m_src, g2m_dst, g2m_coef, halo_send)
     ]
     groups = [
-        (meets_three,), (meets_other_three,), (meets_two, meets_other_two), (meets_next, None), (meets_core,)
+        (meets_other_three,), (meets_three,), (meets_two, meets_other_two), (meets_next, None), (meets_core,)
     ]
     picked, g2m_src, grid_latent = first_pick(groups[:2], g2m_src, grid_latent)
     arrived = [from_others(rows, group[0]) for group, rows in zip(groups, picked)]
@@ -528,7 +532,7 @@
     def encode_group(place, after=()):
         return encode(groups[place], picked[place], arrived[place], enc_weight, g2m_coef, g2m_dst, after)
 
-    pick_next(2, arrived[0])
+    pick_next(2, [*arrived[0], source_col])
     encoded = encode_group(0) + encode_group(1)
     pick_next(3, encoded)
     encoded += encode_group(2)

time: 89.8 us -> 85.1 us (0.948)
  the two profiles are of different devices: /device:TPU:1 before, /device:TPU:0 now
where the time goes in v6:
time: 85.1 us; the launch traced here: 84.4 us
  starting transfers between devices  41 us (48%)
  Pallas kernels  28.2 us (33%)
  waiting for transfers between devices  14.8 us (17%)
    ppermute x14, starting transfers between devices, swapped(): return lax.ppermute(value, REGION, pairs(meets))  29.6 us
    pallas_call x23, Pallas kernels, call(): pl.pallas_call(kernel, out_shape=shapes, in_specs=[pl.BlockSpec(memory_sp...  23.3 us
    ppermute x9, starting transfers between devices, from_others(): lax.ppermute(value, axes, [(ring[i], ring[(i + k) % n]) for ring in rings...  11.4 us
    ppermute x14, waiting for transfers between devices, swapped(): return lax.ppermute(value, REGION, pairs(meets))  7.6 us
    ppermute x9, waiting for transfers between devices, from_others(): lax.ppermute(value, axes, [(ring[i], ring[(i + k) % n]) for ring in rings...  7.23 us
    pallas_call x1, Pallas kernels, fetch(): pl.pallas_call(fetch_kernel, out_shape=[made_in_vmem(o) for o in outputs]...  2.94 us
    pallas_call x1, Pallas kernels, first_pick(): pl.pallas_call(functools.partial(first_pick_kernel, groups, parts), out_s...  2.01 us
  transfers between devices with their start and end apart: 23, of which 10 were waited for; matrix products, arithmetic and copies ran while one was open for 0% of the time, Pallas kernels for 19%

profile of v6, /device:TPU:0, one launch (start us, length us, event | category | flops | bytes accessed | tf_op | source)
XLA Modules:
  0.0 84.4 jit_solution(5459006483784793496)
XLA Ops:
  0.0 2.0 %shard_map.118 = (bf16[1,256,256]{2,1,0:T(8,128)(2,1)S(1)}, bf16[1,256,256]{2,1,0:T(8,128)(2,1)S(1)}, s32[7,1,256]{2,1,0:T(1,128)S(1)}, bf16[2048,256]{1,0:T(8,128)(2,1)S(1)}) custom-call(s32[7,1,256]{2,1,0:T(1,128)} %bitcast.4, bf16[2048,256]{1,0:T(8,128)(2,1)} %table_hbm.1), custom_call_target="tpu_custom_call" | custom-call | tf_op jit(solution)/shard_map/pallas_call | solution.py:221
  2.0 0.7 collective-permute-start
  2.7 4.8 %collective-permute-start.2 = (bf16[1,256,256]{2,1,0:T(8,128)(2,1)S(1)}, bf16[1,256,256]{2,1,0:T(8,128)(2,1)S(1)}, u32[]{:S(2)}, u32[]{:S(2)}) collective-permute-start(bf16[1,256,256]{2,1,0:T(8,128)(2,1)S(1)} %get-tuple-element.41.refs_0_), channel_id=1, source_target_pairs={{0,2},{2,0},{4,6},{6,4},{5,7},{7,5},{8,10},{10,8},{9,11},{11,9},{1... | collective-permute-start | bytes 393224 | tf_op jit(solution)/shard_map/ppermute | solution.py:97
  7.5 2.9 %shard_map.119 = (s32[1,5120]{1,0:T(1,128)}, s32[1,5120]{1,0:T(1,128)S(1)}, f32[1,5120]{1,0:T(1,128)S(1)}, bf16[512,256]{1,0:T(8,128)(2,1)S(1)}, f32[7,1,256]{2,...) custom-call(s32[7,1,256]{2,1,0:T(1,128)S(1)} %get-tuple-element.32.a, ...), custom_call_target="tpu_custom_call" | custom-call | tf_op jit(solution)/shard_map/pallas_call | solution.py:252
  10.5 0.8 shard_map.123.refs_0_
  11.6 0.7 collective-permute-start.1
  12.6 9.3 %collective-permute-start.3 = (bf16[272,256]{1,0:T(8,128)(2,1)S(1)}, bf16[272,256]{1,0:T(8,128)(2,1)S(1)}, u32[]{:S(2)}, u32[]{:S(2)}) collective-permute-start(bf16[272,256]{1,0:T(8,128)(2,1)S(1)} %shard_map.121.refs_1_), channel_id=1, source_target_pairs={{0,5},{4,9},{5,0},{8,13},{9,4},{13,8},{2,7},{6,11},{7,2},{10,15},{... | collective-permute-start | bytes 417800 | tf_op jit(solution)/shard_map/ppermute | solution.py:79
  21.8 0.8 shard_map.125.refs_0_
  22.6 0.6 collective-permute-start.7
  23.2 2.2 %collective-permute-done.3.refs_1_ = bf16[272,256]{1,0:T(8,128)(2,1)S(1)} collective-permute-done((bf16[272,256]{1,0:T(8,128)(2,1)S(1)}, bf16[272,256]{1,0:T(8,128)(2,1)S(1)}, u32[]{:S(2)}, u32[]{:S(2)}) %collective-permute-start.3) | collective-permute-done | bytes 139296 | tf_op jit(solution)/shard_map/ppermute | solution.py:79
  25.7 0.4 shard_map.124
  26.1 0.5 shard_map.128.refs_0_
  26.6 0.9 %collective-permute-start.9 = (bf16[1,256,256]{2,1,0:T(8,128)(2,1)S(1)}, bf16[1,256,256]{2,1,0:T(8,128)(2,1)S(1)}, u32[]{:S(2)}, u32[]{:S(2)}) collective-permute-start(bf16[1,256,256]{2,1,0:T(8,128)(2,1)S(1)} %shard_map.128.refs_0_), channel_id=1, source_target_pairs={{0,2},{2,0},{1,3},{3,1},{4,6},{6,4},{5,7},{7,5},{8,10},{10,8},{9,1... | collective-permute-start | bytes 393224 | tf_op jit(solution)/shard_map/ppermute | solution.py:97
  27.5 0.7 collective-permute-start.6
  28.2 2.7 %collective-permute-done.7.refs_1_ = bf16[2,256,256]{2,1,0:T(8,128)(2,1)S(1)} collective-permute-done((bf16[2,256,256]{2,1,0:T(8,128)(2,1)S(1)}, bf16[2,256,256]{2,1,0:T(8,128)(2,1)S(1)}, u32[]{:S(2)}, u32[]{:S(2)}) %collective-permute-start.7) | collective-permute-done | bytes 262176 | tf_op jit(solution)/shard_map/ppermute | solution.py:97
  30.9 0.4 shard_map.126
  31.2 0.7 collective-permute-start.8
  31.9 0.4 collective-permute-done.9.refs_1_
  32.5 1.7 %collective-permute-start.10 = (bf16[272,256]{1,0:T(8,128)(2,1)S(1)}, bf16[272,256]{1,0:T(8,128)(2,1)S(1)}, u32[]{:S(2)}, u32[]{:S(2)}) collective-permute-start(bf16[272,256]{1,0:T(8,128)(2,1)S(1)} %shard_map.129), channel_id=1, source_target_pairs={{0,1},{1,0},{4,5},{5,4},{8,9},{9,8},{12,13},{13,12},{2,3},{3,2},{6... | collective-permute-start | bytes 417800 | tf_op jit(solution)/shard_map/ppermute | solution.py:79
  34.2 0.4 shard_map.127.before_ref
  34.7 0.5 collective-permute-done.10.refs_1_
  35.2 0.3 shard_map.130.refs_0_.state_ref
  35.6 1.3 %collective-permute-start.11 = (bf16[640,256]{1,0:T(8,128)(2,1)S(1)}, bf16[640,256]{1,0:T(8,128)(2,1)S(1)}, u32[]{:S(2)}, u32[]{:S(2)}) collective-permute-start(bf16[640,256]{1,0:T(8,128)(2,1)S(1)} %shard_map.130.refs_0_.state_ref), channel_id=1, source_target_pairs={{0,2},{2,0},{1,3},{3,1},{4,6},{6,4},{5,7},{7,5},{8,10},{10,8},{9,1... | collective-permute-start | bytes 983048 | tf_op jit(solution)/shard_map/ppermute | solution.py:97
  36.8 0.5 shard_map.133
  37.3 0.7 collective-permute-start.12
  38.0 3.1 %collective-permute-start.13 = (bf16[2,64,256]{2,1,0:T(8,128)(2,1)S(1)}, bf16[2,64,256]{2,1,0:T(8,128)(2,1)S(1)}, u32[]{:S(2)}, u32[]{:S(2)}) collective-permute-start(bf16[2,64,256]{2,1,0:T(8,128)(2,1)S(1)} %get-tuple-element.52), channel_id=1, source_target_pairs={{0,4},{1,5},{4,0},{5,1},{8,12},{9,13},{12,8},{13,9},{2,6},{3,7},{6... | collective-permute-start | bytes 196616 | tf_op jit(solution)/shard_map/ppermute | solution.py:79
  41.0 0.8 collective-permute-start.14
  41.9 1.4 %collective-permute-done.13.one_ref = bf16[2,64,256]{2,1,0:T(8,128)(2,1)S(1)} collective-permute-done((bf16[2,64,256]{2,1,0:T(8,128)(2,1)S(1)}, bf16[2,64,256]{2,1,0:T(8,128)(2,1)S(1)}, u32[]{:S(2)}, u32[]{:S(2)}) %collective-permute-start.13) | collective-permute-done | bytes 65568 | tf_op jit(solution)/shard_map/ppermute | solution.py:79
  43.3 3.8 %collective-permute-start.15 = (bf16[3,64,256]{2,1,0:T(8,128)(2,1)S(1)}, bf16[3,64,256]{2,1,0:T(8,128)(2,1)S(1)}, u32[]{:S(2)}, u32[]{:S(2)}) collective-permute-start(bf16[3,64,256]{2,1,0:T(8,128)(2,1)S(1)} %shard_map.134), channel_id=1, source_target_pairs={{0,1},{1,0},{4,5},{5,4},{8,9},{9,8},{12,13},{13,12},{2,3},{3,2},{6... | collective-permute-start | bytes 294920 | tf_op jit(solution)/shard_map/ppermute | solution.py:79
  47.1 0.9 %collective-permute-done.15.across_ref = bf16[3,64,256]{2,1,0:T(8,128)(2,1)S(1)} collective-permute-done((bf16[3,64,256]{2,1,0:T(8,128)(2,1)S(1)}, bf16[3,64,256]{2,1,0:T(8,128)(2,1)S(1)}, u32[]{:S(2)}, u32[]{:S(2)}) %collective-permute-start.15) | collective-permute-done | bytes 98336 | tf_op jit(solution)/shard_map/ppermute | solution.py:79
  48.1 0.9 %collective-permute-start.16 = (bf16[384,256]{1,0:T(8,128)(2,1)S(1)}, bf16[384,256]{1,0:T(8,128)(2,1)S(1)}, u32[]{:S(2)}, u32[]{:S(2)}) collective-permute-start(bf16[384,256]{1,0:T(8,128)(2,1)S(1)} %shard_map.135.refs_0_), channel_id=1, source_target_pairs={{0,2},{2,0},{1,3},{3,1},{4,6},{6,4},{5,7},{7,5},{8,10},{10,8},{9,1... | collective-permute-start | bytes 589832 | tf_op jit(solution)/shard_map/ppermute | solution.py:97
  49.0 0.5 shard_map.131.table_ref
  49.5 3.5 %shard_map.132.first_ref = f32[5120,256]{1,0:T(8,128)S(1)} custom-call(s16[5120,128]{1,0:T(8,128)(2,1)S(1)} %get-tuple-element.33.refs_1_.source_ref, s16[5120,128]{1,0:T(8,128)(2,1)S(1)} %get-tuple-element.47.target_ref, bf16[1280,256]{1,0:T(8,128)(2,1)S(1)} %shard_map.131.table_ref), custom_call_target="tpu_custom_call" | custom-call | flops 3355443200 | bytes 8519680 | tf_op jit(solution)/shard_map/pallas_call | solution.py:30
  53.0 2.3 %collective-permute-done.16.refs_1_ = bf16[384,256]{1,0:T(8,128)(2,1)S(1)} collective-permute-done((bf16[384,256]{1,0:T(8,128)(2,1)S(1)}, bf16[384,256]{1,0:T(8,128)(2,1)S(1)}, u32[]{:S(2)}, u32[]{:S(2)}) %collective-permute-start.16) | collective-permute-done | bytes 196640 | tf_op jit(solution)/shard_map/ppermute | solution.py:97
  55.3 4.4 %shard_map.136.refs_0_.state_ref = bf16[640,256]{1,0:T(8,128)(2,1)S(1)} custom-call(s16[5120,128]{1,0:T(8,128)(2,1)S(1)} %get-tuple-element.33.refs_1_.source_ref, s32[1,5120]{1,0:T(1,128)S(1)} %get-tuple-element.34.target_ref, f32[1,5120]{1,0:T(1,128)S(1)} %get-tuple-element.35.coef_ref, bf16[640,256]{1,0:T(8,128)(2,1)S(1)} %shard_map.130.refs_0_.state_ref, ...), custom_call_target="tpu_custom_call" | custom-call | flops 2684354560 | bytes 8167424 | tf_op jit(solution)/shard_map/pallas_call | solution.py:30
  59.7 0.9 %collective-permute-start.17 = (bf16[640,256]{1,0:T(8,128)(2,1)S(1)}, bf16[640,256]{1,0:T(8,128)(2,1)S(1)}, u32[]{:S(2)}, u32[]{:S(2)}) collective-permute-start(bf16[640,256]{1,0:T(8,128)(2,1)S(1)} %shard_map.136.refs_0_.state_ref), channel_id=1, source_target_pairs={{0,2},{2,0},{1,3},{3,1},{4,6},{6,4},{5,7},{7,5},{8,10},{10,8},{9,1... | collective-permute-start | bytes 983048 | tf_op jit(solution)/shard_map/ppermute | solution.py:97
  60.6 0.5 shard_map.139
  61.1 0.7 collective-permute-start.18
  61.8 3.7 %collective-permute-start.19 = (bf16[2,64,256]{2,1,0:T(8,128)(2,1)S(1)}, bf16[2,64,256]{2,1,0:T(8,128)(2,1)S(1)}, u32[]{:S(2)}, u32[]{:S(2)}) collective-permute-start(bf16[2,64,256]{2,1,0:T(8,128)(2,1)S(1)} %get-tuple-element.56), channel_id=1, source_target_pairs={{0,4},{1,5},{4,0},{5,1},{8,12},{9,13},{12,8},{13,9},{2,6},{3,7},{6... | collective-permute-start | bytes 196616 | tf_op jit(solution)/shard_map/ppermute | solution.py:79
  65.4 0.7 collective-permute-start.20
  66.1 1.6 %collective-permute-done.19.one_ref = bf16[2,64,256]{2,1,0:T(8,128)(2,1)S(1)} collective-permute-done((bf16[2,64,256]{2,1,0:T(8,128)(2,1)S(1)}, bf16[2,64,256]{2,1,0:T(8,128)(2,1)S(1)}, u32[]{:S(2)}, u32[]{:S(2)}) %collective-permute-start.19) | collective-permute-done | bytes 65568 | tf_op jit(solution)/shard_map/ppermute | solution.py:79
  67.7 3.3 %collective-permute-start.21 = (bf16[3,64,256]{2,1,0:T(8,128)(2,1)S(1)}, bf16[3,64,256]{2,1,0:T(8,128)(2,1)S(1)}, u32[]{:S(2)}, u32[]{:S(2)}) collective-permute-start(bf16[3,64,256]{2,1,0:T(8,128)(2,1)S(1)} %shard_map.140), channel_id=1, source_target_pairs={{0,1},{1,0},{4,5},{5,4},{8,9},{9,8},{12,13},{13,12},{2,3},{3,2},{6... | collective-permute-start | bytes 294920 | tf_op jit(solution)/shard_map/ppermute | solution.py:79
  71.0 0.9 %collective-permute-done.21.across_ref = bf16[3,64,256]{2,1,0:T(8,128)(2,1)S(1)} collective-permute-done((bf16[3,64,256]{2,1,0:T(8,128)(2,1)S(1)}, bf16[3,64,256]{2,1,0:T(8,128)(2,1)S(1)}, u32[]{:S(2)}, u32[]{:S(2)}) %collective-permute-start.21) | collective-permute-done | bytes 98336 | tf_op jit(solution)/shard_map/ppermute | solution.py:79
  72.0 1.2 %collective-permute-start.22 = (bf16[384,256]{1,0:T(8,128)(2,1)S(1)}, bf16[384,256]{1,0:T(8,128)(2,1)S(1)}, u32[]{:S(2)}, u32[]{:S(2)}) collective-permute-start(bf16[384,256]{1,0:T(8,128)(2,1)S(1)} %shard_map.141.refs_0_), channel_id=1, source_target_pairs={{0,2},{2,0},{1,3},{3,1},{4,6},{6,4},{5,7},{7,5},{8,10},{10,8},{9,1... | collective-permute-start | bytes 589832 | tf_op jit(solution)/shard_map/ppermute | solution.py:97
  73.2 0.5 shard_map.137.table_ref
  73.7 3.5 %shard_map.138.first_ref = f32[5120,256]{1,0:T(8,128)S(1)} custom-call(s16[5120,128]{1,0:T(8,128)(2,1)S(1)} %get-tuple-element.33.refs_1_.source_ref, s16[5120,128]{1,0:T(8,128)(2,1)S(1)} %get-tuple-element.47.target_ref, bf16[1280,256]{1,0:T(8,128)(2,1)S(1)} %shard_map.137.table_ref), custom_call_target="tpu_custom_call" | custom-call | flops 3355443200 | bytes 8519680 | tf_op jit(solution)/shard_map/pallas_call | solution.py:30
  77.3 1.9 %collective-permute-done.22.refs_1_ = bf16[384,256]{1,0:T(8,128)(2,1)S(1)} collective-permute-done((bf16[384,256]{1,0:T(8,128)(2,1)S(1)}, bf16[384,256]{1,0:T(8,128)(2,1)S(1)}, u32[]{:S(2)}, u32[]{:S(2)}) %collective-permute-start.22) | collective-permute-done | bytes 196640 | tf_op jit(solution)/shard_map/ppermute | solution.py:97
  79.2 5.2 %shard_map.142 = bf16[640,256]{1,0:T(8,128)(2,1)} custom-call(s16[5120,128]{1,0:T(8,128)(2,1)S(1)} %get-tuple-element.33.refs_1_.source_ref, s32[1,5120]{1,0:T(1,128)S(1)} %get-tuple-element.34.target_ref, f32[1,5120]{1,0:T(1,128)S(1)} %get-tuple-element.35.coef_ref, bf16[640,256]{1,0:T(8,128)(2,1)S(1)} %shard_map.136.refs_0_.state_ref, ...), custom_call_target="tpu_custom_call" | custom-call | flops 2684354560 | bytes 8167424 | tf_op jit(solution)/shard_map/pallas_call | solution.py:30
  (23 shorter events, 1.3 us)
Async XLA Ops:
  2.0 8.5 %collective-permute-start = (bf16[1,256,256]{2,1,0:T(8,128)(2,1)S(1)}, bf16[1,256,256]{2,1,0:T(8,128)(2,1)S(1)}, u32[]{:S(2)}, u32[]{:S(2)}) collective-permute-start(bf16[1,256,256]{2,1,0:T(8,128)(2,1)S(1)} %get-tuple-element.40.refs_0_), channel_id=1, source_target_pairs={{1,3},{3,1},{5,7},{7,5},{8,10},{10,8},{12,14},{14,12},{17,19},{19,... | collective-permute-start | bytes 393224 | tf_op jit(solution)/shard_map/ppermute | solution.py:97
  2.7 9.6 %collective-permute-start.2 = (bf16[1,256,256]{2,1,0:T(8,128)(2,1)S(1)}, bf16[1,256,256]{2,1,0:T(8,128)(2,1)S(1)}, u32[]{:S(2)}, u32[]{:S(2)}) collective-permute-start(bf16[1,256,256]{2,1,0:T(8,128)(2,1)S(1)} %get-tuple-element.41.refs_0_), channel_id=1, source_target_pairs={{0,2},{2,0},{4,6},{6,4},{5,7},{7,5},{8,10},{10,8},{9,11},{11,9},{1... | collective-permute-start | bytes 393224 | tf_op jit(solution)/shard_map/ppermute | solution.py:97
  11.3 14.4 %collective-permute-start.4 = (bf16[2,256,256]{2,1,0:T(8,128)(2,1)S(1)}, bf16[2,256,256]{2,1,0:T(8,128)(2,1)S(1)}, u32[]{:S(2)}, u32[]{:S(2)}) collective-permute-start(bf16[2,256,256]{2,1,0:T(8,128)(2,1)S(1)} %shard_map.123.refs_0_), channel_id=1, source_target_pairs={{0,2},{2,0},{1,3},{3,1},{4,6},{6,4},{5,7},{7,5},{8,10},{10,8},{9,1... | collective-permute-start | bytes 786440 | tf_op jit(solution)/shard_map/ppermute | solution.py:97
  11.6 11.6 %collective-permute-start.1 = (bf16[272,256]{1,0:T(8,128)(2,1)S(1)}, bf16[272,256]{1,0:T(8,128)(2,1)S(1)}, u32[]{:S(2)}, u32[]{:S(2)}) collective-permute-start(bf16[272,256]{1,0:T(8,128)(2,1)S(1)} %shard_map.120.refs_0_), channel_id=1, source_target_pairs={{1,8},{5,12},{8,1},{12,5},{3,10},{7,14},{10,3},{14,7},{17,24},{21,... | collective-permute-start | bytes 417800 | tf_op jit(solution)/shard_map/ppermute | solution.py:79
  12.6 12.8 %collective-permute-start.3 = (bf16[272,256]{1,0:T(8,128)(2,1)S(1)}, bf16[272,256]{1,0:T(8,128)(2,1)S(1)}, u32[]{:S(2)}, u32[]{:S(2)}) collective-permute-start(bf16[272,256]{1,0:T(8,128)(2,1)S(1)} %shard_map.121.refs_1_), channel_id=1, source_target_pairs={{0,5},{4,9},{5,0},{8,13},{9,4},{13,8},{2,7},{6,11},{7,2},{10,15},{... | collective-permute-start | bytes 417800 | tf_op jit(solution)/shard_map/ppermute | solution.py:79
  22.6 8.3 %collective-permute-start.7 = (bf16[2,256,256]{2,1,0:T(8,128)(2,1)S(1)}, bf16[2,256,256]{2,1,0:T(8,128)(2,1)S(1)}, u32[]{:S(2)}, u32[]{:S(2)}) collective-permute-start(bf16[2,256,256]{2,1,0:T(8,128)(2,1)S(1)} %shard_map.125.refs_0_), channel_id=1, source_target_pairs={{0,2},{2,0},{1,3},{3,1},{4,6},{6,4},{5,7},{7,5},{8,10},{10,8},{9,1... | collective-permute-start | bytes 786440 | tf_op jit(solution)/shard_map/ppermute | solution.py:97
  26.6 5.7 %collective-permute-start.9 = (bf16[1,256,256]{2,1,0:T(8,128)(2,1)S(1)}, bf16[1,256,256]{2,1,0:T(8,128)(2,1)S(1)}, u32[]{:S(2)}, u32[]{:S(2)}) collective-permute-start(bf16[1,256,256]{2,1,0:T(8,128)(2,1)S(1)} %shard_map.128.refs_0_), channel_id=1, source_target_pairs={{0,2},{2,0},{1,3},{3,1},{4,6},{6,4},{5,7},{7,5},{8,10},{10,8},{9,1... | collective-permute-start | bytes 393224 | tf_op jit(solution)/shard_map/ppermute | solution.py:97
  27.5 6.7 %collective-permute-start.5 = (bf16[272,256]{1,0:T(8,128)(2,1)S(1)}, bf16[272,256]{1,0:T(8,128)(2,1)S(1)}, u32[]{:S(2)}, u32[]{:S(2)}) collective-permute-start(bf16[272,256]{1,0:T(8,128)(2,1)S(1)} %get-tuple-element.43.refs_1_), channel_id=1, source_target_pairs={{0,4},{1,5},{4,0},{5,1},{8,12},{9,13},{12,8},{13,9},{2,6},{3,7},{6... | collective-permute-start | bytes 417800 | tf_op jit(solution)/shard_map/ppermute | solution.py:79
  27.5 6.7 %collective-permute-start.6 = (bf16[272,256]{1,0:T(8,128)(2,1)S(1)}, bf16[272,256]{1,0:T(8,128)(2,1)S(1)}, u32[]{:S(2)}, u32[]{:S(2)}) collective-permute-start(bf16[272,256]{1,0:T(8,128)(2,1)S(1)} %get-tuple-element.44.refs_2_), channel_id=1, source_target_pairs={{4,8},{5,9},{8,4},{9,5},{6,10},{7,11},{10,6},{11,7},{20,24},{21,25... | collective-permute-start | bytes 417800 | tf_op jit(solution)/shard_map/ppermute | solution.py:79
  31.2 3.4 %collective-permute-start.8 = (bf16[272,256]{1,0:T(8,128)(2,1)S(1)}, bf16[272,256]{1,0:T(8,128)(2,1)S(1)}, u32[]{:S(2)}, u32[]{:S(2)}) collective-permute-start(bf16[272,256]{1,0:T(8,128)(2,1)S(1)} %get-tuple-element.46), channel_id=1, source_target_pairs={{1,4},{4,1},{5,8},{8,5},{9,12},{12,9},{3,6},{6,3},{7,10},{10,7},{1... | collective-permute-start | bytes 417800 | tf_op jit(solution)/shard_map/ppermute | solution.py:79
  32.5 2.7 %collective-permute-start.10 = (bf16[272,256]{1,0:T(8,128)(2,1)S(1)}, bf16[272,256]{1,0:T(8,128)(2,1)S(1)}, u32[]{:S(2)}, u32[]{:S(2)}) collective-permute-start(bf16[272,256]{1,0:T(8,128)(2,1)S(1)} %shard_map.129), channel_id=1, source_target_pairs={{0,1},{1,0},{4,5},{5,4},{8,9},{9,8},{12,13},{13,12},{2,3},{3,2},{6... | collective-permute-start | bytes 417800 | tf_op jit(solution)/shard_map/ppermute | solution.py:79
  35.6 13.4 %collective-permute-start.11 = (bf16[640,256]{1,0:T(8,128)(2,1)S(1)}, bf16[640,256]{1,0:T(8,128)(2,1)S(1)}, u32[]{:S(2)}, u32[]{:S(2)}) collective-permute-start(bf16[640,256]{1,0:T(8,128)(2,1)S(1)} %shard_map.130.refs_0_.state_ref), channel_id=1, source_target_pairs={{0,2},{2,0},{1,3},{3,1},{4,6},{6,4},{5,7},{7,5},{8,10},{10,8},{9,1... | collective-permute-start | bytes 983048 | tf_op jit(solution)/shard_map/ppermute | solution.py:97
  37.3 6.0 %collective-permute-start.12 = (bf16[144,256]{1,0:T(8,128)(2,1)S(1)}, bf16[144,256]{1,0:T(8,128)(2,1)S(1)}, u32[]{:S(2)}, u32[]{:S(2)}) collective-permute-start(bf16[144,256]{1,0:T(8,128)(2,1)S(1)} %get-tuple-element.51), channel_id=1, source_target_pairs={{1,8},{5,12},{8,1},{12,5},{3,10},{7,14},{10,3},{14,7},{17,24},{21,... | collective-permute-start | bytes 221192 | tf_op jit(solution)/shard_map/ppermute | solution.py:79
  38.0 5.3 %collective-permute-start.13 = (bf16[2,64,256]{2,1,0:T(8,128)(2,1)S(1)}, bf16[2,64,256]{2,1,0:T(8,128)(2,1)S(1)}, u32[]{:S(2)}, u32[]{:S(2)}) collective-permute-start(bf16[2,64,256]{2,1,0:T(8,128)(2,1)S(1)} %get-tuple-element.52), channel_id=1, source_target_pairs={{0,4},{1,5},{4,0},{5,1},{8,12},{9,13},{12,8},{13,9},{2,6},{3,7},{6... | collective-permute-start | bytes 196616 | tf_op jit(solution)/shard_map/ppermute | solution.py:79
  41.0 2.2 %collective-permute-start.14 = (bf16[2,64,256]{2,1,0:T(8,128)(2,1)S(1)}, bf16[2,64,256]{2,1,0:T(8,128)(2,1)S(1)}, u32[]{:S(2)}, u32[]{:S(2)}) collective-permute-start(bf16[2,64,256]{2,1,0:T(8,128)(2,1)S(1)} %get-tuple-element.53), channel_id=1, source_target_pairs={{4,8},{5,9},{8,4},{9,5},{6,10},{7,11},{10,6},{11,7},{20,24},{21,25... | collective-permute-start | bytes 196616 | tf_op jit(solution)/shard_map/ppermute | solution.py:79
  43.3 4.7 %collective-permute-start.15 = (bf16[3,64,256]{2,1,0:T(8,128)(2,1)S(1)}, bf16[3,64,256]{2,1,0:T(8,128)(2,1)S(1)}, u32[]{:S(2)}, u32[]{:S(2)}) collective-permute-start(bf16[3,64,256]{2,1,0:T(8,128)(2,1)S(1)} %shard_map.134), channel_id=1, source_target_pairs={{0,1},{1,0},{4,5},{5,4},{8,9},{9,8},{12,13},{13,12},{2,3},{3,2},{6... | collective-permute-start | bytes 294920 | tf_op jit(solution)/shard_map/ppermute | solution.py:79
  48.1 7.2 %collective-permute-start.16 = (bf16[384,256]{1,0:T(8,128)(2,1)S(1)}, bf16[384,256]{1,0:T(8,128)(2,1)S(1)}, u32[]{:S(2)}, u32[]{:S(2)}) collective-permute-start(bf16[384,256]{1,0:T(8,128)(2,1)S(1)} %shard_map.135.refs_0_), channel_id=1, source_target_pairs={{0,2},{2,0},{1,3},{3,1},{4,6},{6,4},{5,7},{7,5},{8,10},{10,8},{9,1... | collective-permute-start | bytes 589832 | tf_op jit(solution)/shard_map/ppermute | solution.py:97
  59.7 13.5 %collective-permute-start.17 = (bf16[640,256]{1,0:T(8,128)(2,1)S(1)}, bf16[640,256]{1,0:T(8,128)(2,1)S(1)}, u32[]{:S(2)}, u32[]{:S(2)}) collective-permute-start(bf16[640,256]{1,0:T(8,128)(2,1)S(1)} %shard_map.136.refs_0_.state_ref), channel_id=1, source_target_pairs={{0,2},{2,0},{1,3},{3,1},{4,6},{6,4},{5,7},{7,5},{8,10},{10,8},{9,1... | collective-permute-start | bytes 983048 | tf_op jit(solution)/shard_map/ppermute | solution.py:97
  61.1 6.6 %collective-permute-start.18 = (bf16[144,256]{1,0:T(8,128)(2,1)S(1)}, bf16[144,256]{1,0:T(8,128)(2,1)S(1)}, u32[]{:S(2)}, u32[]{:S(2)}) collective-permute-start(bf16[144,256]{1,0:T(8,128)(2,1)S(1)} %get-tuple-element.55), channel_id=1, source_target_pairs={{1,8},{5,12},{8,1},{12,5},{3,10},{7,14},{10,3},{14,7},{17,24},{21,... | collective-permute-start | bytes 221192 | tf_op jit(solution)/shard_map/ppermute | solution.py:79
  61.8 5.9 %collective-permute-start.19 = (bf16[2,64,256]{2,1,0:T(8,128)(2,1)S(1)}, bf16[2,64,256]{2,1,0:T(8,128)(2,1)S(1)}, u32[]{:S(2)}, u32[]{:S(2)}) collective-permute-start(bf16[2,64,256]{2,1,0:T(8,128)(2,1)S(1)} %get-tuple-element.56), channel_id=1, source_target_pairs={{0,4},{1,5},{4,0},{5,1},{8,12},{9,13},{12,8},{13,9},{2,6},{3,7},{6... | collective-permute-start | bytes 196616 | tf_op jit(solution)/shard_map/ppermute | solution.py:79
  65.4 2.2 %collective-permute-start.20 = (bf16[2,64,256]{2,1,0:T(8,128)(2,1)S(1)}, bf16[2,64,256]{2,1,0:T(8,128)(2,1)S(1)}, u32[]{:S(2)}, u32[]{:S(2)}) collective-permute-start(bf16[2,64,256]{2,1,0:T(8,128)(2,1)S(1)} %get-tuple-element.57), channel_id=1, source_target_pairs={{4,8},{5,9},{8,4},{9,5},{6,10},{7,11},{10,6},{11,7},{20,24},{21,25... | collective-permute-start | bytes 196616 | tf_op jit(solution)/shard_map/ppermute | solution.py:79
  67.7 4.2 %collective-permute-start.21 = (bf16[3,64,256]{2,1,0:T(8,128)(2,1)S(1)}, bf16[3,64,256]{2,1,0:T(8,128)(2,1)S(1)}, u32[]{:S(2)}, u32[]{:S(2)}) collective-permute-start(bf16[3,64,256]{2,1,0:T(8,128)(2,1)S(1)} %shard_map.140), channel_id=1, source_target_pairs={{0,1},{1,0},{4,5},{5,4},{8,9},{9,8},{12,13},{13,12},{2,3},{3,2},{6... | collective-permute-start | bytes 294920 | tf_op jit(solution)/shard_map/ppermute | solution.py:79
  72.0 7.2 %collective-permute-start.22 = (bf16[384,256]{1,0:T(8,128)(2,1)S(1)}, bf16[384,256]{1,0:T(8,128)(2,1)S(1)}, u32[]{:S(2)}, u32[]{:S(2)}) collective-permute-start(bf16[384,256]{1,0:T(8,128)(2,1)S(1)} %shard_map.141.refs_0_), channel_id=1, source_target_pairs={{0,2},{2,0},{1,3},{3,1},{4,6},{6,4},{5,7},{7,5},{8,10},{10,8},{9,1... | collective-permute-start | bytes 589832 | tf_op jit(solution)/shard_map/ppermute | solution.py:97

commit v7 on v6

--- a/solution.py
+++ b/solution.py
@@ -363,26 +363,35 @@
     )
 
 
-def forward_kernel(distant_ref, near_ref, one_ref, two_ref, out_ref):
-    other = 1 - lax.axis_index("edge")
-    out_ref[0] = near_ref[...]
-    out_ref[1] = one_ref[other]
-    out_ref[2] = two_ref[other]
-
-
-def order_kernel(distant_ref, one_ref, two_ref, across_ref, out_ref):
-    width = across_ref.shape[1]
+def forward_kernel(distant_ref, near_ref, one_ref, two_ref, sent_ref, mine_ref):
+    width = near_ref.shape[0]
+    core = lax.axis_index("edge")
+    for k, part in enumerate((near_ref[...], one_ref[1 - core], two_ref[1 - core])):
+        sent_ref[pl.ds(k * width, width), :] = part
+    for k, part in enumerate((distant_ref[pl.ds(0, width), :], one_ref[core], two_ref[core])):
+        mine_ref[pl.ds(k * width, width), :] = part
+
+
+def exchange_listed(far, near, one, two):
+    width, channels = near.shape
+    distant = swapped(far, meets_other_three)
+    one, two = swapped(one, meets_two), swapped(two, meets_other_two)
+    half = shape((3 * width, channels))
+    sent, mine = call(forward_kernel, [half, half], [distant, near, one, two], 0)
+    across = swapped(sent, meets_core)
+    return [mine, *from_others(mine)], [across, *from_others(across)]
+
+
+def ordered_rows(direct, across):
+    width = direct.shape[0] // 3
     region = lax.axis_index(REGION)
-    core = region % 2
+    even = region % 2 == 0
     low_even = region // 2 % 2 == 0
-    own = (one_ref[core], two_ref[core])
-    across = (across_ref[1], across_ref[2])
+    distant, *own = [direct[k * width : (k + 1) * width] for k in range(3)]
+    near, *crossed = [across[k * width : (k + 1) * width] for k in range(3)]
     before, after = [
-        [jnp.where(low_even == first, pair[0], pair[1]) for pair in (own, across)] for first in (False, True)
-    ]
-    near = across_ref[0]
-    distant = distant_ref[pl.ds(0, width), :]
-    even = core == 0
+        [jnp.where(low_even == first, pair[0], pair[1]) for pair in (own, crossed)] for first in (False, True)
+    ]
     rows = (
         jnp.where(even, after[1], distant),
         after[0],
@@ -391,19 +400,7 @@
         before[0],
         jnp.where(even, distant, before[1]),
     )
-    for j, part in enumerate(rows):
-        out_ref[pl.ds(j * width, width), :] = part
-
-
-def exchange_listed(far, near, one, two):
-    width, channels = near.shape
-    distant = swapped(far, meets_other_three)
-    one, two = swapped(one, meets_two), swapped(two, meets_other_two)
-    sent = call(forward_kernel, [shape((3, width, channels))], [distant, near, one, two], 0)[0]
-    across = swapped(sent, meets_core)
-    return call(
-        order_kernel, [shape((6 * width, channels))], [distant, one, two, across], 0
-    )[0]
+    return jnp.concatenate(rows, axis=0)
 
 
 def projected_rows(weight_ref, parts):
@@ -453,10 +450,15 @@
     )[0]
 
 
-def message_kernel(turn, layer, source_ref, target_ref, coef_ref, state_ref, first_ref, weight_ref, *refs):
+def message_kernel(
+    turn, turns, layer, source_ref, target_ref, coef_ref, state_ref, first_ref, weight_ref, *refs
+):
     listed, (out_ref, message_ref) = (refs[:-2], refs[-2:])
     nodes, channels = state_ref.shape
-    table = projected_rows(weight_ref.at[layer], listed)
+    half = len(listed) // 2
+    table = ordered_rows(
+        projected_rows(weight_ref.at[layer], listed[:half]), projected_rows(weight_ref.at[layer], listed[half:])
+    )
     lanes = (lane_iota(table.shape[0]).astype(jnp.int32) + nodes).astype(jnp.int16)
     rows16 = row_iota(nodes)
     total = state_ref[...].astype(jnp.float32)
@@ -468,22 +470,24 @@
 
     ahead = gathered(0)
     for start in range(0, edges, turn):
-        here = pl.ds(start, turn)
         summed = ahead
         if start + turn < edges:
             ahead = gathered(start + turn)
-        message_ref[here, :] = silu(summed).astype(jnp.bfloat16)
-        mask = sum_mask(target_ref[:, here], rows16, coef_ref[:, here])
-        total += dot(mask, message_ref[here, :])
+        message_ref[pl.ds(start, turn), :] = silu(summed).astype(jnp.bfloat16)
+        done = start // turn + 1
+        if done % turns == 0:
+            here = pl.ds((done - turns) * turn, turns * turn)
+            mask = sum_mask(target_ref[:, here], rows16, coef_ref[:, here])
+            total += dot(mask, message_ref[here, :])
     out_ref[...] = total.astype(jnp.bfloat16)
 
 
 def messages(layer, source_col, m2m_dst, m2m_coef, state, first, src_weights, listed, final):
     nodes, channels = state.shape
     edges = m2m_dst.shape[1]
-    named = listed[0].shape[0]
-    return call(
-        functools.partial(message_kernel, 512, layer),
+    named = 2 * listed[0].shape[0]
+    return call(
+        functools.partial(message_kernel, 512, 5, layer),
         [shape((nodes, channels))],
         [source_col, m2m_dst, m2m_coef, state, first, src_weights, *listed],
         2 * edges * (named + nodes) * channels,
@@ -533,8 +537,8 @@
         return encode(groups[place], picked[place], arrived[place], enc_weight, g2m_coef, g2m_dst, after)
 
     pick_next(2, [*arrived[0], source_col])
+    pick_next(3, arrived[1])
     encoded = encode_group(0) + encode_group(1)
-    pick_next(3, encoded)
     encoded += encode_group(2)
     blocks = [swapped(block, meets) for block, meets in zip(encoded, groups[0] + groups[1] + groups[2])]
     state = gather_in(mesh_latent, blocks[:2], jnp.float32)
@@ -548,12 +552,11 @@
     layers = src_weights.shape[0]
     for layer in range(layers):
         others = from_others(state)
-        listed = exchange_listed(*list_rows(state, halo_send, reach))
+        direct, across = exchange_listed(*list_rows(state, halo_send, reach))
         table = project(layer, [state, *others], src_weights, dst_weights)
-        listed = [listed, *from_others(listed)]
         first = first_part(source_col, target_col, table)
         state = messages(
-            layer, source_col, m2m_dst, m2m_coef, state, first, src_weights, listed, layer == layers - 1
+            layer, source_col, m2m_dst, m2m_coef, state, first, src_weights, direct + across, layer == layers - 1
         )
     return state
 

time: 85.1 us -> 82.4 us (0.968)
  waiting for transfers between devices: 14.8 us -> 10.4 us
  starting transfers between devices: 41 us -> 43.2 us
    ppermute x9 -> x11, waiting for transfers between devices: 7.23 us -> 4.61 us  [from_others(): lax.ppermute(value, axes, [(ring[i], ring[(i + k) % n]) for ring in rings...]
    ppermute x9 -> x11, starting transfers between devices: 11.4 us -> 13.2 us  [from_others(): lax.ppermute(value, axes, [(ring[i], ring[(i + k) % n]) for ring in rings...]
    ppermute x14, waiting for transfers between devices: 7.6 us -> 5.83 us  [swapped(): return lax.ppermute(value, REGION, pairs(meets))]
    pallas_call x23 -> x21, Pallas kernels: 23.3 us -> 22.9 us  [call(): pl.pallas_call(kernel, out_shape=shapes, in_specs=[pl.BlockSpec(memory_sp...]
  transfers between devices with their start and end apart: 23 -> 25, of which waited for: 10 -> 9; matrix products, arithmetic and copies ran while one was open for 0% -> 0% of each run, Pallas kernels for 19% -> 20%
where the time goes in v7:
time: 82.4 us; the launch traced here: 81.8 us
  starting transfers between devices  43.2 us (52%)
  Pallas kernels  27.8 us (34%)
  waiting for transfers between devices  10.4 us (13%)
    ppermute x14, starting transfers between devices, swapped(): return lax.ppermute(value, REGION, pairs(meets))  30 us
    pallas_call x21, Pallas kernels, call(): pl.pallas_call(kernel, out_shape=shapes, in_specs=[pl.BlockSpec(memory_sp...  22.9 us
    ppermute x11, starting transfers between devices, from_others(): lax.ppermute(value, axes, [(ring[i], ring[(i + k) % n]) for ring in rings...  13.2 us
    ppermute x14, waiting for transfers between devices, swapped(): return lax.ppermute(value, REGION, pairs(meets))  5.83 us
    ppermute x11, waiting for transfers between devices, from_others(): lax.ppermute(value, axes, [(ring[i], ring[(i + k) % n]) for ring in rings...  4.61 us
    pallas_call x1, Pallas kernels, fetch(): pl.pallas_call(fetch_kernel, out_shape=[made_in_vmem(o) for o in outputs]...  2.94 us
    pallas_call x1, Pallas kernels, first_pick(): pl.pallas_call(functools.partial(first_pick_kernel, groups, parts), out_s...  2.01 us
  transfers between devices with their start and end apart: 25, of which 9 were waited for; matrix products, arithmetic and copies ran while one was open for 0% of the time, Pallas kernels for 20%

profile of v7, /device:TPU:0, one launch (start us, length us, event | category | flops | bytes accessed | tf_op | source)
XLA Modules:
  0.0 81.8 jit_solution(8157615922901296789)
XLA Ops:
  0.0 2.0 %shard_map.118 = (bf16[1,256,256]{2,1,0:T(8,128)(2,1)S(1)}, bf16[1,256,256]{2,1,0:T(8,128)(2,1)S(1)}, s32[7,1,256]{2,1,0:T(1,128)S(1)}, bf16[2048,256]{1,0:T(8,128)(2,1)S(1)}) custom-call(s32[7,1,256]{2,1,0:T(1,128)} %bitcast.4, bf16[2048,256]{1,0:T(8,128)(2,1)} %table_hbm.1), custom_call_target="tpu_custom_call" | custom-call | tf_op jit(solution)/shard_map/pallas_call | solution.py:221
  2.0 0.7 collective-permute-start
  2.7 4.8 %collective-permute-start.2 = (bf16[1,256,256]{2,1,0:T(8,128)(2,1)S(1)}, bf16[1,256,256]{2,1,0:T(8,128)(2,1)S(1)}, u32[]{:S(2)}, u32[]{:S(2)}) collective-permute-start(bf16[1,256,256]{2,1,0:T(8,128)(2,1)S(1)} %get-tuple-element.45.refs_0_), channel_id=1, source_target_pairs={{0,2},{2,0},{4,6},{6,4},{5,7},{7,5},{8,10},{10,8},{9,11},{11,9},{1... | collective-permute-start | bytes 393224 | tf_op jit(solution)/shard_map/ppermute | solution.py:97
  7.5 2.9 %shard_map.119 = (s32[1,5120]{1,0:T(1,128)}, s32[1,5120]{1,0:T(1,128)S(1)}, f32[1,5120]{1,0:T(1,128)S(1)}, bf16[512,256]{1,0:T(8,128)(2,1)S(1)}, f32[7,1,256]{2,...) custom-call(s32[7,1,256]{2,1,0:T(1,128)S(1)} %get-tuple-element.36.a, ...), custom_call_target="tpu_custom_call" | custom-call | tf_op jit(solution)/shard_map/pallas_call | solution.py:252
  10.5 0.8 shard_map.123.refs_0_
  11.6 0.7 collective-permute-start.1
  12.6 9.3 %collective-permute-start.3 = (bf16[272,256]{1,0:T(8,128)(2,1)S(1)}, bf16[272,256]{1,0:T(8,128)(2,1)S(1)}, u32[]{:S(2)}, u32[]{:S(2)}) collective-permute-start(bf16[272,256]{1,0:T(8,128)(2,1)S(1)} %shard_map.121), channel_id=1, source_target_pairs={{0,5},{4,9},{5,0},{8,13},{9,4},{13,8},{2,7},{6,11},{7,2},{10,15},{... | collective-permute-start | bytes 417800 | tf_op jit(solution)/shard_map/ppermute | solution.py:79
  21.8 0.8 shard_map.125.refs_0_
  22.6 0.6 collective-permute-start.7
  23.2 2.2 %collective-permute-done.3.refs_1_ = bf16[272,256]{1,0:T(8,128)(2,1)S(1)} collective-permute-done((bf16[272,256]{1,0:T(8,128)(2,1)S(1)}, bf16[272,256]{1,0:T(8,128)(2,1)S(1)}, u32[]{:S(2)}, u32[]{:S(2)}) %collective-permute-start.3) | collective-permute-done | bytes 139296 | tf_op jit(solution)/shard_map/ppermute | solution.py:79
  25.7 0.4 shard_map.124
  26.1 0.5 shard_map.128.refs_0_
  26.6 0.9 %collective-permute-start.9 = (bf16[1,256,256]{2,1,0:T(8,128)(2,1)S(1)}, bf16[1,256,256]{2,1,0:T(8,128)(2,1)S(1)}, u32[]{:S(2)}, u32[]{:S(2)}) collective-permute-start(bf16[1,256,256]{2,1,0:T(8,128)(2,1)S(1)} %shard_map.128.refs_0_), channel_id=1, source_target_pairs={{0,2},{2,0},{1,3},{3,1},{4,6},{6,4},{5,7},{7,5},{8,10},{10,8},{9,1... | collective-permute-start | bytes 393224 | tf_op jit(solution)/shard_map/ppermute | solution.py:97
  27.5 0.7 collective-permute-start.6
  28.2 2.7 %collective-permute-done.7.refs_1_ = bf16[2,256,256]{2,1,0:T(8,128)(2,1)S(1)} collective-permute-done((bf16[2,256,256]{2,1,0:T(8,128)(2,1)S(1)}, bf16[2,256,256]{2,1,0:T(8,128)(2,1)S(1)}, u32[]{:S(2)}, u32[]{:S(2)}) %collective-permute-start.7) | collective-permute-done | bytes 262176 | tf_op jit(solution)/shard_map/ppermute | solution.py:97
  30.9 0.4 shard_map.126
  31.2 0.7 collective-permute-start.8
  31.9 0.4 collective-permute-done.9.refs_1_
  32.5 1.7 %collective-permute-start.10 = (bf16[272,256]{1,0:T(8,128)(2,1)S(1)}, bf16[272,256]{1,0:T(8,128)(2,1)S(1)}, u32[]{:S(2)}, u32[]{:S(2)}) collective-permute-start(bf16[272,256]{1,0:T(8,128)(2,1)S(1)} %shard_map.129), channel_id=1, source_target_pairs={{0,1},{1,0},{4,5},{5,4},{8,9},{9,8},{12,13},{13,12},{2,3},{3,2},{6... | collective-permute-start | bytes 417800 | tf_op jit(solution)/shard_map/ppermute | solution.py:79
  34.2 0.4 shard_map.127.before_ref
  34.7 0.5 collective-permute-done.10.refs_1_
  35.2 0.3 shard_map.130.refs_0_.state_ref
  35.6 1.3 %collective-permute-start.11 = (bf16[640,256]{1,0:T(8,128)(2,1)S(1)}, bf16[640,256]{1,0:T(8,128)(2,1)S(1)}, u32[]{:S(2)}, u32[]{:S(2)}) collective-permute-start(bf16[640,256]{1,0:T(8,128)(2,1)S(1)} %shard_map.130.refs_0_.state_ref), channel_id=1, source_target_pairs={{0,2},{2,0},{1,3},{3,1},{4,6},{6,4},{5,7},{7,5},{8,10},{10,8},{9,1... | collective-permute-start | bytes 983048 | tf_op jit(solution)/shard_map/ppermute | solution.py:97
  36.8 0.5 shard_map.133
  37.3 0.7 collective-permute-start.12
  38.0 3.1 %collective-permute-start.13 = (bf16[2,64,256]{2,1,0:T(8,128)(2,1)S(1)}, bf16[2,64,256]{2,1,0:T(8,128)(2,1)S(1)}, u32[]{:S(2)}, u32[]{:S(2)}) collective-permute-start(bf16[2,64,256]{2,1,0:T(8,128)(2,1)S(1)} %get-tuple-element.57), channel_id=1, source_target_pairs={{0,4},{1,5},{4,0},{5,1},{8,12},{9,13},{12,8},{13,9},{2,6},{3,7},{6... | collective-permute-start | bytes 196616 | tf_op jit(solution)/shard_map/ppermute | solution.py:79
  41.0 0.8 %collective-permute-start.14 = (bf16[2,64,256]{2,1,0:T(8,128)(2,1)S(1)}, bf16[2,64,256]{2,1,0:T(8,128)(2,1)S(1)}, u32[]{:S(2)}, u32[]{:S(2)}) collective-permute-start(bf16[2,64,256]{2,1,0:T(8,128)(2,1)S(1)} %get-tuple-element.58), channel_id=1, source_target_pairs={{4,8},{5,9},{8,4},{9,5},{6,10},{7,11},{10,6},{11,7},{20,24},{21,25... | collective-permute-start | bytes 196616 | tf_op jit(solution)/shard_map/ppermute | solution.py:79
  41.9 1.4 %collective-permute-done.13.one_ref = bf16[2,64,256]{2,1,0:T(8,128)(2,1)S(1)} collective-permute-done((bf16[2,64,256]{2,1,0:T(8,128)(2,1)S(1)}, bf16[2,64,256]{2,1,0:T(8,128)(2,1)S(1)}, u32[]{:S(2)}, u32[]{:S(2)}) %collective-permute-start.13) | collective-permute-done | bytes 65568 | tf_op jit(solution)/shard_map/ppermute | solution.py:79
  43.3 3.8 %collective-permute-start.16 = (bf16[192,256]{1,0:T(8,128)(2,1)S(1)}, bf16[192,256]{1,0:T(8,128)(2,1)S(1)}, u32[]{:S(2)}, u32[]{:S(2)}) collective-permute-start(bf16[192,256]{1,0:T(8,128)(2,1)S(1)} %get-tuple-element.60), channel_id=1, source_target_pairs={{0,1},{1,0},{4,5},{5,4},{8,9},{9,8},{12,13},{13,12},{2,3},{3,2},{6... | collective-permute-start | bytes 294920 | tf_op jit(solution)/shard_map/ppermute | solution.py:79
  47.1 0.8 %collective-permute-start.15 = (bf16[192,256]{1,0:T(8,128)(2,1)S(1)}, bf16[192,256]{1,0:T(8,128)(2,1)S(1)}, u32[]{:S(2)}, u32[]{:S(2)}) collective-permute-start(bf16[192,256]{1,0:T(8,128)(2,1)S(1)} %get-tuple-element.59.refs_0_), channel_id=1, source_target_pairs={{0,2},{2,0},{1,3},{3,1},{4,6},{6,4},{5,7},{7,5},{8,10},{10,8},{9,1... | collective-permute-start | bytes 294920 | tf_op jit(solution)/shard_map/ppermute | solution.py:97
  48.0 1.1 %collective-permute-start.17 = (bf16[192,256]{1,0:T(8,128)(2,1)S(1)}, bf16[192,256]{1,0:T(8,128)(2,1)S(1)}, u32[]{:S(2)}, u32[]{:S(2)}) collective-permute-start(bf16[192,256]{1,0:T(8,128)(2,1)S(1)} %collective-permute-done.16.refs_2_), channel_id=1, source_target_pairs={{0,2},{2,0},{1,3},{3,1},{4,6},{6,4},{5,7},{7,5},{8,10},{10,8},{9,1... | collective-permute-start | bytes 294920 | tf_op jit(solution)/shard_map/ppermute | solution.py:97
  49.1 0.5 shard_map.131.table_ref
  49.6 3.5 %shard_map.132.first_ref = f32[5120,256]{1,0:T(8,128)S(1)} custom-call(s16[5120,128]{1,0:T(8,128)(2,1)S(1)} %get-tuple-element.37.refs_1_.source_ref, s16[5120,128]{1,0:T(8,128)(2,1)S(1)} %get-tuple-element.51.target_ref, bf16[1280,256]{1,0:T(8,128)(2,1)S(1)} %shard_map.131.table_ref), custom_call_target="tpu_custom_call" | custom-call | flops 3355443200 | bytes 8519680 | tf_op jit(solution)/shard_map/pallas_call | solution.py:30
  53.2 0.8 collective-permute-done.17.refs_3_
  54.0 4.3 %shard_map.135.refs_0_.state_ref = bf16[640,256]{1,0:T(8,128)(2,1)S(1)} custom-call(s16[5120,128]{1,0:T(8,128)(2,1)S(1)} %get-tuple-element.37.refs_1_.source_ref, s32[1,5120]{1,0:T(1,128)S(1)} %get-tuple-element.38.target_ref, f32[1,5120]{1,0:T(1,128)S(1)} %get-tuple-element.39.coef_ref, bf16[640,256]{1,0:T(8,128)(2,1)S(1)} %shard_map.130.refs_0_.state_ref, ...), custom_call_target="tpu_custom_call" | custom-call | flops 2684354560 | bytes 8167424 | tf_op jit(solution)/shard_map/pallas_call | solution.py:30
  58.2 0.9 %collective-permute-start.18 = (bf16[640,256]{1,0:T(8,128)(2,1)S(1)}, bf16[640,256]{1,0:T(8,128)(2,1)S(1)}, u32[]{:S(2)}, u32[]{:S(2)}) collective-permute-start(bf16[640,256]{1,0:T(8,128)(2,1)S(1)} %shard_map.135.refs_0_.state_ref), channel_id=1, source_target_pairs={{0,2},{2,0},{1,3},{3,1},{4,6},{6,4},{5,7},{7,5},{8,10},{10,8},{9,1... | collective-permute-start | bytes 983048 | tf_op jit(solution)/shard_map/ppermute | solution.py:97
  59.1 0.5 shard_map.138
  59.6 0.7 collective-permute-start.19
  60.3 3.7 %collective-permute-start.20 = (bf16[2,64,256]{2,1,0:T(8,128)(2,1)S(1)}, bf16[2,64,256]{2,1,0:T(8,128)(2,1)S(1)}, u32[]{:S(2)}, u32[]{:S(2)}) collective-permute-start(bf16[2,64,256]{2,1,0:T(8,128)(2,1)S(1)} %get-tuple-element.63), channel_id=1, source_target_pairs={{0,4},{1,5},{4,0},{5,1},{8,12},{9,13},{12,8},{13,9},{2,6},{3,7},{6... | collective-permute-start | bytes 196616 | tf_op jit(solution)/shard_map/ppermute | solution.py:79
  63.9 0.7 collective-permute-start.21
  64.6 1.6 %collective-permute-done.20.one_ref = bf16[2,64,256]{2,1,0:T(8,128)(2,1)S(1)} collective-permute-done((bf16[2,64,256]{2,1,0:T(8,128)(2,1)S(1)}, bf16[2,64,256]{2,1,0:T(8,128)(2,1)S(1)}, u32[]{:S(2)}, u32[]{:S(2)}) %collective-permute-start.20) | collective-permute-done | bytes 65568 | tf_op jit(solution)/shard_map/ppermute | solution.py:79
  66.2 3.7 %collective-permute-start.23 = (bf16[192,256]{1,0:T(8,128)(2,1)S(1)}, bf16[192,256]{1,0:T(8,128)(2,1)S(1)}, u32[]{:S(2)}, u32[]{:S(2)}) collective-permute-start(bf16[192,256]{1,0:T(8,128)(2,1)S(1)} %get-tuple-element.66), channel_id=1, source_target_pairs={{0,1},{1,0},{4,5},{5,4},{8,9},{9,8},{12,13},{13,12},{2,3},{3,2},{6... | collective-permute-start | bytes 294920 | tf_op jit(solution)/shard_map/ppermute | solution.py:79
  69.9 1.0 %collective-permute-start.22 = (bf16[192,256]{1,0:T(8,128)(2,1)S(1)}, bf16[192,256]{1,0:T(8,128)(2,1)S(1)}, u32[]{:S(2)}, u32[]{:S(2)}) collective-permute-start(bf16[192,256]{1,0:T(8,128)(2,1)S(1)} %get-tuple-element.65.refs_0_), channel_id=1, source_target_pairs={{0,2},{2,0},{1,3},{3,1},{4,6},{6,4},{5,7},{7,5},{8,10},{10,8},{9,1... | collective-permute-start | bytes 294920 | tf_op jit(solution)/shard_map/ppermute | solution.py:97
  70.9 1.0 %collective-permute-start.24 = (bf16[192,256]{1,0:T(8,128)(2,1)S(1)}, bf16[192,256]{1,0:T(8,128)(2,1)S(1)}, u32[]{:S(2)}, u32[]{:S(2)}) collective-permute-start(bf16[192,256]{1,0:T(8,128)(2,1)S(1)} %collective-permute-done.23.refs_2_), channel_id=1, source_target_pairs={{0,2},{2,0},{1,3},{3,1},{4,6},{6,4},{5,7},{7,5},{8,10},{10,8},{9,1... | collective-permute-start | bytes 294920 | tf_op jit(solution)/shard_map/ppermute | solution.py:97
  71.9 0.5 shard_map.136.table_ref
  72.4 3.5 %shard_map.137.first_ref = f32[5120,256]{1,0:T(8,128)S(1)} custom-call(s16[5120,128]{1,0:T(8,128)(2,1)S(1)} %get-tuple-element.37.refs_1_.source_ref, s16[5120,128]{1,0:T(8,128)(2,1)S(1)} %get-tuple-element.51.target_ref, bf16[1280,256]{1,0:T(8,128)(2,1)S(1)} %shard_map.136.table_ref), custom_call_target="tpu_custom_call" | custom-call | flops 3355443200 | bytes 8519680 | tf_op jit(solution)/shard_map/pallas_call | solution.py:30
  76.0 0.8 collective-permute-done.24.refs_3_
  76.8 5.0 %shard_map.140 = bf16[640,256]{1,0:T(8,128)(2,1)} custom-call(s16[5120,128]{1,0:T(8,128)(2,1)S(1)} %get-tuple-element.37.refs_1_.source_ref, s32[1,5120]{1,0:T(1,128)S(1)} %get-tuple-element.38.target_ref, f32[1,5120]{1,0:T(1,128)S(1)} %get-tuple-element.39.coef_ref, bf16[640,256]{1,0:T(8,128)(2,1)S(1)} %shard_map.135.refs_0_.state_ref, ...), custom_call_target="tpu_custom_call" | custom-call | flops 2684354560 | bytes 8167424 | tf_op jit(solution)/shard_map/pallas_call | solution.py:30
  (25 shorter events, 1.4 us)
Async XLA Ops:
  2.0 8.5 %collective-permute-start = (bf16[1,256,256]{2,1,0:T(8,128)(2,1)S(1)}, bf16[1,256,256]{2,1,0:T(8,128)(2,1)S(1)}, u32[]{:S(2)}, u32[]{:S(2)}) collective-permute-start(bf16[1,256,256]{2,1,0:T(8,128)(2,1)S(1)} %get-tuple-element.44.refs_0_), channel_id=1, source_target_pairs={{1,3},{3,1},{5,7},{7,5},{8,10},{10,8},{12,14},{14,12},{17,19},{19,... | collective-permute-start | bytes 393224 | tf_op jit(solution)/shard_map/ppermute | solution.py:97
  2.7 9.6 %collective-permute-start.2 = (bf16[1,256,256]{2,1,0:T(8,128)(2,1)S(1)}, bf16[1,256,256]{2,1,0:T(8,128)(2,1)S(1)}, u32[]{:S(2)}, u32[]{:S(2)}) collective-permute-start(bf16[1,256,256]{2,1,0:T(8,128)(2,1)S(1)} %get-tuple-element.45.refs_0_), channel_id=1, source_target_pairs={{0,2},{2,0},{4,6},{6,4},{5,7},{7,5},{8,10},{10,8},{9,11},{11,9},{1... | collective-permute-start | bytes 393224 | tf_op jit(solution)/shard_map/ppermute | solution.py:97
  11.3 14.4 %collective-permute-start.4 = (bf16[2,256,256]{2,1,0:T(8,128)(2,1)S(1)}, bf16[2,256,256]{2,1,0:T(8,128)(2,1)S(1)}, u32[]{:S(2)}, u32[]{:S(2)}) collective-permute-start(bf16[2,256,256]{2,1,0:T(8,128)(2,1)S(1)} %shard_map.123.refs_0_), channel_id=1, source_target_pairs={{0,2},{2,0},{1,3},{3,1},{4,6},{6,4},{5,7},{7,5},{8,10},{10,8},{9,1... | collective-permute-start | bytes 786440 | tf_op jit(solution)/shard_map/ppermute | solution.py:97
  11.6 11.6 %collective-permute-start.1 = (bf16[272,256]{1,0:T(8,128)(2,1)S(1)}, bf16[272,256]{1,0:T(8,128)(2,1)S(1)}, u32[]{:S(2)}, u32[]{:S(2)}) collective-permute-start(bf16[272,256]{1,0:T(8,128)(2,1)S(1)} %shard_map.120), channel_id=1, source_target_pairs={{1,8},{5,12},{8,1},{12,5},{3,10},{7,14},{10,3},{14,7},{17,24},{21,... | collective-permute-start | bytes 417800 | tf_op jit(solution)/shard_map/ppermute | solution.py:79
  12.6 12.8 %collective-permute-start.3 = (bf16[272,256]{1,0:T(8,128)(2,1)S(1)}, bf16[272,256]{1,0:T(8,128)(2,1)S(1)}, u32[]{:S(2)}, u32[]{:S(2)}) collective-permute-start(bf16[272,256]{1,0:T(8,128)(2,1)S(1)} %shard_map.121), channel_id=1, source_target_pairs={{0,5},{4,9},{5,0},{8,13},{9,4},{13,8},{2,7},{6,11},{7,2},{10,15},{... | collective-permute-start | bytes 417800 | tf_op jit(solution)/shard_map/ppermute | solution.py:79
  22.6 8.3 %collective-permute-start.7 = (bf16[2,256,256]{2,1,0:T(8,128)(2,1)S(1)}, bf16[2,256,256]{2,1,0:T(8,128)(2,1)S(1)}, u32[]{:S(2)}, u32[]{:S(2)}) collective-permute-start(bf16[2,256,256]{2,1,0:T(8,128)(2,1)S(1)} %shard_map.125.refs_0_), channel_id=1, source_target_pairs={{0,2},{2,0},{1,3},{3,1},{4,6},{6,4},{5,7},{7,5},{8,10},{10,8},{9,1... | collective-permute-start | bytes 786440 | tf_op jit(solution)/shard_map/ppermute | solution.py:97
  26.6 5.7 %collective-permute-start.9 = (bf16[1,256,256]{2,1,0:T(8,128)(2,1)S(1)}, bf16[1,256,256]{2,1,0:T(8,128)(2,1)S(1)}, u32[]{:S(2)}, u32[]{:S(2)}) collective-permute-start(bf16[1,256,256]{2,1,0:T(8,128)(2,1)S(1)} %shard_map.128.refs_0_), channel_id=1, source_target_pairs={{0,2},{2,0},{1,3},{3,1},{4,6},{6,4},{5,7},{7,5},{8,10},{10,8},{9,1... | collective-permute-start | bytes 393224 | tf_op jit(solution)/shard_map/ppermute | solution.py:97
  27.5 6.7 %collective-permute-start.5 = (bf16[272,256]{1,0:T(8,128)(2,1)S(1)}, bf16[272,256]{1,0:T(8,128)(2,1)S(1)}, u32[]{:S(2)}, u32[]{:S(2)}) collective-permute-start(bf16[272,256]{1,0:T(8,128)(2,1)S(1)} %get-tuple-element.47.refs_1_), channel_id=1, source_target_pairs={{0,4},{1,5},{4,0},{5,1},{8,12},{9,13},{12,8},{13,9},{2,6},{3,7},{6... | collective-permute-start | bytes 417800 | tf_op jit(solution)/shard_map/ppermute | solution.py:79
  27.5 6.7 %collective-permute-start.6 = (bf16[272,256]{1,0:T(8,128)(2,1)S(1)}, bf16[272,256]{1,0:T(8,128)(2,1)S(1)}, u32[]{:S(2)}, u32[]{:S(2)}) collective-permute-start(bf16[272,256]{1,0:T(8,128)(2,1)S(1)} %get-tuple-element.48.refs_2_), channel_id=1, source_target_pairs={{4,8},{5,9},{8,4},{9,5},{6,10},{7,11},{10,6},{11,7},{20,24},{21,25... | collective-permute-start | bytes 417800 | tf_op jit(solution)/shard_map/ppermute | solution.py:79
  31.2 3.4 %collective-permute-start.8 = (bf16[272,256]{1,0:T(8,128)(2,1)S(1)}, bf16[272,256]{1,0:T(8,128)(2,1)S(1)}, u32[]{:S(2)}, u32[]{:S(2)}) collective-permute-start(bf16[272,256]{1,0:T(8,128)(2,1)S(1)} %get-tuple-element.50), channel_id=1, source_target_pairs={{1,4},{4,1},{5,8},{8,5},{9,12},{12,9},{3,6},{6,3},{7,10},{10,7},{1... | collective-permute-start | bytes 417800 | tf_op jit(solution)/shard_map/ppermute | solution.py:79
  32.5 2.7 %collective-permute-start.10 = (bf16[272,256]{1,0:T(8,128)(2,1)S(1)}, bf16[272,256]{1,0:T(8,128)(2,1)S(1)}, u32[]{:S(2)}, u32[]{:S(2)}) collective-permute-start(bf16[272,256]{1,0:T(8,128)(2,1)S(1)} %shard_map.129), channel_id=1, source_target_pairs={{0,1},{1,0},{4,5},{5,4},{8,9},{9,8},{12,13},{13,12},{2,3},{3,2},{6... | collective-permute-start | bytes 417800 | tf_op jit(solution)/shard_map/ppermute | solution.py:79
  35.6 13.6 %collective-permute-start.11 = (bf16[640,256]{1,0:T(8,128)(2,1)S(1)}, bf16[640,256]{1,0:T(8,128)(2,1)S(1)}, u32[]{:S(2)}, u32[]{:S(2)}) collective-permute-start(bf16[640,256]{1,0:T(8,128)(2,1)S(1)} %shard_map.130.refs_0_.state_ref), channel_id=1, source_target_pairs={{0,2},{2,0},{1,3},{3,1},{4,6},{6,4},{5,7},{7,5},{8,10},{10,8},{9,1... | collective-permute-start | bytes 983048 | tf_op jit(solution)/shard_map/ppermute | solution.py:97
  37.3 6.0 %collective-permute-start.12 = (bf16[144,256]{1,0:T(8,128)(2,1)S(1)}, bf16[144,256]{1,0:T(8,128)(2,1)S(1)}, u32[]{:S(2)}, u32[]{:S(2)}) collective-permute-start(bf16[144,256]{1,0:T(8,128)(2,1)S(1)} %get-tuple-element.55), channel_id=1, source_target_pairs={{1,8},{5,12},{8,1},{12,5},{3,10},{7,14},{10,3},{14,7},{17,24},{21,... | collective-permute-start | bytes 221192 | tf_op jit(solution)/shard_map/ppermute | solution.py:79
  38.0 5.3 %collective-permute-start.13 = (bf16[2,64,256]{2,1,0:T(8,128)(2,1)S(1)}, bf16[2,64,256]{2,1,0:T(8,128)(2,1)S(1)}, u32[]{:S(2)}, u32[]{:S(2)}) collective-permute-start(bf16[2,64,256]{2,1,0:T(8,128)(2,1)S(1)} %get-tuple-element.57), channel_id=1, source_target_pairs={{0,4},{1,5},{4,0},{5,1},{8,12},{9,13},{12,8},{13,9},{2,6},{3,7},{6... | collective-permute-start | bytes 196616 | tf_op jit(solution)/shard_map/ppermute | solution.py:79
  41.0 2.2 %collective-permute-start.14 = (bf16[2,64,256]{2,1,0:T(8,128)(2,1)S(1)}, bf16[2,64,256]{2,1,0:T(8,128)(2,1)S(1)}, u32[]{:S(2)}, u32[]{:S(2)}) collective-permute-start(bf16[2,64,256]{2,1,0:T(8,128)(2,1)S(1)} %get-tuple-element.58), channel_id=1, source_target_pairs={{4,8},{5,9},{8,4},{9,5},{6,10},{7,11},{10,6},{11,7},{20,24},{21,25... | collective-permute-start | bytes 196616 | tf_op jit(solution)/shard_map/ppermute | solution.py:79
  43.3 4.7 %collective-permute-start.16 = (bf16[192,256]{1,0:T(8,128)(2,1)S(1)}, bf16[192,256]{1,0:T(8,128)(2,1)S(1)}, u32[]{:S(2)}, u32[]{:S(2)}) collective-permute-start(bf16[192,256]{1,0:T(8,128)(2,1)S(1)} %get-tuple-element.60), channel_id=1, source_target_pairs={{0,1},{1,0},{4,5},{5,4},{8,9},{9,8},{12,13},{13,12},{2,3},{3,2},{6... | collective-permute-start | bytes 294920 | tf_op jit(solution)/shard_map/ppermute | solution.py:79
  47.1 6.1 %collective-permute-start.15 = (bf16[192,256]{1,0:T(8,128)(2,1)S(1)}, bf16[192,256]{1,0:T(8,128)(2,1)S(1)}, u32[]{:S(2)}, u32[]{:S(2)}) collective-permute-start(bf16[192,256]{1,0:T(8,128)(2,1)S(1)} %get-tuple-element.59.refs_0_), channel_id=1, source_target_pairs={{0,2},{2,0},{1,3},{3,1},{4,6},{6,4},{5,7},{7,5},{8,10},{10,8},{9,1... | collective-permute-start | bytes 294920 | tf_op jit(solution)/shard_map/ppermute | solution.py:97
  48.0 5.9 %collective-permute-start.17 = (bf16[192,256]{1,0:T(8,128)(2,1)S(1)}, bf16[192,256]{1,0:T(8,128)(2,1)S(1)}, u32[]{:S(2)}, u32[]{:S(2)}) collective-permute-start(bf16[192,256]{1,0:T(8,128)(2,1)S(1)} %collective-permute-done.16.refs_2_), channel_id=1, source_target_pairs={{0,2},{2,0},{1,3},{3,1},{4,6},{6,4},{5,7},{7,5},{8,10},{10,8},{9,1... | collective-permute-start | bytes 294920 | tf_op jit(solution)/shard_map/ppermute | solution.py:97
  58.2 13.7 %collective-permute-start.18 = (bf16[640,256]{1,0:T(8,128)(2,1)S(1)}, bf16[640,256]{1,0:T(8,128)(2,1)S(1)}, u32[]{:S(2)}, u32[]{:S(2)}) collective-permute-start(bf16[640,256]{1,0:T(8,128)(2,1)S(1)} %shard_map.135.refs_0_.state_ref), channel_id=1, source_target_pairs={{0,2},{2,0},{1,3},{3,1},{4,6},{6,4},{5,7},{7,5},{8,10},{10,8},{9,1... | collective-permute-start | bytes 983048 | tf_op jit(solution)/shard_map/ppermute | solution.py:97
  59.6 6.6 %collective-permute-start.19 = (bf16[144,256]{1,0:T(8,128)(2,1)S(1)}, bf16[144,256]{1,0:T(8,128)(2,1)S(1)}, u32[]{:S(2)}, u32[]{:S(2)}) collective-permute-start(bf16[144,256]{1,0:T(8,128)(2,1)S(1)} %get-tuple-element.61), channel_id=1, source_target_pairs={{1,8},{5,12},{8,1},{12,5},{3,10},{7,14},{10,3},{14,7},{17,24},{21,... | collective-permute-start | bytes 221192 | tf_op jit(solution)/shard_map/ppermute | solution.py:79
  60.3 5.9 %collective-permute-start.20 = (bf16[2,64,256]{2,1,0:T(8,128)(2,1)S(1)}, bf16[2,64,256]{2,1,0:T(8,128)(2,1)S(1)}, u32[]{:S(2)}, u32[]{:S(2)}) collective-permute-start(bf16[2,64,256]{2,1,0:T(8,128)(2,1)S(1)} %get-tuple-element.63), channel_id=1, source_target_pairs={{0,4},{1,5},{4,0},{5,1},{8,12},{9,13},{12,8},{13,9},{2,6},{3,7},{6... | collective-permute-start | bytes 196616 | tf_op jit(solution)/shard_map/ppermute | solution.py:79
  63.9 2.2 %collective-permute-start.21 = (bf16[2,64,256]{2,1,0:T(8,128)(2,1)S(1)}, bf16[2,64,256]{2,1,0:T(8,128)(2,1)S(1)}, u32[]{:S(2)}, u32[]{:S(2)}) collective-permute-start(bf16[2,64,256]{2,1,0:T(8,128)(2,1)S(1)} %get-tuple-element.64), channel_id=1, source_target_pairs={{4,8},{5,9},{8,4},{9,5},{6,10},{7,11},{10,6},{11,7},{20,24},{21,25... | collective-permute-start | bytes 196616 | tf_op jit(solution)/shard_map/ppermute | solution.py:79
  66.2 4.7 %collective-permute-start.23 = (bf16[192,256]{1,0:T(8,128)(2,1)S(1)}, bf16[192,256]{1,0:T(8,128)(2,1)S(1)}, u32[]{:S(2)}, u32[]{:S(2)}) collective-permute-start(bf16[192,256]{1,0:T(8,128)(2,1)S(1)} %get-tuple-element.66), channel_id=1, source_target_pairs={{0,1},{1,0},{4,5},{5,4},{8,9},{9,8},{12,13},{13,12},{2,3},{3,2},{6... | collective-permute-start | bytes 294920 | tf_op jit(solution)/shard_map/ppermute | solution.py:79
  69.9 6.1 %collective-permute-start.22 = (bf16[192,256]{1,0:T(8,128)(2,1)S(1)}, bf16[192,256]{1,0:T(8,128)(2,1)S(1)}, u32[]{:S(2)}, u32[]{:S(2)}) collective-permute-start(bf16[192,256]{1,0:T(8,128)(2,1)S(1)} %get-tuple-element.65.refs_0_), channel_id=1, source_target_pairs={{0,2},{2,0},{1,3},{3,1},{4,6},{6,4},{5,7},{7,5},{8,10},{10,8},{9,1... | collective-permute-start | bytes 294920 | tf_op jit(solution)/shard_map/ppermute | solution.py:97
  70.9 5.9 %collective-permute-start.24 = (bf16[192,256]{1,0:T(8,128)(2,1)S(1)}, bf16[192,256]{1,0:T(8,128)(2,1)S(1)}, u32[]{:S(2)}, u32[]{:S(2)}) collective-permute-start(bf16[192,256]{1,0:T(8,128)(2,1)S(1)} %collective-permute-done.23.refs_2_), channel_id=1, source_target_pairs={{0,2},{2,0},{1,3},{3,1},{4,6},{6,4},{5,7},{7,5},{8,10},{10,8},{9,1... | collective-permute-start | bytes 294920 | tf_op jit(solution)/shard_map/ppermute | solution.py:97

commit v8 on v7

--- a/solution.py
+++ b/solution.py
@@ -230,25 +230,17 @@
 
 
 def fetch_kernel(after_ref, *refs):
-    count = (len(refs) - 3) // 2
-    sources, copied, (source_col_ref, target_col_ref, sems) = (
-        refs[:count],
-        refs[count : 2 * count],
-        refs[2 * count :],
-    )
+    count = (len(refs) - 1) // 2
+    sources, copied, sems = (refs[:count], refs[count : 2 * count], refs[-1])
     copies = [pltpu.make_async_copy(sources[k], copied[k], sems.at[k]) for k in range(count)]
     for copy in copies:
         copy.start()
-    for copy, row_ref, out_ref in zip(copies, copied, (source_col_ref, target_col_ref)):
-        copy.wait()
-        out_ref[...] = column(row_ref[...]).astype(jnp.int16)
-    for copy in copies[2:]:
+    for copy in copies:
         copy.wait()
 
 
 def fetch(after, *arrays):
     outputs = [shape(a.shape, a.dtype) for a in arrays]
-    outputs += [shape((a.shape[1], 128), jnp.int16) for a in arrays[:2]]
     return pl.pallas_call(
         fetch_kernel,
         out_shape=[made_in_vmem(o) for o in outputs],
@@ -257,6 +249,19 @@
         scratch_shapes=[pltpu.SemaphoreType.DMA((len(arrays),))],
         compiler_params=pltpu.CompilerParams(vmem_limit_bytes=VMEM_BYTES),
     )(taken_from_vmem(after), *[taken_from_hbm(a) for a in arrays])
+
+
+def columns_kernel(*refs):
+    half = len(refs) // 2
+    for row_ref, out_ref in zip(refs[:half], refs[half:]):
+        out_ref[...] = column(row_ref[...]).astype(jnp.int16)
+
+
+def columns(*rows):
+    count = rows[0].shape[1]
+    return call(
+        columns_kernel, [shape((count, 128), jnp.int16)] * len(rows), rows, len(rows) * count * 128 * 8
+    )
 
 
 def encode_kernel(group, others, weight_ref, coef_ref, target_ref, *refs):
@@ -294,8 +299,8 @@
     )
 
 
-def gather_in_kernel(before_ref, *refs):
-    blocks, out_ref = (refs[:-1], refs[-1])
+def gather_in_kernel(count, before_ref, *refs):
+    blocks, out_ref = (refs[:count], refs[-1])
     nodes, channels = before_ref.shape
     capacity = blocks[0].shape[0] - PAD
     rows16 = row_iota(nodes)
@@ -311,13 +316,13 @@
     out_ref[...] = total.astype(out_ref.dtype)
 
 
-def gather_in(before, blocks, dtype):
+def gather_in(before, blocks, dtype, after=()):
     nodes, channels = before.shape
     slots = len(blocks) * blocks[0].shape[0]
     return call(
-        gather_in_kernel,
+        functools.partial(gather_in_kernel, len(blocks)),
         [shape((nodes, channels), dtype)],
-        [before, *blocks],
+        [before, *blocks, *after],
         2 * nodes * slots * channels,
     )[0]
 
@@ -521,13 +526,13 @@
     ]
     picked, g2m_src, grid_latent = first_pick(groups[:2], g2m_src, grid_latent)
     arrived = [from_others(rows, group[0]) for group, rows in zip(groups, picked)]
-    m2m_src, m2m_dst, m2m_coef, enc_weight, g2m_coef, g2m_dst, mesh_latent, halo_send, src_weights, dst_weights, *cols = (
+    m2m_src, m2m_dst, m2m_coef, enc_weight, g2m_coef, g2m_dst, mesh_latent, halo_send, src_weights, dst_weights = (
         fetch(
             g2m_src, m2m_src, m2m_dst, m2m_coef, enc_weight, g2m_coef, g2m_dst, mesh_latent, halo_send,
             src_weights, dst_weights,
         )
     )
-    source_col, target_col = cols
+    source_col, target_col = cols = columns(m2m_src, m2m_dst)
 
     def pick_next(place, after):
         picked.extend(pick(groups[place : place + 1], g2m_src, grid_latent, after))
@@ -536,18 +541,19 @@
     def encode_group(place, after=()):
         return encode(groups[place], picked[place], arrived[place], enc_weight, g2m_coef, g2m_dst, after)
 
-    pick_next(2, [*arrived[0], source_col])
-    pick_next(3, arrived[1])
+    pick_next(2, [*arrived[0], enc_weight])
     encoded = encode_group(0) + encode_group(1)
+    pick_next(3, encoded)
     encoded += encode_group(2)
     blocks = [swapped(block, meets) for block, meets in zip(encoded, groups[0] + groups[1] + groups[2])]
-    state = gather_in(mesh_latent, blocks[:2], jnp.float32)
-    pick_next(4, [state, *encoded[2:]])
-    following, own = encode_group(3)
+    far_sum = gather_in(mesh_latent, blocks[:1], jnp.float32)
+    state = gather_in(far_sum, blocks[1:2], jnp.float32)
+    pick_next(4, [far_sum, *encoded[2:]])
+    following, own = encode_group(3, [state])
     (near,) = encode_group(4)
     blocks.append(swapped(following, meets_next))
     near = swapped(near, meets_core)
-    state = gather_in(state, blocks[2:4] + [own], jnp.float32)
+    state = gather_in(state, blocks[2:4] + [own], jnp.float32, cols)
     state = gather_in(state, [blocks[4], near], jnp.bfloat16)
     layers = src_weights.shape[0]
     for layer in range(layers):

time: 82.4 us -> 81 us (0.983)
  waiting for transfers between devices: 10.4 us -> 7.81 us
  starting transfers between devices: 43.2 us -> 44.1 us
    ppermute x14, waiting for transfers between devices: 5.83 us -> 3.71 us  [swapped(): return lax.ppermute(value, REGION, pairs(meets))]
    ppermute x11, starting transfers between devices: 13.2 us -> 15.2 us  [from_others(): lax.ppermute(value, axes, [(ring[i], ring[(i + k) % n]) for ring in rings...]
    pallas_call x21 -> x23, Pallas kernels: 22.9 us -> 24.5 us  [call(): pl.pallas_call(kernel, out_shape=shapes, in_specs=[pl.BlockSpec(memory_sp...]
    pallas_call x1, Pallas kernels: 2.94 us -> 1.58 us  [fetch(): pl.pallas_call(fetch_kernel, out_shape=[made_in_vmem(o) for o in outputs]...]
    ppermute x14, starting transfers between devices: 30 us -> 28.9 us  [swapped(): return lax.ppermute(value, REGION, pairs(meets))]
  transfers between devices with their start and end apart: 25 -> 25, of which waited for: 9 -> 6; matrix products, arithmetic and copies ran while one was open for 0% -> 0% of each run, Pallas kernels for 20% -> 21%
where the time goes in v8:
time: 81 us; the launch traced here: 80.3 us
  starting transfers between devices  44.1 us (54%)
  Pallas kernels  28.1 us (35%)
  waiting for transfers between devices  7.81 us (10%)
    ppermute x14, starting transfers between devices, swapped(): return lax.ppermute(value, REGION, pairs(meets))  28.9 us
    pallas_call x23, Pallas kernels, call(): pl.pallas_call(kernel, out_shape=shapes, in_specs=[pl.BlockSpec(memory_sp...  24.5 us
    ppermute x11, starting transfers between devices, from_others(): lax.ppermute(value, axes, [(ring[i], ring[(i + k) % n]) for ring in rings...  15.2 us
    ppermute x11, waiting for transfers between devices, from_others(): lax.ppermute(value, axes, [(ring[i], ring[(i + k) % n]) for ring in rings...  4.09 us
    ppermute x14, waiting for transfers between devices, swapped(): return lax.ppermute(value, REGION, pairs(meets))  3.71 us
    pallas_call x1, Pallas kernels, first_pick(): pl.pallas_call(functools.partial(first_pick_kernel, groups, parts), out_s...  2.01 us
  transfers between devices with their start and end apart: 25, of which 6 were waited for; matrix products, arithmetic and copies ran while one was open for 0% of the time, Pallas kernels for 21%

profile of v8, /device:TPU:0, one launch (start us, length us, event | category | flops | bytes accessed | tf_op | source)
XLA Modules:
  0.0 80.3 jit_solution(14600001278284088457)
XLA Ops:
  0.0 2.0 %shard_map.118 = (bf16[1,256,256]{2,1,0:T(8,128)(2,1)S(1)}, bf16[1,256,256]{2,1,0:T(8,128)(2,1)S(1)}, s32[7,1,256]{2,1,0:T(1,128)S(1)}, bf16[2048,256]{1,0:T(8,128)(2,1)S(1)}) custom-call(s32[7,1,256]{2,1,0:T(1,128)} %bitcast.4, bf16[2048,256]{1,0:T(8,128)(2,1)} %table_hbm.1), custom_call_target="tpu_custom_call" | custom-call | tf_op jit(solution)/shard_map/pallas_call | solution.py:221
  2.0 0.7 collective-permute-start
  2.7 4.8 %collective-permute-start.2 = (bf16[1,256,256]{2,1,0:T(8,128)(2,1)S(1)}, bf16[1,256,256]{2,1,0:T(8,128)(2,1)S(1)}, u32[]{:S(2)}, u32[]{:S(2)}) collective-permute-start(bf16[1,256,256]{2,1,0:T(8,128)(2,1)S(1)} %get-tuple-element.47.refs_0_), channel_id=1, source_target_pairs={{0,2},{2,0},{4,6},{6,4},{5,7},{7,5},{8,10},{10,8},{9,11},{11,9},{1... | collective-permute-start | bytes 393224 | tf_op jit(solution)/shard_map/ppermute | solution.py:97
  7.5 1.6 %shard_map.119 = (s32[1,5120]{1,0:T(1,128)S(1)}, s32[1,5120]{1,0:T(1,128)S(1)}, f32[1,5120]{1,0:T(1,128)S(1)}, bf16[512,256]{1,0:T(8,128)(2,1)S(1)}, f32[7,1,256...) custom-call(s32[7,1,256]{2,1,0:T(1,128)S(1)} %get-tuple-element.37.a, ...), custom_call_target="tpu_custom_call" | custom-call | tf_op jit(solution)/shard_map/pallas_call | solution.py:244
  9.1 0.8 shard_map.125.refs_0_
  10.0 0.3 shard_map.121.refs_0_
  10.3 0.7 collective-permute-start.1
  11.2 0.8 shard_map.127.refs_0_
  12.0 2.1 %collective-permute-start.7 = (bf16[2,256,256]{2,1,0:T(8,128)(2,1)S(1)}, bf16[2,256,256]{2,1,0:T(8,128)(2,1)S(1)}, u32[]{:S(2)}, u32[]{:S(2)}) collective-permute-start(bf16[2,256,256]{2,1,0:T(8,128)(2,1)S(1)} %shard_map.127.refs_0_), channel_id=1, source_target_pairs={{0,2},{2,0},{1,3},{3,1},{4,6},{6,4},{5,7},{7,5},{8,10},{10,8},{9,1... | collective-permute-start | bytes 786440 | tf_op jit(solution)/shard_map/ppermute | solution.py:97
  14.0 8.9 %collective-permute-start.3 = (bf16[272,256]{1,0:T(8,128)(2,1)S(1)}, bf16[272,256]{1,0:T(8,128)(2,1)S(1)}, u32[]{:S(2)}, u32[]{:S(2)}) collective-permute-start(bf16[272,256]{1,0:T(8,128)(2,1)S(1)} %shard_map.123.refs_1_), channel_id=1, source_target_pairs={{0,5},{4,9},{5,0},{8,13},{9,4},{13,8},{2,7},{6,11},{7,2},{10,15},{... | collective-permute-start | bytes 417800 | tf_op jit(solution)/shard_map/ppermute | solution.py:79
  23.2 0.4 shard_map.126
  23.6 0.5 shard_map.130.refs_0_
  24.1 1.6 %collective-permute-start.9 = (bf16[1,256,256]{2,1,0:T(8,128)(2,1)S(1)}, bf16[1,256,256]{2,1,0:T(8,128)(2,1)S(1)}, u32[]{:S(2)}, u32[]{:S(2)}) collective-permute-start(bf16[1,256,256]{2,1,0:T(8,128)(2,1)S(1)} %shard_map.130.refs_0_), channel_id=1, source_target_pairs={{0,2},{2,0},{1,3},{3,1},{4,6},{6,4},{5,7},{7,5},{8,10},{10,8},{9,1... | collective-permute-start | bytes 393224 | tf_op jit(solution)/shard_map/ppermute | solution.py:97
  25.6 0.7 collective-permute-start.6
  26.6 0.4 shard_map.128
  27.0 0.7 collective-permute-start.8
  27.6 2.5 %collective-permute-done.9.refs_1_ = bf16[1,256,256]{2,1,0:T(8,128)(2,1)S(1)} collective-permute-done((bf16[1,256,256]{2,1,0:T(8,128)(2,1)S(1)}, bf16[1,256,256]{2,1,0:T(8,128)(2,1)S(1)}, u32[]{:S(2)}, u32[]{:S(2)}) %collective-permute-start.9) | collective-permute-done | bytes 131104 | tf_op jit(solution)/shard_map/ppermute | solution.py:97
  30.4 3.7 %collective-permute-start.10 = (bf16[272,256]{1,0:T(8,128)(2,1)S(1)}, bf16[272,256]{1,0:T(8,128)(2,1)S(1)}, u32[]{:S(2)}, u32[]{:S(2)}) collective-permute-start(bf16[272,256]{1,0:T(8,128)(2,1)S(1)} %shard_map.131), channel_id=1, source_target_pairs={{0,1},{1,0},{4,5},{5,4},{8,9},{9,8},{12,13},{13,12},{2,3},{3,2},{6... | collective-permute-start | bytes 417800 | tf_op jit(solution)/shard_map/ppermute | solution.py:79
  34.1 1.4 %shard_map.120 = (s16[5120,128]{1,0:T(8,128)(2,1)S(1)}, s16[5120,128]{1,0:T(8,128)(2,1)S(1)}) custom-call(s32[1,5120]{1,0:T(1,128)S(1)} %get-tuple-element.38.refs_0_, s32[1,5120]{1,0:T(1,128)S(1)} %get-tuple-element.39.refs_1_.target_ref), custom_call_target="tpu_custom_call" | custom-call | flops 10485760 | bytes 2662400 | tf_op jit(solution)/shard_map/pallas_call | solution.py:30
  35.6 0.4 shard_map.129.before_ref
  36.0 0.3 shard_map.132.refs_0_.state_ref
  36.4 1.9 %collective-permute-start.11 = (bf16[640,256]{1,0:T(8,128)(2,1)S(1)}, bf16[640,256]{1,0:T(8,128)(2,1)S(1)}, u32[]{:S(2)}, u32[]{:S(2)}) collective-permute-start(bf16[640,256]{1,0:T(8,128)(2,1)S(1)} %shard_map.132.refs_0_.state_ref), channel_id=1, source_target_pairs={{0,2},{2,0},{1,3},{3,1},{4,6},{6,4},{5,7},{7,5},{8,10},{10,8},{9,1... | collective-permute-start | bytes 983048 | tf_op jit(solution)/shard_map/ppermute | solution.py:97
  38.2 0.5 shard_map.135
  38.7 0.7 collective-permute-start.12
  39.4 2.2 %collective-permute-start.13 = (bf16[2,64,256]{2,1,0:T(8,128)(2,1)S(1)}, bf16[2,64,256]{2,1,0:T(8,128)(2,1)S(1)}, u32[]{:S(2)}, u32[]{:S(2)}) collective-permute-start(bf16[2,64,256]{2,1,0:T(8,128)(2,1)S(1)} %get-tuple-element.59), channel_id=1, source_target_pairs={{0,4},{1,5},{4,0},{5,1},{8,12},{9,13},{12,8},{13,9},{2,6},{3,7},{6... | collective-permute-start | bytes 196616 | tf_op jit(solution)/shard_map/ppermute | solution.py:79
  41.6 0.8 %collective-permute-start.14 = (bf16[2,64,256]{2,1,0:T(8,128)(2,1)S(1)}, bf16[2,64,256]{2,1,0:T(8,128)(2,1)S(1)}, u32[]{:S(2)}, u32[]{:S(2)}) collective-permute-start(bf16[2,64,256]{2,1,0:T(8,128)(2,1)S(1)} %get-tuple-element.60), channel_id=1, source_target_pairs={{4,8},{5,9},{8,4},{9,5},{6,10},{7,11},{10,6},{11,7},{20,24},{21,25... | collective-permute-start | bytes 196616 | tf_op jit(solution)/shard_map/ppermute | solution.py:79
  42.4 1.6 %collective-permute-done.13.one_ref = bf16[2,64,256]{2,1,0:T(8,128)(2,1)S(1)} collective-permute-done((bf16[2,64,256]{2,1,0:T(8,128)(2,1)S(1)}, bf16[2,64,256]{2,1,0:T(8,128)(2,1)S(1)}, u32[]{:S(2)}, u32[]{:S(2)}) %collective-permute-start.13) | collective-permute-done | bytes 65568 | tf_op jit(solution)/shard_map/ppermute | solution.py:79
  44.1 2.6 %collective-permute-start.16 = (bf16[192,256]{1,0:T(8,128)(2,1)S(1)}, bf16[192,256]{1,0:T(8,128)(2,1)S(1)}, u32[]{:S(2)}, u32[]{:S(2)}) collective-permute-start(bf16[192,256]{1,0:T(8,128)(2,1)S(1)} %get-tuple-element.62), channel_id=1, source_target_pairs={{0,1},{1,0},{4,5},{5,4},{8,9},{9,8},{12,13},{13,12},{2,3},{3,2},{6... | collective-permute-start | bytes 294920 | tf_op jit(solution)/shard_map/ppermute | solution.py:79
  46.7 0.5 collective-permute-start.15
  47.1 0.5 collective-permute-done.16.refs_2_
  47.6 1.1 %collective-permute-start.17 = (bf16[192,256]{1,0:T(8,128)(2,1)S(1)}, bf16[192,256]{1,0:T(8,128)(2,1)S(1)}, u32[]{:S(2)}, u32[]{:S(2)}) collective-permute-start(bf16[192,256]{1,0:T(8,128)(2,1)S(1)} %collective-permute-done.16.refs_2_), channel_id=1, source_target_pairs={{0,2},{2,0},{1,3},{3,1},{4,6},{6,4},{5,7},{7,5},{8,10},{10,8},{9,1... | collective-permute-start | bytes 294920 | tf_op jit(solution)/shard_map/ppermute | solution.py:97
  48.7 0.5 shard_map.133.table_ref
  49.2 3.5 %shard_map.134.first_ref = f32[5120,256]{1,0:T(8,128)S(1)} custom-call(s16[5120,128]{1,0:T(8,128)(2,1)S(1)} %get-tuple-element.40.refs_3_.source_ref, s16[5120,128]{1,0:T(8,128)(2,1)S(1)} %get-tuple-element.52.refs_4_.target_ref, bf16[1280,256]{1,0:T(8,128)(2,1)S(1)} %shard_map.133.table_ref), custom_call_target="tpu_custom_call" | custom-call | flops 3355443200 | bytes 8519680 | tf_op jit(solution)/shard_map/pallas_call | solution.py:30
  52.8 0.8 collective-permute-done.17.refs_3_
  53.6 4.2 %shard_map.137.refs_0_.state_ref = bf16[640,256]{1,0:T(8,128)(2,1)S(1)} custom-call(s16[5120,128]{1,0:T(8,128)(2,1)S(1)} %get-tuple-element.40.refs_3_.source_ref, s32[1,5120]{1,0:T(1,128)S(1)} %get-tuple-element.39.refs_1_.target_ref, f32[1,5120]{1,0:T(1,128)S(1)} %get-tuple-element.41.coef_ref, bf16[640,256]{1,0:T(8,128)(2,1)S(1)} %shard_map.132.refs_0_.state_ref, ...), custom_call_target="tpu_custom_call" | custom-call | flops 2684354560 | bytes 8167424 | tf_op jit(solution)/shard_map/pallas_call | solution.py:30
  57.8 0.5 collective-permute-start.18
  58.3 0.5 shard_map.140
  58.8 0.7 collective-permute-start.19
  59.5 2.8 %collective-permute-start.20 = (bf16[2,64,256]{2,1,0:T(8,128)(2,1)S(1)}, bf16[2,64,256]{2,1,0:T(8,128)(2,1)S(1)}, u32[]{:S(2)}, u32[]{:S(2)}) collective-permute-start(bf16[2,64,256]{2,1,0:T(8,128)(2,1)S(1)} %get-tuple-element.65), channel_id=1, source_target_pairs={{0,4},{1,5},{4,0},{5,1},{8,12},{9,13},{12,8},{13,9},{2,6},{3,7},{6... | collective-permute-start | bytes 196616 | tf_op jit(solution)/shard_map/ppermute | solution.py:79
  62.3 0.7 collective-permute-start.21
  63.0 1.6 %collective-permute-done.20.one_ref = bf16[2,64,256]{2,1,0:T(8,128)(2,1)S(1)} collective-permute-done((bf16[2,64,256]{2,1,0:T(8,128)(2,1)S(1)}, bf16[2,64,256]{2,1,0:T(8,128)(2,1)S(1)}, u32[]{:S(2)}, u32[]{:S(2)}) %collective-permute-start.20) | collective-permute-done | bytes 65568 | tf_op jit(solution)/shard_map/ppermute | solution.py:79
  64.6 3.9 %collective-permute-start.23 = (bf16[192,256]{1,0:T(8,128)(2,1)S(1)}, bf16[192,256]{1,0:T(8,128)(2,1)S(1)}, u32[]{:S(2)}, u32[]{:S(2)}) collective-permute-start(bf16[192,256]{1,0:T(8,128)(2,1)S(1)} %get-tuple-element.68), channel_id=1, source_target_pairs={{0,1},{1,0},{4,5},{5,4},{8,9},{9,8},{12,13},{13,12},{2,3},{3,2},{6... | collective-permute-start | bytes 294920 | tf_op jit(solution)/shard_map/ppermute | solution.py:79
  68.4 1.0 %collective-permute-start.22 = (bf16[192,256]{1,0:T(8,128)(2,1)S(1)}, bf16[192,256]{1,0:T(8,128)(2,1)S(1)}, u32[]{:S(2)}, u32[]{:S(2)}) collective-permute-start(bf16[192,256]{1,0:T(8,128)(2,1)S(1)} %get-tuple-element.67.refs_0_), channel_id=1, source_target_pairs={{0,2},{2,0},{1,3},{3,1},{4,6},{6,4},{5,7},{7,5},{8,10},{10,8},{9,1... | collective-permute-start | bytes 294920 | tf_op jit(solution)/shard_map/ppermute | solution.py:97
  69.5 1.0 %collective-permute-start.24 = (bf16[192,256]{1,0:T(8,128)(2,1)S(1)}, bf16[192,256]{1,0:T(8,128)(2,1)S(1)}, u32[]{:S(2)}, u32[]{:S(2)}) collective-permute-start(bf16[192,256]{1,0:T(8,128)(2,1)S(1)} %collective-permute-done.23.refs_2_), channel_id=1, source_target_pairs={{0,2},{2,0},{1,3},{3,1},{4,6},{6,4},{5,7},{7,5},{8,10},{10,8},{9,1... | collective-permute-start | bytes 294920 | tf_op jit(solution)/shard_map/ppermute | solution.py:97
  70.5 0.5 shard_map.138.table_ref
  71.0 3.5 %shard_map.139.first_ref = f32[5120,256]{1,0:T(8,128)S(1)} custom-call(s16[5120,128]{1,0:T(8,128)(2,1)S(1)} %get-tuple-element.40.refs_3_.source_ref, s16[5120,128]{1,0:T(8,128)(2,1)S(1)} %get-tuple-element.52.refs_4_.target_ref, bf16[1280,256]{1,0:T(8,128)(2,1)S(1)} %shard_map.138.table_ref), custom_call_target="tpu_custom_call" | custom-call | flops 3355443200 | bytes 8519680 | tf_op jit(solution)/shard_map/pallas_call | solution.py:30
  74.5 0.8 collective-permute-done.24.refs_3_
  75.3 5.0 %shard_map.142 = bf16[640,256]{1,0:T(8,128)(2,1)} custom-call(s16[5120,128]{1,0:T(8,128)(2,1)S(1)} %get-tuple-element.40.refs_3_.source_ref, s32[1,5120]{1,0:T(1,128)S(1)} %get-tuple-element.39.refs_1_.target_ref, f32[1,5120]{1,0:T(1,128)S(1)} %get-tuple-element.41.coef_ref, bf16[640,256]{1,0:T(8,128)(2,1)S(1)} %shard_map.137.refs_0_.state_ref, ...), custom_call_target="tpu_custom_call" | custom-call | flops 2684354560 | bytes 8167424 | tf_op jit(solution)/shard_map/pallas_call | solution.py:30
  (27 shorter events, 1.1 us)
Async XLA Ops:
  2.0 7.1 %collective-permute-start = (bf16[1,256,256]{2,1,0:T(8,128)(2,1)S(1)}, bf16[1,256,256]{2,1,0:T(8,128)(2,1)S(1)}, u32[]{:S(2)}, u32[]{:S(2)}) collective-permute-start(bf16[1,256,256]{2,1,0:T(8,128)(2,1)S(1)} %get-tuple-element.46.refs_0_), channel_id=1, source_target_pairs={{1,3},{3,1},{5,7},{7,5},{8,10},{10,8},{12,14},{14,12},{17,19},{19,... | collective-permute-start | bytes 393224 | tf_op jit(solution)/shard_map/ppermute | solution.py:97
  2.7 8.3 %collective-permute-start.2 = (bf16[1,256,256]{2,1,0:T(8,128)(2,1)S(1)}, bf16[1,256,256]{2,1,0:T(8,128)(2,1)S(1)}, u32[]{:S(2)}, u32[]{:S(2)}) collective-permute-start(bf16[1,256,256]{2,1,0:T(8,128)(2,1)S(1)} %get-tuple-element.47.refs_0_), channel_id=1, source_target_pairs={{0,2},{2,0},{4,6},{6,4},{5,7},{7,5},{8,10},{10,8},{9,11},{11,9},{1... | collective-permute-start | bytes 393224 | tf_op jit(solution)/shard_map/ppermute | solution.py:97
  9.9 13.2 %collective-permute-start.4 = (bf16[2,256,256]{2,1,0:T(8,128)(2,1)S(1)}, bf16[2,256,256]{2,1,0:T(8,128)(2,1)S(1)}, u32[]{:S(2)}, u32[]{:S(2)}) collective-permute-start(bf16[2,256,256]{2,1,0:T(8,128)(2,1)S(1)} %shard_map.125.refs_0_), channel_id=1, source_target_pairs={{0,2},{2,0},{1,3},{3,1},{4,6},{6,4},{5,7},{7,5},{8,10},{10,8},{9,1... | collective-permute-start | bytes 786440 | tf_op jit(solution)/shard_map/ppermute | solution.py:97
  10.3 12.6 %collective-permute-start.1 = (bf16[272,256]{1,0:T(8,128)(2,1)S(1)}, bf16[272,256]{1,0:T(8,128)(2,1)S(1)}, u32[]{:S(2)}, u32[]{:S(2)}) collective-permute-start(bf16[272,256]{1,0:T(8,128)(2,1)S(1)} %shard_map.121.refs_0_), channel_id=1, source_target_pairs={{1,8},{5,12},{8,1},{12,5},{3,10},{7,14},{10,3},{14,7},{17,24},{21,... | collective-permute-start | bytes 417800 | tf_op jit(solution)/shard_map/ppermute | solution.py:79
  12.0 14.6 %collective-permute-start.7 = (bf16[2,256,256]{2,1,0:T(8,128)(2,1)S(1)}, bf16[2,256,256]{2,1,0:T(8,128)(2,1)S(1)}, u32[]{:S(2)}, u32[]{:S(2)}) collective-permute-start(bf16[2,256,256]{2,1,0:T(8,128)(2,1)S(1)} %shard_map.127.refs_0_), channel_id=1, source_target_pairs={{0,2},{2,0},{1,3},{3,1},{4,6},{6,4},{5,7},{7,5},{8,10},{10,8},{9,1... | collective-permute-start | bytes 786440 | tf_op jit(solution)/shard_map/ppermute | solution.py:97
  14.0 12.3 %collective-permute-start.3 = (bf16[272,256]{1,0:T(8,128)(2,1)S(1)}, bf16[272,256]{1,0:T(8,128)(2,1)S(1)}, u32[]{:S(2)}, u32[]{:S(2)}) collective-permute-start(bf16[272,256]{1,0:T(8,128)(2,1)S(1)} %shard_map.123.refs_1_), channel_id=1, source_target_pairs={{0,5},{4,9},{5,0},{8,13},{9,4},{13,8},{2,7},{6,11},{7,2},{10,15},{... | collective-permute-start | bytes 417800 | tf_op jit(solution)/shard_map/ppermute | solution.py:79
  24.1 6.1 %collective-permute-start.9 = (bf16[1,256,256]{2,1,0:T(8,128)(2,1)S(1)}, bf16[1,256,256]{2,1,0:T(8,128)(2,1)S(1)}, u32[]{:S(2)}, u32[]{:S(2)}) collective-permute-start(bf16[1,256,256]{2,1,0:T(8,128)(2,1)S(1)} %shard_map.130.refs_0_), channel_id=1, source_target_pairs={{0,2},{2,0},{1,3},{3,1},{4,6},{6,4},{5,7},{7,5},{8,10},{10,8},{9,1... | collective-permute-start | bytes 393224 | tf_op jit(solution)/shard_map/ppermute | solution.py:97
  25.6 9.9 %collective-permute-start.5 = (bf16[272,256]{1,0:T(8,128)(2,1)S(1)}, bf16[272,256]{1,0:T(8,128)(2,1)S(1)}, u32[]{:S(2)}, u32[]{:S(2)}) collective-permute-start(bf16[272,256]{1,0:T(8,128)(2,1)S(1)} %get-tuple-element.49.refs_1_), channel_id=1, source_target_pairs={{0,4},{1,5},{4,0},{5,1},{8,12},{9,13},{12,8},{13,9},{2,6},{3,7},{6... | collective-permute-start | bytes 417800 | tf_op jit(solution)/shard_map/ppermute | solution.py:79
  25.6 9.9 %collective-permute-start.6 = (bf16[272,256]{1,0:T(8,128)(2,1)S(1)}, bf16[272,256]{1,0:T(8,128)(2,1)S(1)}, u32[]{:S(2)}, u32[]{:S(2)}) collective-permute-start(bf16[272,256]{1,0:T(8,128)(2,1)S(1)} %get-tuple-element.50.refs_2_), channel_id=1, source_target_pairs={{4,8},{5,9},{8,4},{9,5},{6,10},{7,11},{10,6},{11,7},{20,24},{21,25... | collective-permute-start | bytes 417800 | tf_op jit(solution)/shard_map/ppermute | solution.py:79
  27.0 9.1 %collective-permute-start.8 = (bf16[272,256]{1,0:T(8,128)(2,1)S(1)}, bf16[272,256]{1,0:T(8,128)(2,1)S(1)}, u32[]{:S(2)}, u32[]{:S(2)}) collective-permute-start(bf16[272,256]{1,0:T(8,128)(2,1)S(1)} %get-tuple-element.53), channel_id=1, source_target_pairs={{1,4},{4,1},{5,8},{8,5},{9,12},{12,9},{3,6},{6,3},{7,10},{10,7},{1... | collective-permute-start | bytes 417800 | tf_op jit(solution)/shard_map/ppermute | solution.py:79
  30.4 5.6 %collective-permute-start.10 = (bf16[272,256]{1,0:T(8,128)(2,1)S(1)}, bf16[272,256]{1,0:T(8,128)(2,1)S(1)}, u32[]{:S(2)}, u32[]{:S(2)}) collective-permute-start(bf16[272,256]{1,0:T(8,128)(2,1)S(1)} %shard_map.131), channel_id=1, source_target_pairs={{0,1},{1,0},{4,5},{5,4},{8,9},{9,8},{12,13},{13,12},{2,3},{3,2},{6... | collective-permute-start | bytes 417800 | tf_op jit(solution)/shard_map/ppermute | solution.py:79
  36.4 12.3 %collective-permute-start.11 = (bf16[640,256]{1,0:T(8,128)(2,1)S(1)}, bf16[640,256]{1,0:T(8,128)(2,1)S(1)}, u32[]{:S(2)}, u32[]{:S(2)}) collective-permute-start(bf16[640,256]{1,0:T(8,128)(2,1)S(1)} %shard_map.132.refs_0_.state_ref), channel_id=1, source_target_pairs={{0,2},{2,0},{1,3},{3,1},{4,6},{6,4},{5,7},{7,5},{8,10},{10,8},{9,1... | collective-permute-start | bytes 983048 | tf_op jit(solution)/shard_map/ppermute | solution.py:97
  38.7 5.3 %collective-permute-start.12 = (bf16[144,256]{1,0:T(8,128)(2,1)S(1)}, bf16[144,256]{1,0:T(8,128)(2,1)S(1)}, u32[]{:S(2)}, u32[]{:S(2)}) collective-permute-start(bf16[144,256]{1,0:T(8,128)(2,1)S(1)} %get-tuple-element.57), channel_id=1, source_target_pairs={{1,8},{5,12},{8,1},{12,5},{3,10},{7,14},{10,3},{14,7},{17,24},{21,... | collective-permute-start | bytes 221192 | tf_op jit(solution)/shard_map/ppermute | solution.py:79
  39.4 4.6 %collective-permute-start.13 = (bf16[2,64,256]{2,1,0:T(8,128)(2,1)S(1)}, bf16[2,64,256]{2,1,0:T(8,128)(2,1)S(1)}, u32[]{:S(2)}, u32[]{:S(2)}) collective-permute-start(bf16[2,64,256]{2,1,0:T(8,128)(2,1)S(1)} %get-tuple-element.59), channel_id=1, source_target_pairs={{0,4},{1,5},{4,0},{5,1},{8,12},{9,13},{12,8},{13,9},{2,6},{3,7},{6... | collective-permute-start | bytes 196616 | tf_op jit(solution)/shard_map/ppermute | solution.py:79
  41.6 2.5 %collective-permute-start.14 = (bf16[2,64,256]{2,1,0:T(8,128)(2,1)S(1)}, bf16[2,64,256]{2,1,0:T(8,128)(2,1)S(1)}, u32[]{:S(2)}, u32[]{:S(2)}) collective-permute-start(bf16[2,64,256]{2,1,0:T(8,128)(2,1)S(1)} %get-tuple-element.60), channel_id=1, source_target_pairs={{4,8},{5,9},{8,4},{9,5},{6,10},{7,11},{10,6},{11,7},{20,24},{21,25... | collective-permute-start | bytes 196616 | tf_op jit(solution)/shard_map/ppermute | solution.py:79
  44.1 3.6 %collective-permute-start.16 = (bf16[192,256]{1,0:T(8,128)(2,1)S(1)}, bf16[192,256]{1,0:T(8,128)(2,1)S(1)}, u32[]{:S(2)}, u32[]{:S(2)}) collective-permute-start(bf16[192,256]{1,0:T(8,128)(2,1)S(1)} %get-tuple-element.62), channel_id=1, source_target_pairs={{0,1},{1,0},{4,5},{5,4},{8,9},{9,8},{12,13},{13,12},{2,3},{3,2},{6... | collective-permute-start | bytes 294920 | tf_op jit(solution)/shard_map/ppermute | solution.py:79
  46.7 6.1 %collective-permute-start.15 = (bf16[192,256]{1,0:T(8,128)(2,1)S(1)}, bf16[192,256]{1,0:T(8,128)(2,1)S(1)}, u32[]{:S(2)}, u32[]{:S(2)}) collective-permute-start(bf16[192,256]{1,0:T(8,128)(2,1)S(1)} %get-tuple-element.61.refs_0_), channel_id=1, source_target_pairs={{0,2},{2,0},{1,3},{3,1},{4,6},{6,4},{5,7},{7,5},{8,10},{10,8},{9,1... | collective-permute-start | bytes 294920 | tf_op jit(solution)/shard_map/ppermute | solution.py:97
  47.6 5.9 %collective-permute-start.17 = (bf16[192,256]{1,0:T(8,128)(2,1)S(1)}, bf16[192,256]{1,0:T(8,128)(2,1)S(1)}, u32[]{:S(2)}, u32[]{:S(2)}) collective-permute-start(bf16[192,256]{1,0:T(8,128)(2,1)S(1)} %collective-permute-done.16.refs_2_), channel_id=1, source_target_pairs={{0,2},{2,0},{1,3},{3,1},{4,6},{6,4},{5,7},{7,5},{8,10},{10,8},{9,1... | collective-permute-start | bytes 294920 | tf_op jit(solution)/shard_map/ppermute | solution.py:97
  57.8 12.7 %collective-permute-start.18 = (bf16[640,256]{1,0:T(8,128)(2,1)S(1)}, bf16[640,256]{1,0:T(8,128)(2,1)S(1)}, u32[]{:S(2)}, u32[]{:S(2)}) collective-permute-start(bf16[640,256]{1,0:T(8,128)(2,1)S(1)} %shard_map.137.refs_0_.state_ref), channel_id=1, source_target_pairs={{0,2},{2,0},{1,3},{3,1},{4,6},{6,4},{5,7},{7,5},{8,10},{10,8},{9,1... | collective-permute-start | bytes 983048 | tf_op jit(solution)/shard_map/ppermute | solution.py:97
  58.8 5.8 %collective-permute-start.19 = (bf16[144,256]{1,0:T(8,128)(2,1)S(1)}, bf16[144,256]{1,0:T(8,128)(2,1)S(1)}, u32[]{:S(2)}, u32[]{:S(2)}) collective-permute-start(bf16[144,256]{1,0:T(8,128)(2,1)S(1)} %get-tuple-element.63), channel_id=1, source_target_pairs={{1,8},{5,12},{8,1},{12,5},{3,10},{7,14},{10,3},{14,7},{17,24},{21,... | collective-permute-start | bytes 221192 | tf_op jit(solution)/shard_map/ppermute | solution.py:79
  59.5 5.1 %collective-permute-start.20 = (bf16[2,64,256]{2,1,0:T(8,128)(2,1)S(1)}, bf16[2,64,256]{2,1,0:T(8,128)(2,1)S(1)}, u32[]{:S(2)}, u32[]{:S(2)}) collective-permute-start(bf16[2,64,256]{2,1,0:T(8,128)(2,1)S(1)} %get-tuple-element.65), channel_id=1, source_target_pairs={{0,4},{1,5},{4,0},{5,1},{8,12},{9,13},{12,8},{13,9},{2,6},{3,7},{6... | collective-permute-start | bytes 196616 | tf_op jit(solution)/shard_map/ppermute | solution.py:79
  62.3 2.2 %collective-permute-start.21 = (bf16[2,64,256]{2,1,0:T(8,128)(2,1)S(1)}, bf16[2,64,256]{2,1,0:T(8,128)(2,1)S(1)}, u32[]{:S(2)}, u32[]{:S(2)}) collective-permute-start(bf16[2,64,256]{2,1,0:T(8,128)(2,1)S(1)} %get-tuple-element.66), channel_id=1, source_target_pairs={{4,8},{5,9},{8,4},{9,5},{6,10},{7,11},{10,6},{11,7},{20,24},{21,25... | collective-permute-start | bytes 196616 | tf_op jit(solution)/shard_map/ppermute | solution.py:79
  64.6 4.9 %collective-permute-start.23 = (bf16[192,256]{1,0:T(8,128)(2,1)S(1)}, bf16[192,256]{1,0:T(8,128)(2,1)S(1)}, u32[]{:S(2)}, u32[]{:S(2)}) collective-permute-start(bf16[192,256]{1,0:T(8,128)(2,1)S(1)} %get-tuple-element.68), channel_id=1, source_target_pairs={{0,1},{1,0},{4,5},{5,4},{8,9},{9,8},{12,13},{13,12},{2,3},{3,2},{6... | collective-permute-start | bytes 294920 | tf_op jit(solution)/shard_map/ppermute | solution.py:79
  68.4 6.1 %collective-permute-start.22 = (bf16[192,256]{1,0:T(8,128)(2,1)S(1)}, bf16[192,256]{1,0:T(8,128)(2,1)S(1)}, u32[]{:S(2)}, u32[]{:S(2)}) collective-permute-start(bf16[192,256]{1,0:T(8,128)(2,1)S(1)} %get-tuple-element.67.refs_0_), channel_id=1, source_target_pairs={{0,2},{2,0},{1,3},{3,1},{4,6},{6,4},{5,7},{7,5},{8,10},{10,8},{9,1... | collective-permute-start | bytes 294920 | tf_op jit(solution)/shard_map/ppermute | solution.py:97
  69.5 5.8 %collective-permute-start.24 = (bf16[192,256]{1,0:T(8,128)(2,1)S(1)}, bf16[192,256]{1,0:T(8,128)(2,1)S(1)}, u32[]{:S(2)}, u32[]{:S(2)}) collective-permute-start(bf16[192,256]{1,0:T(8,128)(2,1)S(1)} %collective-permute-done.23.refs_2_), channel_id=1, source_target_pairs={{0,2},{2,0},{1,3},{3,1},{4,6},{6,4},{5,7},{7,5},{8,10},{10,8},{9,1... | collective-permute-start | bytes 294920 | tf_op jit(solution)/shard_map/ppermute | solution.py:97

commit v9 on v8

--- a/solution.py
+++ b/solution.py
@@ -324,6 +324,20 @@
         [shape((nodes, channels), dtype)],
         [before, *blocks, *after],
         2 * nodes * slots * channels,
+    )[0]
+
+
+def sums_kernel(turn, target_ref, coef_ref, out_ref):
+    rows16 = row_iota(out_ref.shape[0])
+    for start in range(0, out_ref.shape[1], turn):
+        here = pl.ds(start, turn)
+        out_ref[:, here] = sum_mask(target_ref[:, here], rows16, coef_ref[:, here])
+
+
+def edge_sums(m2m_dst, m2m_coef, nodes):
+    edges = m2m_dst.shape[1]
+    return call(
+        functools.partial(sums_kernel, 512), [shape((nodes, edges))], [m2m_dst, m2m_coef], 4 * nodes * edges
     )[0]
 
 
@@ -368,7 +382,8 @@
     )
 
 
-def forward_kernel(distant_ref, near_ref, one_ref, two_ref, sent_ref, mine_ref):
+def forward_kernel(distant_ref, near_ref, one_ref, two_ref, *refs):
+    sent_ref, mine_ref = refs[-2:]
     width = near_ref.shape[0]
     core = lax.axis_index("edge")
     for k, part in enumerate((near_ref[...], one_ref[1 - core], two_ref[1 - core])):
@@ -377,12 +392,12 @@
         mine_ref[pl.ds(k * width, width), :] = part
 
 
-def exchange_listed(far, near, one, two):
+def exchange_listed(far, near, one, two, after):
     width, channels = near.shape
     distant = swapped(far, meets_other_three)
     one, two = swapped(one, meets_two), swapped(two, meets_other_two)
     half = shape((3 * width, channels))
-    sent, mine = call(forward_kernel, [half, half], [distant, near, one, two], 0)
+    sent, mine = call(forward_kernel, [half, half], [distant, near, one, two, *after], 0)
     across = swapped(sent, meets_core)
     return [mine, *from_others(mine)], [across, *from_others(across)]
 
@@ -456,7 +471,7 @@
 
 
 def message_kernel(
-    turn, turns, layer, source_ref, target_ref, coef_ref, state_ref, first_ref, weight_ref, *refs
+    turn, turns, layer, source_ref, sums_ref, state_ref, first_ref, weight_ref, *refs
 ):
     listed, (out_ref, message_ref) = (refs[:-2], refs[-2:])
     nodes, channels = state_ref.shape
@@ -465,7 +480,6 @@
         projected_rows(weight_ref.at[layer], listed[:half]), projected_rows(weight_ref.at[layer], listed[half:])
     )
     lanes = (lane_iota(table.shape[0]).astype(jnp.int32) + nodes).astype(jnp.int16)
-    rows16 = row_iota(nodes)
     total = state_ref[...].astype(jnp.float32)
     edges = source_ref.shape[0]
 
@@ -482,19 +496,18 @@
         done = start // turn + 1
         if done % turns == 0:
             here = pl.ds((done - turns) * turn, turns * turn)
-            mask = sum_mask(target_ref[:, here], rows16, coef_ref[:, here])
-            total += dot(mask, message_ref[here, :])
+            total += dot(sums_ref[:, here], message_ref[here, :])
     out_ref[...] = total.astype(jnp.bfloat16)
 
 
-def messages(layer, source_col, m2m_dst, m2m_coef, state, first, src_weights, listed, final):
+def messages(layer, source_col, sums, state, first, src_weights, listed, final):
     nodes, channels = state.shape
-    edges = m2m_dst.shape[1]
+    edges = source_col.shape[0]
     named = 2 * listed[0].shape[0]
     return call(
         functools.partial(message_kernel, 512, 5, layer),
         [shape((nodes, channels))],
-        [source_col, m2m_dst, m2m_coef, state, first, src_weights, *listed],
+        [source_col, sums, state, first, src_weights, *listed],
         2 * edges * (named + nodes) * channels,
         edges * channels,
         [pltpu.VMEM((edges, channels), jnp.bfloat16)],
@@ -555,14 +568,15 @@
     near = swapped(near, meets_core)
     state = gather_in(state, blocks[2:4] + [own], jnp.float32, cols)
     state = gather_in(state, [blocks[4], near], jnp.bfloat16)
+    sums = edge_sums(m2m_dst, m2m_coef, state.shape[0])
     layers = src_weights.shape[0]
     for layer in range(layers):
         others = from_others(state)
-        direct, across = exchange_listed(*list_rows(state, halo_send, reach))
+        direct, across = exchange_listed(*list_rows(state, halo_send, reach), [] if layer else [sums])
         table = project(layer, [state, *others], src_weights, dst_weights)
         first = first_part(source_col, target_col, table)
         state = messages(
-            layer, source_col, m2m_dst, m2m_coef, state, first, src_weights, direct + across, layer == layers - 1
+            layer, source_col, sums, state, first, src_weights, direct + across, layer == layers - 1
         )
     return state
 

time: 81 us -> 81 us (level)
  waiting for transfers between devices: 7.81 us -> 6.88 us
    ppermute x14, waiting for transfers between devices: 3.71 us -> 2.81 us  [swapped(): return lax.ppermute(value, REGION, pairs(meets))]
    pallas_call x23 -> x24, Pallas kernels: 24.5 us -> 25.2 us  [call(): pl.pallas_call(kernel, out_shape=shapes, in_specs=[pl.BlockSpec(memory_sp...]
where the time goes in v9:
time: 81 us; the launch traced here: 80.3 us
  starting transfers between devices  44.3 us (55%)
  Pallas kernels  28.7 us (35%)
  waiting for transfers between devices  6.88 us (8%)
    ppermute x14, starting transfers between devices, swapped(): return lax.ppermute(value, REGION, pairs(meets))  29.1 us
    pallas_call x24, Pallas kernels, call(): pl.pallas_call(kernel, out_shape=shapes, in_specs=[pl.BlockSpec(memory_sp...  25.2 us
    ppermute x11, starting transfers between devices, from_others(): lax.ppermute(value, axes, [(ring[i], ring[(i + k) % n]) for ring in rings...  15.2 us
    ppermute x11, waiting for transfers between devices, from_others(): lax.ppermute(value, axes, [(ring[i], ring[(i + k) % n]) for ring in rings...  4.07 us
    ppermute x14, waiting for transfers between devices, swapped(): return lax.ppermute(value, REGION, pairs(meets))  2.81 us
    pallas_call x1, Pallas kernels, first_pick(): pl.pallas_call(functools.partial(first_pick_kernel, groups, parts), out_s...  2.01 us
  transfers between devices with their start and end apart: 25, of which 6 were waited for; matrix products, arithmetic and copies ran while one was open for 0% of the time, Pallas kernels for 21%

profile of v9, /device:TPU:0, one launch (start us, length us, event | category | flops | bytes accessed | tf_op | source)
XLA Modules:
  0.0 80.3 jit_solution(17534694939125484681)
XLA Ops:
  0.0 2.0 %shard_map.118 = (bf16[1,256,256]{2,1,0:T(8,128)(2,1)S(1)}, bf16[1,256,256]{2,1,0:T(8,128)(2,1)S(1)}, s32[7,1,256]{2,1,0:T(1,128)S(1)}, bf16[2048,256]{1,0:T(8,128)(2,1)S(1)}) custom-call(s32[7,1,256]{2,1,0:T(1,128)} %bitcast.4, bf16[2048,256]{1,0:T(8,128)(2,1)} %table_hbm.1), custom_call_target="tpu_custom_call" | custom-call | tf_op jit(solution)/shard_map/pallas_call | solution.py:221
  2.0 0.7 collective-permute-start
  2.7 4.8 %collective-permute-start.2 = (bf16[1,256,256]{2,1,0:T(8,128)(2,1)S(1)}, bf16[1,256,256]{2,1,0:T(8,128)(2,1)S(1)}, u32[]{:S(2)}, u32[]{:S(2)}) collective-permute-start(bf16[1,256,256]{2,1,0:T(8,128)(2,1)S(1)} %get-tuple-element.47.refs_0_), channel_id=1, source_target_pairs={{0,2},{2,0},{4,6},{6,4},{5,7},{7,5},{8,10},{10,8},{9,11},{11,9},{1... | collective-permute-start | bytes 393224 | tf_op jit(solution)/shard_map/ppermute | solution.py:97
  7.5 1.6 %shard_map.119 = (s32[1,5120]{1,0:T(1,128)S(1)}, s32[1,5120]{1,0:T(1,128)S(1)}, f32[1,5120]{1,0:T(1,128)S(1)}, bf16[512,256]{1,0:T(8,128)(2,1)S(1)}, f32[7,1,256...) custom-call(s32[7,1,256]{2,1,0:T(1,128)S(1)} %get-tuple-element.37.a, ...), custom_call_target="tpu_custom_call" | custom-call | tf_op jit(solution)/shard_map/pallas_call | solution.py:244
  9.1 0.8 shard_map.126.refs_0_
  10.3 0.7 collective-permute-start.1
  11.2 0.8 shard_map.128.refs_0_
  12.0 2.1 %collective-permute-start.7 = (bf16[2,256,256]{2,1,0:T(8,128)(2,1)S(1)}, bf16[2,256,256]{2,1,0:T(8,128)(2,1)S(1)}, u32[]{:S(2)}, u32[]{:S(2)}) collective-permute-start(bf16[2,256,256]{2,1,0:T(8,128)(2,1)S(1)} %shard_map.128.refs_0_), channel_id=1, source_target_pairs={{0,2},{2,0},{1,3},{3,1},{4,6},{6,4},{5,7},{7,5},{8,10},{10,8},{9,1... | collective-permute-start | bytes 786440 | tf_op jit(solution)/shard_map/ppermute | solution.py:97
  14.0 8.9 %collective-permute-start.3 = (bf16[272,256]{1,0:T(8,128)(2,1)S(1)}, bf16[272,256]{1,0:T(8,128)(2,1)S(1)}, u32[]{:S(2)}, u32[]{:S(2)}) collective-permute-start(bf16[272,256]{1,0:T(8,128)(2,1)S(1)} %shard_map.124.refs_1_), channel_id=1, source_target_pairs={{0,5},{4,9},{5,0},{8,13},{9,4},{13,8},{2,7},{6,11},{7,2},{10,15},{... | collective-permute-start | bytes 417800 | tf_op jit(solution)/shard_map/ppermute | solution.py:79
  23.2 0.4 shard_map.127
  23.6 0.5 shard_map.131.refs_0_
  24.1 1.6 %collective-permute-start.9 = (bf16[1,256,256]{2,1,0:T(8,128)(2,1)S(1)}, bf16[1,256,256]{2,1,0:T(8,128)(2,1)S(1)}, u32[]{:S(2)}, u32[]{:S(2)}) collective-permute-start(bf16[1,256,256]{2,1,0:T(8,128)(2,1)S(1)} %shard_map.131.refs_0_), channel_id=1, source_target_pairs={{0,2},{2,0},{1,3},{3,1},{4,6},{6,4},{5,7},{7,5},{8,10},{10,8},{9,1... | collective-permute-start | bytes 393224 | tf_op jit(solution)/shard_map/ppermute | solution.py:97
  25.6 0.7 collective-permute-start.6
  26.6 0.4 shard_map.129
  27.0 0.7 collective-permute-start.8
  27.6 2.5 %collective-permute-done.9.refs_1_ = bf16[1,256,256]{2,1,0:T(8,128)(2,1)S(1)} collective-permute-done((bf16[1,256,256]{2,1,0:T(8,128)(2,1)S(1)}, bf16[1,256,256]{2,1,0:T(8,128)(2,1)S(1)}, u32[]{:S(2)}, u32[]{:S(2)}) %collective-permute-start.9) | collective-permute-done | bytes 131104 | tf_op jit(solution)/shard_map/ppermute | solution.py:97
  30.4 3.7 %collective-permute-start.10 = (bf16[272,256]{1,0:T(8,128)(2,1)S(1)}, bf16[272,256]{1,0:T(8,128)(2,1)S(1)}, u32[]{:S(2)}, u32[]{:S(2)}) collective-permute-start(bf16[272,256]{1,0:T(8,128)(2,1)S(1)} %shard_map.132), channel_id=1, source_target_pairs={{0,1},{1,0},{4,5},{5,4},{8,9},{9,8},{12,13},{13,12},{2,3},{3,2},{6... | collective-permute-start | bytes 417800 | tf_op jit(solution)/shard_map/ppermute | solution.py:79
  34.1 1.4 %shard_map.120 = (s16[5120,128]{1,0:T(8,128)(2,1)S(1)}, s16[5120,128]{1,0:T(8,128)(2,1)S(1)}) custom-call(s32[1,5120]{1,0:T(1,128)S(1)} %get-tuple-element.38.refs_0_, s32[1,5120]{1,0:T(1,128)S(1)} %get-tuple-element.39.refs_1_.target_ref), custom_call_target="tpu_custom_call" | custom-call | flops 10485760 | bytes 2662400 | tf_op jit(solution)/shard_map/pallas_call | solution.py:30
  35.6 0.4 shard_map.130.before_ref
  36.0 0.3 shard_map.133.refs_0_.state_ref
  36.4 1.9 %collective-permute-start.11 = (bf16[640,256]{1,0:T(8,128)(2,1)S(1)}, bf16[640,256]{1,0:T(8,128)(2,1)S(1)}, u32[]{:S(2)}, u32[]{:S(2)}) collective-permute-start(bf16[640,256]{1,0:T(8,128)(2,1)S(1)} %shard_map.133.refs_0_.state_ref), channel_id=1, source_target_pairs={{0,2},{2,0},{1,3},{3,1},{4,6},{6,4},{5,7},{7,5},{8,10},{10,8},{9,1... | collective-permute-start | bytes 983048 | tf_op jit(solution)/shard_map/ppermute | solution.py:97
  38.2 0.5 shard_map.136
  38.7 0.7 collective-permute-start.12
  39.4 2.2 %collective-permute-start.13 = (bf16[2,64,256]{2,1,0:T(8,128)(2,1)S(1)}, bf16[2,64,256]{2,1,0:T(8,128)(2,1)S(1)}, u32[]{:S(2)}, u32[]{:S(2)}) collective-permute-start(bf16[2,64,256]{2,1,0:T(8,128)(2,1)S(1)} %get-tuple-element.59), channel_id=1, source_target_pairs={{0,4},{1,5},{4,0},{5,1},{8,12},{9,13},{12,8},{13,9},{2,6},{3,7},{6... | collective-permute-start | bytes 196616 | tf_op jit(solution)/shard_map/ppermute | solution.py:79
  41.6 0.8 %collective-permute-start.14 = (bf16[2,64,256]{2,1,0:T(8,128)(2,1)S(1)}, bf16[2,64,256]{2,1,0:T(8,128)(2,1)S(1)}, u32[]{:S(2)}, u32[]{:S(2)}) collective-permute-start(bf16[2,64,256]{2,1,0:T(8,128)(2,1)S(1)} %get-tuple-element.60), channel_id=1, source_target_pairs={{4,8},{5,9},{8,4},{9,5},{6,10},{7,11},{10,6},{11,7},{20,24},{21,25... | collective-permute-start | bytes 196616 | tf_op jit(solution)/shard_map/ppermute | solution.py:79
  42.4 0.7 shard_map.121.refs_0_.sums_ref
  43.1 0.9 %collective-permute-done.13.one_ref = bf16[2,64,256]{2,1,0:T(8,128)(2,1)S(1)} collective-permute-done((bf16[2,64,256]{2,1,0:T(8,128)(2,1)S(1)}, bf16[2,64,256]{2,1,0:T(8,128)(2,1)S(1)}, u32[]{:S(2)}, u32[]{:S(2)}) %collective-permute-start.13) | collective-permute-done | bytes 65568 | tf_op jit(solution)/shard_map/ppermute | solution.py:79
  44.1 2.6 %collective-permute-start.16 = (bf16[192,256]{1,0:T(8,128)(2,1)S(1)}, bf16[192,256]{1,0:T(8,128)(2,1)S(1)}, u32[]{:S(2)}, u32[]{:S(2)}) collective-permute-start(bf16[192,256]{1,0:T(8,128)(2,1)S(1)} %get-tuple-element.62), channel_id=1, source_target_pairs={{0,1},{1,0},{4,5},{5,4},{8,9},{9,8},{12,13},{13,12},{2,3},{3,2},{6... | collective-permute-start | bytes 294920 | tf_op jit(solution)/shard_map/ppermute | solution.py:79
  46.7 0.5 collective-permute-start.15
  47.1 0.5 collective-permute-done.16.refs_2_
  47.6 1.1 %collective-permute-start.17 = (bf16[192,256]{1,0:T(8,128)(2,1)S(1)}, bf16[192,256]{1,0:T(8,128)(2,1)S(1)}, u32[]{:S(2)}, u32[]{:S(2)}) collective-permute-start(bf16[192,256]{1,0:T(8,128)(2,1)S(1)} %collective-permute-done.16.refs_2_), channel_id=1, source_target_pairs={{0,2},{2,0},{1,3},{3,1},{4,6},{6,4},{5,7},{7,5},{8,10},{10,8},{9,1... | collective-permute-start | bytes 294920 | tf_op jit(solution)/shard_map/ppermute | solution.py:97
  48.7 0.5 shard_map.134.table_ref
  49.2 3.6 %shard_map.135.first_ref = f32[5120,256]{1,0:T(8,128)S(1)} custom-call(s16[5120,128]{1,0:T(8,128)(2,1)S(1)} %get-tuple-element.40.refs_3_.source_ref, s16[5120,128]{1,0:T(8,128)(2,1)S(1)} %get-tuple-element.52.refs_4_.target_ref, bf16[1280,256]{1,0:T(8,128)(2,1)S(1)} %shard_map.134.table_ref), custom_call_target="tpu_custom_call" | custom-call | flops 3355443200 | bytes 8519680 | tf_op jit(solution)/shard_map/pallas_call | solution.py:30
  52.8 0.8 collective-permute-done.17.refs_3_
  53.6 4.3 %shard_map.138.refs_0_.state_ref = bf16[640,256]{1,0:T(8,128)(2,1)S(1)} custom-call(s16[5120,128]{1,0:T(8,128)(2,1)S(1)} %get-tuple-element.40.refs_3_.source_ref, bf16[640,5120]{1,0:T(8,128)(2,1)S(1)} %shard_map.121.refs_0_.sums_ref, bf16[640,256]{1,0:T(8,128)(2,1)S(1)} %shard_map.133.refs_0_.state_ref, f32[5120,256]{1,0:T(8,128)S(1)} %shard_map.135.first_ref, ...), custom_call_target="tpu_custom_call" | custom-call | flops 2684354560 | bytes 14680064 | tf_op jit(solution)/shard_map/pallas_call | solution.py:30
  57.8 0.5 collective-permute-start.18
  58.4 0.5 shard_map.141
  58.8 0.7 collective-permute-start.19
  59.5 2.8 %collective-permute-start.20 = (bf16[2,64,256]{2,1,0:T(8,128)(2,1)S(1)}, bf16[2,64,256]{2,1,0:T(8,128)(2,1)S(1)}, u32[]{:S(2)}, u32[]{:S(2)}) collective-permute-start(bf16[2,64,256]{2,1,0:T(8,128)(2,1)S(1)} %get-tuple-element.65), channel_id=1, source_target_pairs={{0,4},{1,5},{4,0},{5,1},{8,12},{9,13},{12,8},{13,9},{2,6},{3,7},{6... | collective-permute-start | bytes 196616 | tf_op jit(solution)/shard_map/ppermute | solution.py:79
  62.3 0.9 %collective-permute-start.21 = (bf16[2,64,256]{2,1,0:T(8,128)(2,1)S(1)}, bf16[2,64,256]{2,1,0:T(8,128)(2,1)S(1)}, u32[]{:S(2)}, u32[]{:S(2)}) collective-permute-start(bf16[2,64,256]{2,1,0:T(8,128)(2,1)S(1)} %get-tuple-element.66), channel_id=1, source_target_pairs={{4,8},{5,9},{8,4},{9,5},{6,10},{7,11},{10,6},{11,7},{20,24},{21,25... | collective-permute-start | bytes 196616 | tf_op jit(solution)/shard_map/ppermute | solution.py:79
  63.2 1.4 %collective-permute-done.20.one_ref = bf16[2,64,256]{2,1,0:T(8,128)(2,1)S(1)} collective-permute-done((bf16[2,64,256]{2,1,0:T(8,128)(2,1)S(1)}, bf16[2,64,256]{2,1,0:T(8,128)(2,1)S(1)}, u32[]{:S(2)}, u32[]{:S(2)}) %collective-permute-start.20) | collective-permute-done | bytes 65568 | tf_op jit(solution)/shard_map/ppermute | solution.py:79
  64.6 3.8 %collective-permute-start.23 = (bf16[192,256]{1,0:T(8,128)(2,1)S(1)}, bf16[192,256]{1,0:T(8,128)(2,1)S(1)}, u32[]{:S(2)}, u32[]{:S(2)}) collective-permute-start(bf16[192,256]{1,0:T(8,128)(2,1)S(1)} %get-tuple-element.68), channel_id=1, source_target_pairs={{0,1},{1,0},{4,5},{5,4},{8,9},{9,8},{12,13},{13,12},{2,3},{3,2},{6... | collective-permute-start | bytes 294920 | tf_op jit(solution)/shard_map/ppermute | solution.py:79
  68.4 1.0 %collective-permute-start.22 = (bf16[192,256]{1,0:T(8,128)(2,1)S(1)}, bf16[192,256]{1,0:T(8,128)(2,1)S(1)}, u32[]{:S(2)}, u32[]{:S(2)}) collective-permute-start(bf16[192,256]{1,0:T(8,128)(2,1)S(1)} %get-tuple-element.67.refs_0_), channel_id=1, source_target_pairs={{0,2},{2,0},{1,3},{3,1},{4,6},{6,4},{5,7},{7,5},{8,10},{10,8},{9,1... | collective-permute-start | bytes 294920 | tf_op jit(solution)/shard_map/ppermute | solution.py:97
  69.5 1.0 %collective-permute-start.24 = (bf16[192,256]{1,0:T(8,128)(2,1)S(1)}, bf16[192,256]{1,0:T(8,128)(2,1)S(1)}, u32[]{:S(2)}, u32[]{:S(2)}) collective-permute-start(bf16[192,256]{1,0:T(8,128)(2,1)S(1)} %collective-permute-done.23.refs_2_), channel_id=1, source_target_pairs={{0,2},{2,0},{1,3},{3,1},{4,6},{6,4},{5,7},{7,5},{8,10},{10,8},{9,1... | collective-permute-start | bytes 294920 | tf_op jit(solution)/shard_map/ppermute | solution.py:97
  70.5 0.5 shard_map.139.table_ref
  71.0 3.6 %shard_map.140.first_ref = f32[5120,256]{1,0:T(8,128)S(1)} custom-call(s16[5120,128]{1,0:T(8,128)(2,1)S(1)} %get-tuple-element.40.refs_3_.source_ref, s16[5120,128]{1,0:T(8,128)(2,1)S(1)} %get-tuple-element.52.refs_4_.target_ref, bf16[1280,256]{1,0:T(8,128)(2,1)S(1)} %shard_map.139.table_ref), custom_call_target="tpu_custom_call" | custom-call | flops 3355443200 | bytes 8519680 | tf_op jit(solution)/shard_map/pallas_call | solution.py:30
  74.6 0.8 collective-permute-done.24.refs_3_
  75.3 5.0 %shard_map.143 = bf16[640,256]{1,0:T(8,128)(2,1)} custom-call(s16[5120,128]{1,0:T(8,128)(2,1)S(1)} %get-tuple-element.40.refs_3_.source_ref, bf16[640,5120]{1,0:T(8,128)(2,1)S(1)} %shard_map.121.refs_0_.sums_ref, bf16[640,256]{1,0:T(8,128)(2,1)S(1)} %shard_map.138.refs_0_.state_ref, f32[5120,256]{1,0:T(8,128)S(1)} %shard_map.140.first_ref, ...), custom_call_target="tpu_custom_call" | custom-call | flops 2684354560 | bytes 14680064 | tf_op jit(solution)/shard_map/pallas_call | solution.py:30
  (28 shorter events, 1.4 us)
Async XLA Ops:
  2.0 7.1 %collective-permute-start = (bf16[1,256,256]{2,1,0:T(8,128)(2,1)S(1)}, bf16[1,256,256]{2,1,0:T(8,128)(2,1)S(1)}, u32[]{:S(2)}, u32[]{:S(2)}) collective-permute-start(bf16[1,256,256]{2,1,0:T(8,128)(2,1)S(1)} %get-tuple-element.46.refs_0_), channel_id=1, source_target_pairs={{1,3},{3,1},{5,7},{7,5},{8,10},{10,8},{12,14},{14,12},{17,19},{19,... | collective-permute-start | bytes 393224 | tf_op jit(solution)/shard_map/ppermute | solution.py:97
  2.7 8.3 %collective-permute-start.2 = (bf16[1,256,256]{2,1,0:T(8,128)(2,1)S(1)}, bf16[1,256,256]{2,1,0:T(8,128)(2,1)S(1)}, u32[]{:S(2)}, u32[]{:S(2)}) collective-permute-start(bf16[1,256,256]{2,1,0:T(8,128)(2,1)S(1)} %get-tuple-element.47.refs_0_), channel_id=1, source_target_pairs={{0,2},{2,0},{4,6},{6,4},{5,7},{7,5},{8,10},{10,8},{9,11},{11,9},{1... | collective-permute-start | bytes 393224 | tf_op jit(solution)/shard_map/ppermute | solution.py:97
  9.9 13.2 %collective-permute-start.4 = (bf16[2,256,256]{2,1,0:T(8,128)(2,1)S(1)}, bf16[2,256,256]{2,1,0:T(8,128)(2,1)S(1)}, u32[]{:S(2)}, u32[]{:S(2)}) collective-permute-start(bf16[2,256,256]{2,1,0:T(8,128)(2,1)S(1)} %shard_map.126.refs_0_), channel_id=1, source_target_pairs={{0,2},{2,0},{1,3},{3,1},{4,6},{6,4},{5,7},{7,5},{8,10},{10,8},{9,1... | collective-permute-start | bytes 786440 | tf_op jit(solution)/shard_map/ppermute | solution.py:97
  10.3 12.6 %collective-permute-start.1 = (bf16[272,256]{1,0:T(8,128)(2,1)S(1)}, bf16[272,256]{1,0:T(8,128)(2,1)S(1)}, u32[]{:S(2)}, u32[]{:S(2)}) collective-permute-start(bf16[272,256]{1,0:T(8,128)(2,1)S(1)} %shard_map.122.refs_0_), channel_id=1, source_target_pairs={{1,8},{5,12},{8,1},{12,5},{3,10},{7,14},{10,3},{14,7},{17,24},{21,... | collective-permute-start | bytes 417800 | tf_op jit(solution)/shard_map/ppermute | solution.py:79
  12.0 14.6 %collective-permute-start.7 = (bf16[2,256,256]{2,1,0:T(8,128)(2,1)S(1)}, bf16[2,256,256]{2,1,0:T(8,128)(2,1)S(1)}, u32[]{:S(2)}, u32[]{:S(2)}) collective-permute-start(bf16[2,256,256]{2,1,0:T(8,128)(2,1)S(1)} %shard_map.128.refs_0_), channel_id=1, source_target_pairs={{0,2},{2,0},{1,3},{3,1},{4,6},{6,4},{5,7},{7,5},{8,10},{10,8},{9,1... | collective-permute-start | bytes 786440 | tf_op jit(solution)/shard_map/ppermute | solution.py:97
  14.0 12.3 %collective-permute-start.3 = (bf16[272,256]{1,0:T(8,128)(2,1)S(1)}, bf16[272,256]{1,0:T(8,128)(2,1)S(1)}, u32[]{:S(2)}, u32[]{:S(2)}) collective-permute-start(bf16[272,256]{1,0:T(8,128)(2,1)S(1)} %shard_map.124.refs_1_), channel_id=1, source_target_pairs={{0,5},{4,9},{5,0},{8,13},{9,4},{13,8},{2,7},{6,11},{7,2},{10,15},{... | collective-permute-start | bytes 417800 | tf_op jit(solution)/shard_map/ppermute | solution.py:79
  24.1 6.1 %collective-permute-start.9 = (bf16[1,256,256]{2,1,0:T(8,128)(2,1)S(1)}, bf16[1,256,256]{2,1,0:T(8,128)(2,1)S(1)}, u32[]{:S(2)}, u32[]{:S(2)}) collective-permute-start(bf16[1,256,256]{2,1,0:T(8,128)(2,1)S(1)} %shard_map.131.refs_0_), channel_id=1, source_target_pairs={{0,2},{2,0},{1,3},{3,1},{4,6},{6,4},{5,7},{7,5},{8,10},{10,8},{9,1... | collective-permute-start | bytes 393224 | tf_op jit(solution)/shard_map/ppermute | solution.py:97
  25.6 9.9 %collective-permute-start.5 = (bf16[272,256]{1,0:T(8,128)(2,1)S(1)}, bf16[272,256]{1,0:T(8,128)(2,1)S(1)}, u32[]{:S(2)}, u32[]{:S(2)}) collective-permute-start(bf16[272,256]{1,0:T(8,128)(2,1)S(1)} %get-tuple-element.49.refs_1_), channel_id=1, source_target_pairs={{0,4},{1,5},{4,0},{5,1},{8,12},{9,13},{12,8},{13,9},{2,6},{3,7},{6... | collective-permute-start | bytes 417800 | tf_op jit(solution)/shard_map/ppermute | solution.py:79
  25.6 9.9 %collective-permute-start.6 = (bf16[272,256]{1,0:T(8,128)(2,1)S(1)}, bf16[272,256]{1,0:T(8,128)(2,1)S(1)}, u32[]{:S(2)}, u32[]{:S(2)}) collective-permute-start(bf16[272,256]{1,0:T(8,128)(2,1)S(1)} %get-tuple-element.50.refs_2_), channel_id=1, source_target_pairs={{4,8},{5,9},{8,4},{9,5},{6,10},{7,11},{10,6},{11,7},{20,24},{21,25... | collective-permute-start | bytes 417800 | tf_op jit(solution)/shard_map/ppermute | solution.py:79
  27.0 9.1 %collective-permute-start.8 = (bf16[272,256]{1,0:T(8,128)(2,1)S(1)}, bf16[272,256]{1,0:T(8,128)(2,1)S(1)}, u32[]{:S(2)}, u32[]{:S(2)}) collective-permute-start(bf16[272,256]{1,0:T(8,128)(2,1)S(1)} %get-tuple-element.53), channel_id=1, source_target_pairs={{1,4},{4,1},{5,8},{8,5},{9,12},{12,9},{3,6},{6,3},{7,10},{10,7},{1... | collective-permute-start | bytes 417800 | tf_op jit(solution)/shard_map/ppermute | solution.py:79
  30.4 5.6 %collective-permute-start.10 = (bf16[272,256]{1,0:T(8,128)(2,1)S(1)}, bf16[272,256]{1,0:T(8,128)(2,1)S(1)}, u32[]{:S(2)}, u32[]{:S(2)}) collective-permute-start(bf16[272,256]{1,0:T(8,128)(2,1)S(1)} %shard_map.132), channel_id=1, source_target_pairs={{0,1},{1,0},{4,5},{5,4},{8,9},{9,8},{12,13},{13,12},{2,3},{3,2},{6... | collective-permute-start | bytes 417800 | tf_op jit(solution)/shard_map/ppermute | solution.py:79
  36.4 12.3 %collective-permute-start.11 = (bf16[640,256]{1,0:T(8,128)(2,1)S(1)}, bf16[640,256]{1,0:T(8,128)(2,1)S(1)}, u32[]{:S(2)}, u32[]{:S(2)}) collective-permute-start(bf16[640,256]{1,0:T(8,128)(2,1)S(1)} %shard_map.133.refs_0_.state_ref), channel_id=1, source_target_pairs={{0,2},{2,0},{1,3},{3,1},{4,6},{6,4},{5,7},{7,5},{8,10},{10,8},{9,1... | collective-permute-start | bytes 983048 | tf_op jit(solution)/shard_map/ppermute | solution.py:97
  38.7 5.3 %collective-permute-start.12 = (bf16[144,256]{1,0:T(8,128)(2,1)S(1)}, bf16[144,256]{1,0:T(8,128)(2,1)S(1)}, u32[]{:S(2)}, u32[]{:S(2)}) collective-permute-start(bf16[144,256]{1,0:T(8,128)(2,1)S(1)} %get-tuple-element.57), channel_id=1, source_target_pairs={{1,8},{5,12},{8,1},{12,5},{3,10},{7,14},{10,3},{14,7},{17,24},{21,... | collective-permute-start | bytes 221192 | tf_op jit(solution)/shard_map/ppermute | solution.py:79
  39.4 4.6 %collective-permute-start.13 = (bf16[2,64,256]{2,1,0:T(8,128)(2,1)S(1)}, bf16[2,64,256]{2,1,0:T(8,128)(2,1)S(1)}, u32[]{:S(2)}, u32[]{:S(2)}) collective-permute-start(bf16[2,64,256]{2,1,0:T(8,128)(2,1)S(1)} %get-tuple-element.59), channel_id=1, source_target_pairs={{0,4},{1,5},{4,0},{5,1},{8,12},{9,13},{12,8},{13,9},{2,6},{3,7},{6... | collective-permute-start | bytes 196616 | tf_op jit(solution)/shard_map/ppermute | solution.py:79
  41.6 2.5 %collective-permute-start.14 = (bf16[2,64,256]{2,1,0:T(8,128)(2,1)S(1)}, bf16[2,64,256]{2,1,0:T(8,128)(2,1)S(1)}, u32[]{:S(2)}, u32[]{:S(2)}) collective-permute-start(bf16[2,64,256]{2,1,0:T(8,128)(2,1)S(1)} %get-tuple-element.60), channel_id=1, source_target_pairs={{4,8},{5,9},{8,4},{9,5},{6,10},{7,11},{10,6},{11,7},{20,24},{21,25... | collective-permute-start | bytes 196616 | tf_op jit(solution)/shard_map/ppermute | solution.py:79
  44.1 3.6 %collective-permute-start.16 = (bf16[192,256]{1,0:T(8,128)(2,1)S(1)}, bf16[192,256]{1,0:T(8,128)(2,1)S(1)}, u32[]{:S(2)}, u32[]{:S(2)}) collective-permute-start(bf16[192,256]{1,0:T(8,128)(2,1)S(1)} %get-tuple-element.62), channel_id=1, source_target_pairs={{0,1},{1,0},{4,5},{5,4},{8,9},{9,8},{12,13},{13,12},{2,3},{3,2},{6... | collective-permute-start | bytes 294920 | tf_op jit(solution)/shard_map/ppermute | solution.py:79
  46.7 6.1 %collective-permute-start.15 = (bf16[192,256]{1,0:T(8,128)(2,1)S(1)}, bf16[192,256]{1,0:T(8,128)(2,1)S(1)}, u32[]{:S(2)}, u32[]{:S(2)}) collective-permute-start(bf16[192,256]{1,0:T(8,128)(2,1)S(1)} %get-tuple-element.61.refs_0_), channel_id=1, source_target_pairs={{0,2},{2,0},{1,3},{3,1},{4,6},{6,4},{5,7},{7,5},{8,10},{10,8},{9,1... | collective-permute-start | bytes 294920 | tf_op jit(solution)/shard_map/ppermute | solution.py:97
  47.6 5.9 %collective-permute-start.17 = (bf16[192,256]{1,0:T(8,128)(2,1)S(1)}, bf16[192,256]{1,0:T(8,128)(2,1)S(1)}, u32[]{:S(2)}, u32[]{:S(2)}) collective-permute-start(bf16[192,256]{1,0:T(8,128)(2,1)S(1)} %collective-permute-done.16.refs_2_), channel_id=1, source_target_pairs={{0,2},{2,0},{1,3},{3,1},{4,6},{6,4},{5,7},{7,5},{8,10},{10,8},{9,1... | collective-permute-start | bytes 294920 | tf_op jit(solution)/shard_map/ppermute | solution.py:97
  57.8 12.7 %collective-permute-start.18 = (bf16[640,256]{1,0:T(8,128)(2,1)S(1)}, bf16[640,256]{1,0:T(8,128)(2,1)S(1)}, u32[]{:S(2)}, u32[]{:S(2)}) collective-permute-start(bf16[640,256]{1,0:T(8,128)(2,1)S(1)} %shard_map.138.refs_0_.state_ref), channel_id=1, source_target_pairs={{0,2},{2,0},{1,3},{3,1},{4,6},{6,4},{5,7},{7,5},{8,10},{10,8},{9,1... | collective-permute-start | bytes 983048 | tf_op jit(solution)/shard_map/ppermute | solution.py:97
  58.8 5.8 %collective-permute-start.19 = (bf16[144,256]{1,0:T(8,128)(2,1)S(1)}, bf16[144,256]{1,0:T(8,128)(2,1)S(1)}, u32[]{:S(2)}, u32[]{:S(2)}) collective-permute-start(bf16[144,256]{1,0:T(8,128)(2,1)S(1)} %get-tuple-element.63), channel_id=1, source_target_pairs={{1,8},{5,12},{8,1},{12,5},{3,10},{7,14},{10,3},{14,7},{17,24},{21,... | collective-permute-start | bytes 221192 | tf_op jit(solution)/shard_map/ppermute | solution.py:79
  59.5 5.1 %collective-permute-start.20 = (bf16[2,64,256]{2,1,0:T(8,128)(2,1)S(1)}, bf16[2,64,256]{2,1,0:T(8,128)(2,1)S(1)}, u32[]{:S(2)}, u32[]{:S(2)}) collective-permute-start(bf16[2,64,256]{2,1,0:T(8,128)(2,1)S(1)} %get-tuple-element.65), channel_id=1, source_target_pairs={{0,4},{1,5},{4,0},{5,1},{8,12},{9,13},{12,8},{13,9},{2,6},{3,7},{6... | collective-permute-start | bytes 196616 | tf_op jit(solution)/shard_map/ppermute | solution.py:79
  62.3 2.2 %collective-permute-start.21 = (bf16[2,64,256]{2,1,0:T(8,128)(2,1)S(1)}, bf16[2,64,256]{2,1,0:T(8,128)(2,1)S(1)}, u32[]{:S(2)}, u32[]{:S(2)}) collective-permute-start(bf16[2,64,256]{2,1,0:T(8,128)(2,1)S(1)} %get-tuple-element.66), channel_id=1, source_target_pairs={{4,8},{5,9},{8,4},{9,5},{6,10},{7,11},{10,6},{11,7},{20,24},{21,25... | collective-permute-start | bytes 196616 | tf_op jit(solution)/shard_map/ppermute | solution.py:79
  64.6 4.9 %collective-permute-start.23 = (bf16[192,256]{1,0:T(8,128)(2,1)S(1)}, bf16[192,256]{1,0:T(8,128)(2,1)S(1)}, u32[]{:S(2)}, u32[]{:S(2)}) collective-permute-start(bf16[192,256]{1,0:T(8,128)(2,1)S(1)} %get-tuple-element.68), channel_id=1, source_target_pairs={{0,1},{1,0},{4,5},{5,4},{8,9},{9,8},{12,13},{13,12},{2,3},{3,2},{6... | collective-permute-start | bytes 294920 | tf_op jit(solution)/shard_map/ppermute | solution.py:79
  68.4 6.1 %collective-permute-start.22 = (bf16[192,256]{1,0:T(8,128)(2,1)S(1)}, bf16[192,256]{1,0:T(8,128)(2,1)S(1)}, u32[]{:S(2)}, u32[]{:S(2)}) collective-permute-start(bf16[192,256]{1,0:T(8,128)(2,1)S(1)} %get-tuple-element.67.refs_0_), channel_id=1, source_target_pairs={{0,2},{2,0},{1,3},{3,1},{4,6},{6,4},{5,7},{7,5},{8,10},{10,8},{9,1... | collective-permute-start | bytes 294920 | tf_op jit(solution)/shard_map/ppermute | solution.py:97
  69.5 5.8 %collective-permute-start.24 = (bf16[192,256]{1,0:T(8,128)(2,1)S(1)}, bf16[192,256]{1,0:T(8,128)(2,1)S(1)}, u32[]{:S(2)}, u32[]{:S(2)}) collective-permute-start(bf16[192,256]{1,0:T(8,128)(2,1)S(1)} %collective-permute-done.23.refs_2_), channel_id=1, source_target_pairs={{0,2},{2,0},{1,3},{3,1},{4,6},{6,4},{5,7},{7,5},{8,10},{10,8},{9,1... | collective-permute-start | bytes 294920 | tf_op jit(solution)/shard_map/ppermute | solution.py:97
